TPU v7x, 32 devices: a whole 2x2x4 slice. The times are simulated.
32 devices in a mesh: section: 2 (over core), gx: 4 (over y, x), gy: 4 (over z).
Axes of the slice: x: 2, y: 2, z: 4, core: 2. Of those that a mesh axis runs over, the one named last changes fastest.
Arguments:
- block_input: bfloat16 [4, 512, 768], P(None, 'gx', 'gy'), may hold values from -6 to 6
- output_grad: bfloat16 [4, 512, 768], P(None, 'gx', 'gy'), may hold values from -6 to 6
- attention_gain: float32 [2, 768], P('section', 'gy'), may hold values from 0.1 to 1.9
- attention_in: bfloat16 [2, 768, 3, 768], P('section', 'gy', None, 'gx'), may hold values from -0.21875 to 0.21875
- attention_out: bfloat16 [2, 768, 768], P('section', 'gx', 'gy'), may hold values from -0.4375 to 0.4375
- feed_gain: float32 [2, 768], P('section', 'gy'), may hold values from 0.1 to 1.9
- router_weight: bfloat16 [2, 768, 16], P('section', 'gy'), may hold values from -0.21875 to 0.21875
- expert_in: bfloat16 [2, 16, 768, 2, 2048], P('section', None, 'gy', None, 'gx'), may hold values from -0.21875 to 0.21875
- expert_down: bfloat16 [2, 16, 2048, 768], P('section', None, 'gx', 'gy'), may hold values from -0.125 to 0.125
- shared_in: bfloat16 [2, 768, 2, 2048], P('section', 'gy', None, 'gx'), may hold values from -0.21875 to 0.21875
- shared_down: bfloat16 [2, 2048, 768], P('section', 'gx', 'gy'), may hold values from -0.125 to 0.125
- routes: int32 [2, 4, 512, 2], P('section'), may hold values from 0 to 15, all different within a row; in each aligned block of 512 rows (0 to 511, 512 to 1023, ..., all dimensions but the last counted through in order) at most 80 rows name the same one
Outputs:
- layer_outputs: bfloat16 [2, 4, 512, 768], P('section', None, 'gx', 'gy')
- input_grads: bfloat16 [2, 4, 512, 768], P('section', None, 'gx', 'gy')
- attention_gain_grad: float32 [2, 768], P('section', 'gy')
- attention_in_grad: float32 [2, 768, 3, 768], P('section', 'gy', None, 'gx')
- attention_out_grad: float32 [2, 768, 768], P('section', 'gx', 'gy')
- feed_gain_grad: float32 [2, 768], P('section', 'gy')
- router_weight_grad: float32 [2, 768, 16], P('section', 'gy')
- expert_in_grad: float32 [2, 16, 768, 2, 2048], P('section', None, 'gy', None, 'gx')
- expert_down_grad: float32 [2, 16, 2048, 768], P('section', None, 'gx', 'gy')
- shared_in_grad: float32 [2, 768, 2, 2048], P('section', 'gy', None, 'gx')
- shared_down_grad: float32 [2, 2048, 768], P('section', 'gx', 'gy')
Inputs may be any that keep to these rules, and one draw needn't show every extreme that they name: `routes`: each token names two different experts; in each layer and micro-batch at most 80 tokens name one expert, a bound that some block reaches of them.
All inputs are finite; a program needn't handle non-finite values.
Results may differ from a plain program's by a relative error of at most 0.024.
Values may be sent and summed in bfloat16 or wider, within the bound.
A program may use at most 384 MiB of HBM per device.

v0:
```python
import jax
import jax.numpy as jnp
from jax import lax
from jax.sharding import PartitionSpec as P

DH = 64


epsilon = 1e-06
highest = lax.Precision.HIGHEST


def from_partner(array, axis, apart):
    return lax.ppermute(array, axis, [(i, i ^ 1 << apart) for i in range(lax.axis_size(axis))])


def token_rows(values):
    return lax.all_gather(values, "gx", axis=0, tiled=True)


def output_rows(values):
    return lax.psum_scatter(values, "gx", scatter_dimension=0, tiled=True)


def width_sum(values):
    return lax.psum(values, "gy")


def pass_section(values):
    return from_partner(values, "section", 0)


def sequence_sums(values):
    return lax.psum_scatter(values, "gy", scatter_dimension=0, tiled=True)


def sequence_rows(values):
    return lax.all_gather(values, "gy", axis=0, tiled=True)


def gather_hidden(hidden, shared_hidden):
    return (
        lax.all_gather(hidden, "gy", axis=0, tiled=True),
        lax.all_gather(shared_hidden, "gy", axis=0, tiled=True),
    )


def rope_turn(values, positions, turn_sign):
    half_size = values.shape[-1] // 2
    frequency = 10000.0 ** (-jnp.arange(half_size, dtype=jnp.float32) / half_size)
    angles = positions[:, None] * frequency[None, :]
    cosine = jnp.cos(angles)[:, None, :]
    sine_part = turn_sign * jnp.sin(angles)[:, None, :]
    first_half = values[..., :half_size]
    second_half = values[..., half_size:]
    return jnp.concatenate(
        [
            first_half * cosine - second_half * sine_part,
            first_half * sine_part + second_half * cosine,
        ],
        axis=-1,
    )


def norm_forward(stream, gain):
    full_width = stream.shape[1] * lax.axis_size("gy")
    square_sum = width_sum(jnp.sum(stream * stream, axis=1))
    inverse_rms = lax.rsqrt(square_sum / full_width + epsilon)
    return ((stream * inverse_rms[:, None] * gain[None, :]).astype(jnp.bfloat16), inverse_rms)


def norm_backward(stream, inverse_rms, gain, grad_normed):
    full_width = stream.shape[1] * lax.axis_size("gy")
    scaled = grad_normed * gain[None, :]
    inner_sum = width_sum(jnp.sum(scaled * stream, axis=1))
    cubed = inverse_rms * inverse_rms * inverse_rms
    grad_stream = inverse_rms[:, None] * scaled - stream * (cubed * inner_sum / full_width)[:, None]
    grad_gain = jnp.sum(grad_normed * stream * inverse_rms[:, None], axis=0)
    return (grad_stream, grad_gain)


def slot_table(route_ids, experts, capacity):
    flat_ids = route_ids.reshape(-1)
    assigned = (flat_ids[:, None] == jnp.arange(experts, dtype=jnp.int32)[None, :]).astype(
        jnp.int32
    )
    earlier = jnp.cumsum(assigned, axis=0) - assigned
    places = flat_ids * capacity + jnp.sum(earlier * assigned, axis=1)
    owners = jnp.arange(flat_ids.shape[0], dtype=jnp.int32) // 2
    slot_token = jnp.zeros((experts * capacity,), jnp.int32).at[places].set(owners)
    slot_valid = jnp.zeros((experts * capacity,), jnp.int32).at[places].set(jnp.ones_like(owners))
    return (places.reshape(-1, 2), slot_token, slot_valid)


def expert_act(gate_up, logits):
    half_size = gate_up.shape[1] // 2
    return (
        jax.nn.silu(gate_up[:, :half_size])
        * gate_up[:, half_size:]
        * jax.nn.sigmoid(logits)[:, None]
    )


def shared_act(gate_up):
    half_size = gate_up.shape[1] // 2
    return jax.nn.silu(gate_up[:, :half_size]) * gate_up[:, half_size:]


def causal_scores(queries, keys_part):
    score_scale = queries.shape[-1] ** (-0.5)
    scores = (
        jnp.einsum("qhd,khd->hqk", queries, keys_part, preferred_element_type=jnp.float32)
        * score_scale
    )
    length = queries.shape[0]
    causal = jnp.arange(length)[:, None] >= jnp.arange(length)[None, :]
    return jnp.where(causal[None], scores, -1e30)


def attend_forward(queries, keys_part, values_part):
    scores = causal_scores(queries, keys_part)
    row_max = jnp.max(scores, axis=-1, keepdims=True)
    exponent = jnp.exp(scores - row_max)
    row_total = jnp.sum(exponent, axis=-1, keepdims=True)
    probabilities = (exponent / row_total).astype(jnp.bfloat16)
    attended = jnp.einsum(
        "hqk,khd->qhd", probabilities, values_part, preferred_element_type=jnp.float32
    )
    return (attended, row_max + jnp.log(row_total))


def attend_backward(queries, keys_part, values_part, log_total, grad_attended):
    score_scale = queries.shape[-1] ** (-0.5)
    probabilities = jnp.exp(causal_scores(queries, keys_part) - log_total)
    grad_values = jnp.einsum(
        "hqk,qhd->khd",
        probabilities.astype(jnp.bfloat16),
        grad_attended,
        preferred_element_type=jnp.float32,
    )
    grad_probs = jnp.einsum(
        "qhd,khd->hqk", grad_attended, values_part, preferred_element_type=jnp.float32
    )
    grad_scores = (
        probabilities * (grad_probs - jnp.sum(grad_probs * probabilities, axis=-1, keepdims=True))
    ).astype(jnp.bfloat16)
    grad_queries = (
        jnp.einsum("hqk,khd->qhd", grad_scores, keys_part, preferred_element_type=jnp.float32)
        * score_scale
    )
    grad_keys = (
        jnp.einsum("hqk,qhd->khd", grad_scores, queries, preferred_element_type=jnp.float32)
        * score_scale
    )
    return (grad_queries, grad_keys, grad_values)


def layer_forward(stream, weights, route_ids):
    (
        attention_gain,
        attention_in,
        attention_out,
        feed_gain,
        router_weight,
        expert_in,
        expert_down,
        shared_in,
        shared_down,
    ) = weights
    local_width = stream.shape[1]
    experts = expert_in.shape[0]
    normed, inverse_first = norm_forward(stream, attention_gain)
    rows_first = token_rows(normed)
    tokens = rows_first.shape[0]
    capacity = 5 * tokens // (2 * experts)
    slot_count = experts * capacity
    projected = sequence_sums(
        jnp.dot(
            rows_first, attention_in.reshape(local_width, -1), preferred_element_type=jnp.float32
        )
    )
    length = projected.shape[0]
    projected = projected.reshape(length, 3, -1, DH)
    positions = jnp.arange(length, dtype=jnp.float32)
    queries = rope_turn(projected[:, 0], positions, 1.0).astype(jnp.bfloat16)
    keys_part = rope_turn(projected[:, 1], positions, 1.0).astype(jnp.bfloat16)
    values_part = projected[:, 2].astype(jnp.bfloat16)
    attended, log_total = attend_forward(queries, keys_part, values_part)
    attended_rows = sequence_rows(attended.astype(jnp.bfloat16).reshape(length, -1))
    middle = stream + output_rows(
        jnp.dot(attended_rows, attention_out, preferred_element_type=jnp.float32)
    )
    normed_feed, inverse_second = norm_forward(middle, feed_gain)
    rows_second = token_rows(normed_feed)
    route_slot, slot_token, slot_valid = slot_table(route_ids, experts, capacity)
    grouped = (rows_second[slot_token] * slot_valid[:, None].astype(jnp.bfloat16)).reshape(
        experts, capacity, local_width
    )
    expert_part = jnp.einsum(
        "ecd,edf->ecf",
        grouped,
        expert_in.reshape(experts, local_width, -1),
        preferred_element_type=jnp.float32,
    )
    router_part = jnp.einsum(
        "ecd,de->ec", grouped, router_weight, preferred_element_type=jnp.float32
    )
    shared_part = jnp.dot(
        rows_second, shared_in.reshape(local_width, -1), preferred_element_type=jnp.float32
    )
    expert_gu, router_logit, shared_gu = (
        lax.psum_scatter(
            expert_part.reshape(slot_count, -1), "gy", scatter_dimension=0, tiled=True
        ),
        lax.psum_scatter(router_part.reshape(slot_count), "gy", scatter_dimension=0, tiled=True),
        lax.psum_scatter(shared_part, "gy", scatter_dimension=0, tiled=True),
    )
    hidden_rows, shared_rows = gather_hidden(
        expert_act(expert_gu, router_logit).astype(jnp.bfloat16),
        shared_act(shared_gu).astype(jnp.bfloat16),
    )
    expert_result = jnp.einsum(
        "ecf,efd->ecd",
        hidden_rows.reshape(experts, capacity, -1),
        expert_down,
        preferred_element_type=jnp.float32,
    ).reshape(slot_count, local_width)
    branch = (
        expert_result[route_slot[:, 0]]
        + expert_result[route_slot[:, 1]]
        + jnp.dot(shared_rows, shared_down, preferred_element_type=jnp.float32)
    )
    result = middle + output_rows(branch)
    kept_items = (
        stream,
        inverse_first,
        rows_first,
        queries,
        keys_part,
        values_part,
        log_total,
        attended_rows,
        middle,
        inverse_second,
        rows_second,
        expert_gu,
        router_logit,
        shared_gu,
    )
    return (result, kept_items)


def layer_backward(grad_out, kept_items, weights, route_ids):
    (
        attention_gain,
        attention_in,
        attention_out,
        feed_gain,
        router_weight,
        expert_in,
        expert_down,
        shared_in,
        shared_down,
    ) = weights
    (
        stream,
        inverse_first,
        rows_first,
        queries,
        keys_part,
        values_part,
        log_total,
        attended_rows,
        middle,
        inverse_second,
        rows_second,
        expert_gu,
        router_logit,
        shared_gu,
    ) = kept_items[:14]
    local_width = stream.shape[1]
    experts = expert_in.shape[0]
    tokens = rows_second.shape[0]
    capacity = 5 * tokens // (2 * experts)
    slot_count = experts * capacity
    hidden_rows, shared_rows = gather_hidden(
        expert_act(expert_gu, router_logit).astype(jnp.bfloat16),
        shared_act(shared_gu).astype(jnp.bfloat16),
    )
    route_slot, slot_token, slot_valid = slot_table(route_ids, experts, capacity)
    valid_rows = slot_valid[:, None].astype(jnp.bfloat16)
    grouped = (rows_second[slot_token] * valid_rows).reshape(experts, capacity, local_width)
    grad_rows = token_rows(grad_out.astype(jnp.bfloat16))
    slot_grad = (grad_rows[slot_token] * valid_rows).reshape(experts, capacity, local_width)
    down_grad = jnp.einsum(
        "ecf,ecd->efd",
        hidden_rows.reshape(experts, capacity, -1),
        slot_grad,
        preferred_element_type=jnp.float32,
    )
    shared_down_grad = jnp.einsum(
        "tf,td->fd", shared_rows, grad_rows, preferred_element_type=jnp.float32
    )
    hidden_part = jnp.einsum(
        "ecd,efd->ecf", slot_grad, expert_down, preferred_element_type=jnp.float32
    ).reshape(slot_count, -1)
    shared_part = jnp.einsum(
        "td,fd->tf", grad_rows, shared_down, preferred_element_type=jnp.float32
    )
    grad_hidden, grad_shared = (
        lax.psum_scatter(
            hidden_part.astype(jnp.bfloat16), "gy", scatter_dimension=0, tiled=True
        ).astype(jnp.float32),
        lax.psum_scatter(
            shared_part.astype(jnp.bfloat16), "gy", scatter_dimension=0, tiled=True
        ).astype(jnp.float32),
    )
    unused_expert, expert_back = jax.vjp(expert_act, expert_gu, router_logit)
    grad_gu, grad_logit = expert_back(grad_hidden)
    unused_shared, shared_back = jax.vjp(shared_act, shared_gu)
    (grad_shared_gu,) = shared_back(grad_shared)
    gu_rows, shared_gu_rows = (
        lax.all_gather(grad_gu.astype(jnp.bfloat16), "gy", axis=0, tiled=True),
        lax.all_gather(grad_shared_gu.astype(jnp.bfloat16), "gy", axis=0, tiled=True),
    )
    logit_rows = lax.all_gather(grad_logit, "gy", axis=0, tiled=True).reshape(experts, capacity)
    gu_grouped = gu_rows.reshape(experts, capacity, -1)
    in_grad = jnp.einsum("ecd,ecf->edf", grouped, gu_grouped, preferred_element_type=jnp.float32)
    router_grad = jnp.einsum(
        "ecd,ec->de", grouped.astype(jnp.float32), logit_rows, precision=highest
    )
    shared_in_grad = jnp.einsum(
        "td,tf->df", rows_second, shared_gu_rows, preferred_element_type=jnp.float32
    )
    slot_back = jnp.einsum(
        "ecf,edf->ecd",
        gu_grouped,
        expert_in.reshape(experts, local_width, -1),
        preferred_element_type=jnp.float32,
    )
    slot_back = slot_back + logit_rows[:, :, None] * router_weight.T.astype(jnp.float32)[:, None, :]
    slot_back = slot_back.reshape(slot_count, local_width)
    rows_back = (
        slot_back[route_slot[:, 0]]
        + slot_back[route_slot[:, 1]]
        + jnp.einsum(
            "tf,df->td",
            shared_gu_rows,
            shared_in.reshape(local_width, -1),
            preferred_element_type=jnp.float32,
        )
    )
    grad_middle_norm, feed_gain_grad = norm_backward(
        middle, inverse_second, feed_gain, output_rows(rows_back)
    )
    grad_middle = grad_out + grad_middle_norm
    middle_rows = token_rows(grad_middle.astype(jnp.bfloat16))
    out_weight_grad = jnp.einsum(
        "tf,td->fd", attended_rows, middle_rows, preferred_element_type=jnp.float32
    )
    grad_attended = sequence_sums(
        jnp.einsum("td,fd->tf", middle_rows, attention_out, preferred_element_type=jnp.float32)
    )
    length = grad_attended.shape[0]
    positions = jnp.arange(length, dtype=jnp.float32)
    grad_queries, grad_keys, grad_values = attend_backward(
        queries,
        keys_part,
        values_part,
        log_total,
        grad_attended.astype(jnp.bfloat16).reshape(queries.shape),
    )
    grad_projected = jnp.stack(
        [
            rope_turn(grad_queries, positions, -1.0),
            rope_turn(grad_keys, positions, -1.0),
            grad_values,
        ],
        axis=1,
    )
    grad_projected = grad_projected.astype(jnp.bfloat16).reshape(length, -1)
    projected_rows = sequence_rows(grad_projected)
    in_weight_grad = jnp.einsum(
        "td,tf->df", rows_first, projected_rows, preferred_element_type=jnp.float32
    )
    grad_normed = output_rows(
        jnp.einsum(
            "tf,df->td",
            projected_rows,
            attention_in.reshape(local_width, -1),
            preferred_element_type=jnp.float32,
        )
    )
    grad_stream_norm, attention_gain_grad = norm_backward(
        stream, inverse_first, attention_gain, grad_normed
    )
    layer_grads = (
        attention_gain_grad,
        in_weight_grad.reshape(attention_in.shape),
        out_weight_grad,
        feed_gain_grad,
        router_grad,
        in_grad.reshape(expert_in.shape),
        down_grad,
        shared_in_grad.reshape(shared_in.shape),
        shared_down_grad,
    )
    return (grad_middle + grad_stream_norm, layer_grads)


def put_item(buffer, value, batch_index, is_valid):
    current = lax.dynamic_index_in_dim(buffer, batch_index, 0, keepdims=False)
    return lax.dynamic_update_index_in_dim(
        buffer, jnp.where(is_valid, value, current), batch_index, 0
    )


def on_device(
    block_input,
    output_grad,
    attention_gain,
    attention_in,
    attention_out,
    feed_gain,
    router_weight,
    expert_in,
    expert_down,
    shared_in,
    shared_down,
    routes,
):
    section_index = lax.axis_index("section")
    batches = block_input.shape[0]
    weights = tuple(
        (
            member[0]
            for member in (
                attention_gain,
                attention_in,
                attention_out,
                feed_gain,
                router_weight,
                expert_in,
                expert_down,
                shared_in,
                shared_down,
            )
        )
    )
    route_table = routes[0]
    outputs = jnp.zeros(block_input.shape, jnp.bfloat16)
    received = jnp.zeros(block_input.shape[1:], jnp.bfloat16)
    stored = None
    for tick_step in range(batches + 1):
        micro_index = tick_step - section_index
        is_valid = (micro_index >= 0) & (micro_index < batches)
        batch_index = jnp.clip(micro_index, 0, batches - 1)
        fresh_input = lax.dynamic_index_in_dim(block_input, batch_index, 0, keepdims=False)
        incoming = jnp.where(section_index == 0, fresh_input, received).astype(jnp.float32)
        route_ids = lax.dynamic_index_in_dim(route_table, batch_index, 0, keepdims=False)
        result, kept_items = layer_forward(incoming, weights, route_ids)
        result_low = result.astype(jnp.bfloat16)
        outputs = put_item(outputs, result_low, batch_index, is_valid)
        if stored is None:
            stored = tuple(
                (jnp.zeros((batches,) + member.shape, member.dtype) for member in kept_items)
            )
        stored = tuple(
            (
                put_item(buffer, member, batch_index, is_valid)
                for buffer, member in zip(stored, kept_items)
            )
        )
        if tick_step < batches:
            received = pass_section(result_low)
    grads_in = jnp.zeros(block_input.shape, jnp.bfloat16)
    received = jnp.zeros(block_input.shape[1:], jnp.bfloat16)
    totals = tuple((jnp.zeros(member.shape, jnp.float32) for member in weights))
    for tick_step in range(batches + 1):
        micro_index = batches - tick_step - section_index
        is_valid = (micro_index >= 0) & (micro_index < batches)
        batch_index = jnp.clip(micro_index, 0, batches - 1)
        given_grad = lax.dynamic_index_in_dim(output_grad, batch_index, 0, keepdims=False)
        incoming = jnp.where(section_index == 1, given_grad, received).astype(jnp.float32)
        kept_items = tuple(
            (lax.dynamic_index_in_dim(buffer, batch_index, 0, keepdims=False) for buffer in stored)
        )
        route_ids = lax.dynamic_index_in_dim(route_table, batch_index, 0, keepdims=False)
        grad_input, layer_grads = layer_backward(incoming, kept_items, weights, route_ids)
        grad_low = grad_input.astype(jnp.bfloat16)
        grads_in = put_item(grads_in, grad_low, batch_index, is_valid)
        totals = tuple(
            (total + jnp.where(is_valid, member, 0.0) for total, member in zip(totals, layer_grads))
        )
        if tick_step < batches:
            received = pass_section(grad_low)
    gain_first, gain_second, router_total = lax.psum((totals[0], totals[3], totals[4]), "gx")
    return (
        outputs[None],
        grads_in[None],
        gain_first[None],
        totals[1][None],
        totals[2][None],
        gain_second[None],
        router_total[None],
        totals[5][None],
        totals[6][None],
        totals[7][None],
        totals[8][None],
    )


def solution(mesh):
    in_specs = (
        P(None, "gx", "gy"),
        P(None, "gx", "gy"),
        P("section", "gy"),
        P("section", "gy", None, "gx"),
        P("section", "gx", "gy"),
        P("section", "gy"),
        P("section", "gy", None),
        P("section", None, "gy", None, "gx"),
        P("section", None, "gx", "gy"),
        P("section", "gy", None, "gx"),
        P("section", "gx", "gy"),
        P("section", None, None, None),
    )
    out_specs = (
        P("section", None, "gx", "gy"),
        P("section", None, "gx", "gy"),
        P("section", "gy"),
        P("section", "gy", None, "gx"),
        P("section", "gx", "gy"),
        P("section", "gy"),
        P("section", "gy", None),
        P("section", None, "gy", None, "gx"),
        P("section", None, "gx", "gy"),
        P("section", "gy", None, "gx"),
        P("section", "gx", "gy"),
    )
    return jax.shard_map(
        on_device, mesh=mesh, in_specs=in_specs, out_specs=out_specs, check_vma=False
    )
```

profile of v0, /device:TPU:0, one launch (start us, length us, event | category | flops | bytes accessed | tf_op | source)
XLA Modules:
  0.0 3370.0 jit_solution(16276498277222629624)
XLA Ops:
  156.8 73.9 %reduce-scatter.55.cloned.1.call-done = f32[320,1024]{1,0:T(8,128)} async-done(((f32[1280,1024]{1,0:T(8,128)}), f32[320,1024]{1,0:T(8,128)}) %reduce-scatter.55.cloned.1.call-update) | async-done | bytes 1310736 | tf_op jit(solution)/shard_map/reduce_scatter | solution.py:212
  235.3 42.0 %reduce-scatter.57.cloned.1.call-done = f32[128,1024]{1,0:T(8,128)} async-done(((f32[512,1024]{1,0:T(8,128)}), f32[128,1024]{1,0:T(8,128)}) %reduce-scatter.57.cloned.1.call-update) | async-done | bytes 524304 | tf_op jit(solution)/shard_map/reduce_scatter | solution.py:216
  278.4 18.2 all_gather.199
  333.0 21.6 reduce-scatter.59.cloned.1.call-done
  514.2 75.6 %reduce-scatter.65.cloned.1.call-done = f32[320,1024]{1,0:T(8,128)} async-done(((f32[1280,1024]{1,0:T(8,128)}), f32[320,1024]{1,0:T(8,128)}) %reduce-scatter.65.cloned.1.call-update) | async-done | bytes 1310736 | tf_op jit(solution)/shard_map/reduce_scatter | solution.py:212
  594.4 41.9 %reduce-scatter.67.cloned.1.call-done = f32[128,1024]{1,0:T(8,128)} async-done(((f32[512,1024]{1,0:T(8,128)}), f32[128,1024]{1,0:T(8,128)}) %reduce-scatter.67.cloned.1.call-update) | async-done | bytes 524304 | tf_op jit(solution)/shard_map/reduce_scatter | solution.py:216
  637.4 17.9 all_gather.204
  655.3 17.4 all-gather.24.cloned.1.call-done
  689.7 23.9 reduce-scatter.69.cloned.1.call-done
  744.7 26.5 reduce-scatter.71.cloned.1.call-done
  866.8 73.9 %reduce-scatter.75.cloned.1.call-done = f32[320,1024]{1,0:T(8,128)} async-done(((f32[1280,1024]{1,0:T(8,128)}), f32[320,1024]{1,0:T(8,128)}) %reduce-scatter.75.cloned.1.call-update) | async-done | bytes 1310736 | tf_op jit(solution)/shard_map/reduce_scatter | solution.py:212
  945.2 42.0 %reduce-scatter.77.cloned.1.call-done = f32[128,1024]{1,0:T(8,128)} async-done(((f32[512,1024]{1,0:T(8,128)}), f32[128,1024]{1,0:T(8,128)}) %reduce-scatter.77.cloned.1.call-update) | async-done | bytes 524304 | tf_op jit(solution)/shard_map/reduce_scatter | solution.py:216
  988.3 18.2 all_gather.209
  1040.6 23.9 reduce-scatter.79.cloned.1.call-done
  1228.2 73.9 %reduce-scatter.85.cloned.1.call-done = f32[320,1024]{1,0:T(8,128)} async-done(((f32[1280,1024]{1,0:T(8,128)}), f32[320,1024]{1,0:T(8,128)}) %reduce-scatter.85.cloned.1.call-update) | async-done | bytes 1310736 | tf_op jit(solution)/shard_map/reduce_scatter | solution.py:212
  1306.7 42.2 %reduce-scatter.87.cloned.1.call-done = f32[128,1024]{1,0:T(8,128)} async-done(((f32[512,1024]{1,0:T(8,128)}), f32[128,1024]{1,0:T(8,128)}) %reduce-scatter.87.cloned.1.call-update) | async-done | bytes 524304 | tf_op jit(solution)/shard_map/reduce_scatter | solution.py:216
  1350.0 17.9 all_gather.214
  1367.9 17.4 all-gather.28.cloned.1.call-done
  1402.4 23.9 reduce-scatter.89.cloned.1.call-done
  1455.9 26.5 reduce-scatter.91.cloned.1.call-done
  1633.3 18.6 reduce-scatter.95.cloned.1.call-done
  1660.3 25.5 reduce-scatter.101.cloned.1.call-done
  1712.7 18.1 reduce-scatter.97.cloned.1.call-done
  1736.0 18.6 reduce-scatter.103.cloned.1.call-done
  1778.0 32.4 all-gather.32.cloned.1.call-done
  1848.2 18.0 reduce-scatter.105.cloned.1.call-done
  1935.3 20.3 reduce-scatter.109.cloned.1.call-done
  1992.3 27.3 reduce-scatter.111.cloned.1.call-done
  2023.2 19.0 reduce-scatter.113.cloned.1.call-done
  2054.3 43.3 %all-gather.36.cloned.1.call-done = bf16[1280,1024]{1,0:T(8,128)(2,1)} async-done(((bf16[320,1024]{1,0:T(8,128)(2,1)}), bf16[1280,1024]{1,0:T(8,128)(2,1)}) %all-gather.36.cloned.1.call-update) | async-done | bytes 2621456 | tf_op jit(solution)/shard_map/all_gather | solution.py:323
  2128.5 24.5 reduce-scatter.115.cloned.1.call-done
  2221.2 23.1 reduce-scatter.119.cloned.1.call-done
  2282.1 27.3 reduce-scatter.121.cloned.1.call-done
  2313.0 19.2 reduce-scatter.123.cloned.1.call-done
  2344.2 43.4 %all-gather.40.cloned.1.call-done = bf16[1280,1024]{1,0:T(8,128)(2,1)} async-done(((bf16[320,1024]{1,0:T(8,128)(2,1)}), bf16[1280,1024]{1,0:T(8,128)(2,1)}) %all-gather.40.cloned.1.call-update) | async-done | bytes 2621456 | tf_op jit(solution)/shard_map/all_gather | solution.py:323
  2418.5 24.6 reduce-scatter.125.cloned.1.call-done
  2511.5 23.1 reduce-scatter.129.cloned.1.call-done
  2572.4 27.4 reduce-scatter.131.cloned.1.call-done
  2603.4 19.0 reduce-scatter.133.cloned.1.call-done
  2634.3 43.3 %all-gather.44.cloned.1.call-done = bf16[1280,1024]{1,0:T(8,128)(2,1)} async-done(((bf16[320,1024]{1,0:T(8,128)(2,1)}), bf16[1280,1024]{1,0:T(8,128)(2,1)}) %all-gather.44.cloned.1.call-update) | async-done | bytes 2621456 | tf_op jit(solution)/shard_map/all_gather | solution.py:323
  2708.6 24.5 reduce-scatter.135.cloned.1.call-done
  2783.8 23.2 all_gather.243
  2815.0 21.8 all_gather.219
  2955.8 21.5 all_gather.255
  3008.7 18.2 all_gather.256
  3059.4 22.5 all_gather.257
  3106.4 20.8 all_gather.258
  3291.6 20.0 select_add_fusion
  (1558 shorter events, 1942.5 us)
Async XLA Ops:
  80.3 150.4 %reduce-scatter.55.cloned.1.call-start = ((), (), s32[]{:S(2)}) async-start(), calls=%async_computation.52 | async-start | bytes 6553600 | tf_op jit(solution)/shard_map/reduce_scatter | solution.py:212
  139.1 138.2 %reduce-scatter.57.cloned.1.call-start = ((), (), s32[]{:S(2)}) async-start(), calls=%async_computation.54 | async-start | bytes 2621440 | tf_op jit(solution)/shard_map/reduce_scatter | solution.py:216
  142.9 170.8 %all-gather.22.cloned.1.call-start = ((), (), s32[]{:S(2)}) async-start(), calls=%async_computation.53 | async-start | bytes 1638400 | tf_op jit(solution)/shard_map/all_gather | solution.py:43
  233.0 121.6 %reduce-scatter.59.cloned.1.call-start = ((), (), s32[]{:S(2)}) async-start(), calls=%async_computation.55 | async-start | bytes 491520 | tf_op jit(solution)/shard_map/reduce_scatter | solution.py:22
  330.7 92.1 %reduce-scatter.61.cloned.1.call-start = ((), (), s32[]{:S(2)}) async-start(), calls=%async_computation.56 | async-start | bytes 1474560 | tf_op jit(solution)/shard_map/reduce_scatter | solution.py:34
  440.4 149.4 %reduce-scatter.65.cloned.1.call-start = ((), (), s32[]{:S(2)}) async-start(), calls=%async_computation.58 | async-start | bytes 6553600 | tf_op jit(solution)/shard_map/reduce_scatter | solution.py:212
  498.4 137.9 %reduce-scatter.67.cloned.1.call-start = ((), (), s32[]{:S(2)}) async-start(), calls=%async_computation.60 | async-start | bytes 2621440 | tf_op jit(solution)/shard_map/reduce_scatter | solution.py:216
  502.2 170.5 %all-gather.24.cloned.1.call-start = ((), (), s32[]{:S(2)}) async-start(), calls=%async_computation.59 | async-start | bytes 1638400 | tf_op jit(solution)/shard_map/all_gather | solution.py:43
  592.1 121.6 %reduce-scatter.69.cloned.1.call-start = ((), (), s32[]{:S(2)}) async-start(), calls=%async_computation.61 | async-start | bytes 491520 | tf_op jit(solution)/shard_map/reduce_scatter | solution.py:22
  789.6 151.0 %reduce-scatter.75.cloned.1.call-start = ((), (), s32[]{:S(2)}) async-start(), calls=%async_computation.64 | async-start | bytes 6553600 | tf_op jit(solution)/shard_map/reduce_scatter | solution.py:212
  849.0 138.1 %reduce-scatter.77.cloned.1.call-start = ((), (), s32[]{:S(2)}) async-start(), calls=%async_computation.66 | async-start | bytes 2621440 | tf_op jit(solution)/shard_map/reduce_scatter | solution.py:216
  852.7 170.8 %all-gather.26.cloned.1.call-start = ((), (), s32[]{:S(2)}) async-start(), calls=%async_computation.65 | async-start | bytes 1638400 | tf_op jit(solution)/shard_map/all_gather | solution.py:43
  942.9 121.6 %reduce-scatter.79.cloned.1.call-start = ((), (), s32[]{:S(2)}) async-start(), calls=%async_computation.67 | async-start | bytes 491520 | tf_op jit(solution)/shard_map/reduce_scatter | solution.py:22
  1040.6 93.1 %reduce-scatter.81.cloned.1.call-start = ((), (), s32[]{:S(2)}) async-start(), calls=%async_computation.68 | async-start | bytes 1474560 | tf_op jit(solution)/shard_map/reduce_scatter | solution.py:34
  1152.0 150.1 %reduce-scatter.85.cloned.1.call-start = ((), (), s32[]{:S(2)}) async-start(), calls=%async_computation.70 | async-start | bytes 6553600 | tf_op jit(solution)/shard_map/reduce_scatter | solution.py:212
  1210.7 138.2 %reduce-scatter.87.cloned.1.call-start = ((), (), s32[]{:S(2)}) async-start(), calls=%async_computation.72 | async-start | bytes 2621440 | tf_op jit(solution)/shard_map/reduce_scatter | solution.py:216
  1214.5 170.8 %all-gather.28.cloned.1.call-start = ((), (), s32[]{:S(2)}) async-start(), calls=%async_computation.71 | async-start | bytes 1638400 | tf_op jit(solution)/shard_map/all_gather | solution.py:43
  1304.4 121.9 %reduce-scatter.89.cloned.1.call-start = ((), (), s32[]{:S(2)}) async-start(), calls=%async_computation.73 | async-start | bytes 491520 | tf_op jit(solution)/shard_map/reduce_scatter | solution.py:22
  1500.8 151.0 %reduce-scatter.95.cloned.1.call-start = ((), (), s32[]{:S(2)}) async-start(), calls=%async_computation.76 | async-start | bytes 6553600 | tf_op jit(solution)/shard_map/reduce_scatter | solution.py:212
  1560.2 125.6 %reduce-scatter.101.cloned.1.call-start = ((), (), s32[]{:S(2)}) async-start(), calls=%async_computation.80 | async-start | bytes 1638400 | tf_op jit(solution)/shard_map/reduce_scatter | solution.py:311
  1578.3 152.4 %reduce-scatter.97.cloned.1.call-start = ((), (), s32[]{:S(2)}) async-start(), calls=%async_computation.78 | async-start | bytes 2621440 | tf_op jit(solution)/shard_map/reduce_scatter | solution.py:216
  1581.2 173.4 %reduce-scatter.103.cloned.1.call-start = ((), (), s32[]{:S(2)}) async-start(), calls=%async_computation.82 | async-start | bytes 655360 | tf_op jit(solution)/shard_map/reduce_scatter | solution.py:314
  1583.4 226.9 %all-gather.32.cloned.1.call-start = ((), (), s32[]{:S(2)}) async-start(), calls=%async_computation.81 | async-start | bytes 3276800 | tf_op jit(solution)/shard_map/all_gather | solution.py:323
  1689.9 148.8 %all-gather.34.cloned.1.call-start = ((), (), s32[]{:S(2)}) async-start(), calls=%async_computation.83 | async-start | bytes 1310720 | tf_op jit(solution)/shard_map/all_gather | solution.py:324
  1757.2 108.9 %reduce-scatter.105.cloned.1.call-start = ((), (), s32[]{:S(2)}) async-start(), calls=%async_computation.84 | async-start | bytes 491520 | tf_op jit(solution)/shard_map/reduce_scatter | solution.py:22
  1932.5 87.0 %reduce-scatter.111.cloned.1.call-start = ((), (), s32[]{:S(2)}) async-start(), calls=%async_computation.87 | async-start | bytes 1638400 | tf_op jit(solution)/shard_map/reduce_scatter | solution.py:311
  1992.3 105.3 %all-gather.36.cloned.1.call-start = ((), (), s32[]{:S(2)}) async-start(), calls=%async_computation.88 | async-start | bytes 3276800 | tf_op jit(solution)/shard_map/all_gather | solution.py:323
  2023.1 102.6 %all-gather.38.cloned.1.call-start = ((), (), s32[]{:S(2)}) async-start(), calls=%async_computation.90 | async-start | bytes 1310720 | tf_op jit(solution)/shard_map/all_gather | solution.py:324
  2044.9 108.1 %reduce-scatter.115.cloned.1.call-start = ((), (), s32[]{:S(2)}) async-start(), calls=%async_computation.91 | async-start | bytes 491520 | tf_op jit(solution)/shard_map/reduce_scatter | solution.py:22
  2221.1 88.3 %reduce-scatter.121.cloned.1.call-start = ((), (), s32[]{:S(2)}) async-start(), calls=%async_computation.94 | async-start | bytes 1638400 | tf_op jit(solution)/shard_map/reduce_scatter | solution.py:311
  2282.1 105.5 %all-gather.40.cloned.1.call-start = ((), (), s32[]{:S(2)}) async-start(), calls=%async_computation.95 | async-start | bytes 3276800 | tf_op jit(solution)/shard_map/all_gather | solution.py:323
  2313.0 102.8 %all-gather.42.cloned.1.call-start = ((), (), s32[]{:S(2)}) async-start(), calls=%async_computation.97 | async-start | bytes 1310720 | tf_op jit(solution)/shard_map/all_gather | solution.py:324
  2334.9 108.2 %reduce-scatter.125.cloned.1.call-start = ((), (), s32[]{:S(2)}) async-start(), calls=%async_computation.98 | async-start | bytes 491520 | tf_op jit(solution)/shard_map/reduce_scatter | solution.py:22
  2511.4 88.3 %reduce-scatter.131.cloned.1.call-start = ((), (), s32[]{:S(2)}) async-start(), calls=%async_computation.101 | async-start | bytes 1638400 | tf_op jit(solution)/shard_map/reduce_scatter | solution.py:311
  2572.3 105.3 %all-gather.44.cloned.1.call-start = ((), (), s32[]{:S(2)}) async-start(), calls=%async_computation.102 | async-start | bytes 3276800 | tf_op jit(solution)/shard_map/all_gather | solution.py:323
  2603.3 102.5 %all-gather.46.cloned.1.call-start = ((), (), s32[]{:S(2)}) async-start(), calls=%async_computation.104 | async-start | bytes 1310720 | tf_op jit(solution)/shard_map/all_gather | solution.py:324
  2625.0 108.0 %reduce-scatter.135.cloned.1.call-start = ((), (), s32[]{:S(2)}) async-start(), calls=%async_computation.105 | async-start | bytes 491520 | tf_op jit(solution)/shard_map/reduce_scatter | solution.py:22
  2763.9 104.5 %reduce-scatter.139.cloned.1.call-start = ((), (), s32[]{:S(2)}) async-start(), calls=%async_computation.107 | async-start | bytes 491520 | tf_op jit(solution)/shard_map/reduce_scatter | solution.py:22
  2809.0 177.4 %all-gather.52.cloned.1.call-start = ((), (), s32[]{:S(2)}) async-start(), calls=%async_computation.115 | async-start | bytes 1638400 | tf_op jit(solution)/shard_map/all_gather | solution.py:43
  2809.6 183.9 %reduce-scatter.99.cloned.1.call-start = ((), (), s32[]{:S(2)}) async-start(), calls=%async_computation.79 | async-start | bytes 491520 | tf_op jit(solution)/shard_map/reduce_scatter | solution.py:22
  2853.8 182.2 %all-gather.54.cloned.1.call-start = ((), (), s32[]{:S(2)}) async-start(), calls=%async_computation.116 | async-start | bytes 1638400 | tf_op jit(solution)/shard_map/all_gather | solution.py:43
  2861.7 180.2 %reduce-scatter.141.cloned.1.call-start = ((), (), s32[]{:S(2)}) async-start(), calls=%async_computation.108 | async-start | bytes 1638400 | tf_op jit(solution)/shard_map/reduce_scatter | solution.py:311
  2902.0 187.2 %all-gather.56.cloned.1.call-start = ((), (), s32[]{:S(2)}) async-start(), calls=%async_computation.117 | async-start | bytes 1638400 | tf_op jit(solution)/shard_map/all_gather | solution.py:43
  2919.9 208.5 %reduce-scatter.143.cloned.1.call-start = ((), (), s32[]{:S(2)}) async-start(), calls=%async_computation.110 | async-start | bytes 655360 | tf_op jit(solution)/shard_map/reduce_scatter | solution.py:314
  2993.5 144.9 %all-gather.58.cloned.1.call-start = ((), (), s32[]{:S(2)}) async-start(), calls=%async_computation.118 | async-start | bytes 1638400 | tf_op jit(solution)/shard_map/all_gather | solution.py:43
  3006.2 149.1 %all-gather.48.cloned.1.call-start = ((), (), s32[]{:S(2)}) async-start(), calls=%async_computation.109 | async-start | bytes 3276800 | tf_op jit(solution)/shard_map/all_gather | solution.py:323
  3046.0 133.2 %all-gather.50.cloned.1.call-start = ((), (), s32[]{:S(2)}) async-start(), calls=%async_computation.111 | async-start | bytes 1310720 | tf_op jit(solution)/shard_map/all_gather | solution.py:324
  3131.0 92.9 %reduce-scatter.145.cloned.1.call-start = ((), (), s32[]{:S(2)}) async-start(), calls=%async_computation.112 | async-start | bytes 491520 | tf_op jit(solution)/shard_map/reduce_scatter | solution.py:22
  (355 other events, 9282.6 us)
Sparse Core Ops, SparseCore 0:
  36.2 26.3 reduce-scatter.50
  139.2 91.5 reduce-scatter.54
  232.9 44.3 reduce-scatter.56
  279.4 34.2 all-gather.21
  388.4 26.4 reduce-scatter.60
  498.5 91.3 reduce-scatter.64
  592.1 44.1 reduce-scatter.66
  638.4 34.1 all-gather.23
  689.8 23.7 reduce-scatter.68
  744.8 26.3 reduce-scatter.70
  849.1 91.5 reduce-scatter.74
  942.8 44.3 reduce-scatter.76
  989.2 34.2 all-gather.25
  1040.7 23.7 reduce-scatter.78
  1094.3 26.4 reduce-scatter.80
  1210.8 91.3 reduce-scatter.84
  1304.5 44.3 reduce-scatter.86
  1351.0 34.1 all-gather.27
  1402.4 23.7 reduce-scatter.88
  1456.0 26.3 reduce-scatter.90
  1560.3 91.5 reduce-scatter.94
  1654.1 31.6 reduce-scatter.100
  1688.1 42.6 reduce-scatter.96
  1756.8 53.5 all-gather.31
  1812.0 26.6 all-gather.33
  1842.2 23.8 reduce-scatter.104
  1991.1 28.4 reduce-scatter.110
  2044.3 53.1 all-gather.35
  2099.0 26.7 all-gather.37
  2129.1 23.8 reduce-scatter.114
  2281.0 28.3 reduce-scatter.120
  2334.3 53.1 all-gather.39
  2389.1 26.6 all-gather.41
  2419.2 23.8 reduce-scatter.124
  2571.2 28.4 reduce-scatter.130
  2624.5 53.0 all-gather.43
  2679.0 26.7 all-gather.45
  2709.2 23.8 reduce-scatter.134
  2780.0 41.0 all-gather.29
  2847.8 32.9 all-gather.51
  2909.4 32.6 all-gather.53
  2945.1 38.6 reduce-scatter.140
  2985.4 36.3 all-gather.55
  3047.4 39.4 all-gather.57
  3088.5 62.3 all-gather.47
  3152.4 26.7 all-gather.49
  3182.1 23.8 reduce-scatter.144
  3212.4 33.3 all-gather.59
  (22 shorter events, 467.6 us)
where the time goes:
time: 3400 us; the launch traced here: 3370 us
  waiting for transfers between devices  1380 us (41%)
  blocking collectives  862 us (25%)
  local copies, waits for them, and re-layouts  458 us (13%)
  matrix products  358 us (11%)
  other arithmetic  290 us (9%)
    reduce_scatter x5, waiting for transfers between devices, layer_forward(): lax.psum_scatter(expert_part.reshape(slot_count, -1), 'gy', scatter_dimen...  316 us
    reduce_scatter x20, waiting for transfers between devices, output_rows(): return lax.psum_scatter(values, 'gx', scatter_dimension=0, tiled=True)  288 us
    psum x20, blocking collectives, width_sum(): return lax.psum(values, 'gy')  230 us
    all_gather x10, blocking collectives, gather_hidden(): lax.all_gather(shared_hidden, 'gy', axis=0, tiled=True)  193 us
    reduce_scatter x5, waiting for transfers between devices, layer_forward(): lax.psum_scatter(shared_part, 'gy', scatter_dimension=0, tiled=True)  186 us
    all_gather x20, blocking collectives, token_rows(): return lax.all_gather(values, 'gx', axis=0, tiled=True)  181 us
    all_gather x5, waiting for transfers between devices, layer_backward(): lax.all_gather(grad_gu.astype(jnp.bfloat16), 'gy', axis=0, tiled=True)  162 us
    all_gather x10, blocking collectives, sequence_rows(): return lax.all_gather(values, 'gy', axis=0, tiled=True)  146 us
  transfers between devices with their start and end apart: 78, of which 58 were waited for; matrix products, arithmetic and copies ran while one was open for 23% of the time, Pallas kernels for 0%

commit v1 on v0

--- a/solution.py
+++ b/solution.py
@@ -1,6 +1,10 @@
+import functools
+
 import jax
 import jax.numpy as jnp
 from jax import lax
+from jax.experimental import pallas as pl
+from jax.experimental.pallas import tpu as pltpu
 from jax.sharding import PartitionSpec as P
 
 DH = 64
@@ -510,6 +514,1065 @@
     )
 
 
+def lanes_up(n):
+    return -(-n // 128) * 128
+
+
+def rot_columns(w):
+    shape = w.shape
+    w = w.reshape(shape[:-1] + (-1, 2, DH // 2))
+    w = jnp.stack([-w[..., 1, :], w[..., 0, :]], axis=-2)
+    return w.reshape(shape)
+
+
+def pad_to(v, axis, n):
+    pads = [(0, 0)] * v.ndim
+    pads[axis] = (0, n - v.shape[axis])
+    return jnp.pad(v, pads)
+
+
+def mm(a, b, dims=((1,), (0,))):
+    return lax.dot_general(a, b, (dims, ((), ())), preferred_element_type=jnp.float32)
+
+
+def bf(v):
+    return v.astype(jnp.bfloat16)
+
+
+def emu_gather_gx(v, mbs):
+    rows = v.shape[0] // mbs
+    g = lax.all_gather(v.reshape(mbs, rows, -1), "gx")
+    return jnp.moveaxis(g, 0, 1).reshape(mbs * 4 * rows, -1)
+
+
+def emu_scatter_gx(v, mbs):
+    n = lax.axis_size("gx")
+    rows = v.shape[0] // mbs // n
+    v = bf(v).astype(jnp.float32).reshape(mbs, n, rows, -1)
+    v = lax.psum_scatter(v, "gx", scatter_dimension=1, tiled=False)
+    return v.reshape(mbs * rows, -1)
+
+
+def head_mask(pw, h):
+    lane = lax.broadcasted_iota(jnp.int32, (1, pw), 1)
+    return (lane >= h * DH) & (lane < (h + 1) * DH)
+
+
+def rms(x, features):
+    return lax.rsqrt(jnp.sum(x * x, axis=1, keepdims=True) / features + epsilon)
+
+
+def norm_back(x, inv, gain, d, features):
+    u = d * gain
+    inner = jnp.sum(u * x, axis=1, keepdims=True) / features
+    dx = inv * u - x * (inv * inv * inv * inner)
+    return dx, jnp.sum(d * x * inv, axis=0, keepdims=True)
+
+
+def emu_attn_fwd(x, gain, wqkv, wout, fgain, rwx, cos, sin, mbs, heads, features):
+    pw = cos.shape[1]
+    n1 = bf(x * rms(x, features) * gain)
+    rows = emu_gather_gx(n1, mbs)
+    proj = mm(rows, wqkv)
+    length = rows.shape[0] // mbs
+    cos2 = jnp.concatenate([cos] * mbs, 0)
+    sin2 = jnp.concatenate([sin] * mbs, 0)
+    q = bf(proj[:, :pw] * cos2 + proj[:, 3 * pw : 4 * pw] * sin2)
+    k = bf(proj[:, pw : 2 * pw] * cos2 + proj[:, 4 * pw : 5 * pw] * sin2)
+    v = bf(proj[:, 2 * pw : 3 * pw])
+    outs = []
+    for m in range(mbs):
+        rs = slice(m * length, (m + 1) * length)
+        acc = jnp.zeros((length, pw), jnp.float32)
+        for h in range(heads):
+            mask = head_mask(pw, h)
+            p = probs_of(jnp.where(mask, q[rs], 0), k[rs])
+            acc = acc + mm(bf(p), jnp.where(mask, v[rs], 0))
+        outs.append(acc)
+    att = bf(jnp.concatenate(outs, 0))
+    mid = x + emu_scatter_gx(mm(att, wout), mbs)
+    n2 = bf(mid * rms(mid, features) * fgain)
+    rx = mm(n2, rwx)
+    return mid, n2, rx, rows, q, k, v, att
+
+
+def probs_of(q, k):
+    s = mm(q, k, ((1,), (1,))) * DH ** -0.5
+    n = s.shape[0]
+    causal = lax.broadcasted_iota(jnp.int32, (n, n), 0) >= lax.broadcasted_iota(jnp.int32, (n, n), 1)
+    s = jnp.where(causal, s, -1e30)
+    e = jnp.exp(s - jnp.max(s, axis=1, keepdims=True))
+    return e / jnp.sum(e, axis=1, keepdims=True)
+
+
+def emu_attn_bwd(dn2, g, mid, fgain, x, gain, rows, q, k, v, att, wqkv, wout, cos, sin, rot, mbs, heads, features):
+    pw = cos.shape[1]
+    dx2, fgain_grad = norm_back(mid, rms(mid, features), fgain, dn2, features)
+    dm = g + dx2
+    dmr = emu_gather_gx(bf(dm), mbs)
+    wout_grad = mm(att, dmr, ((0,), (0,)))
+    datt = bf(mm(dmr, wout, ((1,), (1,))))
+    length = rows.shape[0] // mbs
+    parts = []
+    for m in range(mbs):
+        rs = slice(m * length, (m + 1) * length)
+        dq = jnp.zeros((length, pw), jnp.float32)
+        dk = dq
+        dv = dq
+        for h in range(heads):
+            mask = head_mask(pw, h)
+            qh = jnp.where(mask, q[rs], 0)
+            kh = jnp.where(mask, k[rs], 0)
+            da = jnp.where(mask, datt[rs], 0)
+            p = probs_of(qh, k[rs])
+            dp = mm(da, v[rs], ((1,), (1,)))
+            ds = bf(p * (dp - jnp.sum(dp * p, axis=1, keepdims=True)))
+            dv = dv + mm(bf(p), da, ((0,), (0,)))
+            dq = dq + mm(ds, kh) * DH ** -0.5
+            dk = dk + mm(ds, qh, ((0,), (0,))) * DH ** -0.5
+
+        def back(t):
+            hi = bf(t)
+            lo = bf(t - hi.astype(jnp.float32))
+            return t * cos - (mm(hi, rot) + mm(lo, rot)) * sin
+
+        parts.append(jnp.concatenate([bf(back(dq)), bf(back(dk)), bf(dv)], 1))
+    dqkv = jnp.concatenate(parts, 0)
+    wqkv_grad = mm(rows, dqkv, ((0,), (0,)))
+    dn1 = emu_scatter_gx(mm(dqkv, wqkv[:, : 3 * pw], ((1,), (1,))), mbs)
+    dx1, gain_grad = norm_back(x, rms(x, features), gain, dn1, features)
+    return dm + dx1, wqkv_grad, wout_grad, gain_grad, fgain_grad
+
+
+def emu_spread(v, mbs, pw):
+    n = lax.axis_size("gy")
+    rows = v.shape[0] // mbs
+    t = lax.all_to_all(v.reshape(mbs, rows, n, pw), "gy", split_axis=2, concat_axis=0, tiled=False)
+    t = lax.all_gather(t, "gx")
+    return t.transpose(2, 1, 0, 3, 4).reshape(mbs, -1, pw)
+
+
+def emu_return(v, mbs):
+    nx, ny = lax.axis_size("gx"), lax.axis_size("gy")
+    pw = v.shape[-1]
+    t = bf(v).astype(jnp.float32).reshape(mbs, ny, nx, -1, pw)
+    t = lax.psum_scatter(t, "gx", scatter_dimension=2, tiled=False)
+    rows = t.shape[2]
+    t = lax.all_to_all(t, "gy", split_axis=1, concat_axis=0, tiled=False)
+    return t.transpose(1, 2, 0, 3).reshape(mbs * rows, ny * pw)
+
+
+def place_matrix(place_row, slots):
+    i = lax.broadcasted_iota(jnp.int32, (slots, place_row.shape[1]), 0)
+    return bf(((place_row[0:1] == i) | (place_row[1:2] == i)).astype(jnp.float32))
+
+
+def ext_block(n2, rx, j, width, pw, experts):
+    lane = lax.broadcasted_iota(jnp.int32, (1, pw), 1)
+    hi = bf(rx)
+    lo = bf(rx - hi.astype(jnp.float32))
+    v = jnp.where(lane < width + experts, hi, lo)
+    return jnp.where(lane < width, n2[:, j * pw : (j + 1) * pw], v)
+
+
+def emu_ff_fwd(mid, n2, rx, place, win, wdt, sin_w, sdt, mbs, dims):
+    width, pw, experts, cap = dims
+    f = wdt.shape[-1]
+    xe = jnp.concatenate([ext_block(n2, rx, j, width, pw, experts) for j in range(4)], 1)
+    xs_all = emu_spread(xe, mbs, pw)
+    slots_all, gu_all, hid_all, branch = [], [], [], []
+    for m in range(mbs):
+        pm = place_matrix(place[m], experts * cap)
+        slots = bf(mm(pm, xs_all[m]))
+        se = slots.reshape(experts, cap, pw)
+        gu = jnp.einsum("ecd,edf->ecf", se[..., :width], win, preferred_element_type=jnp.float32)
+        gu = lax.psum(bf(gu).astype(jnp.float32), "gy")
+        lane = lax.broadcasted_iota(jnp.int32, (experts, 1, pw), 2)
+        ex = lax.broadcasted_iota(jnp.int32, (experts, 1, pw), 0)
+        rmask = (lane == width + ex) | (lane == width + experts + ex)
+        r = jnp.sum(jnp.where(rmask, se.astype(jnp.float32), 0), -1, keepdims=True)
+        hid = bf(jax.nn.silu(gu[..., :f]) * gu[..., f:] * jax.nn.sigmoid(r))
+        eo = bf(jnp.einsum("ecf,edf->ecd", hid, wdt, preferred_element_type=jnp.float32)).reshape(-1, width)
+        branch.append(pad_to(mm(pm, eo, ((0,), (0,))), 1, pw))
+        slots_all.append(se)
+        gu_all.append(bf(gu))
+        hid_all.append(hid)
+    ret = emu_return(jnp.stack(branch), mbs)
+    rows2 = emu_gather_gx(n2, mbs)
+    sgu = mm(rows2, sin_w)
+    shid = bf(jax.nn.silu(sgu[:, :f]) * sgu[:, f:])
+    sout = emu_scatter_gx(mm(shid, sdt, ((1,), (1,))), mbs)
+    out = mid + ret + sout
+    return out, (jnp.stack(slots_all), jnp.stack(gu_all), jnp.stack(hid_all), rows2, bf(sgu), shid)
+
+
+def emu_ff_bwd(g, kept, n2, place, win, wdt, sin_w, sdt, rwx, mbs, dims):
+    width, pw, experts, cap = dims
+    slots_all, gu_all, hid_all, rows2, sgu, shid = kept
+    f = wdt.shape[-1]
+    gb = bf(g)
+    g_all = emu_spread(gb, mbs, pw)
+    comb = []
+    win_grad = jnp.zeros((experts, width, 2 * f), jnp.float32)
+    wdt_grad = jnp.zeros((experts, width, f), jnp.float32)
+    for m in range(mbs):
+        pm = place_matrix(place[m], experts * cap)
+        gs = bf(mm(pm, g_all[m])).reshape(experts, cap, pw)[..., :width]
+        dh = jnp.einsum("ecd,edf->ecf", gs, wdt, preferred_element_type=jnp.float32)
+        dh = lax.psum(bf(dh).astype(jnp.float32), "gy")
+        gu = gu_all[m].astype(jnp.float32)
+        se = slots_all[m]
+        lane = lax.broadcasted_iota(jnp.int32, (experts, 1, pw), 2)
+        ex = lax.broadcasted_iota(jnp.int32, (experts, 1, pw), 0)
+        rmask = (lane == width + ex) | (lane == width + experts + ex)
+        r = jnp.sum(jnp.where(rmask, se.astype(jnp.float32), 0), -1, keepdims=True)
+        gate, up = gu[..., :f], gu[..., f:]
+        dgate, dup, dr = act_back(gate, up, dh, jax.nn.sigmoid(r))
+        dgu = jnp.concatenate([bf(dgate), bf(dup)], -1)
+        dslot = jnp.einsum("ecf,edf->ecd", dgu, win, preferred_element_type=jnp.float32)
+        dslot = pad_to(dslot, 2, pw)
+        hi = bf(dr).astype(jnp.float32)
+        owner = (lax.axis_index("gy") == 0).astype(jnp.float32)
+        dslot = dslot + owner * jnp.where(lane == width + ex, hi, jnp.where(lane == width + experts + ex, dr - hi, 0.0))
+        comb.append(mm(pm, bf(dslot).reshape(-1, pw), ((0,), (0,))))
+        win_grad = win_grad + jnp.einsum("ecd,ecf->edf", se[..., :width], dgu, preferred_element_type=jnp.float32)
+        wdt_grad = wdt_grad + jnp.einsum("ecd,ecf->edf", gs, hid_all[m], preferred_element_type=jnp.float32)
+    ret = emu_return(jnp.stack(comb), mbs)
+    g_rows = emu_gather_gx(gb, mbs)
+    dsh = mm(g_rows, sdt)
+    sgu_f = sgu.astype(jnp.float32)
+    dsg, dsu, _ = act_back(sgu_f[:, :f], sgu_f[:, f:], dsh, None)
+    dsgu = jnp.concatenate([bf(dsg), bf(dsu)], 1)
+    sin_grad = mm(rows2, dsgu, ((0,), (0,)))
+    sdt_grad = mm(g_rows, shid, ((0,), (0,)))
+    sback = emu_scatter_gx(mm(dsgu, sin_w, ((1,), (1,))), mbs)
+    dn2, rw_grad = router_back(ret, n2, rwx, width, pw)
+    return dn2 + sback, win_grad, wdt_grad, sin_grad, sdt_grad, rw_grad
+
+
+def router_back(ret, n2, rwx, width, pw):
+    lane = lax.broadcasted_iota(jnp.int32, (1, ret.shape[1]), 1)
+    ret_x = sum(ret[:, j * pw : (j + 1) * pw] for j in range(ret.shape[1] // pw))
+    lane1 = lax.broadcasted_iota(jnp.int32, (1, pw), 1)
+    dlog = jnp.where(lane1 >= width, ret_x, 0.0)
+    hi = bf(dlog)
+    lo = bf(dlog - hi.astype(jnp.float32))
+    main = jnp.where(lane % pw < width, ret, 0.0)
+    dn2 = main + mm(hi, rwx, ((1,), (1,))) + mm(lo, rwx, ((1,), (1,)))
+    rw_grad = mm(n2, hi, ((0,), (0,))) + mm(n2, lo, ((0,), (0,)))
+    return dn2, rw_grad
+
+
+def act_back(gate, up, dh, s):
+    sg = jax.nn.sigmoid(gate)
+    silu = gate * sg
+    if s is None:
+        return dh * up * (sg * (1.0 + gate * (1.0 - sg))), dh * silu, None
+    dr = jnp.sum(dh * silu * up, axis=-1, keepdims=True) * s * (1.0 - s)
+    ds = dh * s
+    return ds * up * (sg * (1.0 + gate * (1.0 - sg))), ds * silu, dr
+
+
+def places_of(routes, experts, capacity):
+    lead = routes.shape[:-2]
+    ids = routes.reshape((-1, routes.shape[-2] * 2))
+    n = ids.shape[1]
+    hot = (ids[..., None] == jnp.arange(experts, dtype=jnp.int32)).astype(jnp.bfloat16)
+    before = (jnp.arange(n)[:, None] > jnp.arange(n)[None, :]).astype(jnp.bfloat16)
+    earlier = jnp.einsum("ij,bje->bie", before, hot, preferred_element_type=jnp.float32)
+    rank = jnp.sum(earlier * hot.astype(jnp.float32), -1).astype(jnp.int32)
+    place = (ids * capacity + rank).reshape(lead + (-1, 2))
+    return jnp.moveaxis(place, -1, -2)
+
+
+def fast_device(block_input, output_grad, attention_gain, attention_in, attention_out, feed_gain,
+                router_weight, expert_in, expert_down, shared_in, shared_down, routes):
+    s = lax.axis_index("section")
+    a = lax.axis_index("gx")
+    b = lax.axis_index("gy")
+    ny = lax.axis_size("gy")
+    nx = lax.axis_size("gx")
+    mbs = block_input.shape[0] // 2
+    width = block_input.shape[2]
+    features = width * ny
+    experts = expert_in.shape[1]
+    f = expert_in.shape[-1]
+    pw = lanes_up(width + 2 * experts)
+    tokens = routes.shape[2]
+    cap = 5 * tokens // (2 * experts)
+    sub = tokens // (nx * ny)
+    heads = attention_in.shape[-1] // DH
+    dims = (width, pw, experts, cap)
+    length = sub * nx
+
+    def both(v):
+        other = pass_section(v)
+        return jnp.where(s == 0, v, other), jnp.where(s == 0, other, v)
+
+    def wide(v, axis):
+        v = pad_to(v, axis, pw)
+        return lax.all_gather(v, "gy", axis=axis, tiled=True)
+
+    ai = wide(attention_in[0], 0)
+    rotq = rot_columns(ai[:, :2])
+    ai = pad_to(jnp.concatenate([ai, rotq], 1), 2, pw).reshape(ny * pw, 5 * pw)
+    wqkv = both(ai)
+    wout = both(pad_to(wide(attention_out[0], 1), 0, pw))
+    gain = both(wide(attention_gain, 1))
+    fgain = both(wide(feed_gain, 1))
+    rwx = wide(router_weight[0], 0)
+    rwx = jnp.concatenate([jnp.zeros((ny * pw, width), jnp.bfloat16), rwx, rwx], 1)
+    rwx = both(pad_to(rwx, 1, pw))
+    win_pair = (expert_in[0].reshape(experts, width, 2 * f),)
+    win_pair = win_pair + (pass_section(win_pair[0]),)
+    wdt_pair = (expert_down[0].transpose(0, 2, 1),)
+    wdt_pair = wdt_pair + (pass_section(wdt_pair[0]),)
+    sin_w = both(wide(shared_in[0].reshape(width, 2 * f), 0))
+    sdt = both(wide(shared_down[0].T, 0))
+    place = places_of(jnp.stack([lax.dynamic_slice_in_dim(r, s * mbs, mbs, 0) for r in both(routes[0])]), experts, cap)
+
+    def tokens_in(v):
+        t = lax.dynamic_slice_in_dim(v, s * mbs, mbs, 0)
+        t = lax.all_gather(t, "gx", axis=1, tiled=True)
+        t = lax.all_gather(pad_to(t, 2, pw), "gy", axis=2, tiled=True)
+        t = lax.dynamic_slice_in_dim(t, b * length + a * sub, sub, 1)
+        return t.reshape(mbs * sub, ny * pw).astype(jnp.float32)
+
+    def tokens_out(pair):
+        v0, v1 = pair
+        keep = jnp.where(s == 0, v0, v1)
+        send = jnp.where(s == 0, v1, v0)
+        got = pass_section(send)
+        both_mb = jnp.where(s == 0, jnp.stack([keep, got]), jnp.stack([got, keep]))
+        t = bf(both_mb).reshape(2 * mbs, sub, ny, pw)[..., :width]
+        t = lax.all_gather(t, "gx", axis=1, tiled=True)
+        t = lax.all_gather(t, "gy", axis=1, tiled=True)
+        t = lax.dynamic_slice_in_dim(t, a * (tokens // nx), tokens // nx, 1)
+        return lax.dynamic_index_in_dim(t, b, 2, keepdims=False)[None]
+
+    half = DH // 2
+    freq = 10000.0 ** (-jnp.arange(half, dtype=jnp.float32) / half)
+    ang = jnp.arange(length, dtype=jnp.float32)[:, None] * freq[None]
+    lanes = jnp.tile(ang, (1, 2 * heads))
+    cos = pad_to(jnp.cos(lanes), 1, pw)
+    sin = pad_to(jnp.sin(lanes), 1, pw)
+    rot = pad_to(pad_to(rot_columns(jnp.eye(heads * DH, dtype=jnp.float32)), 0, pw), 1, pw).astype(jnp.bfloat16)
+
+    x = tokens_in(block_input)
+    kept, outs = [], []
+    for l in range(2):
+        mid, n2, rx, rows, q, k, v, att = emu_attn_fwd(
+            x, gain[l], wqkv[l], wout[l], fgain[l], rwx[l], cos, sin, mbs, heads, features)
+        out, ff = ff_fwd(l, mid, n2, rx, place[l], win_pair, wdt_pair, sin_w[l], sdt[l], mbs, dims, l)
+        kept.append((x, mid, n2, rows, q, k, v, att, ff))
+        x = bf(out).astype(jnp.float32)
+        outs.append(x)
+    g = tokens_in(output_grad)
+    gouts, grads = [None, None], [None, None]
+    expert_grads = (jnp.zeros((experts, width, 2 * f), jnp.float32), jnp.zeros((experts, width, f), jnp.float32))
+    for l in (1, 0):
+        x, mid, n2, rows, q, k, v, att, ff = kept[l]
+        dn2, expert_grads, sin_g, sdt_g, rw_g = ff_bwd(
+            l, g, ff, n2, place[l], win_pair, wdt_pair, sin_w[l], sdt[l], rwx[l], expert_grads, mbs, dims, 2 + l)
+        dx, wqkv_g, wout_g, gain_g, fgain_g = emu_attn_bwd(
+            dn2, g, mid, fgain[l], x, gain[l], rows, q, k, v, att, wqkv[l], wout[l], cos, sin, rot, mbs, heads, features)
+        g = bf(dx).astype(jnp.float32)
+        gouts[l] = g
+        grads[l] = (gain_g, wqkv_g, wout_g, fgain_g, rw_g, sin_g.astype(jnp.float32), sdt_g.astype(jnp.float32))
+
+    own = [jnp.where(s == 0, p, q_) for p, q_ in zip(*grads)]
+    other = [jnp.where(s == 0, q_, p) for p, q_ in zip(*grads)]
+    own = [p + pass_section(q_) for p, q_ in zip(own, other)]
+    gain_g, wqkv_g, wout_g, fgain_g, rw_g, sin_g, sdt_g = own
+    win_g, wdt_g = expert_grads
+
+    def narrow(v, axis):
+        v = lax.psum_scatter(v, "gy", scatter_dimension=axis, tiled=True)
+        return lax.slice_in_dim(v, 0, width, axis=axis)
+
+    gain_g, fgain_g, rw_g = lax.psum((gain_g, fgain_g, rw_g), "gx")
+    rw_g = rw_g[:, width : width + experts] + rw_g[:, width + experts : width + 2 * experts]
+    hd = heads * DH
+    return (
+        tokens_out(outs),
+        tokens_out(gouts),
+        narrow(gain_g, 1),
+        narrow(wqkv_g, 0).reshape(width, 3, pw)[..., :hd][None],
+        narrow(wout_g, 1)[:hd][None],
+        narrow(fgain_g, 1),
+        narrow(rw_g, 0)[None],
+        win_g.reshape(experts, width, 2, f)[None],
+        wdt_g.transpose(0, 2, 1)[None],
+        narrow(sin_g, 0).reshape(width, 2, f)[None],
+        narrow(sdt_g, 0).T[None],
+    )
+
+
+MESH = pl.DeviceIdType.MESH
+VMEM_BYTES = 60 * 2**20
+
+
+def greet(targets):
+    barrier = pltpu.get_barrier_semaphore()
+    for target in targets:
+        pl.semaphore_signal(barrier, inc=1, device_id=target, device_id_type=MESH)
+    return barrier
+
+
+def remote(src, dst, send, recv, target):
+    return pltpu.make_async_remote_copy(
+        src_ref=src, dst_ref=dst, send_sem=send, recv_sem=recv, device_id=target, device_id_type=MESH
+    )
+
+
+def router_column(rows, e, width, experts):
+    lane = lax.broadcasted_iota(jnp.int32, rows.shape, rows.ndim - 1)
+    mask = (lane == width + e) | (lane == width + experts + e)
+    return jnp.sum(jnp.where(mask, rows.astype(jnp.float32), 0.0), axis=-1, keepdims=True)
+
+
+class Position:
+    def __init__(self, nx, ny):
+        self.s = lax.axis_index("section")
+        self.a = lax.axis_index("gx")
+        self.b = lax.axis_index("gy")
+        self.nx, self.ny = nx, ny
+        self.n = nx * ny
+        self.me = self.a * ny + self.b
+
+    def device(self, index):
+        return (self.s, index // self.ny, lax.rem(index, self.ny))
+
+    def others(self, do):
+        def step(i, c):
+            index = lax.rem(self.me + i, self.n)
+            do(index, index // self.ny, lax.rem(index, self.ny))
+            return c
+
+        lax.fori_loop(1, self.n, step, 0)
+
+    def peers(self, do):
+        for i in range(1, self.nx):
+            do(lax.rem(self.a + i, self.nx))
+
+
+def greet_section(pos):
+    barrier = pltpu.get_barrier_semaphore()
+
+    def one(index, ai, bi):
+        pl.semaphore_signal(barrier, inc=1, device_id=(pos.s, ai, bi), device_id_type=MESH)
+
+    pos.others(one)
+    return barrier
+
+
+def ff_fwd_kernel(cfg, mid, n2, rx, place, place_t, win_a, win_b, wdt_a, wdt_b, sin_w, sdt,
+                  out, slots_o, gu_o, hid_o, rows_o, sgu_o, shid_o,
+                  win, wdt, xsend, xall, nrows, pm, pt, slots, acc, gu, hid, eo, shid, rsend, rrecv, ssend, srecv,
+                  w_sem, x_send, x_recv, n_send, n_recv, rs_send, rs_recv, ag_send, ag_recv,
+                  r_send, r_recv, s_send, s_recv, o_sem):
+    layer, nx, ny, mbs, sub, width, pw, experts, cap, f, sk, ak = cfg
+    pos = Position(nx, ny)
+    s, a, b, me = pos.s, pos.a, pos.b, pos.me
+    slots_n = experts * cap
+    tokens = nx * ny * sub
+    d = ny * pw
+    barrier = greet_section(pos)
+
+    for j, (dst, own, oth) in enumerate(((win, win_a, win_b), (wdt, wdt_a, wdt_b))):
+        @pl.when(s == layer)
+        def _():
+            pltpu.make_async_copy(own, dst, w_sem.at[j]).start()
+
+        @pl.when(s != layer)
+        def _():
+            pltpu.make_async_copy(oth, dst, w_sem.at[j]).start()
+
+    lane = lax.broadcasted_iota(jnp.int32, (1, pw), 1)
+    rv = rx[...]
+    hi = bf(rv)
+    lo = bf(rv - hi.astype(jnp.float32))
+    tail = jnp.where(lane < width + experts, hi, lo)
+    for j in range(ny):
+        block = jnp.where(lane < width, n2[...].reshape(mbs * sub, d)[:, j * pw : (j + 1) * pw], tail)
+        xsend[j] = block.reshape(mbs, sub, pw)
+    pl.semaphore_wait(barrier, pos.n - 1)
+
+    def send_x(index, ai, bi):
+        remote(xsend.at[bi], xall.at[:, b, a], x_send.at[index], x_recv.at[me], (s, ai, bi)).start()
+
+    pos.others(send_x)
+
+    def send_n(ai):
+        remote(n2, nrows.at[:, a], n_send.at[ai], n_recv.at[a], (s, ai, b)).start()
+
+    pos.peers(send_n)
+    xall[:, b, a] = xsend[b]
+    nrows[:, a] = n2[...]
+
+    for m in range(mbs):
+        i0 = lax.broadcasted_iota(jnp.int32, (slots_n, tokens), 0)
+        pm[m] = bf(((place[m, 0:1] == i0) | (place[m, 1:2] == i0)).astype(jnp.float32))
+        i1 = lax.broadcasted_iota(jnp.int32, (tokens, slots_n), 1)
+        pt[m] = bf(((place_t[m, :, 0:1] == i1) | (place_t[m, :, 1:2] == i1)).astype(jnp.float32))
+
+    def wait_x(index, ai, bi):
+        remote(xsend.at[0], xall.at[:, bi, ai], x_send.at[index], x_recv.at[index], (s, ai, bi)).wait()
+
+    pos.others(wait_x)
+    for m in range(mbs):
+        slots[m] = bf(mm(pm[m], xall[m].reshape(tokens, pw))).reshape(experts, cap, pw)
+    for j, (dst, own) in enumerate(((win, win_a), (wdt, wdt_a))):
+        pltpu.make_async_copy(own, dst, w_sem.at[j]).wait()
+    pltpu.make_async_copy(slots, slots_o, o_sem.at[0]).start()
+
+    def gu_copy(m, e):
+        to = b - 1 if m == 0 else b + 1
+        return remote(gu.at[m, e], gu.at[m, e], rs_send.at[m, e], rs_recv.at[m, e], (s, a, to))
+
+    def hid_copy(m, e):
+        to = b + 1 if m == 0 else b - 1
+        return remote(hid.at[m, e], hid.at[m, e], ag_send.at[m, e], ag_recv.at[m, e], (s, a, to))
+
+    first = (b == ny - 1, b == 0)
+    last = (b == 0, b == ny - 1)
+
+    up = (ny - 1 - b, b)
+    down = (b, ny - 1 - b)
+
+    def step(i, c):
+        for m in range(mbs):
+            e0 = i - sk * up[m]
+
+            @pl.when((e0 >= 0) & (e0 < experts))
+            def _():
+                e = jnp.clip(e0, 0, experts - 1)
+                acc[m] = mm(slots[m, e, :, :width], win[e])
+
+                @pl.when(jnp.logical_not(first[m]))
+                def _():
+                    gu_copy(m, e).wait_recv()
+                    acc[m] += gu[m, e].astype(jnp.float32)
+
+                gu[m, e] = bf(acc[m])
+
+                @pl.when(jnp.logical_not(last[m]))
+                def _():
+                    gu_copy(m, e).start()
+
+                @pl.when(last[m])
+                def _():
+                    r = router_column(slots[m, e], e, width, experts)
+                    gate = acc[m, :, :f]
+                    hid[m, e] = bf(gate * jax.nn.sigmoid(gate) * acc[m, :, f:] * jax.nn.sigmoid(r))
+                    hid_copy(m, e).start()
+
+        for m in range(mbs):
+            e1 = i - sk * (ny - 1) - ak * down[m]
+
+            @pl.when((e1 >= 0) & (e1 < experts))
+            def _():
+                e = jnp.clip(e1, 0, experts - 1)
+
+                @pl.when(jnp.logical_not(last[m]))
+                def _():
+                    hid_copy(m, e).wait_recv()
+
+                    @pl.when(jnp.logical_not(first[m]))
+                    def _():
+                        hid_copy(m, e).start()
+
+                eo[m, e] = bf(mm(hid[m, e], wdt[e], ((1,), (1,))))
+
+        return c
+
+    lax.fori_loop(0, experts + (sk + ak) * (ny - 1), step, 0)
+
+    def wait_n(ai):
+        remote(n2, nrows.at[:, ai], n_send.at[ai], n_recv.at[ai], (s, ai, b)).wait()
+
+    for m in range(mbs):
+        @pl.when(last[m])
+        def _():
+            pltpu.make_async_copy(gu.at[m], gu_o.at[m], o_sem.at[1]).start()
+
+    pltpu.make_async_copy(hid, hid_o, o_sem.at[2]).start()
+    for m in range(mbs):
+        br = mm(pt[m], eo[m].reshape(slots_n, width))
+        rsend[m, ..., :width] = bf(br).reshape(ny, nx, sub, width)
+
+    def send_r(index, ai, bi):
+        remote(rsend.at[:, bi, ai], rrecv.at[a, b], r_send.at[index], r_recv.at[me], (s, ai, bi)).start()
+
+    pos.others(send_r)
+    rrecv[a, b] = rsend[:, b, a]
+
+    pos.peers(wait_n)
+    sgu = mm(nrows[...].reshape(mbs * nx * sub, d), sin_w[...])
+    sgu_o[...] = bf(sgu)
+    gate = sgu[:, :f]
+    shid[...] = bf(gate * jax.nn.sigmoid(gate) * sgu[:, f:])
+    shid_o[...] = shid[...]
+    rows_o[...] = nrows[...]
+    ssend[...] = bf(mm(shid[...], sdt[...], ((1,), (1,)))).reshape(mbs, nx, sub, d)
+
+    def send_s(ai):
+        remote(ssend.at[:, ai], srecv.at[a], s_send.at[ai], s_recv.at[a], (s, ai, b)).start()
+
+    pos.peers(send_s)
+    srecv[a] = ssend[:, a]
+
+    def wait_s(ai):
+        remote(ssend.at[:, ai], srecv.at[ai], s_send.at[ai], s_recv.at[ai], (s, ai, b)).wait()
+
+    pos.peers(wait_s)
+
+    def wait_r(index, ai, bi):
+        remote(rsend.at[:, bi, ai], rrecv.at[ai, bi], r_send.at[index], r_recv.at[index], (s, ai, bi)).wait()
+
+    pos.others(wait_r)
+    total = mid[...]
+    for ai in range(nx):
+        total = total + srecv[ai].astype(jnp.float32)
+    for j in range(ny):
+        part = total[:, :, j * pw : (j + 1) * pw]
+        for ai in range(nx):
+            part = part + jnp.where(lane < width, rrecv[ai, j].astype(jnp.float32), 0.0)
+        out[:, :, j * pw : (j + 1) * pw] = part
+
+    def finish(e, c):
+        for m in range(mbs):
+            @pl.when(jnp.logical_not(last[m]))
+            def _():
+                gu_copy(m, e).wait_send()
+
+            @pl.when(jnp.logical_not(first[m]))
+            def _():
+                hid_copy(m, e).wait_send()
+
+        return c
+
+    lax.fori_loop(0, experts, finish, 0)
+    for m in range(mbs):
+        @pl.when(last[m])
+        def _():
+            pltpu.make_async_copy(gu.at[m], gu_o.at[m], o_sem.at[1]).wait()
+
+    pltpu.make_async_copy(hid, hid_o, o_sem.at[2]).wait()
+    pltpu.make_async_copy(slots, slots_o, o_sem.at[0]).wait()
+
+
+def ff_fwd(layer, mid, n2, rx, place, win, wdt, sin_w, sdt, mbs, dims, ids):
+    width, pw, experts, cap = dims
+    nx, ny = lax.axis_size("gx"), lax.axis_size("gy")
+    f = wdt[0].shape[-1]
+    d = ny * pw
+    sub = n2.shape[0] // mbs
+    tokens = nx * ny * sub
+    slots = experts * cap
+    cfg = (layer, nx, ny, mbs, sub, width, pw, experts, cap, f, *FWD_SKEW)
+    vm = pl.BlockSpec(memory_space=pltpu.VMEM)
+    hbm = pl.BlockSpec(memory_space=pl.ANY)
+    b16, f32 = jnp.bfloat16, jnp.float32
+    dma = pltpu.SemaphoreType.DMA
+    n = nx * ny
+    outs = pl.pallas_call(
+        functools.partial(ff_fwd_kernel, cfg),
+        out_shape=(
+            jax.ShapeDtypeStruct((mbs, sub, d), f32),
+            jax.ShapeDtypeStruct((mbs, experts, cap, pw), b16),
+            jax.ShapeDtypeStruct((mbs, experts, cap, 2 * f), b16),
+            jax.ShapeDtypeStruct((mbs, experts, cap, f), b16),
+            jax.ShapeDtypeStruct((mbs, nx, sub, d), b16),
+            jax.ShapeDtypeStruct((mbs * nx * sub, 2 * f), b16),
+            jax.ShapeDtypeStruct((mbs * nx * sub, f), b16),
+        ),
+        in_specs=[vm] * 5 + [hbm] * 4 + [vm] * 2,
+        out_specs=(vm, hbm, hbm, hbm, vm, vm, vm),
+        scratch_shapes=[
+            pltpu.VMEM((experts, width, 2 * f), b16),
+            pltpu.VMEM((experts, width, f), b16),
+            pltpu.VMEM((ny, mbs, sub, pw), b16),
+            pltpu.VMEM((mbs, ny, nx, sub, pw), b16),
+            pltpu.VMEM((mbs, nx, sub, d), b16),
+            pltpu.VMEM((mbs, slots, tokens), b16),
+            pltpu.VMEM((mbs, tokens, slots), b16),
+            pltpu.VMEM((mbs, experts, cap, pw), b16),
+            pltpu.VMEM((mbs, cap, 2 * f), f32),
+            pltpu.VMEM((mbs, experts, cap, 2 * f), b16),
+            pltpu.VMEM((mbs, experts, cap, f), b16),
+            pltpu.VMEM((mbs, experts, cap, width), b16),
+            pltpu.VMEM((mbs * nx * sub, f), b16),
+            pltpu.VMEM((mbs, ny, nx, sub, pw), b16),
+            pltpu.VMEM((nx, ny, mbs, sub, pw), b16),
+            pltpu.VMEM((mbs, nx, sub, d), b16),
+            pltpu.VMEM((nx, mbs, sub, d), b16),
+            dma((2,)), dma((n,)), dma((n,)), dma((nx,)), dma((nx,)),
+            dma((mbs, experts)), dma((mbs, experts)), dma((mbs, experts)), dma((mbs, experts)),
+            dma((n,)), dma((n,)), dma((nx,)), dma((nx,)), dma((3,)),
+        ],
+        compiler_params=pltpu.CompilerParams(collective_id=ids, has_side_effects=True, vmem_limit_bytes=VMEM_BYTES),
+        cost_estimate=pl.CostEstimate(flops=4 * 10**9, bytes_accessed=30 * 10**6, transcendentals=10**6),
+        name="experts_forward",
+    )(
+        mid.reshape(mbs, sub, d), n2.reshape(mbs, sub, d), rx, place, jnp.swapaxes(place, 1, 2),
+        win[0], win[1], wdt[0], wdt[1], sin_w, sdt,
+    )
+    out, slots_k, gu, hid, rows2, sgu, shid = outs
+    return out.reshape(mbs * sub, d), (slots_k, gu, hid, rows2.reshape(-1, d), sgu, shid)
+
+
+FWD_SKEW = (1, 1)
+
+
+def ff_bwd_kernel(cfg, g, n2, place, place_t, rwx, slots_i, gu_i, hid_i, rows2, sgu, shid,
+                  win_a, win_b, wdt_a, wdt_b, sin_w, sdt, win_g_i, wdt_g_i,
+                  out, rw_g, sin_g, sdt_g, win_g, wdt_g,
+                  win, wdt, gsend, gall, grows, pm, pt, slots, gslots, gown, hid, acc, dh, dgu, deo,
+                  wxi, wxd, sti, std, dsgu, rsend, rrecv, ssend, srecv,
+                  w_sem, x_send, x_recv, n_send, n_recv, rs_send, rs_recv, ag_send, ag_recv,
+                  wi_send, wi_recv, wd_send, wd_recv, r_send, r_recv, s_send, s_recv, l_sem, st_sem):
+    layer, nx, ny, mbs, sub, width, pw, experts, cap, f, sk, ak = cfg
+    pos = Position(nx, ny)
+    s, a, b, me = pos.s, pos.a, pos.b, pos.me
+    keeper = s == layer
+    slots_n = experts * cap
+    tokens = nx * ny * sub
+    d = ny * pw
+    first = (b == ny - 1, b == 0)
+    last = (b == 0, b == ny - 1)
+    barrier = greet_section(pos)
+
+    @pl.when(keeper)
+    def _():
+        pl.semaphore_signal(barrier, inc=1, device_id=(1 - s, a, b), device_id_type=MESH)
+
+    for j, (dst, own, oth) in enumerate(((win, win_a, win_b), (wdt, wdt_a, wdt_b))):
+        @pl.when(keeper)
+        def _():
+            pltpu.make_async_copy(own, dst, w_sem.at[j]).start()
+
+        @pl.when(jnp.logical_not(keeper))
+        def _():
+            pltpu.make_async_copy(oth, dst, w_sem.at[j]).start()
+
+    pltpu.make_async_copy(slots_i, slots, l_sem.at[0]).start()
+    pltpu.make_async_copy(hid_i, hid, l_sem.at[1]).start()
+    for m in range(mbs):
+        @pl.when(last[m])
+        def _():
+            pltpu.make_async_copy(gu_i.at[m], gown, l_sem.at[2]).start()
+
+    lane = lax.broadcasted_iota(jnp.int32, (1, pw), 1)
+    for j in range(ny):
+        gsend[j] = g[:, :, j * pw : (j + 1) * pw]
+
+    @pl.when(keeper)
+    def _():
+        pl.semaphore_wait(barrier, pos.n - 1)
+
+    @pl.when(jnp.logical_not(keeper))
+    def _():
+        pl.semaphore_wait(barrier, pos.n)
+
+    def send_x(index, ai, bi):
+        remote(gsend.at[bi], gall.at[:, b, a], x_send.at[index], x_recv.at[me], (s, ai, bi)).start()
+
+    pos.others(send_x)
+
+    def send_n(ai):
+        remote(g, grows.at[:, a], n_send.at[ai], n_recv.at[a], (s, ai, b)).start()
+
+    pos.peers(send_n)
+    gall[:, b, a] = gsend[b]
+    grows[:, a] = g[...]
+    deo[...] = jnp.zeros_like(deo)
+
+    def wait_x(index, ai, bi):
+        remote(gsend.at[0], gall.at[:, bi, ai], x_send.at[index], x_recv.at[index], (s, ai, bi)).wait()
+
+    i0 = lax.broadcasted_iota(jnp.int32, (slots_n, tokens), 0)
+    pm[...] = bf(((place[0, 0:1] == i0) | (place[0, 1:2] == i0)).astype(jnp.float32))
+    pos.others(wait_x)
+    for m in range(mbs):
+        if m:
+            pm[...] = bf(((place[m, 0:1] == i0) | (place[m, 1:2] == i0)).astype(jnp.float32))
+        gslots[m] = bf(mm(pm[...], gall[m].reshape(tokens, pw))).reshape(experts, cap, pw)
+    for j, (dst, own) in enumerate(((win, win_a), (wdt, wdt_a))):
+        pltpu.make_async_copy(own, dst, w_sem.at[j]).wait()
+    pltpu.make_async_copy(slots_i, slots, l_sem.at[0]).wait()
+    pltpu.make_async_copy(hid_i, hid, l_sem.at[1]).wait()
+    for m in range(mbs):
+        @pl.when(last[m])
+        def _():
+            pltpu.make_async_copy(gu_i.at[m], gown, l_sem.at[2]).wait()
+
+    def dh_copy(m, e):
+        to = b - 1 if m == 0 else b + 1
+        return remote(dh.at[m, e], dh.at[m, e], rs_send.at[m, e], rs_recv.at[m, e], (s, a, to))
+
+    def dgu_copy(m, e):
+        to = b + 1 if m == 0 else b - 1
+        return remote(dgu.at[m, e], dgu.at[m, e], ag_send.at[m, e], ag_recv.at[m, e], (s, a, to))
+
+    def wi_copy(e):
+        return remote(wxi.at[e], wxi.at[e], wi_send.at[e], wi_recv.at[e], (layer, a, b))
+
+    def wd_copy(e):
+        return remote(wxd.at[e], wxd.at[e], wd_send.at[e], wd_recv.at[e], (layer, a, b))
+
+    def st_copies(e, slot):
+        return (pltpu.make_async_copy(sti.at[slot], win_g.at[e], st_sem.at[0, slot]),
+                pltpu.make_async_copy(std.at[slot], wdt_g.at[e], st_sem.at[1, slot]))
+
+    def weight_grads(e):
+        gi = mm(slots[:, e, :, :width].reshape(mbs * cap, width), dgu[:, e].reshape(mbs * cap, 2 * f), ((0,), (0,)))
+        gd = mm(gslots[:, e, :, :width].reshape(mbs * cap, width), hid[:, e].reshape(mbs * cap, f), ((0,), (0,)))
+        return gi, gd
+
+    up = (ny - 1 - b, b)
+    down = (b, ny - 1 - b)
+    full = (sk + ak) * (ny - 1)
+    late = 2
+
+    def step(i, c):
+        for m in range(mbs):
+            e0 = i - sk * up[m]
+
+            @pl.when((e0 >= 0) & (e0 < experts))
+            def _():
+                e = jnp.clip(e0, 0, experts - 1)
+                acc[m] = mm(gslots[m, e, :, :width], wdt[e])
+
+                @pl.when(jnp.logical_not(first[m]))
+                def _():
+                    dh_copy(m, e).wait_recv()
+                    acc[m] += dh[m, e].astype(jnp.float32)
+
+                @pl.when(jnp.logical_not(last[m]))
+                def _():
+                    dh[m, e] = bf(acc[m])
+                    dh_copy(m, e).start()
+
+                @pl.when(last[m])
+                def _():
+                    r = router_column(slots[m, e], e, width, experts)
+                    gate = gown[e, :, :f].astype(jnp.float32)
+                    upv = gown[e, :, f:].astype(jnp.float32)
+                    dgate, dup, dr = act_back(gate, upv, acc[m], jax.nn.sigmoid(r))
+                    dgu[m, e, :, :f] = bf(dgate)
+                    dgu[m, e, :, f:] = bf(dup)
+                    dgu_copy(m, e).start()
+                    hi = bf(dr).astype(jnp.float32)
+                    deo[m, e] = bf(jnp.where(lane == width + e, hi, jnp.where(lane == width + experts + e, dr - hi, 0.0)))
+
+        for m in range(mbs):
+            e1 = i - sk * (ny - 1) - ak * down[m]
+
+            @pl.when((e1 >= 0) & (e1 < experts))
+            def _():
+                e = jnp.clip(e1, 0, experts - 1)
+
+                @pl.when(jnp.logical_not(last[m]))
+                def _():
+                    dgu_copy(m, e).wait_recv()
+
+                    @pl.when(jnp.logical_not(first[m]))
+                    def _():
+                        dgu_copy(m, e).start()
+
+                deo[m, e, :, :width] = bf(mm(dgu[m, e], win[e], ((1,), (1,))))
+
+        e2 = i - full
+
+        @pl.when((e2 >= 0) & (e2 < experts) & jnp.logical_not(keeper))
+        def _():
+            e = jnp.clip(e2, 0, experts - 1)
+            gi, gd = weight_grads(e)
+            wxi[e] = bf(gi)
+            wi_copy(e).start()
+            wxd[e] = bf(gd)
+            wd_copy(e).start()
+
+        e3 = i - full - late
+
+        @pl.when((e3 >= 0) & (e3 < experts) & keeper)
+        def _():
+            e = jnp.clip(e3, 0, experts - 1)
+            slot = lax.rem(e, 2)
+
+            @pl.when(e >= 2)
+            def _():
+                for copy in st_copies(e - 2, slot):
+                    copy.wait()
+
+            gi, gd = weight_grads(e)
+            wi_copy(e).wait_recv()
+            sti[slot] = gi + wxi[e].astype(jnp.float32)
+            wd_copy(e).wait_recv()
+            std[slot] = gd + wxd[e].astype(jnp.float32)
+            for copy in st_copies(e, slot):
+                copy.start()
+
+        return c
+
+    lax.fori_loop(0, experts + full + late, step, 0)
+
+    for m in range(mbs):
+        i1 = lax.broadcasted_iota(jnp.int32, (tokens, slots_n), 1)
+        pt[...] = bf(((place_t[m, :, 0:1] == i1) | (place_t[m, :, 1:2] == i1)).astype(jnp.float32))
+        br = mm(pt[...], deo[m].reshape(slots_n, pw))
+        rsend[m] = bf(br).reshape(ny, nx, sub, pw)
+
+    def send_r(index, ai, bi):
+        remote(rsend.at[:, bi, ai], rrecv.at[a, b], r_send.at[index], r_recv.at[me], (s, ai, bi)).start()
+
+    pos.others(send_r)
+    rrecv[a, b] = rsend[:, b, a]
+
+    def wait_n(ai):
+        remote(g, grows.at[:, ai], n_send.at[ai], n_recv.at[ai], (s, ai, b)).wait()
+
+    pos.peers(wait_n)
+    gr = grows[...].reshape(mbs * nx * sub, d)
+    dsg, dsu, _ = act_back(sgu[:, :f].astype(jnp.float32), sgu[:, f:].astype(jnp.float32), mm(gr, sdt[...]), None)
+    dsgu[:, :f] = bf(dsg)
+    dsgu[:, f:] = bf(dsu)
+    ssend[...] = bf(mm(dsgu[...], sin_w[...], ((1,), (1,)))).reshape(mbs, nx, sub, d)
+
+    def send_s(ai):
+        remote(ssend.at[:, ai], srecv.at[a], s_send.at[ai], s_recv.at[a], (s, ai, b)).start()
+
+    pos.peers(send_s)
+    srecv[a] = ssend[:, a]
+    sin_g[...] = bf(mm(rows2[...], dsgu[...], ((0,), (0,))))
+    sdt_g[...] = bf(mm(gr, shid[...], ((0,), (0,))))
+
+    def wait_s(ai):
+        remote(ssend.at[:, ai], srecv.at[ai], s_send.at[ai], s_recv.at[ai], (s, ai, b)).wait()
+
+    pos.peers(wait_s)
+
+    def wait_r(index, ai, bi):
+        remote(rsend.at[:, bi, ai], rrecv.at[ai, bi], r_send.at[index], r_recv.at[index], (s, ai, bi)).wait()
+
+    pos.others(wait_r)
+    dlog = jnp.zeros((mbs * sub, pw), jnp.float32)
+    parts = []
+    for j in range(ny):
+        part = jnp.zeros((mbs, sub, pw), jnp.float32)
+        for ai in range(nx):
+            part = part + rrecv[ai, j].astype(jnp.float32)
+        part = part.reshape(mbs * sub, pw)
+        dlog = dlog + jnp.where(lane >= width, part, 0.0)
+        parts.append(jnp.where(lane < width, part, 0.0))
+    hi = bf(dlog)
+    lo = bf(dlog - hi.astype(jnp.float32))
+    total = mm(hi, rwx[...], ((1,), (1,))) + mm(lo, rwx[...], ((1,), (1,)))
+    for ai in range(nx):
+        total = total + srecv[ai].astype(jnp.float32).reshape(mbs * sub, d)
+    for j in range(ny):
+        out[:, j * pw : (j + 1) * pw] = total[:, j * pw : (j + 1) * pw] + parts[j]
+    n2v = n2[...].reshape(mbs * sub, d)
+    rw_g[...] = mm(n2v, hi, ((0,), (0,))) + mm(n2v, lo, ((0,), (0,)))
+
+    def finish(e, c):
+        for m in range(mbs):
+            @pl.when(jnp.logical_not(last[m]))
+            def _():
+                dh_copy(m, e).wait_send()
+
+            @pl.when(jnp.logical_not(first[m]))
+            def _():
+                dgu_copy(m, e).wait_send()
+
+        @pl.when(jnp.logical_not(keeper))
+        def _():
+            wi_copy(e).wait_send()
+            wd_copy(e).wait_send()
+
+        return c
+
+    lax.fori_loop(0, experts, finish, 0)
+
+    @pl.when(keeper)
+    def _():
+        for e in (experts - 2, experts - 1):
+            for copy in st_copies(e, e % 2):
+                copy.wait()
+
+
+def ff_bwd(layer, g, kept, n2, place, win, wdt, sin_w, sdt, rwx, grads, mbs, dims, ids):
+    width, pw, experts, cap = dims
+    slots_k, gu, hid, rows2, sgu, shid = kept
+    nx, ny = lax.axis_size("gx"), lax.axis_size("gy")
+    f = wdt[0].shape[-1]
+    d = ny * pw
+    sub = n2.shape[0] // mbs
+    tokens = nx * ny * sub
+    slots = experts * cap
+    cfg = (layer, nx, ny, mbs, sub, width, pw, experts, cap, f, *BWD_SKEW)
+    vm = pl.BlockSpec(memory_space=pltpu.VMEM)
+    hbm = pl.BlockSpec(memory_space=pl.ANY)
+    b16, f32 = jnp.bfloat16, jnp.float32
+    dma = pltpu.SemaphoreType.DMA
+    n = nx * ny
+    out, rw_g, sin_g, sdt_g, win_g, wdt_g = pl.pallas_call(
+        functools.partial(ff_bwd_kernel, cfg),
+        out_shape=(
+            jax.ShapeDtypeStruct((mbs * sub, d), f32),
+            jax.ShapeDtypeStruct((d, pw), f32),
+            jax.ShapeDtypeStruct((d, 2 * f), b16),
+            jax.ShapeDtypeStruct((d, f), b16),
+            jax.ShapeDtypeStruct((experts, width, 2 * f), f32),
+            jax.ShapeDtypeStruct((experts, width, f), f32),
+        ),
+        in_specs=[vm] * 5 + [hbm] * 3 + [vm] * 3 + [hbm] * 4 + [vm] * 2 + [hbm] * 2,
+        out_specs=(vm, vm, vm, vm, hbm, hbm),
+        scratch_shapes=[
+            pltpu.VMEM((experts, width, 2 * f), b16),
+            pltpu.VMEM((experts, width, f), b16),
+            pltpu.VMEM((ny, mbs, sub, pw), b16),
+            pltpu.VMEM((mbs, ny, nx, sub, pw), b16),
+            pltpu.VMEM((mbs, nx, sub, d), b16),
+            pltpu.VMEM((slots, tokens), b16),
+            pltpu.VMEM((tokens, slots), b16),
+            pltpu.VMEM((mbs, experts, cap, pw), b16),
+            pltpu.VMEM((mbs, experts, cap, pw), b16),
+            pltpu.VMEM((experts, cap, 2 * f), b16),
+            pltpu.VMEM((mbs, experts, cap, f), b16),
+            pltpu.VMEM((mbs, cap, f), f32),
+            pltpu.VMEM((mbs, experts, cap, f), b16),
+            pltpu.VMEM((mbs, experts, cap, 2 * f), b16),
+            pltpu.VMEM((mbs, experts, cap, pw), b16),
+            pltpu.VMEM((experts, width, 2 * f), b16),
+            pltpu.VMEM((experts, width, f), b16),
+            pltpu.VMEM((2, width, 2 * f), f32),
+            pltpu.VMEM((2, width, f), f32),
+            pltpu.VMEM((mbs * nx * sub, 2 * f), b16),
+            pltpu.VMEM((mbs, ny, nx, sub, pw), b16),
+            pltpu.VMEM((nx, ny, mbs, sub, pw), b16),
+            pltpu.VMEM((mbs, nx, sub, d), b16),
+            pltpu.VMEM((nx, mbs, sub, d), b16),
+            dma((2,)), dma((n,)), dma((n,)), dma((nx,)), dma((nx,)),
+            dma((mbs, experts)), dma((mbs, experts)), dma((mbs, experts)), dma((mbs, experts)),
+            dma((experts,)), dma((experts,)), dma((experts,)), dma((experts,)),
+            dma((n,)), dma((n,)), dma((nx,)), dma((nx,)), dma((3,)), dma((2, 2)),
+        ],
+        input_output_aliases={17: 4, 18: 5},
+        compiler_params=pltpu.CompilerParams(collective_id=ids, has_side_effects=True, vmem_limit_bytes=VMEM_BYTES),
+        cost_estimate=pl.CostEstimate(flops=8 * 10**9, bytes_accessed=60 * 10**6, transcendentals=10**6),
+        name="experts_backward",
+    )(
+        bf(g).reshape(mbs, sub, d), n2.reshape(mbs, sub, d), place, jnp.swapaxes(place, 1, 2), rwx,
+        slots_k, gu, hid, rows2, sgu, shid, win[0], win[1], wdt[0], wdt[1], sin_w, sdt, *grads,
+    )
+    return out, (win_g, wdt_g), sin_g, sdt_g, rw_g
+
+
+BWD_SKEW = (2, 2)
+
+
 def solution(mesh):
     in_specs = (
         P(None, "gx", "gy"),
@@ -538,6 +1601,7 @@
         P("section", "gy", None, "gx"),
         P("section", "gx", "gy"),
     )
+    fast = mesh.shape["gx"] == mesh.shape["gy"]
     return jax.shard_map(
-        on_device, mesh=mesh, in_specs=in_specs, out_specs=out_specs, check_vma=False
-    )
+        fast_device if fast else on_device, mesh=mesh, in_specs=in_specs, out_specs=out_specs, check_vma=False
+    )

time: 3400 us -> 1500 us (0.44)
  waiting for transfers between devices: 1380 us -> 504 us
  blocking collectives: 862 us -> 160 us
  Pallas kernels: 0 us -> 598 us
  local copies, waits for them, and re-layouts: 458 us -> 110 us
  matrix products: 358 us -> 31.2 us
  other arithmetic: 290 us -> 63.5 us
    reduce_scatter x50 -> x5, waiting for transfers between devices: 1090 us -> 204 us  [narrow(): v = lax.psum_scatter(v, 'gy', scatter_dimension=axis, tiled=True)]
    pallas_call x0 -> x4, Pallas kernels: none -> 598 us  [the longest x2 313 us: ff_fwd(): pl.pallas_call(functools.partial(ff_fwd_kernel, cfg), out_shape=(jax.Shap...]
    all_gather x40 -> x12, blocking collectives: 520 us -> 150 us  [the longest x4 59.9 us: wide(): return lax.all_gather(v, 'gy', axis=axis, tiled=True)]
    dot_general x135 -> x103, matrix products: 358 us -> 31.2 us  [the longest x102 29.8 us: mm(): lax.dot_general(a, b, (dims, ((), ())), preferred_element_type=jnp.float32)]
    psum x21 -> x1, blocking collectives: 247 us -> 9.66 us  [fast_device(): gain_g, fgain_g, rw_g = lax.psum((gain_g, fgain_g, rw_g), 'gx')]
    gather x55 -> x0, local copies, waits for them, and re-layouts: 183 us -> none  [the longest x10 28 us: layer_backward(): slot_back[route_slot[:, 1]]]
    all_gather x20 -> x7, waiting for transfers between devices: 278 us -> 153 us  [the longest x2 129 us: tokens_out(): t = lax.all_gather(t, 'gy', axis=1, tiled=True)]
    unnamed x10 -> x0, blocking collectives: 95.5 us -> none
  transfers between devices with their start and end apart: 78 -> 38, of which waited for: 58 -> 21; matrix products, arithmetic and copies ran while one was open for 23% -> 10% of each run, Pallas kernels for 0% -> 11%
where the time goes in v1:
time: 1500 us; the launch traced here: 1490 us
  Pallas kernels  598 us (40%)
  waiting for transfers between devices  504 us (34%)
  blocking collectives  160 us (11%)
  local copies, waits for them, and re-layouts  110 us (7%)
  other arithmetic  63.5 us (4%)
  matrix products  31.2 us (2%)
  between operations  17.3 us (1%)
    pallas_call x2, Pallas kernels, ff_fwd(): pl.pallas_call(functools.partial(ff_fwd_kernel, cfg), out_shape=(jax.Shap...  313 us
    pallas_call x2, Pallas kernels, ff_bwd(): pl.pallas_call(functools.partial(ff_bwd_kernel, cfg), out_shape=(jax.Shap...  285 us
    reduce_scatter x5, waiting for transfers between devices, narrow(): v = lax.psum_scatter(v, 'gy', scatter_dimension=axis, tiled=True)  204 us
    all_gather x2, waiting for transfers between devices, tokens_out(): t = lax.all_gather(t, 'gy', axis=1, tiled=True)  129 us
    unnamed x25, waiting for transfers between devices  74.6 us
    all_gather x4, blocking collectives, wide(): return lax.all_gather(v, 'gy', axis=axis, tiled=True)  59.9 us
    psum x1, waiting for transfers between devices, fast_device(): gain_g, fgain_g, rw_g = lax.psum((gain_g, fgain_g, rw_g), 'gx')  52.6 us
    all_gather x4, blocking collectives, emu_gather_gx(): g = lax.all_gather(v.reshape(mbs, rows, -1), 'gx')  38.8 us
  transfers between devices with their start and end apart: 38, of which 21 were waited for; matrix products, arithmetic and copies ran while one was open for 10% of the time, Pallas kernels for 11%

profile of v1, /device:TPU:0, one launch (start us, length us, event | category | flops | bytes accessed | tf_op | source)
XLA Modules:
  0.0 1489.0 jit_solution(6680013365999165718)
XLA Ops:
  9.4 11.5 all_gather.57
  22.9 21.8 %all-gather.12.cloned.1.call-done = bf16[1024,3,192]{0,2,1:T(8,128)(2,1)} async-done(((bf16[256,3,192]{0,2,1:T(8,128)(2,1)}), bf16[1024,3,192]{0,2,1:T(8,128)(2,1)}) %all-gather.12.cloned.1.call-update) | async-done | bytes 1179664 | tf_op jit(solution)/shard_map/all_gather | solution.py:814
  47.0 17.3 %all_gather.62 = bf16[192,1024]{1,0:T(8,128)(2,1)S(1)} all-gather(bf16[192,256]{1,0:T(8,128)(2,1)S(1)} %pad.68), channel_id=1, replica_groups=mesh['section'=2,'gx'=4,'gy'=4] {'gy'}, dimensions={1}, use_global_device_ids=true | all-gather | bytes 491520 | tf_op jit(solution)/shard_map/all_gather | solution.py:814
  65.3 16.3 %all_gather.59 = f32[1,1024]{1,0:T(1,128)S(1)} all-gather(f32[1,256]{1,0:T(1,128)S(1)} %pad.63), channel_id=1, replica_groups=mesh['section'=2,'gx'=4,'gy'=4] {'gy'}, dimensions={1}, use_global_device_ids=true | all-gather | bytes 5120 | tf_op jit(solution)/shard_map/all_gather | solution.py:814
  81.6 11.0 reshape_squeeze.6.win_a
  99.3 8.8 all-gather
  108.2 3.8 broadcast_select_fusion
  119.3 9.9 all_gather.63
  131.5 16.3 %all_gather.64 = bf16[1024,16]{1,0:T(8,128)(2,1)} all-gather(bf16[256,16]{1,0:T(8,128)(2,1)S(1)} %pad.71), channel_id=1, replica_groups=mesh['section'=2,'gx'=4,'gy'=4] {'gy'}, dimensions={0}, use_global_device_ids=true | all-gather | bytes 40960 | tf_op jit(solution)/shard_map/all_gather | solution.py:814
  154.5 11.0 all_gather.70
  168.9 2.4 all-gather.16.cloned.1.call-done
  176.8 2.4 eq.16
  181.2 2.7 convert_element_type.533
  188.9 2.5 broadcast_select_fusion.8
  191.4 2.9 broadcast_select_fusion.5
  194.2 4.0 broadcast_select_fusion.2
  198.3 3.1 reduce-scatter.38.cloned.1.call-done
  209.2 170.7 %experts_forward.2 = (f32[2,32,1024]{2,1,0:T(8,128)}, bf16[2,16,80,256]{3,2,1,0:T(8,128)(2,1)}, bf16[2,16,80,1024]{3,2,1,0:T(8,128)(2,1)}, bf16[2,16,80,512]{3,2...) custom-call(f32[2,32,1024]{2,1,0:T(8,128)} %get-tuple-element.135.mid, ...), custom_call_target="tpu_custom_call" | custom-call | flops 4000000000 | bytes 30000000 | tf_op jit(solution)/shard_map/experts_forward/pallas_call | solution.py:1179
  381.1 11.0 all-gather.1
  402.4 24.1 %reduce-scatter.40.cloned.1.call-done = f32[2,1,32,1024]{3,2,0,1:T(8,128)} async-done(((f32[2,4,32,1024]{3,2,0,1:T(8,128)}), f32[2,1,32,1024]{3,2,0,1:T(8,128)}) %reduce-scatter.40.cloned.1.call-update) | async-done | bytes 262160
  432.4 142.7 %experts_forward.3 = (f32[2,32,1024]{2,1,0:T(8,128)}, bf16[2,16,80,256]{3,2,1,0:T(8,128)(2,1)}, bf16[2,16,80,1024]{3,2,1,0:T(8,128)(2,1)}, bf16[2,16,80,512]{3,2...) custom-call(f32[2,32,1024]{2,1,0:T(8,128)} %get-tuple-element.131.mid, ...), custom_call_target="tpu_custom_call" | custom-call | flops 4000000000 | bytes 30000000 | tf_op jit(solution)/shard_map/experts_forward/pallas_call | solution.py:1179
  575.1 6.2 broadcast_in_dim.487.win_g_i
  581.3 3.5 broadcast_in_dim.488.wdt_g_i
  584.8 140.2 %experts_backward.2 = (f32[64,1024]{1,0:T(8,128)}, f32[1024,256]{1,0:T(8,128)}, bf16[1024,1024]{1,0:T(8,128)(2,1)}, bf16[1024,512]{1,0:T(8,128)(2,1)}, f32[16,19...) custom-call(bf16[2,32,1024]{2,1,0:T(8,128)(2,1)} %constant_dynamic-slice_fusion.1.g, ...), custom_call_target="tpu_custom_call", output_to_operand_aliasing={{4}: (17, {}), {5}: (18, {})} | custom-call | flops 8000000000 | bytes 60000000 | tf_op jit(solution)/shard_map/experts_backward/pallas_call | solution.py:1520
  728.0 9.6 all_gather.72
  747.7 27.1 %reduce-scatter.42.cloned.1.call-done = f32[2,1,32,1024]{3,2,0,1:T(8,128)} async-done(((f32[2,4,32,1024]{3,2,0,1:T(8,128)}), f32[2,1,32,1024]{3,2,0,1:T(8,128)}) %reduce-scatter.42.cloned.1.call-update) | async-done | bytes 262160
  778.4 144.9 %experts_backward.3 = (f32[64,1024]{1,0:T(8,128)}, f32[1024,256]{1,0:T(8,128)}, bf16[1024,1024]{1,0:T(8,128)(2,1)}, bf16[1024,512]{1,0:T(8,128)(2,1)}, f32[16,19...) custom-call(bf16[2,32,1024]{2,1,0:T(8,128)(2,1)} %bitcast.293, ...), custom_call_target="tpu_custom_call", output_to_operand_aliasing={{4}: (17, {}), {5}: (18, {})} | custom-call | flops 8000000000 | bytes 60000000 | tf_op jit(solution)/shard_map/experts_backward/pallas_call | solution.py:1520
  926.7 9.4 all_gather.73
  945.6 2.6 collective-permute-done.16
  952.3 19.9 %reduce-scatter.44.cloned.1.call-done = f32[2,1,32,1024]{3,2,0,1:T(8,128)} async-done(((f32[2,4,32,1024]{3,2,0,1:T(8,128)}), f32[2,1,32,1024]{3,2,0,1:T(8,128)}) %reduce-scatter.44.cloned.1.call-update) | async-done | bytes 262160
  975.7 52.6 %all-reduce.23.cloned.1.call-done = f32[1024,256]{1,0:T(8,128)} async-done(((f32[1024,256]{1,0:T(8,128)}), f32[1024,256]{1,0:T(8,128)}) %all-reduce.23.cloned.1.call-update) | async-done | bytes 1048592 | tf_op jit(solution)/shard_map/psum | solution.py:893
  1028.4 2.4 slice_add_fusion
  1030.9 14.1 all_gather.68
  1053.3 3.3 fusion.7
  1059.8 15.0 %all_gather.74 = bf16[4,128,4,192]{3,2,1,0:T(4,128)(2,1)} all-gather(bf16[4,32,4,192]{3,2,1,0:T(4,128)(2,1)S(1)} %bitcast.307), channel_id=1, replica_groups=mesh['section'=2,'gx'=4,'gy'=4] {'gx'}, dimensions={1}, use_global_device_ids=true | all-gather | bytes 983040 | tf_op jit(solution)/shard_map/all_gather | solution.py:848
  1076.7 5.6 collective-permute-done.13
  1086.1 2.6 convert_select_fusion
  1089.0 7.0 collective-permute-done.17
  1096.0 3.1 fusion.2
  1099.2 17.0 %broadcast_in_dim_reshape.7 = f32[1,16,192,2,512]{4,3,2,1,0:T(2,128)} reshape(f32[16,192,1024]{2,1,0:T(8,128)} %get-tuple-element.57) | data formatting | bytes 25165824 | tf_op jit(solution)/shard_map/broadcast_in_dim;reshape | solution.py:904
  1118.1 9.7 all-reduce.20
  1129.4 48.8 %all-gather.18.cloned.1.call-done = bf16[4,512,4,192]{3,2,1,0:T(4,128)(2,1)} async-done(((bf16[4,128,4,192]{3,2,1,0:T(4,128)(2,1)}), bf16[4,512,4,192]{3,2,1,0:T(4,128)(2,1)}) %all-gather.18.cloned.1.call-update) | async-done | bytes 3145744 | tf_op jit(solution)/shard_map/all_gather | solution.py:849
  1180.9 25.1 %reduce-scatter.26.cloned.1.call-done = f32[256,256]{1,0:T(8,128)} async-done(((f32[256,1024]{1,0:T(8,128)}), f32[256,256]{1,0:T(8,128)}) %reduce-scatter.26.cloned.1.call-update) | async-done | bytes 262160 | tf_op jit(solution)/shard_map/reduce_scatter | solution.py:890
  1207.6 43.2 %reduce-scatter.32.cloned.1.call-done = f32[256,512]{1,0:T(8,128)} async-done(((f32[1024,512]{1,0:T(8,128)}), f32[256,512]{1,0:T(8,128)}) %reduce-scatter.32.cloned.1.call-update) | async-done | bytes 524304 | tf_op jit(solution)/shard_map/reduce_scatter | solution.py:890
  1252.6 79.8 %all-gather.22.cloned.1.call-done = bf16[4,512,4,192]{3,2,1,0:T(4,128)(2,1)} async-done(((bf16[4,128,4,192]{3,2,1,0:T(4,128)(2,1)}), bf16[4,512,4,192]{3,2,1,0:T(4,128)(2,1)}) %all-gather.22.cloned.1.call-update) | async-done | bytes 3145744 | tf_op jit(solution)/shard_map/all_gather | solution.py:849
  1335.1 58.3 %reduce-scatter.24.cloned.1.call-done = f32[256,768]{1,0:T(8,128)} async-done(((f32[1024,768]{1,0:T(8,128)}), f32[256,768]{1,0:T(8,128)}) %reduce-scatter.24.cloned.1.call-update) | async-done | bytes 786448 | tf_op jit(solution)/shard_map/reduce_scatter | solution.py:890
  1395.8 77.2 %reduce-scatter.30.cloned.1.call-done = f32[256,1024]{1,0:T(8,128)} async-done(((f32[1024,1024]{1,0:T(8,128)}), f32[256,1024]{1,0:T(8,128)}) %reduce-scatter.30.cloned.1.call-update) | async-done | bytes 1048592 | tf_op jit(solution)/shard_map/reduce_scatter | solution.py:890
  1475.7 6.5 copy.149
  (699 shorter events, 140.7 us)
Async XLA Ops:
  7.2 37.5 %all-gather.12.cloned.1.call-start = ((), (), s32[]{:S(2)}) async-start(), calls=%async_computation.12 | async-start | bytes 1474560 | tf_op jit(solution)/shard_map/all_gather | solution.py:814
  9.2 88.0 %all-gather.10.cloned.1.call-start = ((), (), s32[]{:S(2)}) async-start(), calls=%async_computation.11 | async-start | bytes 2621440 | tf_op jit(solution)/shard_map/all_gather | solution.py:837
  21.9 125.9 %all-gather.14.cloned.1.call-start = ((), (), s32[]{:S(2)}) async-start(), calls=%async_computation.13 | async-start | bytes 2621440 | tf_op jit(solution)/shard_map/all_gather | solution.py:814
  22.8 148.5 %all-gather.16.cloned.1.call-start = ((), (), s32[]{:S(2)}) async-start(), calls=%async_computation.14 | async-start | bytes 1310720 | tf_op jit(solution)/shard_map/all_gather | solution.py:814
  46.5 61.6 %collective-permute-start.1 = (bf16[1024,1280]{0,1:T(8,128)(2,1)S(1)}, bf16[1024,1280]{0,1:T(8,128)(2,1)}, u32[]{:S(2)}, u32[]{:S(2)}) collective-permute-start(bf16[1024,1280]{0,1:T(8,128)(2,1)S(1)} %bitcast.288), channel_id=1, source_target_pairs={{0,16},{16,0},{1,17},{17,1},{2,18},{18,2},{3,19},{19,3},{4,20},{20... | collective-permute-start | bytes 7864328 | tf_op jit(solution)/shard_map/ppermute | solution.py:18
  65.3 51.3 %collective-permute-start.2 = (bf16[256,1024]{1,0:T(8,128)(2,1)}, bf16[256,1024]{1,0:T(8,128)(2,1)}, u32[]{:S(2)}, u32[]{:S(2)}) collective-permute-start(bf16[256,1024]{1,0:T(8,128)(2,1)} %pad.69), channel_id=1, source_target_pairs={{0,16},{16,0},{1,17},{17,1},{2,18},{18,2},{3,19},{19,3},{4,20},{20... | collective-permute-start | bytes 1572872 | tf_op jit(solution)/shard_map/ppermute | solution.py:18
  81.6 15.0 %collective-permute-start = (f32[1,1024]{1,0:T(1,128)S(1)}, f32[1,1024]{1,0:T(1,128)S(1)}, u32[]{:S(2)}, u32[]{:S(2)}) collective-permute-start(f32[1,1024]{1,0:T(1,128)S(1)} %all_gather.59), channel_id=1, source_target_pairs={{0,16},{16,0},{1,17},{17,1},{2,18},{18,2},{3,19},{19,3},{4,20},{20... | collective-permute-start | bytes 12296 | tf_op jit(solution)/shard_map/ppermute | solution.py:18
  92.7 116.5 %collective-permute-start.6 = (bf16[16,192,1024]{2,1,0:T(8,128)(2,1)}, bf16[16,192,1024]{2,1,0:T(8,128)(2,1)}, u32[]{:S(2)}, u32[]{:S(2)}) collective-permute-start(bf16[16,192,1024]{2,1,0:T(8,128)(2,1)} %reshape_squeeze.6.win_a), channel_id=1, source_target_pairs={{0,16},{16,0},{1,17},{17,1},{2,18},{18,2},{3,19},{19,3},{4,20},{20... | collective-permute-start | bytes 18874376 | tf_op jit(solution)/shard_map/ppermute | solution.py:18
  93.9 107.5 %reduce-scatter.38.cloned.1.call-start = ((), (), s32[]{:S(2)}) async-start(), calls=%async_computation.26 | async-start | bytes 1310720
  118.4 282.5 %all-gather.20.cloned.1.call-start = ((), (), s32[]{:S(2)}) async-start(), calls=%async_computation.16 | async-start | bytes 2621440 | tf_op jit(solution)/shard_map/all_gather | solution.py:837
  129.2 37.6 %collective-permute-start.3 = (f32[1,1024]{1,0:T(1,128)S(1)}, f32[1,1024]{1,0:T(1,128)}, u32[]{:S(2)}, u32[]{:S(2)}) collective-permute-start(f32[1,1024]{1,0:T(1,128)S(1)} %all_gather.63), channel_id=1, source_target_pairs={{0,16},{16,0},{1,17},{17,1},{2,18},{18,2},{3,19},{19,3},{4,20},{20... | collective-permute-start | bytes 12296 | tf_op jit(solution)/shard_map/ppermute | solution.py:18
  147.8 46.5 %collective-permute-start.8 = (bf16[1024,1024]{1,0:T(8,128)(2,1)}, bf16[1024,1024]{1,0:T(8,128)(2,1)}, u32[]{:S(2)}, u32[]{:S(2)}) collective-permute-start(bf16[1024,1024]{1,0:T(8,128)(2,1)} %all-gather.14.cloned.1.call-done), channel_id=1, source_target_pairs={{0,16},{16,0},{1,17},{17,1},{2,18},{18,2},{3,19},{19,3},{4,20},{20... | collective-permute-start | bytes 6291464 | tf_op jit(solution)/shard_map/ppermute | solution.py:18
  150.8 38.1 %collective-permute-start.4 = (bf16[1024,256]{1,0:T(8,128)(2,1)}, bf16[1024,256]{1,0:T(8,128)(2,1)}, u32[]{:S(2)}, u32[]{:S(2)}) collective-permute-start(bf16[1024,256]{1,0:T(8,128)(2,1)} %pad.72), channel_id=1, source_target_pairs={{0,16},{16,0},{1,17},{17,1},{2,18},{18,2},{3,19},{19,3},{4,20},{20... | collective-permute-start | bytes 1572872 | tf_op jit(solution)/shard_map/ppermute | solution.py:18
  151.3 16.3 %collective-permute-start.5 = (s32[4,512,2]{1,2,0:T(2,128)}, s32[4,512,2]{1,2,0:T(2,128)}, u32[]{:S(2)}, u32[]{:S(2)}) collective-permute-start(s32[4,512,2]{1,2,0:T(2,128)} %bitcast.347), channel_id=1, source_target_pairs={{0,16},{16,0},{1,17},{17,1},{2,18},{18,2},{3,19},{19,3},{4,20},{20... | collective-permute-start | bytes 49160 | tf_op jit(solution)/shard_map/ppermute | solution.py:18
  166.4 260.2 %reduce-scatter.40.cloned.1.call-start = ((), (), s32[]{:S(2)}) async-start(), calls=%async_computation.27 | async-start | bytes 1310720
  166.8 42.4 %collective-permute-start.7 = (bf16[16,192,512]{2,1,0:T(8,128)(2,1)S(1)}, bf16[16,192,512]{2,1,0:T(8,128)(2,1)}, u32[]{:S(2)}, u32[]{:S(2)}) collective-permute-start(bf16[16,192,512]{2,1,0:T(8,128)(2,1)S(1)} %bitcast.271), channel_id=1, source_target_pairs={{0,16},{16,0},{1,17},{17,1},{2,18},{18,2},{3,19},{19,3},{4,20},{20... | collective-permute-start | bytes 9437192 | tf_op jit(solution)/shard_map/ppermute | solution.py:18
  171.3 20.0 %collective-permute-start.9 = (bf16[1024,512]{1,0:T(8,128)(2,1)}, bf16[1024,512]{1,0:T(8,128)(2,1)}, u32[]{:S(2)}, u32[]{:S(2)}) collective-permute-start(bf16[1024,512]{1,0:T(8,128)(2,1)} %all-gather.16.cloned.1.call-done), channel_id=1, source_target_pairs={{0,16},{16,0},{1,17},{17,1},{2,18},{18,2},{3,19},{19,3},{4,20},{20... | collective-permute-start | bytes 3145736 | tf_op jit(solution)/shard_map/ppermute | solution.py:18
  209.2 171.8 %copy-start.99 = (f32[1,1024]{1,0:T(1,128)S(1)}, f32[1,1024]{1,0:T(1,128)}, u32[]{:S(2)}) copy-start(f32[1,1024]{1,0:T(1,128)} %get-tuple-element.162) | copy-start | bytes 12292
  209.2 182.9 %copy-start.7 = (bf16[1024,1280]{0,1:T(8,128)(2,1)S(1)}, bf16[1024,1280]{0,1:T(8,128)(2,1)}, u32[]{:S(2)}) copy-start(bf16[1024,1280]{0,1:T(8,128)(2,1)} %get-tuple-element.136) | copy-start | bytes 7864324
  393.7 346.0 %copy-start.141 = (f32[128]{0:T(128)}, f32[128]{0:T(128)S(1)}, u32[]{:S(2)}) copy-start(f32[128]{0:T(128)S(1)} %get-tuple-element.186) | copy-start | bytes 1540
  393.8 345.9 %copy-start.143 = (f32[128]{0:T(128)}, f32[128]{0:T(128)S(1)}, u32[]{:S(2)}) copy-start(f32[128]{0:T(128)S(1)} %fusion.233) | copy-start | bytes 1540
  394.0 345.9 %copy-start.167 = (f32[128]{0:T(128)}, f32[128]{0:T(128)S(1)}, u32[]{:S(2)}) copy-start(f32[128]{0:T(128)S(1)} %get-tuple-element.188) | copy-start | bytes 1540
  394.1 345.9 %copy-start.169 = (f32[128]{0:T(128)}, f32[128]{0:T(128)S(1)}, u32[]{:S(2)}) copy-start(f32[128]{0:T(128)S(1)} %fusion.235) | copy-start | bytes 1540
  398.8 376.0 %reduce-scatter.42.cloned.1.call-start = ((), (), s32[]{:S(2)}) async-start(), calls=%async_computation.28 | async-start | bytes 1310720
  427.7 299.1 %copy-start.127 = (f32[64]{0:T(128)}, f32[64]{0:T(128)S(1)}, u32[]{:S(2)}) copy-start(f32[64]{0:T(128)S(1)} %rsqrt.69) | copy-start | bytes 772
  584.8 152.9 %copy-start.43 = (bf16[192,1024]{1,0:T(8,128)(2,1)S(1)}, bf16[192,1024]{1,0:T(8,128)(2,1)}, u32[]{:S(2)}) copy-start(bf16[192,1024]{1,0:T(8,128)(2,1)} %copy-done.41) | copy-start | bytes 1179652
  747.5 224.7 %reduce-scatter.44.cloned.1.call-start = ((), (), s32[]{:S(2)}) async-start(), calls=%async_computation.29 | async-start | bytes 1310720
  778.4 147.2 %copy-start.22 = (bf16[64,1024]{1,0:T(8,128)(2,1)S(1)}, bf16[64,1024]{1,0:T(8,128)(2,1)}, u32[]{:S(2)}) copy-start(bf16[64,1024]{1,0:T(8,128)(2,1)} %fusion.108) | copy-start | bytes 393220
  778.4 157.8 %copy-start.44 = (bf16[192,1024]{1,0:T(8,128)(2,1)S(1)}, bf16[192,1024]{1,0:T(8,128)(2,1)}, u32[]{:S(2)}) copy-start(bf16[192,1024]{1,0:T(8,128)(2,1)} %copy-done.41) | copy-start | bytes 1179652
  944.6 83.8 %all-reduce.23.cloned.1.call-start = ((), (), s32[]{:S(2)}) async-start(), calls=%async_computation.20 | async-start | bytes 2097152 | tf_op jit(solution)/shard_map/psum | solution.py:893
  945.5 2.7 collective-permute-start.16
  949.5 166.7 %reduce-scatter.36.cloned.1.call-start = ((), (), s32[]{:S(2)}) async-start(), calls=%async_computation.25 | async-start | bytes 655360
  950.0 1.2 collective-permute-start.15
  950.2 23.2 %collective-permute-start.10 = (bf16[64,1024]{1,0:T(8,128)(2,1)S(1)}, bf16[64,1024]{1,0:T(8,128)(2,1)S(1)}, u32[]{:S(2)}, u32[]{:S(2)}) collective-permute-start(bf16[64,1024]{1,0:T(8,128)(2,1)S(1)} %bitcast_select_fusion), channel_id=1, source_target_pairs={{0,16},{16,0},{1,17},{17,1},{2,18},{18,2},{3,19},{19,3},{4,20},{20... | collective-permute-start | bytes 393224 | tf_op jit(solution)/shard_map/ppermute | solution.py:18
  952.3 164.8 %reduce-scatter.34.cloned.1.call-start = ((), (), s32[]{:S(2)}) async-start(), calls=%async_computation.24 | async-start | bytes 655360
  973.4 1.2 collective-permute-start.12
  975.7 152.1 %reduce-scatter.28.cloned.1.call-start = ((), (), s32[]{:S(2)}) async-start(), calls=%async_computation.21 | async-start | bytes 655360 | tf_op jit(solution)/shard_map/reduce_scatter | solution.py:890
  1030.8 147.4 %all-gather.18.cloned.1.call-start = ((), (), s32[]{:S(2)}) async-start(), calls=%async_computation.15 | async-start | bytes 5242880 | tf_op jit(solution)/shard_map/all_gather | solution.py:849
  1045.0 161.0 %reduce-scatter.26.cloned.1.call-start = ((), (), s32[]{:S(2)}) async-start(), calls=%async_computation.19 | async-start | bytes 1310720 | tf_op jit(solution)/shard_map/reduce_scatter | solution.py:890
  1047.0 2.7 collective-permute-start.14
  1048.7 4.6 collective-permute-start.18
  1051.0 199.8 %reduce-scatter.32.cloned.1.call-start = ((), (), s32[]{:S(2)}) async-start(), calls=%async_computation.23 | async-start | bytes 2621440 | tf_op jit(solution)/shard_map/reduce_scatter | solution.py:890
  1056.7 275.6 %all-gather.22.cloned.1.call-start = ((), (), s32[]{:S(2)}) async-start(), calls=%async_computation.17 | async-start | bytes 5242880 | tf_op jit(solution)/shard_map/all_gather | solution.py:849
  1058.2 1.4 collective-permute-start.11
  1074.9 318.4 %reduce-scatter.24.cloned.1.call-start = ((), (), s32[]{:S(2)}) async-start(), calls=%async_computation.18 | async-start | bytes 3932160 | tf_op jit(solution)/shard_map/reduce_scatter | solution.py:890
  1076.6 5.7 collective-permute-start.13
  1084.6 388.4 %reduce-scatter.30.cloned.1.call-start = ((), (), s32[]{:S(2)}) async-start(), calls=%async_computation.22 | async-start | bytes 5242880 | tf_op jit(solution)/shard_map/reduce_scatter | solution.py:890
  1088.8 7.2 collective-permute-start.17
  (172 other events, 2093.3 us)
Sparse Core Ops, SparseCore 0:
  10.2 34.4 all-gather.11
  46.8 47.7 all-gather.9
  96.2 46.7 all-gather.13
  144.5 26.8 all-gather.15
  174.1 27.2 reduce-scatter.37
  202.8 68.9 all-gather.19
  398.9 27.6 reduce-scatter.39
  747.6 27.0 reduce-scatter.41
  944.7 27.5 reduce-scatter.43
  975.8 52.5 all-reduce.22
  1031.2 21.6 reduce-scatter.35
  1055.6 19.8 reduce-scatter.33
  1077.8 19.8 reduce-scatter.27
  1099.1 79.0 all-gather.17
  1180.3 25.6 reduce-scatter.25
  1208.2 42.5 reduce-scatter.31
  1252.2 80.0 all-gather.21
  1334.5 58.7 reduce-scatter.23
  1396.2 76.7 reduce-scatter.29

commit v2 on v1

--- a/solution.py
+++ b/solution.py
@@ -861,50 +861,42 @@
     x = tokens_in(block_input)
     kept, outs = [], []
     for l in range(2):
-        mid, n2, rx, rows, q, k, v, att = emu_attn_fwd(
-            x, gain[l], wqkv[l], wout[l], fgain[l], rwx[l], cos, sin, mbs, heads, features)
+        mid, n2, rx, rows, q, k, v, att = attn_fwd(
+            x, gain[l], wqkv[l], wout[l], fgain[l], rwx[l], cos, sin, mbs, heads, features, 4)
         out, ff = ff_fwd(l, mid, n2, rx, place[l], win_pair, wdt_pair, sin_w[l], sdt[l], mbs, dims, l)
         kept.append((x, mid, n2, rows, q, k, v, att, ff))
         x = bf(out).astype(jnp.float32)
         outs.append(x)
     g = tokens_in(output_grad)
-    gouts, grads = [None, None], [None, None]
+    gouts = [None, None]
+    dense_grads = tuple(jnp.zeros(v.shape, v.dtype) for v in grad_shapes(experts, width, pw, f))
     expert_grads = (jnp.zeros((experts, width, 2 * f), jnp.float32), jnp.zeros((experts, width, f), jnp.float32))
     for l in (1, 0):
         x, mid, n2, rows, q, k, v, att, ff = kept[l]
         dn2, expert_grads, sin_g, sdt_g, rw_g = ff_bwd(
             l, g, ff, n2, place[l], win_pair, wdt_pair, sin_w[l], sdt[l], rwx[l], expert_grads, mbs, dims, 2 + l)
-        dx, wqkv_g, wout_g, gain_g, fgain_g = emu_attn_bwd(
-            dn2, g, mid, fgain[l], x, gain[l], rows, q, k, v, att, wqkv[l], wout[l], cos, sin, rot, mbs, heads, features)
+        dx, dense_grads = attn_bwd(
+            l, dn2, g, mid, fgain[l], x, gain[l], rows, q, k, v, att, wqkv[l], wout[l], cos, sin, rot,
+            sin_g, sdt_g, rw_g, dense_grads, mbs, heads, features, 5 + l)
         g = bf(dx).astype(jnp.float32)
         gouts[l] = g
-        grads[l] = (gain_g, wqkv_g, wout_g, fgain_g, rw_g, sin_g.astype(jnp.float32), sdt_g.astype(jnp.float32))
-
-    own = [jnp.where(s == 0, p, q_) for p, q_ in zip(*grads)]
-    other = [jnp.where(s == 0, q_, p) for p, q_ in zip(*grads)]
-    own = [p + pass_section(q_) for p, q_ in zip(own, other)]
-    gain_g, wqkv_g, wout_g, fgain_g, rw_g, sin_g, sdt_g = own
+
+    wqkv_g, wout_g, sin_g, sdt_g, small_g = dense_grads
     win_g, wdt_g = expert_grads
 
-    def narrow(v, axis):
-        v = lax.psum_scatter(v, "gy", scatter_dimension=axis, tiled=True)
-        return lax.slice_in_dim(v, 0, width, axis=axis)
-
-    gain_g, fgain_g, rw_g = lax.psum((gain_g, fgain_g, rw_g), "gx")
-    rw_g = rw_g[:, width : width + experts] + rw_g[:, width + experts : width + 2 * experts]
     hd = heads * DH
     return (
         tokens_out(outs),
         tokens_out(gouts),
-        narrow(gain_g, 1),
-        narrow(wqkv_g, 0).reshape(width, 3, pw)[..., :hd][None],
-        narrow(wout_g, 1)[:hd][None],
-        narrow(fgain_g, 1),
-        narrow(rw_g, 0)[None],
+        small_g[experts + 1 : experts + 2, :width],
+        wqkv_g.reshape(width, 3, pw)[..., :hd][None],
+        wout_g[:hd, :width][None],
+        small_g[experts : experts + 1, :width],
+        small_g[:experts, :width].T[None],
         win_g.reshape(experts, width, 2, f)[None],
         wdt_g.transpose(0, 2, 1)[None],
-        narrow(sin_g, 0).reshape(width, 2, f)[None],
-        narrow(sdt_g, 0).T[None],
+        sin_g.reshape(width, 2, f)[None],
+        sdt_g.T[None],
     )
 
 
@@ -1474,7 +1466,8 @@
     for j in range(ny):
         out[:, j * pw : (j + 1) * pw] = total[:, j * pw : (j + 1) * pw] + parts[j]
     n2v = n2[...].reshape(mbs * sub, d)
-    rw_g[...] = mm(n2v, hi, ((0,), (0,))) + mm(n2v, lo, ((0,), (0,)))
+    rw_t = mm(hi, n2v, ((0,), (0,))) + mm(lo, n2v, ((0,), (0,)))
+    rw_g[...] = rw_t[width : width + experts] + rw_t[width + experts : width + 2 * experts]
 
     def finish(e, c):
         for m in range(mbs):
@@ -1521,7 +1514,7 @@
         functools.partial(ff_bwd_kernel, cfg),
         out_shape=(
             jax.ShapeDtypeStruct((mbs * sub, d), f32),
-            jax.ShapeDtypeStruct((d, pw), f32),
+            jax.ShapeDtypeStruct((experts, d), f32),
             jax.ShapeDtypeStruct((d, 2 * f), b16),
             jax.ShapeDtypeStruct((d, f), b16),
             jax.ShapeDtypeStruct((experts, width, 2 * f), f32),
@@ -1573,6 +1566,333 @@
 BWD_SKEW = (2, 2)
 
 
+def attn_fwd_kernel(cfg, x, gain, fgain, wqkv, wout, rwx, cos, sin,
+                    mid, n2, rx, rows_o, q, k, v, att,
+                    nsend, nall, proj, osend, orecv, n_send, n_recv, o_send, o_recv):
+    nx, ny, mbs, sub, pw, heads, features = cfg
+    pos = Position(nx, ny)
+    s, a, b = pos.s, pos.a, pos.b
+    d = ny * pw
+    length = nx * sub
+    barrier = pltpu.get_barrier_semaphore()
+    pos.peers(lambda ai: pl.semaphore_signal(barrier, inc=1, device_id=(s, ai, b), device_id_type=MESH))
+    xv = x[...].reshape(mbs * sub, d)
+    nsend[...] = bf(xv * rms(xv, features) * gain[...]).reshape(mbs, sub, d)
+    pl.semaphore_wait(barrier, nx - 1)
+
+    def copy_n(ai, slot):
+        return remote(nsend, nall.at[:, slot], n_send.at[ai], n_recv.at[slot], (s, ai, b))
+
+    pos.peers(lambda ai: copy_n(ai, a).start())
+    nall[:, a] = nsend[...]
+    pos.peers(lambda ai: copy_n(ai, ai).wait())
+    rows = nall[...].reshape(mbs * length, d)
+    proj[...] = mm(rows, wqkv[...])
+    rows_o[...] = nall[...]
+    v[...] = bf(proj[:, 2 * pw : 3 * pw])
+    for m in range(mbs):
+        rs = slice(m * length, (m + 1) * length)
+        q[rs] = bf(proj[rs, :pw] * cos[...] + proj[rs, 3 * pw : 4 * pw] * sin[...])
+        k[rs] = bf(proj[rs, pw : 2 * pw] * cos[...] + proj[rs, 4 * pw : 5 * pw] * sin[...])
+        acc = jnp.zeros((length, pw), jnp.float32)
+        for h in range(heads):
+            mask = head_mask(pw, h)
+            p = probs_of(jnp.where(mask, q[rs], 0), k[rs])
+            acc = acc + mm(bf(p), jnp.where(mask, v[rs], 0))
+        att[rs] = bf(acc)
+    osend[...] = bf(mm(att[...], wout[...])).reshape(mbs, nx, sub, d)
+
+    def copy_o(ai, slot):
+        return remote(osend.at[:, ai], orecv.at[slot], o_send.at[ai], o_recv.at[slot], (s, ai, b))
+
+    pos.peers(lambda ai: copy_o(ai, a).start())
+    orecv[a] = osend[:, a]
+    pos.peers(lambda ai: copy_o(ai, ai).wait())
+    mv = x[...]
+    for ai in range(nx):
+        mv = mv + orecv[ai].astype(jnp.float32)
+    mv = mv.reshape(mbs * sub, d)
+    mid[...] = mv
+    n2v = bf(mv * rms(mv, features) * fgain[...])
+    n2[...] = n2v
+    rx[...] = mm(n2v, rwx[...])
+
+
+def attn_fwd(x, gain, wqkv, wout, fgain, rwx, cos, sin, mbs, heads, features, ids):
+    nx, ny = lax.axis_size("gx"), lax.axis_size("gy")
+    pw = cos.shape[1]
+    d = ny * pw
+    sub = x.shape[0] // mbs
+    length = nx * sub
+    b16, f32 = jnp.bfloat16, jnp.float32
+    dma = pltpu.SemaphoreType.DMA
+    vm = pl.BlockSpec(memory_space=pltpu.VMEM)
+    outs = pl.pallas_call(
+        functools.partial(attn_fwd_kernel, (nx, ny, mbs, sub, pw, heads, features)),
+        out_shape=(
+            jax.ShapeDtypeStruct((mbs * sub, d), f32),
+            jax.ShapeDtypeStruct((mbs * sub, d), b16),
+            jax.ShapeDtypeStruct((mbs * sub, pw), f32),
+            jax.ShapeDtypeStruct((mbs, nx, sub, d), b16),
+            jax.ShapeDtypeStruct((mbs * length, pw), b16),
+            jax.ShapeDtypeStruct((mbs * length, pw), b16),
+            jax.ShapeDtypeStruct((mbs * length, pw), b16),
+            jax.ShapeDtypeStruct((mbs * length, pw), b16),
+        ),
+        in_specs=[vm] * 8,
+        out_specs=(vm,) * 8,
+        scratch_shapes=[
+            pltpu.VMEM((mbs, sub, d), b16),
+            pltpu.VMEM((mbs, nx, sub, d), b16),
+            pltpu.VMEM((mbs * length, 5 * pw), f32),
+            pltpu.VMEM((mbs, nx, sub, d), b16),
+            pltpu.VMEM((nx, mbs, sub, d), b16),
+            dma((nx,)), dma((nx,)), dma((nx,)), dma((nx,)),
+        ],
+        compiler_params=pltpu.CompilerParams(collective_id=ids, has_side_effects=True, vmem_limit_bytes=VMEM_BYTES),
+        cost_estimate=pl.CostEstimate(flops=10**9, bytes_accessed=10**7, transcendentals=10**6),
+        name="attention_forward",
+    )(x.reshape(mbs, sub, d), gain, fgain, wqkv, wout, rwx, cos, sin)
+    mid, n2, rx, rows, q, k, v, att = outs
+    return mid, n2, rx, rows.reshape(mbs * length, d), q, k, v, att
+
+
+def attn_bwd_kernel(cfg, dn2, g, mid, x, gain, fgain, rows, q, k, v, att, wqkv, wout, cos, sin, rot,
+                    sin_p, sdt_p, rw_p, wqkv_i, wout_i, sin_i, sdt_i, small_i,
+                    dx_o, wqkv_o, wout_o, sin_o, sdt_o, small_o,
+                    msend, mall, dqkv, dsend, drecv, datt,
+                    wqkv_p, wout_p, small_p, wqkv_x, wout_x, sin_x, sdt_x, small_x,
+                    wqkv_t, wout_t, sin_t, sdt_t, small_t, wqkv_r, wout_r, sin_r, sdt_r, small_r,
+                    wqkv_f, wout_f, sin_f, sdt_f, small_f, small_a,
+                    m_send, m_recv, d_send, d_recv, c_send, c_recv, r_send, r_recv, a_send, a_recv, f_sem):
+    layer, nx, ny, mbs, sub, width, pw, heads, features, experts = cfg
+    pos = Position(nx, ny)
+    s, a, b = pos.s, pos.a, pos.b
+    keeper = s == layer
+    helper = jnp.logical_not(keeper)
+    d = ny * pw
+    length = nx * sub
+    scale = DH ** -0.5
+    barrier = pltpu.get_barrier_semaphore()
+    pos.peers(lambda ai: pl.semaphore_signal(barrier, inc=1, device_id=(s, ai, b), device_id_type=MESH))
+
+    def line(do):
+        for i in range(1, ny):
+            do(lax.rem(b + i, ny))
+
+    @pl.when(keeper)
+    def _():
+        line(lambda bi: pl.semaphore_signal(barrier, inc=1, device_id=(s, a, bi), device_id_type=MESH))
+        pl.semaphore_signal(barrier, inc=1, device_id=(1 - s, a, b), device_id_type=MESH)
+
+    xv = x[...]
+    mv = mid[...]
+    dx2, fgain_g = norm_back(mv, rms(mv, features), fgain[...], dn2[...], features)
+    dm = g[...] + dx2
+    msend[...] = bf(dm).reshape(mbs, sub, d)
+    dx_o[...] = dm
+
+    @pl.when(keeper)
+    def _():
+        pl.semaphore_wait(barrier, nx - 1 + ny - 1)
+
+    @pl.when(helper)
+    def _():
+        pl.semaphore_wait(barrier, nx)
+
+    def copy_m(ai, slot):
+        return remote(msend, mall.at[:, slot], m_send.at[ai], m_recv.at[slot], (s, ai, b))
+
+    pos.peers(lambda ai: copy_m(ai, a).start())
+
+    crossing = ((sin_p, sin_x), (sdt_p, sdt_x), (wqkv_p, wqkv_x), (wout_p, wout_x), (small_p, small_x))
+
+    def cross(i):
+        return remote(crossing[i][0], crossing[i][1], c_send.at[i], c_recv.at[i], (layer, a, b))
+
+    def rows_of(ref, bi, n):
+        return ref.at[pl.ds(pl.multiple_of(bi * pw, pw), n)]
+
+    def lanes_of(ref, bi):
+        return ref.at[:, pl.ds(pl.multiple_of(bi * pw, pw), pw)]
+
+    blocks = (
+        lambda bi: rows_of(sin_t, bi, width), lambda bi: rows_of(sdt_t, bi, width),
+        lambda bi: rows_of(wqkv_t, bi, width), lambda bi: lanes_of(wout_t, bi), lambda bi: lanes_of(small_t, bi),
+    )
+    totals = (sin_t, sdt_t, wqkv_t, wout_t, small_t)
+    places = (sin_r, sdt_r, wqkv_r, wout_r, small_r)
+    finals = (sin_f, sdt_f, wqkv_f, wout_f, small_f)
+    results = (sin_o, sdt_o, wqkv_o, wout_o, small_o)
+
+    def spread(i, bi, slot):
+        return remote(blocks[i](bi), places[i].at[slot], r_send.at[i, bi], r_recv.at[i, slot], (s, a, bi))
+
+    def join(i):
+        cross(i).wait_recv()
+        part, other = crossing[i]
+        totals[i][...] = (part[...].astype(jnp.float32) + other[...].astype(jnp.float32)).astype(totals[i].dtype)
+        line(lambda bi: spread(i, bi, b).start())
+
+    @pl.when(helper)
+    def _():
+        cross(0).start()
+        cross(1).start()
+
+    mall[:, a] = msend[...]
+    pos.peers(lambda ai: copy_m(ai, ai).wait())
+    dmr = mall[...].reshape(mbs * length, d)
+    datt[...] = bf(mm(dmr, wout[...], ((1,), (1,))))
+    wout_p[...] = bf(mm(att[...], dmr, ((0,), (0,))))
+
+    @pl.when(keeper)
+    def _():
+        join(0)
+        join(1)
+
+    def back(t):
+        hi = bf(t)
+        lo = bf(t - hi.astype(jnp.float32))
+        return bf(t * cos[...] - (mm(hi, rot[...]) + mm(lo, rot[...])) * sin[...])
+
+    for m in range(mbs):
+        rs = slice(m * length, (m + 1) * length)
+        dq = jnp.zeros((length, pw), jnp.float32)
+        dk = dq
+        dv = dq
+        for h in range(heads):
+            mask = head_mask(pw, h)
+            qh = jnp.where(mask, q[rs], 0)
+            kh = jnp.where(mask, k[rs], 0)
+            da = jnp.where(mask, datt[rs], 0)
+            p = probs_of(qh, k[rs])
+            dp = mm(da, v[rs], ((1,), (1,)))
+            ds = bf(p * (dp - jnp.sum(dp * p, axis=1, keepdims=True)))
+            dv = dv + mm(bf(p), da, ((0,), (0,)))
+            dq = dq + mm(ds, kh)
+            dk = dk + mm(ds, qh, ((0,), (0,)))
+        dqkv[rs, :pw] = back(dq * scale)
+        dqkv[rs, pw : 2 * pw] = back(dk * scale)
+        dqkv[rs, 2 * pw :] = bf(dv)
+    dsend[...] = bf(mm(dqkv[...], wqkv[:, : 3 * pw], ((1,), (1,)))).reshape(mbs, nx, sub, d)
+
+    def copy_d(ai, slot):
+        return remote(dsend.at[:, ai], drecv.at[slot], d_send.at[ai], d_recv.at[slot], (s, ai, b))
+
+    pos.peers(lambda ai: copy_d(ai, a).start())
+    drecv[a] = dsend[:, a]
+    wqkv_p[...] = bf(mm(rows[...], dqkv[...], ((0,), (0,))))
+
+    @pl.when(helper)
+    def _():
+        cross(2).start()
+        cross(3).start()
+
+    pos.peers(lambda ai: copy_d(ai, ai).wait())
+    dn1 = drecv[0].astype(jnp.float32)
+    for ai in range(1, nx):
+        dn1 = dn1 + drecv[ai].astype(jnp.float32)
+    dn1 = dn1.reshape(mbs * sub, d)
+    dx1, gain_g = norm_back(xv, rms(xv, features), gain[...], dn1, features)
+    dx_o[...] += dx1
+    small_p[: experts] = rw_p[...]
+    row = lax.broadcasted_iota(jnp.int32, (8, d), 0)
+    small_p[experts:] = jnp.where(row == 0, fgain_g, jnp.where(row == 1, gain_g, 0.0))
+
+    @pl.when(helper)
+    def _():
+        cross(4).start()
+        for i in range(5):
+            cross(i).wait_send()
+
+    @pl.when(keeper)
+    def _():
+        join(2)
+        join(3)
+        join(4)
+        for i in range(5):
+            line(lambda bi: spread(i, bi, bi).wait())
+            total = blocks[i](b)[...].astype(jnp.float32)
+            for k in range(1, ny):
+                total = total + places[i][lax.rem(b + k, ny)].astype(jnp.float32)
+            finals[i][...] = total
+            if i < 4:
+                pltpu.make_async_copy(finals[i], results[i], f_sem.at[i]).start()
+
+        def copy_a(ai, slot):
+            return remote(small_f, small_a.at[slot], a_send.at[ai], a_recv.at[slot], (s, ai, b))
+
+        pos.peers(lambda ai: copy_a(ai, a).start())
+        small_a[a] = small_f[...]
+        pos.peers(lambda ai: copy_a(ai, ai).wait())
+        total = small_a[0]
+        for ai in range(1, nx):
+            total = total + small_a[ai]
+        small_f[...] = total
+        pltpu.make_async_copy(small_f, small_o, f_sem.at[4]).start()
+        for i in range(5):
+            pltpu.make_async_copy(finals[i], results[i], f_sem.at[i]).wait()
+
+
+def grad_shapes(experts, width, pw, f):
+    return (
+        jax.ShapeDtypeStruct((width, 3 * pw), jnp.float32),
+        jax.ShapeDtypeStruct((pw, pw), jnp.float32),
+        jax.ShapeDtypeStruct((width, 2 * f), jnp.float32),
+        jax.ShapeDtypeStruct((width, f), jnp.float32),
+        jax.ShapeDtypeStruct((experts + 8, pw), jnp.float32),
+    )
+
+
+def attn_bwd(layer, dn2, g, mid, fgain, x, gain, rows, q, k, v, att, wqkv, wout, cos, sin, rot,
+             sin_g, sdt_g, rw_g, grads, mbs, heads, features, ids):
+    nx, ny = lax.axis_size("gx"), lax.axis_size("gy")
+    pw = cos.shape[1]
+    d = ny * pw
+    width = features // ny
+    sub = x.shape[0] // mbs
+    length = nx * sub
+    f = sdt_g.shape[1]
+    experts = rw_g.shape[0]
+    b16, f32 = jnp.bfloat16, jnp.float32
+    dma = pltpu.SemaphoreType.DMA
+    vm = pl.BlockSpec(memory_space=pltpu.VMEM)
+    hbm = pl.BlockSpec(memory_space=pl.ANY)
+    shapes = grad_shapes(experts, width, pw, f)
+    n = experts + 8
+    outs = pl.pallas_call(
+        functools.partial(attn_bwd_kernel, (layer, nx, ny, mbs, sub, width, pw, heads, features, experts)),
+        out_shape=(jax.ShapeDtypeStruct((mbs * sub, d), f32),) + shapes,
+        in_specs=[vm] * 19 + [hbm] * 5,
+        out_specs=(vm,) + (hbm,) * 5,
+        scratch_shapes=[
+            pltpu.VMEM((mbs, sub, d), b16),
+            pltpu.VMEM((mbs, nx, sub, d), b16),
+            pltpu.VMEM((mbs * length, 3 * pw), b16),
+            pltpu.VMEM((mbs, nx, sub, d), b16),
+            pltpu.VMEM((nx, mbs, sub, d), b16),
+            pltpu.VMEM((mbs * length, pw), b16),
+            pltpu.VMEM((d, 3 * pw), b16), pltpu.VMEM((pw, d), b16), pltpu.VMEM((n, d), f32),
+            pltpu.VMEM((d, 3 * pw), b16), pltpu.VMEM((pw, d), b16), pltpu.VMEM((d, 2 * f), b16),
+            pltpu.VMEM((d, f), b16), pltpu.VMEM((n, d), f32),
+            pltpu.VMEM((d, 3 * pw), b16), pltpu.VMEM((pw, d), b16), pltpu.VMEM((d, 2 * f), b16),
+            pltpu.VMEM((d, f), b16), pltpu.VMEM((n, d), f32),
+            pltpu.VMEM((ny, width, 3 * pw), b16), pltpu.VMEM((ny, pw, pw), b16), pltpu.VMEM((ny, width, 2 * f), b16),
+            pltpu.VMEM((ny, width, f), b16), pltpu.VMEM((ny, n, pw), f32),
+            pltpu.VMEM((width, 3 * pw), f32), pltpu.VMEM((pw, pw), f32), pltpu.VMEM((width, 2 * f), f32),
+            pltpu.VMEM((width, f), f32), pltpu.VMEM((n, pw), f32),
+            pltpu.VMEM((nx, n, pw), f32),
+            dma((nx,)), dma((nx,)), dma((nx,)), dma((nx,)), dma((5,)), dma((5,)),
+            dma((5, ny)), dma((5, ny)), dma((nx,)), dma((nx,)), dma((5,)),
+        ],
+        input_output_aliases={19 + i: 1 + i for i in range(5)},
+        compiler_params=pltpu.CompilerParams(collective_id=ids, has_side_effects=True, vmem_limit_bytes=VMEM_BYTES),
+        cost_estimate=pl.CostEstimate(flops=2 * 10**9, bytes_accessed=2 * 10**7, transcendentals=10**6),
+        name="attention_backward",
+    )(dn2, g, mid, x, gain, fgain, rows, q, k, v, att, wqkv, wout, cos, sin, rot, sin_g, sdt_g, rw_g, *grads)
+    return outs[0], outs[1:]
+
+
 def solution(mesh):
     in_specs = (
         P(None, "gx", "gy"),

time: 1500 us -> 1130 us (0.75)
  waiting for transfers between devices: 504 us -> 91.3 us
  Pallas kernels: 598 us -> 788 us
  blocking collectives: 160 us -> 104 us
  matrix products: 31.2 us -> 0.6 us
  other arithmetic: 63.5 us -> 33.3 us
  local copies, waits for them, and re-layouts: 110 us -> 93.7 us
    reduce_scatter x5 -> x0, waiting for transfers between devices: 204 us -> none  [narrow(): v = lax.psum_scatter(v, 'gy', scatter_dimension=axis, tiled=True)]
    pallas_call x0 -> x4, Pallas kernels: none -> 137 us  [the longest x2 93.5 us: attn_bwd(): pl.pallas_call(functools.partial(attn_bwd_kernel, (layer, nx, ny, mbs, su...]
    pallas_call x2, Pallas kernels: 285 us -> 365 us  [ff_bwd(): pl.pallas_call(functools.partial(ff_bwd_kernel, cfg), out_shape=(jax.Shap...]
    unnamed x25 -> x7, waiting for transfers between devices: 74.6 us -> 0.12 us
    all_gather x2, waiting for transfers between devices: 129 us -> 54.7 us  [tokens_out(): t = lax.all_gather(t, 'gy', axis=1, tiled=True)]
    psum x1 -> x0, waiting for transfers between devices: 52.6 us -> none  [fast_device(): gain_g, fgain_g, rw_g = lax.psum((gain_g, fgain_g, rw_g), 'gx')]
    all_gather x4 -> x0, blocking collectives: 38.8 us -> none  [emu_gather_gx(): g = lax.all_gather(v.reshape(mbs, rows, -1), 'gx')]
    all_gather x2, waiting for transfers between devices: 0.01 us -> 33.1 us  [tokens_in(): t = lax.all_gather(pad_to(t, 2, pw), 'gy', axis=2, tiled=True)]
  transfers between devices with their start and end apart: 38 -> 19, of which waited for: 21 -> 6; matrix products, arithmetic and copies ran while one was open for 10% -> 10% of each run, Pallas kernels for 11% -> 70%
where the time goes in v2:
time: 1130 us
  Pallas kernels  788 us (70%)
  blocking collectives  104 us (9%)
  local copies, waits for them, and re-layouts  93.7 us (8%)
  waiting for transfers between devices  91.3 us (8%)
  other arithmetic  33.3 us (3%)
  between operations  15.1 us (1%)
    pallas_call x2, Pallas kernels, ff_bwd(): pl.pallas_call(functools.partial(ff_bwd_kernel, cfg), out_shape=(jax.Shap...  365 us
    pallas_call x2, Pallas kernels, ff_fwd(): pl.pallas_call(functools.partial(ff_fwd_kernel, cfg), out_shape=(jax.Shap...  286 us
    pallas_call x2, Pallas kernels, attn_bwd(): pl.pallas_call(functools.partial(attn_bwd_kernel, (layer, nx, ny, mbs, su...  93.5 us
    all_gather x2, waiting for transfers between devices, tokens_out(): t = lax.all_gather(t, 'gy', axis=1, tiled=True)  54.7 us
    all_gather x4, blocking collectives, wide(): return lax.all_gather(v, 'gy', axis=axis, tiled=True)  52.9 us
    pallas_call x2, Pallas kernels, attn_fwd(): pl.pallas_call(functools.partial(attn_fwd_kernel, (nx, ny, mbs, sub, pw,...  43.4 us
    all_gather x2, waiting for transfers between devices, tokens_in(): t = lax.all_gather(pad_to(t, 2, pw), 'gy', axis=2, tiled=True)  33.1 us
    all_gather x2, blocking collectives, tokens_out(): t = lax.all_gather(t, 'gx', axis=1, tiled=True)  29.1 us
  transfers between devices with their start and end apart: 19, of which 6 were waited for; matrix products, arithmetic and copies ran while one was open for 10% of the time, Pallas kernels for 70%

profile of v2, /device:TPU:0, one launch (start us, length us, event | category | flops | bytes accessed | tf_op | source)
XLA Modules:
  0.0 1127.9 jit_solution(2934860929877927124)
XLA Ops:
  9.2 1.6 pad.74
  13.1 11.5 %all_gather.45 = bf16[2,512,192]{2,1,0:T(8,128)(2,1)S(1)} all-gather(bf16[2,128,192]{2,1,0:T(8,128)(2,1)S(1)} %copy.108), channel_id=1, replica_groups=mesh['section'=2,'gx'=4,'gy'=4] {'gx'}, dimensions={1}, use_global_device_ids=true | all-gather | bytes 491520 | tf_op jit(solution)/shard_map/all_gather | solution.py:836
  25.6 11.1 reshape_squeeze.6.win_a
  36.7 11.2 all_gather.47
  47.9 7.6 all_gather.48
  55.5 18.3 %all_gather.50 = bf16[192,1024]{1,0:T(8,128)(2,1)S(1)} all-gather(bf16[192,256]{1,0:T(8,128)(2,1)S(1)} %pad.67), channel_id=1, replica_groups=mesh['section'=2,'gx'=4,'gy'=4] {'gy'}, dimensions={1}, use_global_device_ids=true | all-gather | bytes 491520 | tf_op jit(solution)/shard_map/all_gather | solution.py:814
  75.6 10.7 all_gather.56
  87.4 15.8 %all_gather.51 = bf16[1024,16]{1,0:T(8,128)(2,1)S(1)} all-gather(bf16[256,16]{1,0:T(8,128)(2,1)S(1)} %pad.69), channel_id=1, replica_groups=mesh['section'=2,'gx'=4,'gy'=4] {'gy'}, dimensions={0}, use_global_device_ids=true | all-gather | bytes 40960 | tf_op jit(solution)/shard_map/all_gather | solution.py:814
  104.3 1.3 slice.59
  105.9 1.8 fusion.5
  107.7 4.8 copy.92
  112.6 2.0 pad.70
  118.6 1.3 copy.97
  120.0 1.4 copy.96
  121.3 1.8 eq.16
  123.7 2.1 convert_element_type.141
  126.2 2.6 add_bitcast_fusion
  129.9 2.6 slice_bitcast_fusion.1
  132.5 1.8 copy.98.place
  134.3 1.8 copy.100.place
  136.1 2.5 broadcast_select_fusion.8
  138.7 2.4 broadcast_select_fusion.6
  141.1 2.8 broadcast_select_fusion.4
  143.9 33.1 %all-gather.8.cloned.1.call-done = bf16[2,512,1024]{2,1,0:T(8,128)(2,1)} async-done(((bf16[2,512,256]{2,1,0:T(8,128)(2,1)}), bf16[2,512,1024]{2,1,0:T(8,128)(2,1)}) %all-gather.8.cloned.1.call-update) | async-done | bytes 2097168 | tf_op jit(solution)/shard_map/all_gather | solution.py:837
  176.9 1.6 dynamic-slice_convert_fusion.x
  178.6 5.2 broadcast_select_fusion
  183.8 23.5 %attention_forward.2 = (f32[64,1024]{1,0:T(8,128)}, bf16[64,1024]{1,0:T(8,128)(2,1)}, f32[64,256]{1,0:T(8,128)}, bf16[2,4,32,1024]{3,2,1,0:T(8,128)(2,1)}, bf16[...) custom-call(f32[2,32,1024]{2,1,0:T(8,128)} %dynamic-slice_convert_fusion.x,, ...), custom_call_target="tpu_custom_call" | custom-call | flops 1000000000 | bytes 10000000 | tf_op jit(solution)/shard_map/attention_forward/pallas_call | solution.py:1630
  207.3 4.5 broadcast_select_fusion.2
  211.8 148.1 %experts_forward.2 = (f32[2,32,1024]{2,1,0:T(8,128)}, bf16[2,16,80,256]{3,2,1,0:T(8,128)(2,1)}, bf16[2,16,80,1024]{3,2,1,0:T(8,128)(2,1)}, bf16[2,16,80,512]{3,2...) custom-call(f32[2,32,1024]{2,1,0:T(8,128)} %bitcast.107, ...), custom_call_target="tpu_custom_call" | custom-call | flops 4000000000 | bytes 30000000 | tf_op jit(solution)/shard_map/experts_forward/pallas_call | solution.py:1171
  359.9 1.7 convert_convert_fusion.1.x
  361.5 19.9 %attention_forward.3 = (f32[64,1024]{1,0:T(8,128)}, bf16[64,1024]{1,0:T(8,128)(2,1)}, f32[64,256]{1,0:T(8,128)}, bf16[2,4,32,1024]{3,2,1,0:T(8,128)(2,1)}, bf16[...) custom-call(f32[2,32,1024]{2,1,0:T(8,128)} %convert_convert_fusion.1.x, ...), custom_call_target="tpu_custom_call" | custom-call | flops 1000000000 | bytes 10000000 | tf_op jit(solution)/shard_map/attention_forward/pallas_call | solution.py:1630
  381.5 138.3 %experts_forward.3 = (f32[2,32,1024]{2,1,0:T(8,128)}, bf16[2,16,80,256]{3,2,1,0:T(8,128)(2,1)}, bf16[2,16,80,1024]{3,2,1,0:T(8,128)(2,1)}, bf16[2,16,80,512]{3,2...) custom-call(f32[2,32,1024]{2,1,0:T(8,128)} %bitcast.108, ...), custom_call_target="tpu_custom_call" | custom-call | flops 4000000000 | bytes 30000000 | tf_op jit(solution)/shard_map/experts_forward/pallas_call | solution.py:1171
  522.5 14.6 %all_gather.54 = bf16[4,128,4,192]{3,2,1,0:T(4,128)(2,1)} all-gather(bf16[4,32,4,192]{3,2,1,0:T(4,128)(2,1)S(1)} %bitcast.109), channel_id=1, replica_groups=mesh['section'=2,'gx'=4,'gy'=4] {'gx'}, dimensions={1}, use_global_device_ids=true | all-gather | bytes 983040 | tf_op jit(solution)/shard_map/all_gather | solution.py:848
  539.9 6.7 broadcast_in_dim.52.win_g_i
  546.6 3.5 broadcast_in_dim.53.wdt_g_i
  550.1 196.8 %experts_backward.2 = (f32[64,1024]{1,0:T(8,128)}, f32[16,1024]{1,0:T(8,128)}, bf16[1024,1024]{1,0:T(8,128)(2,1)}, bf16[1024,512]{1,0:T(8,128)(2,1)}, f32[16,192,1024]{2,1,0:T(8,128)}, /*index=5*/f32[16,192,512]{2,1,0:T(8,128)}) custom-call(bf16[2,32,1024]{2,1,0:T(8,128)(2,1)} %copy-done.10, ...), custom_call_target="tpu_custom_call", output_to_operand_aliasing={{4}: (17, {}), {5}: (18, {})} | custom-call | flops 8000000000 | bytes 60000000 | tf_op jit(solution)/shard_map/experts_backward/pallas_call | solution.py:1513
  750.9 27.5 %attention_backward.2 = (f32[64,1024]{1,0:T(8,128)}, f32[192,768]{1,0:T(8,128)}, f32[256,256]{1,0:T(8,128)}, f32[192,1024]{1,0:T(8,128)}, f32[192,512]{1,0:T(8,128)}, /*index=5*/f32[24,256]{1,0:T(8,128)}) custom-call(f32[64,1024]{1,0:T(8,128)} %get-tuple-element.79.dn2, ...), custom_call_target="tpu_custom_call", output_to_operand_aliasing={{1}: (19, {}), {2}: (20, {}), {3}: (21, {}), {4}: (22, {}),... | custom-call | flops 2000000000 | bytes 20000000 | tf_op jit(solution)/shard_map/attention_backward/pallas_call | solution.py:1863
  778.4 1.7 fusion.24
  780.1 167.8 %experts_backward.3 = (f32[64,1024]{1,0:T(8,128)}, f32[16,1024]{1,0:T(8,128)}, bf16[1024,1024]{1,0:T(8,128)(2,1)}, bf16[1024,512]{1,0:T(8,128)(2,1)}, f32[16,192,1024]{2,1,0:T(8,128)}, /*index=5*/f32[16,192,512]{2,1,0:T(8,128)}) custom-call(bf16[2,32,1024]{2,1,0:T(8,128)(2,1)} %bitcast.105, ...), custom_call_target="tpu_custom_call", output_to_operand_aliasing={{4}: (17, {}), {5}: (18, {})} | custom-call | flops 8000000000 | bytes 60000000 | tf_op jit(solution)/shard_map/experts_backward/pallas_call | solution.py:1513
  948.0 66.0 %attention_backward.3 = (f32[64,1024]{1,0:T(8,128)}, f32[192,768]{1,0:T(8,128)}, f32[256,256]{1,0:T(8,128)}, f32[192,1024]{1,0:T(8,128)}, f32[192,512]{1,0:T(8,128)}, /*index=5*/f32[24,256]{1,0:T(8,128)}) custom-call(f32[64,1024]{1,0:T(8,128)} %get-tuple-element.97.dn2, ...), custom_call_target="tpu_custom_call", output_to_operand_aliasing={{1}: (19, {}), {2}: (20, {}), {3}: (21, {}), {4}: (22, {}),... | custom-call | flops 2000000000 | bytes 20000000 | tf_op jit(solution)/shard_map/attention_backward/pallas_call | solution.py:1863
  1015.1 1.3 collective-permute-done.11
  1016.7 14.5 %all_gather.58 = bf16[4,128,4,192]{3,2,1,0:T(4,128)(2,1)} all-gather(bf16[4,32,4,192]{3,2,1,0:T(4,128)(2,1)S(1)} %bitcast.110), channel_id=1, replica_groups=mesh['section'=2,'gx'=4,'gy'=4] {'gx'}, dimensions={1}, use_global_device_ids=true | all-gather | bytes 983040 | tf_op jit(solution)/shard_map/all_gather | solution.py:848
  1032.6 17.1 %broadcast_in_dim_reshape.7 = f32[1,16,192,2,512]{4,3,2,1,0:T(2,128)} reshape(f32[16,192,1024]{2,1,0:T(8,128)} %get-tuple-element.115) | data formatting | bytes 25165824 | tf_op jit(solution)/shard_map/broadcast_in_dim;reshape | solution.py:896
  1049.7 1.5 broadcast_in_dim_reshape.8
  1053.1 1.8 constant_dynamic-slice_fusion.3
  1055.8 54.7 %all-gather.20.cloned.1.call-done = bf16[4,512,4,192]{3,2,1,0:T(4,128)(2,1)} async-done(((bf16[4,128,4,192]{3,2,1,0:T(4,128)(2,1)}), bf16[4,512,4,192]{3,2,1,0:T(4,128)(2,1)}) %all-gather.20.cloned.1.call-update) | async-done | bytes 3145744 | tf_op jit(solution)/shard_map/all_gather | solution.py:849
  1110.6 1.8 constant_dynamic-slice_fusion
  1113.3 6.5 copy.127
  (149 shorter events, 32.2 us)
Async XLA Ops:
  7.2 5.8 copy-start
  7.2 97.1 %all-gather.10.cloned.1.call-start = ((), (), s32[]{:S(2)}) async-start(), calls=%async_computation.1 | async-start | bytes 1474560 | tf_op jit(solution)/shard_map/all_gather | solution.py:814
  9.2 116.6 %all-gather.14.cloned.1.call-start = ((), (), s32[]{:S(2)}) async-start(), calls=%async_computation.3 | async-start | bytes 1310720 | tf_op jit(solution)/shard_map/all_gather | solution.py:814
  10.9 118.9 %all-gather.12.cloned.1.call-start = ((), (), s32[]{:S(2)}) async-start(), calls=%async_computation.2 | async-start | bytes 2621440 | tf_op jit(solution)/shard_map/all_gather | solution.py:814
  12.9 164.0 %all-gather.8.cloned.1.call-start = ((), (), s32[]{:S(2)}) async-start(), calls=%async_computation | async-start | bytes 2621440 | tf_op jit(solution)/shard_map/all_gather | solution.py:837
  25.5 11.2 copy-start.19
  25.5 22.4 %copy-start.20 = (f32[1,192]{1,0:T(1,128)S(1)}, f32[1,192]{1,0:T(1,128)}, u32[]{:S(2)}) copy-start(f32[1,192]{1,0:T(1,128)} %param.17) | copy-start | bytes 2308
  25.6 29.9 %copy-start.15 = (bf16[1,192,192]{2,1,0:T(8,128)(2,1)S(1)}, bf16[1,192,192]{2,1,0:T(8,128)(2,1)}, u32[]{:S(2)}) copy-start(bf16[1,192,192]{2,1,0:T(8,128)(2,1)} %param.16) | copy-start | bytes 221188
  25.6 49.9 %copy-start.16 = (bf16[4,128,192]{1,2,0:T(8,128)(2,1)S(1)}, bf16[4,128,192]{1,2,0:T(8,128)(2,1)}, u32[]{:S(2)}) copy-start(bf16[4,128,192]{1,2,0:T(8,128)(2,1)} %param.13) | copy-start | bytes 589828
  25.6 512.7 %all-gather.18.cloned.1.call-start = ((), (), s32[]{:S(2)}) async-start(), calls=%async_computation.5 | async-start | bytes 2621440 | tf_op jit(solution)/shard_map/all_gather | solution.py:837
  36.7 50.6 %copy-start.17 = (bf16[1,192,16]{1,2,0:T(8,128)(2,1)S(1)}, bf16[1,192,16]{1,2,0:T(8,128)(2,1)}, u32[]{:S(2)}) copy-start(bf16[1,192,16]{1,2,0:T(8,128)(2,1)} %param.18) | copy-start | bytes 18436
  36.7 175.1 %collective-permute-start.6 = (bf16[16,192,1024]{2,1,0:T(8,128)(2,1)}, bf16[16,192,1024]{2,1,0:T(8,128)(2,1)}, u32[]{:S(2)}, u32[]{:S(2)}) collective-permute-start(bf16[16,192,1024]{2,1,0:T(8,128)(2,1)} %reshape_squeeze.6.win_a), channel_id=1, source_target_pairs={{0,16},{16,0},{1,17},{17,1},{2,18},{18,2},{3,19},{19,3},{4,20},{20... | collective-permute-start | bytes 18874376 | tf_op jit(solution)/shard_map/ppermute | solution.py:18
  47.9 68.2 %collective-permute-start = (f32[1,1024]{1,0:T(1,128)S(1)}, f32[1,1024]{1,0:T(1,128)S(1)}, u32[]{:S(2)}, u32[]{:S(2)}) collective-permute-start(f32[1,1024]{1,0:T(1,128)S(1)} %all_gather.47), channel_id=1, source_target_pairs={{0,16},{16,0},{1,17},{17,1},{2,18},{18,2},{3,19},{19,3},{4,20},{20... | collective-permute-start | bytes 12296 | tf_op jit(solution)/shard_map/ppermute | solution.py:18
  55.5 61.8 %collective-permute-start.1 = (f32[1,1024]{1,0:T(1,128)S(1)}, f32[1,1024]{1,0:T(1,128)S(1)}, u32[]{:S(2)}, u32[]{:S(2)}) collective-permute-start(f32[1,1024]{1,0:T(1,128)S(1)} %all_gather.48), channel_id=1, source_target_pairs={{0,16},{16,0},{1,17},{17,1},{2,18},{18,2},{3,19},{19,3},{4,20},{20... | collective-permute-start | bytes 12296 | tf_op jit(solution)/shard_map/ppermute | solution.py:18
  73.8 0.7 copy-start.8
  75.4 50.4 %collective-permute-start.3 = (bf16[256,1024]{1,0:T(8,128)(2,1)}, bf16[256,1024]{1,0:T(8,128)(2,1)}, u32[]{:S(2)}, u32[]{:S(2)}) collective-permute-start(bf16[256,1024]{1,0:T(8,128)(2,1)} %pad.68), channel_id=1, source_target_pairs={{0,16},{16,0},{1,17},{17,1},{2,18},{18,2},{3,19},{19,3},{4,20},{20... | collective-permute-start | bytes 1572872 | tf_op jit(solution)/shard_map/ppermute | solution.py:18
  87.2 965.9 %all-gather.16.cloned.1.call-start = ((), (), s32[]{:S(2)}) async-start(), calls=%async_computation.4 | async-start | bytes 5242880 | tf_op jit(solution)/shard_map/all_gather | solution.py:849
  104.3 1.5 copy-start.9
  107.6 9.6 copy-start.18
  107.6 10.8 copy-start.2
  112.4 66.2 %collective-permute-start.2 = (bf16[1024,1280]{1,0:T(8,128)(2,1)}, bf16[1024,1280]{1,0:T(8,128)(2,1)}, u32[]{:S(2)}, u32[]{:S(2)}) collective-permute-start(bf16[1024,1280]{1,0:T(8,128)(2,1)} %copy.92), channel_id=1, source_target_pairs={{0,16},{16,0},{1,17},{17,1},{2,18},{18,2},{3,19},{19,3},{4,20},{20... | collective-permute-start | bytes 7864328 | tf_op jit(solution)/shard_map/ppermute | solution.py:18
  116.1 12.7 %collective-permute-start.4 = (bf16[1024,256]{1,0:T(8,128)(2,1)}, bf16[1024,256]{1,0:T(8,128)(2,1)}, u32[]{:S(2)}, u32[]{:S(2)}) collective-permute-start(bf16[1024,256]{1,0:T(8,128)(2,1)} %pad.70), channel_id=1, source_target_pairs={{0,16},{16,0},{1,17},{17,1},{2,18},{18,2},{3,19},{19,3},{4,20},{20... | collective-permute-start | bytes 1572872 | tf_op jit(solution)/shard_map/ppermute | solution.py:18
  117.2 1.2 collective-permute-start.5
  118.4 93.3 %collective-permute-start.7 = (bf16[16,192,512]{2,1,0:T(8,128)(2,1)S(1)}, bf16[16,192,512]{2,1,0:T(8,128)(2,1)}, u32[]{:S(2)}, u32[]{:S(2)}) collective-permute-start(bf16[16,192,512]{2,1,0:T(8,128)(2,1)S(1)} %bitcast.97), channel_id=1, source_target_pairs={{0,16},{16,0},{1,17},{17,1},{2,18},{18,2},{3,19},{19,3},{4,20},{20... | collective-permute-start | bytes 9437192 | tf_op jit(solution)/shard_map/ppermute | solution.py:18
  125.8 15.3 %collective-permute-start.9 = (bf16[1024,512]{1,0:T(8,128)(2,1)}, bf16[1024,512]{1,0:T(8,128)(2,1)}, u32[]{:S(2)}, u32[]{:S(2)}) collective-permute-start(bf16[1024,512]{1,0:T(8,128)(2,1)} %all-gather.14.cloned.1.call-done), channel_id=1, source_target_pairs={{0,16},{16,0},{1,17},{17,1},{2,18},{18,2},{3,19},{19,3},{4,20},{20... | collective-permute-start | bytes 3145736 | tf_op jit(solution)/shard_map/ppermute | solution.py:18
  129.9 77.4 %collective-permute-start.8 = (bf16[1024,1024]{1,0:T(8,128)(2,1)}, bf16[1024,1024]{1,0:T(8,128)(2,1)}, u32[]{:S(2)}, u32[]{:S(2)}) collective-permute-start(bf16[1024,1024]{1,0:T(8,128)(2,1)} %all-gather.12.cloned.1.call-done), channel_id=1, source_target_pairs={{0,16},{16,0},{1,17},{17,1},{2,18},{18,2},{3,19},{19,3},{4,20},{20... | collective-permute-start | bytes 6291464 | tf_op jit(solution)/shard_map/ppermute | solution.py:18
  136.1 5.0 copy-start.12
  381.5 138.4 %copy-start.6 = (f32[2,32,1024]{2,1,0:T(8,128)S(1)}, f32[2,32,1024]{2,1,0:T(8,128)}, u32[]{:S(2)}) copy-start(f32[2,32,1024]{2,1,0:T(8,128)} %convert_convert_fusion.1.x) | copy-start | bytes 786436
  381.5 139.4 %copy-start.13 = (f32[2,32,1024]{2,1,0:T(8,128)S(1)}, f32[2,32,1024]{2,1,0:T(8,128)}, u32[]{:S(2)}) copy-start(f32[2,32,1024]{2,1,0:T(8,128)} %get-tuple-element.68) | copy-start | bytes 786436
  520.8 1.4 collective-permute-start.10
  537.1 573.5 %all-gather.20.cloned.1.call-start = ((), (), s32[]{:S(2)}) async-start(), calls=%async_computation.6 | async-start | bytes 5242880 | tf_op jit(solution)/shard_map/all_gather | solution.py:849
  539.2 7.4 copy-start.10
  948.0 66.0 %copy-start.11 = (bf16[64,1024]{1,0:T(8,128)(2,1)S(1)}, bf16[64,1024]{1,0:T(8,128)(2,1)}, u32[]{:S(2)}) copy-start(bf16[64,1024]{1,0:T(8,128)(2,1)} %get-tuple-element.153) | copy-start | bytes 393220
  1014.0 17.2 %copy-start.4 = (f32[192,768]{1,0:T(8,128)S(1)}, f32[192,768]{1,0:T(8,128)}, u32[]{:S(2)}) copy-start(f32[192,768]{1,0:T(8,128)} %get-tuple-element.113) | copy-start | bytes 1769476
  1015.0 1.4 collective-permute-start.11
  1032.6 17.1 %copy-start.3 = (f32[192,1024]{1,0:T(8,128)S(1)}, f32[192,1024]{1,0:T(8,128)}, u32[]{:S(2)}) copy-start(f32[192,1024]{1,0:T(8,128)} %get-tuple-element.117) | copy-start | bytes 2359300
  1032.6 18.6 %copy-start.14 = (f32[24,256]{1,0:T(8,128)S(1)}, f32[24,256]{1,0:T(8,128)}, u32[]{:S(2)}) copy-start(f32[24,256]{1,0:T(8,128)} %get-tuple-element.112) | copy-start | bytes 73732
  1032.6 19.8 %copy-start.7 = (f32[256,256]{1,0:T(8,128)S(1)}, f32[256,256]{1,0:T(8,128)}, u32[]{:S(2)}) copy-start(f32[256,256]{1,0:T(8,128)} %get-tuple-element.114) | copy-start | bytes 786436
  1113.3 6.5 copy-start.5
  1113.3 7.3 copy-start.1
Sparse Core Ops, SparseCore 0:
  10.2 34.4 all-gather.9
  46.2 32.5 all-gather.13
  80.4 49.3 all-gather.11
  131.9 45.0 all-gather.7
  178.4 54.6 all-gather.17
  537.2 123.8 all-gather.15
  1031.3 79.2 all-gather.19

commit v3 on v1

--- a/solution.py
+++ b/solution.py
@@ -539,20 +539,6 @@
     return v.astype(jnp.bfloat16)
 
 
-def emu_gather_gx(v, mbs):
-    rows = v.shape[0] // mbs
-    g = lax.all_gather(v.reshape(mbs, rows, -1), "gx")
-    return jnp.moveaxis(g, 0, 1).reshape(mbs * 4 * rows, -1)
-
-
-def emu_scatter_gx(v, mbs):
-    n = lax.axis_size("gx")
-    rows = v.shape[0] // mbs // n
-    v = bf(v).astype(jnp.float32).reshape(mbs, n, rows, -1)
-    v = lax.psum_scatter(v, "gx", scatter_dimension=1, tiled=False)
-    return v.reshape(mbs * rows, -1)
-
-
 def head_mask(pw, h):
     lane = lax.broadcasted_iota(jnp.int32, (1, pw), 1)
     return (lane >= h * DH) & (lane < (h + 1) * DH)
@@ -567,33 +553,6 @@
     inner = jnp.sum(u * x, axis=1, keepdims=True) / features
     dx = inv * u - x * (inv * inv * inv * inner)
     return dx, jnp.sum(d * x * inv, axis=0, keepdims=True)
-
-
-def emu_attn_fwd(x, gain, wqkv, wout, fgain, rwx, cos, sin, mbs, heads, features):
-    pw = cos.shape[1]
-    n1 = bf(x * rms(x, features) * gain)
-    rows = emu_gather_gx(n1, mbs)
-    proj = mm(rows, wqkv)
-    length = rows.shape[0] // mbs
-    cos2 = jnp.concatenate([cos] * mbs, 0)
-    sin2 = jnp.concatenate([sin] * mbs, 0)
-    q = bf(proj[:, :pw] * cos2 + proj[:, 3 * pw : 4 * pw] * sin2)
-    k = bf(proj[:, pw : 2 * pw] * cos2 + proj[:, 4 * pw : 5 * pw] * sin2)
-    v = bf(proj[:, 2 * pw : 3 * pw])
-    outs = []
-    for m in range(mbs):
-        rs = slice(m * length, (m + 1) * length)
-        acc = jnp.zeros((length, pw), jnp.float32)
-        for h in range(heads):
-            mask = head_mask(pw, h)
-            p = probs_of(jnp.where(mask, q[rs], 0), k[rs])
-            acc = acc + mm(bf(p), jnp.where(mask, v[rs], 0))
-        outs.append(acc)
-    att = bf(jnp.concatenate(outs, 0))
-    mid = x + emu_scatter_gx(mm(att, wout), mbs)
-    n2 = bf(mid * rms(mid, features) * fgain)
-    rx = mm(n2, rwx)
-    return mid, n2, rx, rows, q, k, v, att
 
 
 def probs_of(q, k):
@@ -605,15 +564,534 @@
     return e / jnp.sum(e, axis=1, keepdims=True)
 
 
-def emu_attn_bwd(dn2, g, mid, fgain, x, gain, rows, q, k, v, att, wqkv, wout, cos, sin, rot, mbs, heads, features):
-    pw = cos.shape[1]
-    dx2, fgain_grad = norm_back(mid, rms(mid, features), fgain, dn2, features)
-    dm = g + dx2
-    dmr = emu_gather_gx(bf(dm), mbs)
-    wout_grad = mm(att, dmr, ((0,), (0,)))
-    datt = bf(mm(dmr, wout, ((1,), (1,))))
-    length = rows.shape[0] // mbs
-    parts = []
+def act_back(gate, up, dh, s):
+    sg = jax.nn.sigmoid(gate)
+    silu = gate * sg
+    if s is None:
+        return dh * up * (sg * (1.0 + gate * (1.0 - sg))), dh * silu, None
+    dr = jnp.sum(dh * silu * up, axis=-1, keepdims=True) * s * (1.0 - s)
+    ds = dh * s
+    return ds * up * (sg * (1.0 + gate * (1.0 - sg))), ds * silu, dr
+
+
+def places_of(routes, experts, capacity):
+    lead = routes.shape[:-2]
+    ids = routes.reshape((-1, routes.shape[-2] * 2))
+    n = ids.shape[1]
+    hot = (ids[..., None] == jnp.arange(experts, dtype=jnp.int32)).astype(jnp.bfloat16)
+    before = (jnp.arange(n)[:, None] > jnp.arange(n)[None, :]).astype(jnp.bfloat16)
+    earlier = jnp.einsum("ij,bje->bie", before, hot, preferred_element_type=jnp.float32)
+    rank = jnp.sum(earlier * hot.astype(jnp.float32), -1).astype(jnp.int32)
+    place = (ids * capacity + rank).reshape(lead + (-1, 2))
+    return jnp.moveaxis(place, -1, -2)
+
+
+MESH = pl.DeviceIdType.MESH
+VMEM_BYTES = 60 * 2**20
+
+
+def remote(src, dst, send, recv, target):
+    return pltpu.make_async_remote_copy(
+        src_ref=src, dst_ref=dst, send_sem=send, recv_sem=recv, device_id=target, device_id_type=MESH
+    )
+
+
+def router_column(rows, e, width, experts):
+    lane = lax.broadcasted_iota(jnp.int32, rows.shape, rows.ndim - 1)
+    mask = (lane == width + e) | (lane == width + experts + e)
+    return jnp.sum(jnp.where(mask, rows.astype(jnp.float32), 0.0), axis=-1, keepdims=True)
+
+
+class Position:
+    def __init__(self, nx, ny):
+        self.s = lax.axis_index("section")
+        self.a = lax.axis_index("gx")
+        self.b = lax.axis_index("gy")
+        self.nx, self.ny = nx, ny
+        self.n = nx * ny
+        self.me = self.a * ny + self.b
+
+    def device(self, index):
+        return (self.s, index // self.ny, lax.rem(index, self.ny))
+
+    def others(self, do):
+        def step(i, c):
+            index = lax.rem(self.me + i, self.n)
+            do(index, index // self.ny, lax.rem(index, self.ny))
+            return c
+
+        lax.fori_loop(1, self.n, step, 0)
+
+    def peers(self, do):
+        for i in range(1, self.nx):
+            do(lax.rem(self.a + i, self.nx))
+
+
+def greet_section(pos):
+    barrier = pltpu.get_barrier_semaphore()
+
+    def one(index, ai, bi):
+        pl.semaphore_signal(barrier, inc=1, device_id=(pos.s, ai, bi), device_id_type=MESH)
+
+    pos.others(one)
+    return barrier
+
+
+def flags(count):
+    return pltpu.SemaphoreType.DMA(count)
+
+
+class Share:
+    def __init__(self, pos, layer, block, full, sems):
+        self.pos, self.layer, self.block, self.full = pos, layer, block, full
+        self.sems = sems
+        self.source = pos.s == layer
+
+    def line(self, do):
+        for i in range(1, self.pos.ny):
+            do(lax.rem(self.pos.b + i, self.pos.ny))
+
+    def signal(self, barrier, with_line):
+        pos = self.pos
+        if with_line:
+            @pl.when(self.source)
+            def _():
+                self.line(lambda bi: pl.semaphore_signal(
+                    barrier, inc=1, device_id=(pos.s, pos.a, bi), device_id_type=MESH))
+
+        @pl.when(jnp.logical_not(self.source))
+        def _():
+            pl.semaphore_signal(barrier, inc=1, device_id=(1 - pos.s, pos.a, pos.b), device_id_type=MESH)
+
+    def wait_barrier(self, barrier, count, with_line):
+        @pl.when(self.source)
+        def _():
+            pl.semaphore_wait(barrier, count + 1 + (self.pos.ny - 1 if with_line else 0))
+
+        @pl.when(jnp.logical_not(self.source))
+        def _():
+            pl.semaphore_wait(barrier, count)
+
+    def along(self, bi, slot):
+        pos = self.pos
+        return remote(self.block, self.full.at[slot], self.sems[0].at[bi], self.sems[1].at[slot], (pos.s, pos.a, bi))
+
+    def across(self, src, slot):
+        pos = self.pos
+        return remote(src, self.full.at[slot], self.sems[2].at[slot], self.sems[3].at[slot], (1 - pos.s, pos.a, pos.b))
+
+    def start(self):
+        b = self.pos.b
+
+        @pl.when(self.source)
+        def _():
+            self.line(lambda bi: self.along(bi, b).start())
+            self.across(self.block, b).start()
+            self.full[b] = self.block[...]
+
+    def forward(self):
+        @pl.when(self.source)
+        def _():
+            def one(bi):
+                self.along(bi, bi).wait_recv()
+                self.across(self.full.at[bi], bi).start()
+
+            self.line(one)
+
+    def finish(self):
+        b = self.pos.b
+
+        @pl.when(self.source)
+        def _():
+            def one(bi):
+                self.along(bi, bi).wait_send()
+                self.across(self.full.at[bi], bi).wait_send()
+
+            self.line(one)
+            self.across(self.block, b).wait_send()
+
+        @pl.when(jnp.logical_not(self.source))
+        def _():
+            for j in range(self.pos.ny):
+                self.across(self.full.at[j], j).wait_recv()
+
+
+def share_sems(ny):
+    return [flags((ny,))] * 4
+
+
+def params(ids):
+    return pltpu.CompilerParams(collective_id=ids, has_side_effects=True, vmem_limit_bytes=VMEM_BYTES)
+
+
+def greet_all(pos):
+    barrier = pltpu.get_barrier_semaphore()
+    total = 2 * pos.n
+    mine = pos.s * pos.n + pos.me
+
+    def one(i, c):
+        index = lax.rem(mine + i, total)
+        rest = lax.rem(index, pos.n)
+        pl.semaphore_signal(
+            barrier, inc=1, device_id=(index // pos.n, rest // pos.ny, lax.rem(rest, pos.ny)), device_id_type=MESH)
+        return c
+
+    lax.fori_loop(1, total, one, 0)
+    pl.semaphore_wait(barrier, total - 1)
+
+
+def entry_kernel(cfg, tin, watt, small, tok, watt0, small_o, tbuf, wbuf, sbuf,
+                 t_send, t_recv, s_send, s_recv, *w_sems):
+    nx, ny, mbs, sub, pw = cfg
+    pos = Position(nx, ny)
+    s, a, b = pos.s, pos.a, pos.b
+    greet_all(pos)
+    share = Share(pos, 0, watt, wbuf, w_sems)
+
+    def tokens(i, slot, seq):
+        src = tin.at[:, :, pl.ds(pl.multiple_of(i * sub, sub), sub), :]
+        return remote(src, tbuf.at[slot], t_send.at[i], t_recv.at[slot], (s, i, seq))
+
+    for k in range(nx):
+        i = lax.rem(a + k, nx)
+
+        @pl.when(jnp.logical_or(i != a, a != b))
+        def _():
+            tokens(i, b, a).start()
+
+    @pl.when(a == b)
+    def _():
+        tbuf[b] = tin[:, :, pl.ds(pl.multiple_of(a * sub, sub), sub), :]
+
+    def gains(so, bi, s_slot, b_slot):
+        return remote(small, sbuf.at[s_slot, b_slot], s_send.at[so, bi], s_recv.at[s_slot, b_slot], (so, a, bi))
+
+    def each_gain(do):
+        for so in range(2):
+            for bi in range(ny):
+                @pl.when(jnp.logical_or(s != so, b != bi))
+                def _():
+                    do(so, bi)
+
+    each_gain(lambda so, bi: gains(so, bi, s, b).start())
+    sbuf[s, b] = small[...]
+    share.start()
+    share.forward()
+    each_gain(lambda so, bi: gains(so, bi, so, bi).wait())
+    for l in range(2):
+        for j in range(ny):
+            small_o[l, :, j * pw : (j + 1) * pw] = sbuf[l, j]
+    for k in range(nx):
+        i = lax.rem(a + k, nx)
+
+        @pl.when(jnp.logical_or(i != a, a != b))
+        def _():
+            tokens(i, b, a).wait_send()
+
+    for j in range(ny):
+        @pl.when(jnp.logical_or(a != b, b != j))
+        def _():
+            tokens(a, j, j).wait_recv()
+
+        tok[:, :, :, j * pw : (j + 1) * pw] = tbuf[j]
+    share.finish()
+    watt0[...] = wbuf[...]
+
+
+def entry(tin, watt, small, ids):
+    nx, ny = lax.axis_size("gx"), lax.axis_size("gy")
+    kinds, mbs, length, pw = tin.shape
+    sub = length // nx
+    width, cols = watt.shape
+    vm = pl.BlockSpec(memory_space=pltpu.VMEM)
+    b16, f32 = jnp.bfloat16, jnp.float32
+    return pl.pallas_call(
+        functools.partial(entry_kernel, (nx, ny, mbs, sub, pw)),
+        out_shape=(
+            jax.ShapeDtypeStruct((kinds, mbs, sub, ny * pw), b16),
+            jax.ShapeDtypeStruct((ny, width, cols), b16),
+            jax.ShapeDtypeStruct((2, small.shape[0], ny * pw), f32),
+        ),
+        in_specs=[vm] * 3,
+        out_specs=(vm,) * 3,
+        scratch_shapes=[
+            pltpu.VMEM((ny, kinds, mbs, sub, pw), b16),
+            pltpu.VMEM((ny, width, cols), b16),
+            pltpu.VMEM((2, ny, small.shape[0], pw), f32),
+            flags((nx,)), flags((ny,)), flags((2, ny)), flags((2, ny)),
+        ] + share_sems(ny),
+        compiler_params=params(ids),
+        name="entry",
+    )(tin, watt, small)
+
+
+def leave_kernel(cfg, pair0, pair1, out, buf, t_send, t_recv):
+    nx, ny, mbs, sub, pw = cfg
+    pos = Position(nx, ny)
+    s, a, b = pos.s, pos.a, pos.b
+    greet_all(pos)
+    pairs = (pair0, pair1)
+
+    def copy(l, j, s_slot, a_slot, seq):
+        src = pairs[l].at[:, :, :, pl.ds(pl.multiple_of(j * pw, pw), pw)]
+        return remote(src, buf.at[s_slot, a_slot], t_send.at[l, j], t_recv.at[s_slot, a_slot], (l, seq, j))
+
+    for l in range(2):
+        for j in range(ny):
+            @pl.when((l != s) | (a != b) | (j != b))
+            def _():
+                copy(l, j, s, a, b).start()
+
+        @pl.when((l == s) & (a == b))
+        def _():
+            buf[s, a] = pairs[l][:, :, :, pl.ds(pl.multiple_of(b * pw, pw), pw)]
+
+    for so in range(2):
+        for i in range(nx):
+            @pl.when((so != s) | (a != b) | (i != a))
+            def _():
+                copy(0, 0, so, i, i).wait_recv()
+
+            out[:, so * mbs : (so + 1) * mbs, i * sub : (i + 1) * sub, :] = buf[so, i]
+    for l in range(2):
+        for j in range(ny):
+            @pl.when((l != s) | (a != b) | (j != b))
+            def _():
+                copy(l, j, s, a, b).wait_send()
+
+
+def leave(pair0, pair1, pw, ids):
+    nx, ny = lax.axis_size("gx"), lax.axis_size("gy")
+    kinds, mbs, sub, d = pair0.shape
+    vm = pl.BlockSpec(memory_space=pltpu.VMEM)
+    return pl.pallas_call(
+        functools.partial(leave_kernel, (nx, ny, mbs, sub, pw)),
+        out_shape=jax.ShapeDtypeStruct((kinds, 2 * mbs, nx * sub, pw), jnp.bfloat16),
+        in_specs=[vm] * 2,
+        out_specs=vm,
+        scratch_shapes=[
+            pltpu.VMEM((2, nx, kinds, mbs, sub, pw), jnp.bfloat16),
+            flags((2, ny)), flags((2, nx)),
+        ],
+        compiler_params=params(ids),
+        name="leave",
+    )(pair0, pair1)
+
+
+def turn(t, cos, sin, rot, sign):
+    hi = bf(t)
+    lo = bf(t - hi.astype(jnp.float32))
+    return bf(t * cos + sign * ((mm(hi, rot) + mm(lo, rot)) * sin))
+
+
+def by_blocks(rows, full, cols, width, pw):
+    total = None
+    for j in range(full.shape[0]):
+        part = mm(rows[:, j * pw : j * pw + width], full[j, :, cols])
+        total = part if total is None else total + part
+    return total
+
+
+def attn_fwd_kernel(cfg, x, small, watt, shw, cos, sin, rot,
+                    mid, n2, rx, rows_o, q, k, v, att, shw_o,
+                    nsend, nall, proj, osend, orecv, rwx, shfull,
+                    n_send, n_recv, o_send, o_recv, w_sem, *w_sems):
+    layer, nx, ny, mbs, sub, width, pw, heads, features, experts = cfg
+    pos = Position(nx, ny)
+    s, a, b = pos.s, pos.a, pos.b
+    d = ny * pw
+    length = nx * sub
+    barrier = pltpu.get_barrier_semaphore()
+    share = Share(pos, layer, shw, shfull, w_sems)
+    pos.peers(lambda ai: pl.semaphore_signal(barrier, inc=1, device_id=(s, ai, b), device_id_type=MESH))
+    share.signal(barrier, True)
+    xv = x[...].reshape(mbs * sub, d).astype(jnp.float32)
+    gain = small[experts + 1 : experts + 2]
+    fgain = small[experts : experts + 1]
+    nsend[...] = bf(xv * rms(xv, features) * gain).reshape(mbs, sub, d)
+    share.wait_barrier(barrier, nx - 1, True)
+
+    def copy_n(ai, slot):
+        return remote(nsend, nall.at[:, slot], n_send.at[ai], n_recv.at[slot], (s, ai, b))
+
+    pos.peers(lambda ai: copy_n(ai, a).start())
+    share.start()
+    nall[:, a] = nsend[...]
+    osend[...] = jnp.zeros_like(osend)
+    rwx[...] = jnp.zeros_like(rwx)
+    rwx[width : width + experts] = bf(small[:experts])
+    rwx[width + experts : width + 2 * experts] = bf(small[:experts])
+    pos.peers(lambda ai: copy_n(ai, ai).wait())
+    rows = nall[...].reshape(mbs * length, d)
+    proj[...] = by_blocks(rows, watt, slice(0, 3 * pw), width, pw)
+    rows_o[...] = nall[...]
+    v[...] = bf(proj[:, 2 * pw : 3 * pw])
+    for m in range(mbs):
+        rs = slice(m * length, (m + 1) * length)
+        q[rs] = turn(proj[rs, :pw], cos[...], sin[...], rot[...], 1.0)
+        k[rs] = turn(proj[rs, pw : 2 * pw], cos[...], sin[...], rot[...], 1.0)
+        acc = jnp.zeros((length, pw), jnp.float32)
+        for h in range(heads):
+            mask = head_mask(pw, h)
+            p = probs_of(jnp.where(mask, q[rs], 0), k[rs])
+            acc = acc + mm(bf(p), jnp.where(mask, v[rs], 0))
+        att[rs] = bf(acc)
+    for j in range(ny):
+        part = mm(att[...], watt[j, :, 3 * pw : 4 * pw], ((1,), (1,)))
+        osend[..., j * pw : j * pw + width] = bf(part).reshape(mbs, nx, sub, width)
+
+    def copy_o(ai, slot):
+        return remote(osend.at[:, ai], orecv.at[slot], o_send.at[ai], o_recv.at[slot], (s, ai, b))
+
+    pos.peers(lambda ai: copy_o(ai, a).start())
+    orecv[a] = osend[:, a]
+    share.forward()
+    pos.peers(lambda ai: copy_o(ai, ai).wait())
+    mv = xv.reshape(mbs, sub, d)
+    for ai in range(nx):
+        mv = mv + orecv[ai].astype(jnp.float32)
+    mv = mv.reshape(mbs * sub, d)
+    mid[...] = mv
+    n2v = bf(mv * rms(mv, features) * fgain)
+    n2[...] = n2v
+    rx[...] = mm(n2v, rwx[...], ((1,), (1,)))
+    share.finish()
+    keep = pltpu.make_async_copy(shfull, shw_o, w_sem)
+    keep.start()
+    keep.wait()
+
+
+def attn_fwd(layer, x, small, watt, shw, cos, sin, rot, dims, heads, features, ids):
+    width, pw, experts, cap = dims
+    nx, ny = lax.axis_size("gx"), lax.axis_size("gy")
+    d = ny * pw
+    mbs, sub = x.shape[:2]
+    length = nx * sub
+    b16, f32 = jnp.bfloat16, jnp.float32
+    vm = pl.BlockSpec(memory_space=pltpu.VMEM)
+    hbm = pl.BlockSpec(memory_space=pl.ANY)
+    return pl.pallas_call(
+        functools.partial(attn_fwd_kernel, (layer, nx, ny, mbs, sub, width, pw, heads, features, experts)),
+        out_shape=(
+            jax.ShapeDtypeStruct((mbs * sub, d), f32),
+            jax.ShapeDtypeStruct((mbs * sub, d), b16),
+            jax.ShapeDtypeStruct((mbs * sub, pw), f32),
+            jax.ShapeDtypeStruct((mbs, nx, sub, d), b16),
+            jax.ShapeDtypeStruct((mbs * length, pw), b16),
+            jax.ShapeDtypeStruct((mbs * length, pw), b16),
+            jax.ShapeDtypeStruct((mbs * length, pw), b16),
+            jax.ShapeDtypeStruct((mbs * length, pw), b16),
+            jax.ShapeDtypeStruct((ny,) + shw.shape, b16),
+        ),
+        in_specs=[vm] * 7,
+        out_specs=(vm,) * 8 + (hbm,),
+        scratch_shapes=[
+            pltpu.VMEM((mbs, sub, d), b16),
+            pltpu.VMEM((mbs, nx, sub, d), b16),
+            pltpu.VMEM((mbs * length, 3 * pw), f32),
+            pltpu.VMEM((mbs, nx, sub, d), b16),
+            pltpu.VMEM((nx, mbs, sub, d), b16),
+            pltpu.VMEM((pw, d), b16),
+            pltpu.VMEM((ny,) + shw.shape, b16),
+            flags((nx,)), flags((nx,)), flags((nx,)), flags((nx,)), pltpu.SemaphoreType.DMA,
+        ] + share_sems(ny),
+        compiler_params=params(ids),
+        cost_estimate=pl.CostEstimate(flops=10**9, bytes_accessed=10**7, transcendentals=10**6),
+        name="attention_forward",
+    )(x, small, watt, shw, cos, sin, rot)
+
+
+def attn_bwd_kernel(cfg, *refs):
+    layer, nx, ny, mbs, sub, width, pw, heads, features, experts = cfg
+    (dn2, g, mid, x, small, rows, q, k, v, att, watt, cos, sin, rot, sh_p, rw_p) = refs[:16]
+    refs = refs[16 + (0 if layer else 3) :]
+    (dx_o, att_o, sh_o, small_o,
+     msend, mall, dqkv, dsend, drecv, datt,
+     att_p, small_p, sh_x, att_x, small_x, sh_t, att_t, small_t, sh_r, att_r, small_r,
+     sh_f, att_f, small_f, small_a,
+     m_send, m_recv, d_send, d_recv, c_send, c_recv, r_send, r_recv, a_send, a_recv, f_sem) = refs
+    pos = Position(nx, ny)
+    s, a, b = pos.s, pos.a, pos.b
+    keeper = s == layer
+    helper = jnp.logical_not(keeper)
+    d = ny * pw
+    length = nx * sub
+    scale = DH ** -0.5
+    barrier = pltpu.get_barrier_semaphore()
+    pos.peers(lambda ai: pl.semaphore_signal(barrier, inc=1, device_id=(s, ai, b), device_id_type=MESH))
+
+    def line(do):
+        for i in range(1, ny):
+            do(lax.rem(b + i, ny))
+
+    @pl.when(keeper)
+    def _():
+        line(lambda bi: pl.semaphore_signal(barrier, inc=1, device_id=(s, a, bi), device_id_type=MESH))
+        pl.semaphore_signal(barrier, inc=1, device_id=(1 - s, a, b), device_id_type=MESH)
+
+    xv = x[...].reshape(mbs * sub, d).astype(jnp.float32)
+    mv = mid[...]
+    gain = small[experts + 1 : experts + 2]
+    fgain = small[experts : experts + 1]
+    dx2, fgain_g = norm_back(mv, rms(mv, features), fgain, dn2[...], features)
+    dm = g[...].reshape(mbs * sub, d).astype(jnp.float32) + dx2
+    msend[...] = bf(dm).reshape(mbs, sub, d)
+
+    @pl.when(keeper)
+    def _():
+        pl.semaphore_wait(barrier, nx - 1 + ny - 1)
+
+    @pl.when(helper)
+    def _():
+        pl.semaphore_wait(barrier, nx)
+
+    def copy_m(ai, slot):
+        return remote(msend, mall.at[:, slot], m_send.at[ai], m_recv.at[slot], (s, ai, b))
+
+    pos.peers(lambda ai: copy_m(ai, a).start())
+
+    crossing = ((sh_p, sh_x), (att_p, att_x), (small_p, small_x))
+    totals = (sh_t, att_t, small_t)
+    places = (sh_r, att_r, small_r)
+    finals = (sh_f, att_f, small_f)
+    results = (sh_o, att_o, small_o)
+
+    def cross(i):
+        return remote(crossing[i][0], crossing[i][1], c_send.at[i], c_recv.at[i], (layer, a, b))
+
+    def block(i, bi):
+        if i == 2:
+            return small_t.at[:, pl.ds(pl.multiple_of(bi * pw, pw), pw)]
+        return totals[i].at[bi]
+
+    def spread(i, bi, slot):
+        return remote(block(i, bi), places[i].at[slot], r_send.at[i, bi], r_recv.at[i, slot], (s, a, bi))
+
+    def copy_a(ai, slot):
+        return remote(small_f, small_a.at[slot], a_send.at[ai], a_recv.at[slot], (s, ai, b))
+
+    def join(i):
+        cross(i).wait_recv()
+        part, other = crossing[i]
+        totals[i][...] = (part[...].astype(jnp.float32) + other[...].astype(jnp.float32)).astype(totals[i].dtype)
+        line(lambda bi: spread(i, bi, b).start())
+
+    @pl.when(helper)
+    def _():
+        cross(0).start()
+
+    mall[:, a] = msend[...]
+    dsend[...] = jnp.zeros_like(dsend)
+    pos.peers(lambda ai: copy_m(ai, ai).wait())
+    dmr = mall[...].reshape(mbs * length, d)
+    datt[...] = bf(by_blocks(dmr, watt, slice(3 * pw, 4 * pw), width, pw))
+    for j in range(ny):
+        att_p[j, :, 3 * pw :] = bf(mm(dmr[:, j * pw : j * pw + width], att[...], ((0,), (0,))))
+
+    @pl.when(keeper)
+    def _():
+        join(0)
+
     for m in range(mbs):
         rs = slice(m * length, (m + 1) * length)
         dq = jnp.zeros((length, pw), jnp.float32)
@@ -628,356 +1106,141 @@
             dp = mm(da, v[rs], ((1,), (1,)))
             ds = bf(p * (dp - jnp.sum(dp * p, axis=1, keepdims=True)))
             dv = dv + mm(bf(p), da, ((0,), (0,)))
-            dq = dq + mm(ds, kh) * DH ** -0.5
-            dk = dk + mm(ds, qh, ((0,), (0,))) * DH ** -0.5
-
-        def back(t):
-            hi = bf(t)
-            lo = bf(t - hi.astype(jnp.float32))
-            return t * cos - (mm(hi, rot) + mm(lo, rot)) * sin
-
-        parts.append(jnp.concatenate([bf(back(dq)), bf(back(dk)), bf(dv)], 1))
-    dqkv = jnp.concatenate(parts, 0)
-    wqkv_grad = mm(rows, dqkv, ((0,), (0,)))
-    dn1 = emu_scatter_gx(mm(dqkv, wqkv[:, : 3 * pw], ((1,), (1,))), mbs)
-    dx1, gain_grad = norm_back(x, rms(x, features), gain, dn1, features)
-    return dm + dx1, wqkv_grad, wout_grad, gain_grad, fgain_grad
-
-
-def emu_spread(v, mbs, pw):
-    n = lax.axis_size("gy")
-    rows = v.shape[0] // mbs
-    t = lax.all_to_all(v.reshape(mbs, rows, n, pw), "gy", split_axis=2, concat_axis=0, tiled=False)
-    t = lax.all_gather(t, "gx")
-    return t.transpose(2, 1, 0, 3, 4).reshape(mbs, -1, pw)
-
-
-def emu_return(v, mbs):
+            dq = dq + mm(ds, kh)
+            dk = dk + mm(ds, qh, ((0,), (0,)))
+        dqkv[rs, :pw] = turn(dq * scale, cos[...], sin[...], rot[...], -1.0)
+        dqkv[rs, pw : 2 * pw] = turn(dk * scale, cos[...], sin[...], rot[...], -1.0)
+        dqkv[rs, 2 * pw :] = bf(dv)
+    for j in range(ny):
+        part = mm(dqkv[...], watt[j, :, : 3 * pw], ((1,), (1,)))
+        dsend[..., j * pw : j * pw + width] = bf(part).reshape(mbs, nx, sub, width)
+
+    def copy_d(ai, slot):
+        return remote(dsend.at[:, ai], drecv.at[slot], d_send.at[ai], d_recv.at[slot], (s, ai, b))
+
+    pos.peers(lambda ai: copy_d(ai, a).start())
+    drecv[a] = dsend[:, a]
+    rv = rows[...].reshape(mbs * length, d)
+    for j in range(ny):
+        att_p[j, :, : 3 * pw] = bf(mm(rv[:, j * pw : j * pw + width], dqkv[...], ((0,), (0,))))
+
+    @pl.when(helper)
+    def _():
+        cross(1).start()
+
+    @pl.when(keeper)
+    def _():
+        join(1)
+
+    pos.peers(lambda ai: copy_d(ai, ai).wait())
+    dn1 = drecv[0].astype(jnp.float32)
+    for ai in range(1, nx):
+        dn1 = dn1 + drecv[ai].astype(jnp.float32)
+    dn1 = dn1.reshape(mbs * sub, d)
+    dx1, gain_g = norm_back(xv, rms(xv, features), gain, dn1, features)
+    dx_o[...] = bf(dm + dx1).reshape(mbs, sub, d)
+    small_p[: experts] = rw_p[...]
+    row = lax.broadcasted_iota(jnp.int32, (8, d), 0)
+    small_p[experts:] = jnp.where(row == 0, fgain_g, jnp.where(row == 1, gain_g, 0.0))
+
+    @pl.when(helper)
+    def _():
+        cross(2).start()
+        for i in range(3):
+            cross(i).wait_send()
+
+    @pl.when(keeper)
+    def _():
+        join(2)
+        for i in (2, 0, 1):
+            line(lambda bi: spread(i, bi, bi).wait())
+            total = block(i, b)[...].astype(jnp.float32)
+            for c in range(1, ny):
+                total = total + places[i][lax.rem(b + c, ny)].astype(jnp.float32)
+            finals[i][...] = total
+            if i < 2:
+                pltpu.make_async_copy(finals[i], results[i], f_sem.at[i]).start()
+            else:
+                pos.peers(lambda ai: copy_a(ai, a).start())
+        small_a[a] = small_f[...]
+        pos.peers(lambda ai: copy_a(ai, ai).wait())
+        total = small_a[0]
+        for ai in range(1, nx):
+            total = total + small_a[ai]
+        small_f[...] = total
+        pltpu.make_async_copy(small_f, small_o, f_sem.at[2]).start()
+        for i in range(3):
+            pltpu.make_async_copy(finals[i], results[i], f_sem.at[i]).wait()
+
+
+def attn_bwd(layer, dn2, g, mid, x, small, rows, q, k, v, att, watt, cos, sin, rot, sh_g, rw_g, grads, dims,
+             heads, features, ids):
+    width, pw, experts, cap = dims
     nx, ny = lax.axis_size("gx"), lax.axis_size("gy")
-    pw = v.shape[-1]
-    t = bf(v).astype(jnp.float32).reshape(mbs, ny, nx, -1, pw)
-    t = lax.psum_scatter(t, "gx", scatter_dimension=2, tiled=False)
-    rows = t.shape[2]
-    t = lax.all_to_all(t, "gy", split_axis=1, concat_axis=0, tiled=False)
-    return t.transpose(1, 2, 0, 3).reshape(mbs * rows, ny * pw)
-
-
-def place_matrix(place_row, slots):
-    i = lax.broadcasted_iota(jnp.int32, (slots, place_row.shape[1]), 0)
-    return bf(((place_row[0:1] == i) | (place_row[1:2] == i)).astype(jnp.float32))
-
-
-def ext_block(n2, rx, j, width, pw, experts):
-    lane = lax.broadcasted_iota(jnp.int32, (1, pw), 1)
-    hi = bf(rx)
-    lo = bf(rx - hi.astype(jnp.float32))
-    v = jnp.where(lane < width + experts, hi, lo)
-    return jnp.where(lane < width, n2[:, j * pw : (j + 1) * pw], v)
-
-
-def emu_ff_fwd(mid, n2, rx, place, win, wdt, sin_w, sdt, mbs, dims):
-    width, pw, experts, cap = dims
-    f = wdt.shape[-1]
-    xe = jnp.concatenate([ext_block(n2, rx, j, width, pw, experts) for j in range(4)], 1)
-    xs_all = emu_spread(xe, mbs, pw)
-    slots_all, gu_all, hid_all, branch = [], [], [], []
-    for m in range(mbs):
-        pm = place_matrix(place[m], experts * cap)
-        slots = bf(mm(pm, xs_all[m]))
-        se = slots.reshape(experts, cap, pw)
-        gu = jnp.einsum("ecd,edf->ecf", se[..., :width], win, preferred_element_type=jnp.float32)
-        gu = lax.psum(bf(gu).astype(jnp.float32), "gy")
-        lane = lax.broadcasted_iota(jnp.int32, (experts, 1, pw), 2)
-        ex = lax.broadcasted_iota(jnp.int32, (experts, 1, pw), 0)
-        rmask = (lane == width + ex) | (lane == width + experts + ex)
-        r = jnp.sum(jnp.where(rmask, se.astype(jnp.float32), 0), -1, keepdims=True)
-        hid = bf(jax.nn.silu(gu[..., :f]) * gu[..., f:] * jax.nn.sigmoid(r))
-        eo = bf(jnp.einsum("ecf,edf->ecd", hid, wdt, preferred_element_type=jnp.float32)).reshape(-1, width)
-        branch.append(pad_to(mm(pm, eo, ((0,), (0,))), 1, pw))
-        slots_all.append(se)
-        gu_all.append(bf(gu))
-        hid_all.append(hid)
-    ret = emu_return(jnp.stack(branch), mbs)
-    rows2 = emu_gather_gx(n2, mbs)
-    sgu = mm(rows2, sin_w)
-    shid = bf(jax.nn.silu(sgu[:, :f]) * sgu[:, f:])
-    sout = emu_scatter_gx(mm(shid, sdt, ((1,), (1,))), mbs)
-    out = mid + ret + sout
-    return out, (jnp.stack(slots_all), jnp.stack(gu_all), jnp.stack(hid_all), rows2, bf(sgu), shid)
-
-
-def emu_ff_bwd(g, kept, n2, place, win, wdt, sin_w, sdt, rwx, mbs, dims):
-    width, pw, experts, cap = dims
-    slots_all, gu_all, hid_all, rows2, sgu, shid = kept
-    f = wdt.shape[-1]
-    gb = bf(g)
-    g_all = emu_spread(gb, mbs, pw)
-    comb = []
-    win_grad = jnp.zeros((experts, width, 2 * f), jnp.float32)
-    wdt_grad = jnp.zeros((experts, width, f), jnp.float32)
-    for m in range(mbs):
-        pm = place_matrix(place[m], experts * cap)
-        gs = bf(mm(pm, g_all[m])).reshape(experts, cap, pw)[..., :width]
-        dh = jnp.einsum("ecd,edf->ecf", gs, wdt, preferred_element_type=jnp.float32)
-        dh = lax.psum(bf(dh).astype(jnp.float32), "gy")
-        gu = gu_all[m].astype(jnp.float32)
-        se = slots_all[m]
-        lane = lax.broadcasted_iota(jnp.int32, (experts, 1, pw), 2)
-        ex = lax.broadcasted_iota(jnp.int32, (experts, 1, pw), 0)
-        rmask = (lane == width + ex) | (lane == width + experts + ex)
-        r = jnp.sum(jnp.where(rmask, se.astype(jnp.float32), 0), -1, keepdims=True)
-        gate, up = gu[..., :f], gu[..., f:]
-        dgate, dup, dr = act_back(gate, up, dh, jax.nn.sigmoid(r))
-        dgu = jnp.concatenate([bf(dgate), bf(dup)], -1)
-        dslot = jnp.einsum("ecf,edf->ecd", dgu, win, preferred_element_type=jnp.float32)
-        dslot = pad_to(dslot, 2, pw)
-        hi = bf(dr).astype(jnp.float32)
-        owner = (lax.axis_index("gy") == 0).astype(jnp.float32)
-        dslot = dslot + owner * jnp.where(lane == width + ex, hi, jnp.where(lane == width + experts + ex, dr - hi, 0.0))
-        comb.append(mm(pm, bf(dslot).reshape(-1, pw), ((0,), (0,))))
-        win_grad = win_grad + jnp.einsum("ecd,ecf->edf", se[..., :width], dgu, preferred_element_type=jnp.float32)
-        wdt_grad = wdt_grad + jnp.einsum("ecd,ecf->edf", gs, hid_all[m], preferred_element_type=jnp.float32)
-    ret = emu_return(jnp.stack(comb), mbs)
-    g_rows = emu_gather_gx(gb, mbs)
-    dsh = mm(g_rows, sdt)
-    sgu_f = sgu.astype(jnp.float32)
-    dsg, dsu, _ = act_back(sgu_f[:, :f], sgu_f[:, f:], dsh, None)
-    dsgu = jnp.concatenate([bf(dsg), bf(dsu)], 1)
-    sin_grad = mm(rows2, dsgu, ((0,), (0,)))
-    sdt_grad = mm(g_rows, shid, ((0,), (0,)))
-    sback = emu_scatter_gx(mm(dsgu, sin_w, ((1,), (1,))), mbs)
-    dn2, rw_grad = router_back(ret, n2, rwx, width, pw)
-    return dn2 + sback, win_grad, wdt_grad, sin_grad, sdt_grad, rw_grad
-
-
-def router_back(ret, n2, rwx, width, pw):
-    lane = lax.broadcasted_iota(jnp.int32, (1, ret.shape[1]), 1)
-    ret_x = sum(ret[:, j * pw : (j + 1) * pw] for j in range(ret.shape[1] // pw))
-    lane1 = lax.broadcasted_iota(jnp.int32, (1, pw), 1)
-    dlog = jnp.where(lane1 >= width, ret_x, 0.0)
-    hi = bf(dlog)
-    lo = bf(dlog - hi.astype(jnp.float32))
-    main = jnp.where(lane % pw < width, ret, 0.0)
-    dn2 = main + mm(hi, rwx, ((1,), (1,))) + mm(lo, rwx, ((1,), (1,)))
-    rw_grad = mm(n2, hi, ((0,), (0,))) + mm(n2, lo, ((0,), (0,)))
-    return dn2, rw_grad
-
-
-def act_back(gate, up, dh, s):
-    sg = jax.nn.sigmoid(gate)
-    silu = gate * sg
-    if s is None:
-        return dh * up * (sg * (1.0 + gate * (1.0 - sg))), dh * silu, None
-    dr = jnp.sum(dh * silu * up, axis=-1, keepdims=True) * s * (1.0 - s)
-    ds = dh * s
-    return ds * up * (sg * (1.0 + gate * (1.0 - sg))), ds * silu, dr
-
-
-def places_of(routes, experts, capacity):
-    lead = routes.shape[:-2]
-    ids = routes.reshape((-1, routes.shape[-2] * 2))
-    n = ids.shape[1]
-    hot = (ids[..., None] == jnp.arange(experts, dtype=jnp.int32)).astype(jnp.bfloat16)
-    before = (jnp.arange(n)[:, None] > jnp.arange(n)[None, :]).astype(jnp.bfloat16)
-    earlier = jnp.einsum("ij,bje->bie", before, hot, preferred_element_type=jnp.float32)
-    rank = jnp.sum(earlier * hot.astype(jnp.float32), -1).astype(jnp.int32)
-    place = (ids * capacity + rank).reshape(lead + (-1, 2))
-    return jnp.moveaxis(place, -1, -2)
-
-
-def fast_device(block_input, output_grad, attention_gain, attention_in, attention_out, feed_gain,
-                router_weight, expert_in, expert_down, shared_in, shared_down, routes):
-    s = lax.axis_index("section")
-    a = lax.axis_index("gx")
-    b = lax.axis_index("gy")
-    ny = lax.axis_size("gy")
-    nx = lax.axis_size("gx")
-    mbs = block_input.shape[0] // 2
-    width = block_input.shape[2]
-    features = width * ny
-    experts = expert_in.shape[1]
-    f = expert_in.shape[-1]
-    pw = lanes_up(width + 2 * experts)
-    tokens = routes.shape[2]
-    cap = 5 * tokens // (2 * experts)
-    sub = tokens // (nx * ny)
-    heads = attention_in.shape[-1] // DH
-    dims = (width, pw, experts, cap)
-    length = sub * nx
-
-    def both(v):
-        other = pass_section(v)
-        return jnp.where(s == 0, v, other), jnp.where(s == 0, other, v)
-
-    def wide(v, axis):
-        v = pad_to(v, axis, pw)
-        return lax.all_gather(v, "gy", axis=axis, tiled=True)
-
-    ai = wide(attention_in[0], 0)
-    rotq = rot_columns(ai[:, :2])
-    ai = pad_to(jnp.concatenate([ai, rotq], 1), 2, pw).reshape(ny * pw, 5 * pw)
-    wqkv = both(ai)
-    wout = both(pad_to(wide(attention_out[0], 1), 0, pw))
-    gain = both(wide(attention_gain, 1))
-    fgain = both(wide(feed_gain, 1))
-    rwx = wide(router_weight[0], 0)
-    rwx = jnp.concatenate([jnp.zeros((ny * pw, width), jnp.bfloat16), rwx, rwx], 1)
-    rwx = both(pad_to(rwx, 1, pw))
-    win_pair = (expert_in[0].reshape(experts, width, 2 * f),)
-    win_pair = win_pair + (pass_section(win_pair[0]),)
-    wdt_pair = (expert_down[0].transpose(0, 2, 1),)
-    wdt_pair = wdt_pair + (pass_section(wdt_pair[0]),)
-    sin_w = both(wide(shared_in[0].reshape(width, 2 * f), 0))
-    sdt = both(wide(shared_down[0].T, 0))
-    place = places_of(jnp.stack([lax.dynamic_slice_in_dim(r, s * mbs, mbs, 0) for r in both(routes[0])]), experts, cap)
-
-    def tokens_in(v):
-        t = lax.dynamic_slice_in_dim(v, s * mbs, mbs, 0)
-        t = lax.all_gather(t, "gx", axis=1, tiled=True)
-        t = lax.all_gather(pad_to(t, 2, pw), "gy", axis=2, tiled=True)
-        t = lax.dynamic_slice_in_dim(t, b * length + a * sub, sub, 1)
-        return t.reshape(mbs * sub, ny * pw).astype(jnp.float32)
-
-    def tokens_out(pair):
-        v0, v1 = pair
-        keep = jnp.where(s == 0, v0, v1)
-        send = jnp.where(s == 0, v1, v0)
-        got = pass_section(send)
-        both_mb = jnp.where(s == 0, jnp.stack([keep, got]), jnp.stack([got, keep]))
-        t = bf(both_mb).reshape(2 * mbs, sub, ny, pw)[..., :width]
-        t = lax.all_gather(t, "gx", axis=1, tiled=True)
-        t = lax.all_gather(t, "gy", axis=1, tiled=True)
-        t = lax.dynamic_slice_in_dim(t, a * (tokens // nx), tokens // nx, 1)
-        return lax.dynamic_index_in_dim(t, b, 2, keepdims=False)[None]
-
-    half = DH // 2
-    freq = 10000.0 ** (-jnp.arange(half, dtype=jnp.float32) / half)
-    ang = jnp.arange(length, dtype=jnp.float32)[:, None] * freq[None]
-    lanes = jnp.tile(ang, (1, 2 * heads))
-    cos = pad_to(jnp.cos(lanes), 1, pw)
-    sin = pad_to(jnp.sin(lanes), 1, pw)
-    rot = pad_to(pad_to(rot_columns(jnp.eye(heads * DH, dtype=jnp.float32)), 0, pw), 1, pw).astype(jnp.bfloat16)
-
-    x = tokens_in(block_input)
-    kept, outs = [], []
-    for l in range(2):
-        mid, n2, rx, rows, q, k, v, att = emu_attn_fwd(
-            x, gain[l], wqkv[l], wout[l], fgain[l], rwx[l], cos, sin, mbs, heads, features)
-        out, ff = ff_fwd(l, mid, n2, rx, place[l], win_pair, wdt_pair, sin_w[l], sdt[l], mbs, dims, l)
-        kept.append((x, mid, n2, rows, q, k, v, att, ff))
-        x = bf(out).astype(jnp.float32)
-        outs.append(x)
-    g = tokens_in(output_grad)
-    gouts, grads = [None, None], [None, None]
-    expert_grads = (jnp.zeros((experts, width, 2 * f), jnp.float32), jnp.zeros((experts, width, f), jnp.float32))
-    for l in (1, 0):
-        x, mid, n2, rows, q, k, v, att, ff = kept[l]
-        dn2, expert_grads, sin_g, sdt_g, rw_g = ff_bwd(
-            l, g, ff, n2, place[l], win_pair, wdt_pair, sin_w[l], sdt[l], rwx[l], expert_grads, mbs, dims, 2 + l)
-        dx, wqkv_g, wout_g, gain_g, fgain_g = emu_attn_bwd(
-            dn2, g, mid, fgain[l], x, gain[l], rows, q, k, v, att, wqkv[l], wout[l], cos, sin, rot, mbs, heads, features)
-        g = bf(dx).astype(jnp.float32)
-        gouts[l] = g
-        grads[l] = (gain_g, wqkv_g, wout_g, fgain_g, rw_g, sin_g.astype(jnp.float32), sdt_g.astype(jnp.float32))
-
-    own = [jnp.where(s == 0, p, q_) for p, q_ in zip(*grads)]
-    other = [jnp.where(s == 0, q_, p) for p, q_ in zip(*grads)]
-    own = [p + pass_section(q_) for p, q_ in zip(own, other)]
-    gain_g, wqkv_g, wout_g, fgain_g, rw_g, sin_g, sdt_g = own
-    win_g, wdt_g = expert_grads
-
-    def narrow(v, axis):
-        v = lax.psum_scatter(v, "gy", scatter_dimension=axis, tiled=True)
-        return lax.slice_in_dim(v, 0, width, axis=axis)
-
-    gain_g, fgain_g, rw_g = lax.psum((gain_g, fgain_g, rw_g), "gx")
-    rw_g = rw_g[:, width : width + experts] + rw_g[:, width + experts : width + 2 * experts]
-    hd = heads * DH
-    return (
-        tokens_out(outs),
-        tokens_out(gouts),
-        narrow(gain_g, 1),
-        narrow(wqkv_g, 0).reshape(width, 3, pw)[..., :hd][None],
-        narrow(wout_g, 1)[:hd][None],
-        narrow(fgain_g, 1),
-        narrow(rw_g, 0)[None],
-        win_g.reshape(experts, width, 2, f)[None],
-        wdt_g.transpose(0, 2, 1)[None],
-        narrow(sin_g, 0).reshape(width, 2, f)[None],
-        narrow(sdt_g, 0).T[None],
-    )
-
-
-MESH = pl.DeviceIdType.MESH
-VMEM_BYTES = 60 * 2**20
-
-
-def greet(targets):
-    barrier = pltpu.get_barrier_semaphore()
-    for target in targets:
-        pl.semaphore_signal(barrier, inc=1, device_id=target, device_id_type=MESH)
-    return barrier
-
-
-def remote(src, dst, send, recv, target):
-    return pltpu.make_async_remote_copy(
-        src_ref=src, dst_ref=dst, send_sem=send, recv_sem=recv, device_id=target, device_id_type=MESH
-    )
-
-
-def router_column(rows, e, width, experts):
-    lane = lax.broadcasted_iota(jnp.int32, rows.shape, rows.ndim - 1)
-    mask = (lane == width + e) | (lane == width + experts + e)
-    return jnp.sum(jnp.where(mask, rows.astype(jnp.float32), 0.0), axis=-1, keepdims=True)
-
-
-class Position:
-    def __init__(self, nx, ny):
-        self.s = lax.axis_index("section")
-        self.a = lax.axis_index("gx")
-        self.b = lax.axis_index("gy")
-        self.nx, self.ny = nx, ny
-        self.n = nx * ny
-        self.me = self.a * ny + self.b
-
-    def device(self, index):
-        return (self.s, index // self.ny, lax.rem(index, self.ny))
-
-    def others(self, do):
-        def step(i, c):
-            index = lax.rem(self.me + i, self.n)
-            do(index, index // self.ny, lax.rem(index, self.ny))
-            return c
-
-        lax.fori_loop(1, self.n, step, 0)
-
-    def peers(self, do):
-        for i in range(1, self.nx):
-            do(lax.rem(self.a + i, self.nx))
-
-
-def greet_section(pos):
-    barrier = pltpu.get_barrier_semaphore()
-
-    def one(index, ai, bi):
-        pl.semaphore_signal(barrier, inc=1, device_id=(pos.s, ai, bi), device_id_type=MESH)
-
-    pos.others(one)
-    return barrier
-
-
-def ff_fwd_kernel(cfg, mid, n2, rx, place, place_t, win_a, win_b, wdt_a, wdt_b, sin_w, sdt,
-                  out, slots_o, gu_o, hid_o, rows_o, sgu_o, shid_o,
-                  win, wdt, xsend, xall, nrows, pm, pt, slots, acc, gu, hid, eo, shid, rsend, rrecv, ssend, srecv,
-                  w_sem, x_send, x_recv, n_send, n_recv, rs_send, rs_recv, ag_send, ag_recv,
-                  r_send, r_recv, s_send, s_recv, o_sem):
+    d = ny * pw
+    mbs, sub = x.shape[:2]
+    length = nx * sub
+    b16, f32 = jnp.bfloat16, jnp.float32
+    vm = pl.BlockSpec(memory_space=pltpu.VMEM)
+    hbm = pl.BlockSpec(memory_space=pl.ANY)
+    ac, sc, n = watt.shape[2], sh_g.shape[2], small.shape[0]
+    outs = pl.pallas_call(
+        functools.partial(attn_bwd_kernel, (layer, nx, ny, mbs, sub, width, pw, heads, features, experts)),
+        out_shape=(
+            jax.ShapeDtypeStruct((mbs, sub, d), b16),
+            jax.ShapeDtypeStruct((width, ac), f32),
+            jax.ShapeDtypeStruct((width, sc), f32),
+            jax.ShapeDtypeStruct((n, pw), f32),
+        ),
+        in_specs=[vm] * 16 + [hbm] * len(grads),
+        out_specs=(vm,) + (hbm,) * 3,
+        scratch_shapes=[
+            pltpu.VMEM((mbs, sub, d), b16),
+            pltpu.VMEM((mbs, nx, sub, d), b16),
+            pltpu.VMEM((mbs * length, 3 * pw), b16),
+            pltpu.VMEM((mbs, nx, sub, d), b16),
+            pltpu.VMEM((nx, mbs, sub, d), b16),
+            pltpu.VMEM((mbs * length, pw), b16),
+            pltpu.VMEM((ny, width, ac), b16), pltpu.VMEM((n, d), f32),
+            pltpu.VMEM((ny, width, sc), b16), pltpu.VMEM((ny, width, ac), b16), pltpu.VMEM((n, d), f32),
+            pltpu.VMEM((ny, width, sc), b16), pltpu.VMEM((ny, width, ac), b16), pltpu.VMEM((n, d), f32),
+            pltpu.VMEM((ny, width, sc), b16), pltpu.VMEM((ny, width, ac), b16), pltpu.VMEM((ny, n, pw), f32),
+            pltpu.VMEM((width, sc), f32), pltpu.VMEM((width, ac), f32), pltpu.VMEM((n, pw), f32),
+            pltpu.VMEM((nx, n, pw), f32),
+            flags((nx,)), flags((nx,)), flags((nx,)), flags((nx,)), flags((3,)), flags((3,)),
+            flags((3, ny)), flags((3, ny)), flags((nx,)), flags((nx,)), flags((3,)),
+        ],
+        input_output_aliases={16 + i: 1 + i for i in range(len(grads))},
+        compiler_params=params(ids),
+        cost_estimate=pl.CostEstimate(flops=2 * 10**9, bytes_accessed=2 * 10**7, transcendentals=10**6),
+        name="attention_backward",
+    )(dn2, g, mid, x, small, rows, q, k, v, att, watt, cos, sin, rot, sh_g, rw_g, *grads)
+    return outs[0], outs[1:]
+
+
+def ff_fwd_kernel(cfg, *refs):
     layer, nx, ny, mbs, sub, width, pw, experts, cap, f, sk, ak = cfg
+    (mid, n2, rx, place, place_t, win_a, win_b, wdt_a, wdt_b, shw) = refs[:10]
+    refs = refs[10:]
+    if layer == 0:
+        watt1, refs = refs[0], refs[1:]
+    (out, slots_o, gu_o, hid_o, rows_o, sgu_o, shid_o), refs = refs[:7], refs[7:]
+    if layer == 0:
+        watt_o, refs = refs[0], refs[1:]
+    (win, wdt, xsend, xall, nrows, pm, pt, slots, acc, gu, hid, eo, rsend, rrecv, ssend, srecv,
+     w_sem, x_send, x_recv, n_send, n_recv, rs_send, rs_recv, ag_send, ag_recv,
+     r_send, r_recv, s_send, s_recv, o_sem) = refs[:30]
+    refs = refs[30:]
     pos = Position(nx, ny)
     s, a, b, me = pos.s, pos.a, pos.b, pos.me
     slots_n = experts * cap
     tokens = nx * ny * sub
     d = ny * pw
     barrier = greet_section(pos)
+    if layer == 0:
+        wfull, *w_sems = refs
+        share = Share(pos, 1, watt1, wfull, w_sems)
+        share.signal(barrier, False)
 
     for j, (dst, own, oth) in enumerate(((win, win_a, win_b), (wdt, wdt_a, wdt_b))):
         @pl.when(s == layer)
@@ -993,20 +1256,25 @@
     hi = bf(rv)
     lo = bf(rv - hi.astype(jnp.float32))
     tail = jnp.where(lane < width + experts, hi, lo)
+    n2v = n2[...].reshape(mbs * sub, d)
     for j in range(ny):
-        block = jnp.where(lane < width, n2[...].reshape(mbs * sub, d)[:, j * pw : (j + 1) * pw], tail)
-        xsend[j] = block.reshape(mbs, sub, pw)
-    pl.semaphore_wait(barrier, pos.n - 1)
+        xsend[j] = jnp.where(lane < width, n2v[:, j * pw : (j + 1) * pw], tail).reshape(mbs, sub, pw)
+    if layer == 0:
+        share.wait_barrier(barrier, pos.n - 1, False)
+    else:
+        pl.semaphore_wait(barrier, pos.n - 1)
 
     def send_x(index, ai, bi):
         remote(xsend.at[bi], xall.at[:, b, a], x_send.at[index], x_recv.at[me], (s, ai, bi)).start()
 
     pos.others(send_x)
 
-    def send_n(ai):
-        remote(n2, nrows.at[:, a], n_send.at[ai], n_recv.at[a], (s, ai, b)).start()
-
-    pos.peers(send_n)
+    def copy_n(ai, slot):
+        return remote(n2, nrows.at[:, slot], n_send.at[ai], n_recv.at[slot], (s, ai, b))
+
+    pos.peers(lambda ai: copy_n(ai, a).start())
+    if layer == 0:
+        share.start()
     xall[:, b, a] = xsend[b]
     nrows[:, a] = n2[...]
 
@@ -1036,9 +1304,37 @@
 
     first = (b == ny - 1, b == 0)
     last = (b == 0, b == ny - 1)
-
     up = (ny - 1 - b, b)
     down = (b, ny - 1 - b)
+
+    def shared_part(i):
+        @pl.when(i == 2)
+        def _():
+            pos.peers(lambda ai: copy_n(ai, ai).wait())
+            rows_o[...] = nrows[...]
+            sgu_o[...] = bf(by_blocks(nrows[...].reshape(mbs * nx * sub, d), shw, slice(0, 2 * f), width, pw))
+
+        @pl.when(i == 4)
+        def _():
+            gate = sgu_o[:, :f].astype(jnp.float32)
+            shid_o[...] = bf(gate * jax.nn.sigmoid(gate) * sgu_o[:, f:].astype(jnp.float32))
+            ssend[...] = jnp.zeros_like(ssend)
+
+        @pl.when(i == 6)
+        def _():
+            for j in range(ny):
+                part = mm(shid_o[...], shw[j, :, 2 * f :], ((1,), (1,)))
+                ssend[..., j * pw : j * pw + width] = bf(part).reshape(mbs, nx, sub, width)
+            pos.peers(lambda ai: copy_s(ai, a).start())
+            srecv[a] = ssend[:, a]
+
+        if layer == 0:
+            @pl.when(i == 8)
+            def _():
+                share.forward()
+
+    def copy_s(ai, slot):
+        return remote(ssend.at[:, ai], srecv.at[slot], s_send.at[ai], s_recv.at[slot], (s, ai, b))
 
     def step(i, c):
         for m in range(mbs):
@@ -1084,12 +1380,10 @@
 
                 eo[m, e] = bf(mm(hid[m, e], wdt[e], ((1,), (1,))))
 
+        shared_part(i)
         return c
 
     lax.fori_loop(0, experts + (sk + ak) * (ny - 1), step, 0)
-
-    def wait_n(ai):
-        remote(n2, nrows.at[:, ai], n_send.at[ai], n_recv.at[ai], (s, ai, b)).wait()
 
     for m in range(mbs):
         @pl.when(last[m])
@@ -1106,26 +1400,10 @@
 
     pos.others(send_r)
     rrecv[a, b] = rsend[:, b, a]
-
-    pos.peers(wait_n)
-    sgu = mm(nrows[...].reshape(mbs * nx * sub, d), sin_w[...])
-    sgu_o[...] = bf(sgu)
-    gate = sgu[:, :f]
-    shid[...] = bf(gate * jax.nn.sigmoid(gate) * sgu[:, f:])
-    shid_o[...] = shid[...]
-    rows_o[...] = nrows[...]
-    ssend[...] = bf(mm(shid[...], sdt[...], ((1,), (1,)))).reshape(mbs, nx, sub, d)
-
-    def send_s(ai):
-        remote(ssend.at[:, ai], srecv.at[a], s_send.at[ai], s_recv.at[a], (s, ai, b)).start()
-
-    pos.peers(send_s)
-    srecv[a] = ssend[:, a]
-
-    def wait_s(ai):
-        remote(ssend.at[:, ai], srecv.at[ai], s_send.at[ai], s_recv.at[ai], (s, ai, b)).wait()
-
-    pos.peers(wait_s)
+    if layer == 0:
+        share.finish()
+        pltpu.make_async_copy(wfull, watt_o, o_sem.at[3]).start()
+    pos.peers(lambda ai: copy_s(ai, ai).wait())
 
     def wait_r(index, ai, bi):
         remote(rsend.at[:, bi, ai], rrecv.at[ai, bi], r_send.at[index], r_recv.at[index], (s, ai, bi)).wait()
@@ -1138,7 +1416,7 @@
         part = total[:, :, j * pw : (j + 1) * pw]
         for ai in range(nx):
             part = part + jnp.where(lane < width, rrecv[ai, j].astype(jnp.float32), 0.0)
-        out[:, :, j * pw : (j + 1) * pw] = part
+        out[:, :, j * pw : (j + 1) * pw] = bf(part)
 
     def finish(e, c):
         for m in range(mbs):
@@ -1160,9 +1438,11 @@
 
     pltpu.make_async_copy(hid, hid_o, o_sem.at[2]).wait()
     pltpu.make_async_copy(slots, slots_o, o_sem.at[0]).wait()
-
-
-def ff_fwd(layer, mid, n2, rx, place, win, wdt, sin_w, sdt, mbs, dims, ids):
+    if layer == 0:
+        pltpu.make_async_copy(wfull, watt_o, o_sem.at[3]).wait()
+
+
+def ff_fwd(layer, mid, n2, rx, place, win, wdt, shw, watt1, mbs, dims, ids):
     width, pw, experts, cap = dims
     nx, ny = lax.axis_size("gx"), lax.axis_size("gy")
     f = wdt[0].shape[-1]
@@ -1174,21 +1454,23 @@
     vm = pl.BlockSpec(memory_space=pltpu.VMEM)
     hbm = pl.BlockSpec(memory_space=pl.ANY)
     b16, f32 = jnp.bfloat16, jnp.float32
-    dma = pltpu.SemaphoreType.DMA
     n = nx * ny
+    extra = [watt1] if layer == 0 else []
+    wide = [jax.ShapeDtypeStruct((ny,) + v.shape, b16) for v in extra]
     outs = pl.pallas_call(
         functools.partial(ff_fwd_kernel, cfg),
         out_shape=(
-            jax.ShapeDtypeStruct((mbs, sub, d), f32),
+            jax.ShapeDtypeStruct((mbs, sub, d), b16),
             jax.ShapeDtypeStruct((mbs, experts, cap, pw), b16),
             jax.ShapeDtypeStruct((mbs, experts, cap, 2 * f), b16),
             jax.ShapeDtypeStruct((mbs, experts, cap, f), b16),
             jax.ShapeDtypeStruct((mbs, nx, sub, d), b16),
             jax.ShapeDtypeStruct((mbs * nx * sub, 2 * f), b16),
             jax.ShapeDtypeStruct((mbs * nx * sub, f), b16),
+            *wide,
         ),
-        in_specs=[vm] * 5 + [hbm] * 4 + [vm] * 2,
-        out_specs=(vm, hbm, hbm, hbm, vm, vm, vm),
+        in_specs=[vm] * 5 + [hbm] * 4 + [vm] + [vm] * len(extra),
+        out_specs=(vm, hbm, hbm, hbm, vm, vm, vm) + (hbm,) * len(extra),
         scratch_shapes=[
             pltpu.VMEM((experts, width, 2 * f), b16),
             pltpu.VMEM((experts, width, f), b16),
@@ -1202,37 +1484,37 @@
             pltpu.VMEM((mbs, experts, cap, 2 * f), b16),
             pltpu.VMEM((mbs, experts, cap, f), b16),
             pltpu.VMEM((mbs, experts, cap, width), b16),
-            pltpu.VMEM((mbs * nx * sub, f), b16),
             pltpu.VMEM((mbs, ny, nx, sub, pw), b16),
             pltpu.VMEM((nx, ny, mbs, sub, pw), b16),
             pltpu.VMEM((mbs, nx, sub, d), b16),
             pltpu.VMEM((nx, mbs, sub, d), b16),
-            dma((2,)), dma((n,)), dma((n,)), dma((nx,)), dma((nx,)),
-            dma((mbs, experts)), dma((mbs, experts)), dma((mbs, experts)), dma((mbs, experts)),
-            dma((n,)), dma((n,)), dma((nx,)), dma((nx,)), dma((3,)),
-        ],
-        compiler_params=pltpu.CompilerParams(collective_id=ids, has_side_effects=True, vmem_limit_bytes=VMEM_BYTES),
+            flags((2,)), flags((n,)), flags((n,)), flags((nx,)), flags((nx,)),
+            flags((mbs, experts)), flags((mbs, experts)), flags((mbs, experts)), flags((mbs, experts)),
+            flags((n,)), flags((n,)), flags((nx,)), flags((nx,)), flags((4,)),
+        ] + ([pltpu.VMEM(wide[0].shape, b16)] + share_sems(ny) if extra else []),
+        compiler_params=params(ids),
         cost_estimate=pl.CostEstimate(flops=4 * 10**9, bytes_accessed=30 * 10**6, transcendentals=10**6),
         name="experts_forward",
     )(
         mid.reshape(mbs, sub, d), n2.reshape(mbs, sub, d), rx, place, jnp.swapaxes(place, 1, 2),
-        win[0], win[1], wdt[0], wdt[1], sin_w, sdt,
-    )
-    out, slots_k, gu, hid, rows2, sgu, shid = outs
-    return out.reshape(mbs * sub, d), (slots_k, gu, hid, rows2.reshape(-1, d), sgu, shid)
-
-
-FWD_SKEW = (1, 1)
-
-
-def ff_bwd_kernel(cfg, g, n2, place, place_t, rwx, slots_i, gu_i, hid_i, rows2, sgu, shid,
-                  win_a, win_b, wdt_a, wdt_b, sin_w, sdt, win_g_i, wdt_g_i,
-                  out, rw_g, sin_g, sdt_g, win_g, wdt_g,
-                  win, wdt, gsend, gall, grows, pm, pt, slots, gslots, gown, hid, acc, dh, dgu, deo,
-                  wxi, wxd, sti, std, dsgu, rsend, rrecv, ssend, srecv,
-                  w_sem, x_send, x_recv, n_send, n_recv, rs_send, rs_recv, ag_send, ag_recv,
-                  wi_send, wi_recv, wd_send, wd_recv, r_send, r_recv, s_send, s_recv, l_sem, st_sem):
+        win[0], win[1], wdt[0], wdt[1], shw, *extra,
+    )
+    return outs[0], outs[1:7], outs[7] if extra else None
+
+
+FWD_SKEW = (2, 2)
+
+
+def ff_bwd_kernel(cfg, *refs):
     layer, nx, ny, mbs, sub, width, pw, experts, cap, f, sk, ak = cfg
+    (g, n2, place, place_t, small, slots_i, gu_i, hid_i, rows2, sgu, shid,
+     win_a, win_b, wdt_a, wdt_b, shw) = refs[:16]
+    refs = refs[16 + (0 if layer else 2) :]
+    (out, rw_g, sh_g, win_g, wdt_g,
+     win, wdt, gsend, gall, grows, pm, pt, slots, gslots, gown, hid, acc, dh, dgu, deo,
+     wxi, wxd, sti, std, dsgu, rsend, rrecv, ssend, srecv, rwx,
+     w_sem, x_send, x_recv, n_send, n_recv, rs_send, rs_recv, ag_send, ag_recv,
+     wi_send, wi_recv, wd_send, wd_recv, r_send, r_recv, s_send, s_recv, l_sem, st_sem) = refs
     pos = Position(nx, ny)
     s, a, b, me = pos.s, pos.a, pos.b, pos.me
     keeper = s == layer
@@ -1280,13 +1562,16 @@
 
     pos.others(send_x)
 
-    def send_n(ai):
-        remote(g, grows.at[:, a], n_send.at[ai], n_recv.at[a], (s, ai, b)).start()
-
-    pos.peers(send_n)
+    def copy_n(ai, slot):
+        return remote(g, grows.at[:, slot], n_send.at[ai], n_recv.at[slot], (s, ai, b))
+
+    pos.peers(lambda ai: copy_n(ai, a).start())
     gall[:, b, a] = gsend[b]
     grows[:, a] = g[...]
     deo[...] = jnp.zeros_like(deo)
+    rwx[...] = jnp.zeros_like(rwx)
+    rwx[width : width + experts] = bf(small[:experts])
+    rwx[width + experts : width + 2 * experts] = bf(small[:experts])
 
     def wait_x(index, ai, bi):
         remote(gsend.at[0], gall.at[:, bi, ai], x_send.at[index], x_recv.at[index], (s, ai, bi)).wait()
@@ -1335,6 +1620,39 @@
     full = (sk + ak) * (ny - 1)
     late = 2
 
+    def copy_s(ai, slot):
+        return remote(ssend.at[:, ai], srecv.at[slot], s_send.at[ai], s_recv.at[slot], (s, ai, b))
+
+    def shared_part(i):
+        @pl.when(i == 2)
+        def _():
+            pos.peers(lambda ai: copy_n(ai, ai).wait())
+            ssend[...] = jnp.zeros_like(ssend)
+            dsh = by_blocks(grows[...].reshape(mbs * nx * sub, d), shw, slice(2 * f, 3 * f), width, pw)
+            dsg, dsu, _ = act_back(sgu[:, :f].astype(jnp.float32), sgu[:, f:].astype(jnp.float32), dsh, None)
+            dsgu[:, :f] = bf(dsg)
+            dsgu[:, f:] = bf(dsu)
+
+        @pl.when(i == 4)
+        def _():
+            for j in range(ny):
+                part = mm(dsgu[...], shw[j, :, : 2 * f], ((1,), (1,)))
+                ssend[..., j * pw : j * pw + width] = bf(part).reshape(mbs, nx, sub, width)
+            pos.peers(lambda ai: copy_s(ai, a).start())
+            srecv[a] = ssend[:, a]
+
+        @pl.when(i == 6)
+        def _():
+            for j in range(ny):
+                rj = rows2[:, :, :, j * pw : j * pw + width].reshape(mbs * nx * sub, width)
+                sh_g[j, :, : 2 * f] = bf(mm(rj, dsgu[...], ((0,), (0,))))
+
+        @pl.when(i == 8)
+        def _():
+            for j in range(ny):
+                gj = grows[:, :, :, j * pw : j * pw + width].reshape(mbs * nx * sub, width)
+                sh_g[j, :, 2 * f :] = bf(mm(gj, shid[...], ((0,), (0,))))
+
     def step(i, c):
         for m in range(mbs):
             e0 = i - sk * up[m]
@@ -1414,6 +1732,7 @@
             for copy in st_copies(e, slot):
                 copy.start()
 
+        shared_part(i)
         return c
 
     lax.fori_loop(0, experts + full + late, step, 0)
@@ -1430,28 +1749,7 @@
     pos.others(send_r)
     rrecv[a, b] = rsend[:, b, a]
 
-    def wait_n(ai):
-        remote(g, grows.at[:, ai], n_send.at[ai], n_recv.at[ai], (s, ai, b)).wait()
-
-    pos.peers(wait_n)
-    gr = grows[...].reshape(mbs * nx * sub, d)
-    dsg, dsu, _ = act_back(sgu[:, :f].astype(jnp.float32), sgu[:, f:].astype(jnp.float32), mm(gr, sdt[...]), None)
-    dsgu[:, :f] = bf(dsg)
-    dsgu[:, f:] = bf(dsu)
-    ssend[...] = bf(mm(dsgu[...], sin_w[...], ((1,), (1,)))).reshape(mbs, nx, sub, d)
-
-    def send_s(ai):
-        remote(ssend.at[:, ai], srecv.at[a], s_send.at[ai], s_recv.at[a], (s, ai, b)).start()
-
-    pos.peers(send_s)
-    srecv[a] = ssend[:, a]
-    sin_g[...] = bf(mm(rows2[...], dsgu[...], ((0,), (0,))))
-    sdt_g[...] = bf(mm(gr, shid[...], ((0,), (0,))))
-
-    def wait_s(ai):
-        remote(ssend.at[:, ai], srecv.at[ai], s_send.at[ai], s_recv.at[ai], (s, ai, b)).wait()
-
-    pos.peers(wait_s)
+    pos.peers(lambda ai: copy_s(ai, ai).wait())
 
     def wait_r(index, ai, bi):
         remote(rsend.at[:, bi, ai], rrecv.at[ai, bi], r_send.at[index], r_recv.at[index], (s, ai, bi)).wait()
@@ -1468,13 +1766,14 @@
         parts.append(jnp.where(lane < width, part, 0.0))
     hi = bf(dlog)
     lo = bf(dlog - hi.astype(jnp.float32))
-    total = mm(hi, rwx[...], ((1,), (1,))) + mm(lo, rwx[...], ((1,), (1,)))
+    total = mm(hi, rwx[...]) + mm(lo, rwx[...])
     for ai in range(nx):
         total = total + srecv[ai].astype(jnp.float32).reshape(mbs * sub, d)
     for j in range(ny):
         out[:, j * pw : (j + 1) * pw] = total[:, j * pw : (j + 1) * pw] + parts[j]
     n2v = n2[...].reshape(mbs * sub, d)
-    rw_g[...] = mm(n2v, hi, ((0,), (0,))) + mm(n2v, lo, ((0,), (0,)))
+    rw_t = mm(hi, n2v, ((0,), (0,))) + mm(lo, n2v, ((0,), (0,)))
+    rw_g[...] = rw_t[width : width + experts] + rw_t[width + experts : width + 2 * experts]
 
     def finish(e, c):
         for m in range(mbs):
@@ -1502,7 +1801,7 @@
                 copy.wait()
 
 
-def ff_bwd(layer, g, kept, n2, place, win, wdt, sin_w, sdt, rwx, grads, mbs, dims, ids):
+def ff_bwd(layer, g, kept, n2, place, win, wdt, shw, small, grads, mbs, dims, ids):
     width, pw, experts, cap = dims
     slots_k, gu, hid, rows2, sgu, shid = kept
     nx, ny = lax.axis_size("gx"), lax.axis_size("gy")
@@ -1515,20 +1814,18 @@
     vm = pl.BlockSpec(memory_space=pltpu.VMEM)
     hbm = pl.BlockSpec(memory_space=pl.ANY)
     b16, f32 = jnp.bfloat16, jnp.float32
-    dma = pltpu.SemaphoreType.DMA
     n = nx * ny
-    out, rw_g, sin_g, sdt_g, win_g, wdt_g = pl.pallas_call(
+    out, rw_g, sh_g, win_g, wdt_g = pl.pallas_call(
         functools.partial(ff_bwd_kernel, cfg),
         out_shape=(
             jax.ShapeDtypeStruct((mbs * sub, d), f32),
-            jax.ShapeDtypeStruct((d, pw), f32),
-            jax.ShapeDtypeStruct((d, 2 * f), b16),
-            jax.ShapeDtypeStruct((d, f), b16),
+            jax.ShapeDtypeStruct((experts, d), f32),
+            jax.ShapeDtypeStruct(shw.shape, b16),
             jax.ShapeDtypeStruct((experts, width, 2 * f), f32),
             jax.ShapeDtypeStruct((experts, width, f), f32),
         ),
-        in_specs=[vm] * 5 + [hbm] * 3 + [vm] * 3 + [hbm] * 4 + [vm] * 2 + [hbm] * 2,
-        out_specs=(vm, vm, vm, vm, hbm, hbm),
+        in_specs=[vm] * 5 + [hbm] * 3 + [vm] * 3 + [hbm] * 4 + [vm] + [hbm] * len(grads),
+        out_specs=(vm, vm, vm, hbm, hbm),
         scratch_shapes=[
             pltpu.VMEM((experts, width, 2 * f), b16),
             pltpu.VMEM((experts, width, f), b16),
@@ -1554,23 +1851,106 @@
             pltpu.VMEM((nx, ny, mbs, sub, pw), b16),
             pltpu.VMEM((mbs, nx, sub, d), b16),
             pltpu.VMEM((nx, mbs, sub, d), b16),
-            dma((2,)), dma((n,)), dma((n,)), dma((nx,)), dma((nx,)),
-            dma((mbs, experts)), dma((mbs, experts)), dma((mbs, experts)), dma((mbs, experts)),
-            dma((experts,)), dma((experts,)), dma((experts,)), dma((experts,)),
-            dma((n,)), dma((n,)), dma((nx,)), dma((nx,)), dma((3,)), dma((2, 2)),
+            pltpu.VMEM((pw, d), b16),
+            flags((2,)), flags((n,)), flags((n,)), flags((nx,)), flags((nx,)),
+            flags((mbs, experts)), flags((mbs, experts)), flags((mbs, experts)), flags((mbs, experts)),
+            flags((experts,)), flags((experts,)), flags((experts,)), flags((experts,)),
+            flags((n,)), flags((n,)), flags((nx,)), flags((nx,)), flags((3,)), flags((2, 2)),
         ],
-        input_output_aliases={17: 4, 18: 5},
-        compiler_params=pltpu.CompilerParams(collective_id=ids, has_side_effects=True, vmem_limit_bytes=VMEM_BYTES),
+        input_output_aliases={16 + i: 3 + i for i in range(len(grads))},
+        compiler_params=params(ids),
         cost_estimate=pl.CostEstimate(flops=8 * 10**9, bytes_accessed=60 * 10**6, transcendentals=10**6),
         name="experts_backward",
     )(
-        bf(g).reshape(mbs, sub, d), n2.reshape(mbs, sub, d), place, jnp.swapaxes(place, 1, 2), rwx,
-        slots_k, gu, hid, rows2, sgu, shid, win[0], win[1], wdt[0], wdt[1], sin_w, sdt, *grads,
-    )
-    return out, (win_g, wdt_g), sin_g, sdt_g, rw_g
+        g, n2.reshape(mbs, sub, d), place, jnp.swapaxes(place, 1, 2), small,
+        slots_k, gu, hid, rows2, sgu, shid, win[0], win[1], wdt[0], wdt[1], shw, *grads,
+    )
+    return out, (win_g, wdt_g), sh_g, rw_g
 
 
 BWD_SKEW = (2, 2)
+
+
+def fast_device(block_input, output_grad, attention_gain, attention_in, attention_out, feed_gain,
+                router_weight, expert_in, expert_down, shared_in, shared_down, routes):
+    s = lax.axis_index("section")
+    ny = lax.axis_size("gy")
+    nx = lax.axis_size("gx")
+    mbs = block_input.shape[0] // 2
+    width = block_input.shape[2]
+    features = width * ny
+    experts = expert_in.shape[1]
+    f = expert_in.shape[-1]
+    pw = lanes_up(width + 2 * experts)
+    tokens = routes.shape[2]
+    cap = 5 * tokens // (2 * experts)
+    length = tokens // ny
+    heads = attention_in.shape[-1] // DH
+    dims = (width, pw, experts, cap)
+
+    att_block = jnp.concatenate([
+        pad_to(attention_in[0], 2, pw).reshape(width, 3 * pw), pad_to(attention_out[0].T, 1, pw)], 1)
+    sh_block = jnp.concatenate([shared_in[0].reshape(width, 2 * f), shared_down[0].T], 1)
+    small = jnp.concatenate([
+        router_weight[0].T.astype(jnp.float32), feed_gain, attention_gain, jnp.zeros((6, width), jnp.float32)], 0)
+    tin = lax.dynamic_slice_in_dim(jnp.stack([block_input, output_grad]), s * mbs, mbs, 1)
+    tok, watt0, small = entry(pad_to(tin, 3, pw), att_block, pad_to(small, 1, pw), 0)
+
+    win = expert_in[0].reshape(experts, width, 2 * f)
+    win = (win, pass_section(win))
+    wdt = expert_down[0].transpose(0, 2, 1)
+    wdt = (wdt, pass_section(wdt))
+    other = pass_section(routes[0])
+    pair = jnp.stack([jnp.where(s == 0, routes[0], other), jnp.where(s == 0, other, routes[0])])
+    place = places_of(lax.dynamic_slice_in_dim(pair, s * mbs, mbs, 1), experts, cap)
+
+    half = DH // 2
+    freq = 10000.0 ** (-jnp.arange(half, dtype=jnp.float32) / half)
+    ang = jnp.arange(length, dtype=jnp.float32)[:, None] * freq[None]
+    lanes = jnp.tile(ang, (1, 2 * heads))
+    cos = pad_to(jnp.cos(lanes), 1, pw)
+    sin = pad_to(jnp.sin(lanes), 1, pw)
+    rot = pad_to(pad_to(rot_columns(jnp.eye(heads * DH, dtype=jnp.float32)), 0, pw), 1, pw).astype(jnp.bfloat16)
+
+    x, watt = tok[0], [watt0, None]
+    kept, outs = [], []
+    for l in range(2):
+        mid, n2, rx, rows, q, k, v, att, shw = attn_fwd(
+            l, x, small[l], watt[l], sh_block, cos, sin, rot, dims, heads, features, 1 + l)
+        out, ff, wide = ff_fwd(l, mid, n2, rx, place[l], win, wdt, shw, att_block, mbs, dims, 3 + l)
+        watt[1] = wide if l == 0 else watt[1]
+        kept.append((x, mid, n2, rows, q, k, v, att, shw, ff))
+        x = out
+        outs.append(x)
+    g = tok[1]
+    gouts = [None, None]
+    expert_grads = dense_grads = ()
+    for l in (1, 0):
+        x, mid, n2, rows, q, k, v, att, shw, ff = kept[l]
+        dn2, expert_grads, sh_g, rw_g = ff_bwd(
+            l, g, ff, n2, place[l], win, wdt, shw, small[l], expert_grads, mbs, dims, 5 + l)
+        g, dense_grads = attn_bwd(
+            l, dn2, g, mid, x, small[l], rows, q, k, v, att, watt[l], cos, sin, rot, sh_g, rw_g, dense_grads,
+            dims, heads, features, 7 + l)
+        gouts[l] = g
+
+    both = leave(jnp.stack([outs[0], gouts[0]]), jnp.stack([outs[1], gouts[1]]), pw, 9)[..., :width]
+    att_g, sh_g, small_g = dense_grads
+    win_g, wdt_g = expert_grads
+    hd = heads * DH
+    return (
+        both[0][None],
+        both[1][None],
+        small_g[experts + 1 : experts + 2, :width],
+        att_g[:, : 3 * pw].reshape(width, 3, pw)[..., :hd][None],
+        att_g[:, 3 * pw : 3 * pw + hd].T[None],
+        small_g[experts : experts + 1, :width],
+        small_g[:experts, :width].T[None],
+        win_g.reshape(experts, width, 2, f)[None],
+        wdt_g.transpose(0, 2, 1)[None],
+        sh_g[:, : 2 * f].reshape(width, 2, f)[None],
+        sh_g[:, 2 * f :].T[None],
+    )
 
 
 def solution(mesh):

time: 1500 us -> 900 us (0.60)
  waiting for transfers between devices: 504 us -> 0.01 us
  Pallas kernels: 598 us -> 809 us
  blocking collectives: 160 us -> 0 us
  other arithmetic: 63.5 us -> 5.48 us
  local copies, waits for them, and re-layouts: 110 us -> 71.6 us
  matrix products: 31.2 us -> 0.6 us
  between operations: 17.3 us -> 1.49 us
    pallas_call x0 -> x6, Pallas kernels: none -> 213 us  [the longest x2 86.8 us: attn_bwd(): pl.pallas_call(functools.partial(attn_bwd_kernel, (layer, nx, ny, mbs, su...]
    reduce_scatter x5 -> x0, waiting for transfers between devices: 204 us -> none  [narrow(): v = lax.psum_scatter(v, 'gy', scatter_dimension=axis, tiled=True)]
    all_gather x7 -> x0, waiting for transfers between devices: 153 us -> none  [the longest x2 129 us: tokens_out(): t = lax.all_gather(t, 'gy', axis=1, tiled=True)]
    all_gather x12 -> x0, blocking collectives: 150 us -> none  [the longest x4 59.9 us: wide(): return lax.all_gather(v, 'gy', axis=axis, tiled=True)]
    unnamed x25 -> x0, waiting for transfers between devices: 74.6 us -> none
    psum x1 -> x0, waiting for transfers between devices: 52.6 us -> none  [fast_device(): gain_g, fgain_g, rw_g = lax.psum((gain_g, fgain_g, rw_g), 'gx')]
    dot_general x102 -> x0, matrix products: 29.8 us -> none  [mm(): lax.dot_general(a, b, (dims, ((), ())), preferred_element_type=jnp.float32)]
    pallas_call x2, Pallas kernels: 313 us -> 288 us  [ff_fwd(): pl.pallas_call(functools.partial(ff_fwd_kernel, cfg), out_shape=(jax.Shap...]
  transfers between devices with their start and end apart: 38 -> 3, of which waited for: 21 -> 0; matrix products, arithmetic and copies ran while one was open for 10% -> 3% of each run, Pallas kernels for 11% -> 9%
where the time goes in v3:
time: 900 us; the launch traced here: 890 us
  Pallas kernels  809 us (90%)
  local copies, waits for them, and re-layouts  71.6 us (8%)
    pallas_call x2, Pallas kernels, ff_bwd(): pl.pallas_call(functools.partial(ff_bwd_kernel, cfg), out_shape=(jax.Shap...  309 us
    pallas_call x2, Pallas kernels, ff_fwd(): pl.pallas_call(functools.partial(ff_fwd_kernel, cfg), out_shape=(jax.Shap...  288 us
    pallas_call x2, Pallas kernels, attn_bwd(): pl.pallas_call(functools.partial(attn_bwd_kernel, (layer, nx, ny, mbs, su...  86.8 us
    pallas_call x2, Pallas kernels, attn_fwd(): pl.pallas_call(functools.partial(attn_fwd_kernel, (layer, nx, ny, mbs, su...  66.1 us
    pallas_call x1, Pallas kernels, entry(): pl.pallas_call(functools.partial(entry_kernel, (nx, ny, mbs, sub, pw)), o...  46.1 us
  transfers between devices with their start and end apart: 3, of which 0 were waited for; matrix products, arithmetic and copies ran while one was open for 3% of the time, Pallas kernels for 9%

profile of v3, /device:TPU:0, one launch (start us, length us, event | category | flops | bytes accessed | tf_op | source)
XLA Modules:
  0.0 889.6 jit_solution(4432808495780266916)
XLA Ops:
  0.7 11.1 %reshape_squeeze.7.refs_5_.refs_11_ = bf16[16,192,1024]{2,1,0:T(8,128)(2,1)} reshape(bf16[1,16,192,2,512]{4,3,2,1,0:T(2,128)(2,1)} %param.19) | data formatting | bytes 12582912 | tf_op jit(solution)/shard_map/reshape;squeeze | solution.py:1899
  13.0 0.6 pad.36.small
  13.9 0.6 pad.38.sin.refs_12_
  14.7 0.7 pad.37.cos.refs_11_
  15.3 1.0 copy.60
  16.5 0.7 copy.63
  17.3 1.1 copy.57
  18.3 1.8 copy.58
  20.1 1.6 pad.60.rot.refs_13_
  21.7 0.9 fusion.14
  22.7 0.7 pad.33.tin
  23.4 1.3 copy.75
  25.0 0.8 fusion.13.watt.refs_10_
  25.8 46.1 %entry.1 = (bf16[2,2,32,1024]{3,2,1,0:T(8,128)(2,1)}, bf16[4,192,1024]{2,1,0:T(8,128)(2,1)}, f32[2,24,1024]{2,1,0:T(8,128)}) custom-call(bf16[2,2,128,256]{3,2,1,0:T(8,128)(2,1)} %pad.33.tin, bf16[192,1024]{1,0:T(8,128)(2,1)} %fusion.13.watt.refs_10_, f32[24,256]{1,0:T(8,128)} %pad.36.small), custom_call_target="tpu_custom_call" | custom-call | tf_op jit(solution)/shard_map/entry/pallas_call | solution.py:808
  71.9 1.6 slice_bitcast_fusion.9
  73.5 1.7 slice_bitcast_fusion.8
  75.2 0.9 pad_maximum_fusion.shw
  76.0 30.5 %attention_forward.2 = (f32[64,1024]{1,0:T(8,128)}, bf16[64,1024]{1,0:T(8,128)(2,1)}, f32[64,256]{1,0:T(8,128)}, bf16[2,4,32,1024]{3,2,1,0:T(8,128)(2,1)}, bf16[...) custom-call(bf16[2,32,1024]{2,1,0:T(8,128)(2,1)} %get-tuple-element., ...), custom_call_target="tpu_custom_call" | custom-call | flops 1000000000 | bytes 10000000 | tf_op jit(solution)/shard_map/attention_forward/pallas_call | solution.py:973
  106.6 1.3 copy.74
  108.0 1.8 eq.27
  109.7 0.6 fusion.9
  110.3 2.0 convert_element_type.52
  112.4 1.6 add_bitcast_fusion
  114.0 1.4 slice_bitcast_fusion.1
  115.4 1.8 copy.68.refs_3_.refs_2_
  117.2 1.8 copy.66.refs_3_.refs_2_
  119.0 144.9 %experts_forward.2 = (bf16[2,32,1024]{2,1,0:T(8,128)(2,1)}, bf16[2,16,80,256]{3,2,1,0:T(8,128)(2,1)}, bf16[2,16,80,1024]{3,2,1,0:T(8,128)(2,1)}, bf16[2,16,80,51...) custom-call(f32[2,32,1024]{2,1,0:T(8,128)} %bitcast.108, ...), custom_call_target="tpu_custom_call" | custom-call | flops 4000000000 | bytes 30000000 | tf_op jit(solution)/shard_map/experts_forward/pallas_call | solution.py:1460
  264.0 35.6 %attention_forward.3 = (f32[64,1024]{1,0:T(8,128)}, bf16[64,1024]{1,0:T(8,128)(2,1)}, f32[64,256]{1,0:T(8,128)}, bf16[2,4,32,1024]{3,2,1,0:T(8,128)(2,1)}, bf16[...) custom-call(bf16[2,32,1024]{2,1,0:T(8,128)(2,1)} %get-tuple-element., ...), custom_call_target="tpu_custom_call" | custom-call | flops 1000000000 | bytes 10000000 | tf_op jit(solution)/shard_map/attention_forward/pallas_call | solution.py:973
  299.6 142.7 %experts_forward.3 = (bf16[2,32,1024]{2,1,0:T(8,128)(2,1)}, bf16[2,16,80,256]{3,2,1,0:T(8,128)(2,1)}, bf16[2,16,80,1024]{3,2,1,0:T(8,128)(2,1)}, bf16[2,16,80,51...) custom-call(f32[2,32,1024]{2,1,0:T(8,128)} %bitcast.121, ...), custom_call_target="tpu_custom_call" | custom-call | flops 4000000000 | bytes 30000000 | tf_op jit(solution)/shard_map/experts_forward/pallas_call | solution.py:1460
  442.3 136.1 %experts_backward.2 = (f32[64,1024]{1,0:T(8,128)}, f32[16,1024]{1,0:T(8,128)}, bf16[4,192,1536]{2,1,0:T(8,128)(2,1)}, f32[16,192,1024]{2,1,0:T(8,128)}, f32[16,192,512]{2,1,0:T(8,128)}) custom-call(bf16[2,32,1024]{2,1,0:T(8,128)(2,1)} %get-tuple-element.159.refs_0_.refs_1_, bf16[2,32,1024]{2,1,0:T(8,128)(2,1)} %bitcast.114, ...), custom_call_target="tpu_custom_call" | custom-call | flops 8000000000 | bytes 60000000 | tf_op jit(solution)/shard_map/experts_backward/pallas_call | solution.py:1818
  578.3 21.7 %attention_backward.2 = (bf16[2,32,1024]{2,1,0:T(8,128)(2,1)}, f32[192,1024]{1,0:T(8,128)}, f32[192,1536]{1,0:T(8,128)}, f32[24,256]{1,0:T(8,128)}) custom-call(f32[64,1024]{1,0:T(8,128)} %get-tuple-element.84.refs_0_, bf16[2,32,1024]{2,1,0:T(8,128)(2,1)} %get-tuple-element.159.refs_0_.refs_1_, f32[64,1024]{1,0:T(8,128)} %get-tuple-element.75.refs_2_, ...), custom_call_target="tpu_custom_call" | custom-call | flops 2000000000 | bytes 20000000 | tf_op jit(solution)/shard_map/attention_backward/pallas_call | solution.py:1187
  600.0 173.1 %experts_backward.3 = (f32[64,1024]{1,0:T(8,128)}, f32[16,1024]{1,0:T(8,128)}, bf16[4,192,1536]{2,1,0:T(8,128)(2,1)}, f32[16,192,1024]{2,1,0:T(8,128)}, f32[16,192,512]{2,1,0:T(8,128)}) custom-call(bf16[2,32,1024]{2,1,0:T(8,128)(2,1)} %get-tuple-element.92.refs_0_.refs_1_, ...), custom_call_target="tpu_custom_call", output_to_operand_aliasing={{3}: (16, {}), {4}: (17, {})} | custom-call | flops 8000000000 | bytes 60000000 | tf_op jit(solution)/shard_map/experts_backward/pallas_call | solution.py:1818
  773.1 65.1 %attention_backward.3 = (bf16[2,32,1024]{2,1,0:T(8,128)(2,1)}, f32[192,1024]{1,0:T(8,128)}, f32[192,1536]{1,0:T(8,128)}, f32[24,256]{1,0:T(8,128)}) custom-call(f32[64,1024]{1,0:T(8,128)} %get-tuple-element.101.refs_0_, bf16[2,32,1024]{2,1,0:T(8,128)(2,1)} %get-tuple-element.92.refs_0_.refs_1_, ...), custom_call_target="tpu_custom_call", output_to_operand_aliasing={{1}: (16, {}), {2}: (17, {}), {3}: (18, {})} | custom-call | flops 2000000000 | bytes 20000000 | tf_op jit(solution)/shard_map/attention_backward/pallas_call | solution.py:1187
  838.3 1.4 fusion.23
  839.7 1.3 slice_bitcast_fusion.11
  841.0 0.9 slice_bitcast_fusion.6
  842.0 1.1 slice.75
  843.1 1.8 slice_bitcast_fusion.5
  844.9 0.8 pad_maximum_fusion.1
  845.8 13.6 %leave.1 = bf16[2,4,128,256]{3,2,1,0:T(8,128)(2,1)} custom-call(bf16[2,2,32,1024]{3,2,1,0:T(8,128)(2,1)} %get-tuple-element.168.pair0, bf16[2,2,32,1024]{3,2,1,0:T(8,128)(2,1)} %get-tuple-element.169.pair1), custom_call_target="tpu_custom_call" | custom-call | tf_op jit(solution)/shard_map/leave/pallas_call | solution.py:867
  859.4 1.1 fusion.22
  860.5 0.8 copy.71
  861.3 0.8 copy.70
  862.1 0.8 copy.73
  863.4 0.9 copy.72
  864.3 1.5 broadcast_in_dim_reshape.8
  865.8 16.9 %broadcast_in_dim_reshape.7 = f32[1,16,192,2,512]{4,3,2,1,0:T(2,128)} reshape(f32[16,192,1024]{2,1,0:T(8,128)} %get-tuple-element.116) | data formatting | bytes 25165824 | tf_op jit(solution)/shard_map/broadcast_in_dim;reshape | solution.py:1949
  882.7 6.5 copy.90
  (55 shorter events, 2.5 us)
Async XLA Ops:
  0.6 11.6 %copy-start.8 = (s32[1,4,512,2]{2,3,1,0:T(2,128)S(1)}, s32[1,4,512,2]{2,3,1,0:T(2,128)}, u32[]{:S(2)}) copy-start(s32[1,4,512,2]{2,3,1,0:T(2,128)} %param.23) | copy-start | bytes 49156
  0.7 11.7 %copy-start = (bf16[1,16,512,192]{2,3,1,0:T(8,128)(2,1)S(1)}, bf16[1,16,512,192]{2,3,1,0:T(8,128)(2,1)}, u32[]{:S(2)}) copy-start(bf16[1,16,512,192]{2,3,1,0:T(8,128)(2,1)} %param.20) | copy-start | bytes 9437188
  0.7 12.3 %copy-start.9 = (bf16[1,192,16]{1,2,0:T(8,128)(2,1)S(1)}, bf16[1,192,16]{1,2,0:T(8,128)(2,1)}, u32[]{:S(2)}) copy-start(bf16[1,192,16]{1,2,0:T(8,128)(2,1)} %param.18) | copy-start | bytes 18436
  0.7 12.3 %copy-start.11 = (f32[1,192]{1,0:T(1,128)S(1)}, f32[1,192]{1,0:T(1,128)}, u32[]{:S(2)}) copy-start(f32[1,192]{1,0:T(1,128)} %param.17) | copy-start | bytes 2308
  0.7 12.3 %copy-start.10 = (f32[1,192]{1,0:T(1,128)S(1)}, f32[1,192]{1,0:T(1,128)}, u32[]{:S(2)}) copy-start(f32[1,192]{1,0:T(1,128)} %param.14) | copy-start | bytes 2308
  11.8 107.2 %collective-permute-start.1 = (bf16[16,192,1024]{2,1,0:T(8,128)(2,1)}, bf16[16,192,1024]{2,1,0:T(8,128)(2,1)}, u32[]{:S(2)}, u32[]{:S(2)}) collective-permute-start(bf16[16,192,1024]{2,1,0:T(8,128)(2,1)} %reshape_squeeze.7.refs_5_.refs_11_), channel_id=1, source_target_pairs={{0,16},{16,0},{1,17},{17,1},{2,18},{18,2},{3,19},{19,3},{4,20},{20... | collective-permute-start | bytes 18874376 | tf_op jit(solution)/shard_map/ppermute | solution.py:18
  12.3 94.3 %collective-permute-start = (s32[4,512,2]{1,0,2:T(4,128)S(1)}, s32[4,512,2]{1,0,2:T(4,128)S(1)}, u32[]{:S(2)}, u32[]{:S(2)}) collective-permute-start(s32[4,512,2]{1,0,2:T(4,128)S(1)} %bitcast.126), channel_id=1, source_target_pairs={{0,16},{16,0},{1,17},{17,1},{2,18},{18,2},{3,19},{19,3},{4,20},{20... | collective-permute-start | bytes 49160 | tf_op jit(solution)/shard_map/ppermute | solution.py:18
  12.4 106.6 %collective-permute-start.2 = (bf16[16,192,512]{2,1,0:T(8,128)(2,1)S(1)}, bf16[16,192,512]{2,1,0:T(8,128)(2,1)}, u32[]{:S(2)}, u32[]{:S(2)}) collective-permute-start(bf16[16,192,512]{2,1,0:T(8,128)(2,1)S(1)} %bitcast.102), channel_id=1, source_target_pairs={{0,16},{16,0},{1,17},{17,1},{2,18},{18,2},{3,19},{19,3},{4,20},{20... | collective-permute-start | bytes 9437192 | tf_op jit(solution)/shard_map/ppermute | solution.py:18
  20.1 4.8 copy-start.3
  23.4 51.8 %copy-start.4 = (bf16[1,512,192]{1,2,0:T(8,128)(2,1)S(1)}, bf16[1,512,192]{1,2,0:T(8,128)(2,1)}, u32[]{:S(2)}) copy-start(bf16[1,512,192]{1,2,0:T(8,128)(2,1)} %param.22) | copy-start | bytes 589828
  838.2 6.6 copy-start.1
  838.3 6.7 copy-start.2
  838.3 6.7 copy-start.5
  838.3 6.7 copy-start.6
  838.3 6.7 copy-start.7

commit v4 on v0

--- a/solution.py
+++ b/solution.py
@@ -1,6 +1,10 @@
+import functools
+
 import jax
 import jax.numpy as jnp
 from jax import lax
+from jax.experimental import pallas as pl
+from jax.experimental.pallas import tpu as pltpu
 from jax.sharding import PartitionSpec as P
 
 DH = 64
@@ -510,6 +514,1437 @@
     )
 
 
+def lanes_up(n):
+    return -(-n // 128) * 128
+
+
+def rot_columns(w):
+    shape = w.shape
+    w = w.reshape(shape[:-1] + (-1, 2, DH // 2))
+    w = jnp.stack([-w[..., 1, :], w[..., 0, :]], axis=-2)
+    return w.reshape(shape)
+
+
+def pad_to(v, axis, n):
+    pads = [(0, 0)] * v.ndim
+    pads[axis] = (0, n - v.shape[axis])
+    return jnp.pad(v, pads)
+
+
+def mm(a, b, dims=((1,), (0,))):
+    return lax.dot_general(a, b, (dims, ((), ())), preferred_element_type=jnp.float32)
+
+
+def bf(v):
+    return v.astype(jnp.bfloat16)
+
+
+def head_mask(pw, h):
+    lane = lax.broadcasted_iota(jnp.int32, (1, pw), 1)
+    return (lane >= h * DH) & (lane < (h + 1) * DH)
+
+
+def rms(x, features):
+    return lax.rsqrt(jnp.sum(x * x, axis=1, keepdims=True) / features + epsilon)
+
+
+def norm_back(x, inv, gain, d, features):
+    u = d * gain
+    inner = jnp.sum(u * x, axis=1, keepdims=True) / features
+    dx = inv * u - x * (inv * inv * inv * inner)
+    return dx, jnp.sum(d * x * inv, axis=0, keepdims=True)
+
+
+def probs_of(q, k):
+    s = mm(q, k, ((1,), (1,))) * DH ** -0.5
+    n = s.shape[0]
+    causal = lax.broadcasted_iota(jnp.int32, (n, n), 0) >= lax.broadcasted_iota(jnp.int32, (n, n), 1)
+    s = jnp.where(causal, s, -1e30)
+    e = jnp.exp(s - jnp.max(s, axis=1, keepdims=True))
+    return e / jnp.sum(e, axis=1, keepdims=True)
+
+
+def act_back(gate, up, dh, s):
+    sg = jax.nn.sigmoid(gate)
+    silu = gate * sg
+    if s is None:
+        return dh * up * (sg * (1.0 + gate * (1.0 - sg))), dh * silu, None
+    dr = jnp.sum(dh * silu * up, axis=-1, keepdims=True) * s * (1.0 - s)
+    ds = dh * s
+    return ds * up * (sg * (1.0 + gate * (1.0 - sg))), ds * silu, dr
+
+
+MESH = pl.DeviceIdType.MESH
+VMEM_BYTES = 62 * 2**20
+
+
+def remote(src, dst, send, recv, target):
+    return pltpu.make_async_remote_copy(
+        src_ref=src, dst_ref=dst, send_sem=send, recv_sem=recv, device_id=target, device_id_type=MESH
+    )
+
+
+def router_column(rows, e, width, experts):
+    lane = lax.broadcasted_iota(jnp.int32, rows.shape, rows.ndim - 1)
+    mask = (lane == width + e) | (lane == width + experts + e)
+    return jnp.sum(jnp.where(mask, rows.astype(jnp.float32), 0.0), axis=-1, keepdims=True)
+
+
+class Position:
+    def __init__(self, nx, ny):
+        self.s = lax.axis_index("section")
+        self.a = lax.axis_index("gx")
+        self.b = lax.axis_index("gy")
+        self.nx, self.ny = nx, ny
+        self.n = nx * ny
+        self.me = self.a * ny + self.b
+
+    def device(self, index):
+        return (self.s, index // self.ny, lax.rem(index, self.ny))
+
+    def others(self, do):
+        def step(i, c):
+            index = lax.rem(self.me + i, self.n)
+            do(index, index // self.ny, lax.rem(index, self.ny))
+            return c
+
+        lax.fori_loop(1, self.n, step, 0)
+
+    def peers(self, do):
+        for i in range(1, self.nx):
+            do(lax.rem(self.a + i, self.nx))
+
+    def line(self, do):
+        for i in range(1, self.ny):
+            do(lax.rem(self.b + i, self.ny))
+
+
+def greet_section(pos):
+    barrier = pltpu.get_barrier_semaphore()
+
+    def one(index, ai, bi):
+        pl.semaphore_signal(barrier, inc=1, device_id=(pos.s, ai, bi), device_id_type=MESH)
+
+    pos.others(one)
+    return barrier
+
+
+def flags(count):
+    return pltpu.SemaphoreType.DMA(count)
+
+
+class Share:
+    def __init__(self, pos, layer, block, full, sems):
+        self.pos, self.layer, self.block, self.full = pos, layer, block, full
+        self.sems = sems
+        self.source = pos.s == layer
+
+    def along(self, way, h):
+        pos = self.pos
+        j = pos.b - way * h
+        to = pos.b + way
+        real = (j >= 0) & (j < pos.ny) & (to >= 0) & (to < pos.ny)
+        j = jnp.clip(j, 0, pos.ny - 1)
+        src = self.block if h == 0 else self.full.at[j]
+        copy = remote(src, self.full.at[j], self.sems[0].at[(way + 1) // 2, h], self.sems[1].at[j], (pos.s, pos.a, to))
+        return real, j, copy
+
+    def across(self, src, slot):
+        pos = self.pos
+        return remote(src, self.full.at[slot], self.sems[2].at[slot], self.sems[3].at[slot], (1 - pos.s, pos.a, pos.b))
+
+    def start(self):
+        b = self.pos.b
+
+        @pl.when(self.source)
+        def _():
+            self.full[b] = self.block[...]
+            for way in (-1, 1):
+                real, _, copy = self.along(way, 0)
+                pl.when(real)(copy.start)
+            self.across(self.block, b).start()
+
+    def hop(self, h):
+        pos = self.pos
+
+        @pl.when(self.source)
+        def _():
+            for way in (-1, 1):
+                j = pos.b - way * h
+
+                @pl.when((j >= 0) & (j < pos.ny))
+                def _():
+                    real, jc, copy = self.along(way, h)
+                    copy.wait_recv()
+                    pl.when(real)(copy.start)
+                    self.across(self.full.at[jc], jc).start()
+
+    def finish(self):
+        pos = self.pos
+
+        @pl.when(self.source)
+        def _():
+            for h in range(pos.ny - 1):
+                for way in (-1, 1):
+                    real, _, copy = self.along(way, h)
+                    pl.when(real)(copy.wait_send)
+            for j in range(pos.ny):
+                self.across(self.block, j).wait_send()
+
+        @pl.when(jnp.logical_not(self.source))
+        def _():
+            for j in range(pos.ny):
+                self.across(self.full.at[j], j).wait_recv()
+
+
+def share_sems(ny):
+    return [flags((2, ny)), flags((ny,)), flags((ny,)), flags((ny,))]
+
+
+def params(ids):
+    return pltpu.CompilerParams(collective_id=ids, has_side_effects=True, vmem_limit_bytes=VMEM_BYTES)
+
+
+def greet_all(pos):
+    barrier = pltpu.get_barrier_semaphore()
+    total = 2 * pos.n
+    mine = pos.s * pos.n + pos.me
+
+    def one(i, c):
+        index = lax.rem(mine + i, total)
+        rest = lax.rem(index, pos.n)
+        pl.semaphore_signal(
+            barrier, inc=1, device_id=(index // pos.n, rest // pos.ny, lax.rem(rest, pos.ny)), device_id_type=MESH)
+        return c
+
+    lax.fori_loop(1, total, one, 0)
+    pl.semaphore_wait(barrier, total - 1)
+
+
+def leave_kernel(cfg, pair0, pair1, out, buf, t_send, t_recv):
+    nx, ny, mbs, sub, pw = cfg
+    pos = Position(nx, ny)
+    s, a, b = pos.s, pos.a, pos.b
+    greet_all(pos)
+    pairs = (pair0, pair1)
+
+    def copy(l, j, s_slot, a_slot, seq):
+        src = pairs[l].at[:, :, :, pl.ds(pl.multiple_of(j * pw, pw), pw)]
+        return remote(src, buf.at[s_slot, a_slot], t_send.at[l, j], t_recv.at[s_slot, a_slot], (l, seq, j))
+
+    for l in range(2):
+        for j in range(ny):
+            @pl.when((l != s) | (a != b) | (j != b))
+            def _():
+                copy(l, j, s, a, b).start()
+
+        @pl.when((l == s) & (a == b))
+        def _():
+            buf[s, a] = pairs[l][:, :, :, pl.ds(pl.multiple_of(b * pw, pw), pw)]
+
+    for so in range(2):
+        for i in range(nx):
+            @pl.when((so != s) | (a != b) | (i != a))
+            def _():
+                copy(0, 0, so, i, i).wait_recv()
+
+            out[:, so * mbs : (so + 1) * mbs, i * sub : (i + 1) * sub, :] = buf[so, i]
+    for l in range(2):
+        for j in range(ny):
+            @pl.when((l != s) | (a != b) | (j != b))
+            def _():
+                copy(l, j, s, a, b).wait_send()
+
+
+def leave(pair0, pair1, pw, ids):
+    nx, ny = lax.axis_size("gx"), lax.axis_size("gy")
+    kinds, mbs, sub, d = pair0.shape
+    vm = pl.BlockSpec(memory_space=pltpu.VMEM)
+    return pl.pallas_call(
+        functools.partial(leave_kernel, (nx, ny, mbs, sub, pw)),
+        out_shape=jax.ShapeDtypeStruct((kinds, 2 * mbs, nx * sub, pw), jnp.bfloat16),
+        in_specs=[vm] * 2,
+        out_specs=vm,
+        scratch_shapes=[
+            pltpu.VMEM((2, nx, kinds, mbs, sub, pw), jnp.bfloat16),
+            flags((2, ny)), flags((2, nx)),
+        ],
+        compiler_params=params(ids),
+        name="leave",
+    )(pair0, pair1)
+
+
+def turn(t, cos, sin, rot, sign):
+    hi = bf(t)
+    lo = bf(t - hi.astype(jnp.float32))
+    return bf(t * cos + sign * ((mm(hi, rot) + mm(lo, rot)) * sin))
+
+
+def by_blocks(rows, full, cols, width, pw):
+    total = None
+    for j in range(full.shape[0]):
+        part = mm(rows[:, j * pw : j * pw + width], full[j, :, cols])
+        total = part if total is None else total + part
+    return total
+
+
+def forward_kernel(cfg, *refs):
+    nx, ny, mbs, sub, width, pw, heads, features, experts, cap, f, sk, ak = cfg
+    (tin, small_b, att_b, sh_b, routes, cos, sin, rot, win_a, win_b, wdt_a, wdt_b,
+     tok_o, small_o, place_o, place_to, watt0_o, y_o, mid_o, n2_o, rows_o, q_o, k_o, v_o, att_o, slots_o, gu_o, hid_o, rows2_o, sgu_o, shid_o, shw_o, watt_o,
+     y, mid, n2, rx, nsend, nall, proj, q, k, v, att, osend, orecv, rwx,
+     xsend, xline, xall, nrows, pm, pt, slots, acc, gu, hid, eo, sgu, shid, ssend, srecv, rsend, rpeer, rline, rrecv,
+     win, wdt, shw0, shw1, watt0, watt1, tbuf, tok, rts, place, place_t, sm0, sm1, small,
+     n_send, n_recv, o_send, o_recv, x_send, x_recv, u_send, u_recv, t_send, t_recv, s_send, s_recv, g_send, g_recv, r_send, r_recv,
+     rs_send, rs_recv, ag_send, ag_recv, wi_sem, wd_sem, g_sem, k_sem, i_send, i_recv, q_send, q_recv, *w_sems) = refs
+    pos = Position(nx, ny)
+    s, a, b, me = pos.s, pos.a, pos.b, pos.me
+    slots_n = experts * cap
+    tokens = nx * ny * sub
+    d = ny * pw
+    length = nx * sub
+    half = experts // 2
+    lane = lax.broadcasted_iota(jnp.int32, (1, pw), 1)
+    shares = (
+        Share(pos, 0, sh_b, shw0, w_sems[0:4]),
+        Share(pos, 1, att_b, watt1, w_sems[4:8]),
+        Share(pos, 1, sh_b, shw1, w_sems[8:12]),
+    )
+    entry_shares = (
+        Share(pos, 0, small_b, sm0, w_sems[12:16]),
+        Share(pos, 1, small_b, sm1, w_sems[16:20]),
+        Share(pos, 0, att_b, watt0, w_sems[20:24]),
+    )
+    watts, shws = (watt0, watt1), (shw0, shw1)
+    barrier = pltpu.get_barrier_semaphore()
+    pos.peers(lambda ai: pl.semaphore_signal(barrier, inc=1, device_id=(s, ai, b), device_id_type=MESH))
+    pos.line(lambda bi: pl.semaphore_signal(barrier, inc=1, device_id=(s, a, bi), device_id_type=MESH))
+    pl.semaphore_signal(barrier, inc=1, device_id=(1 - s, a, b), device_id_type=MESH)
+    for j in range(ny):
+        @pl.when((a != b) | (b != j))
+        def _():
+            pl.semaphore_signal(barrier, inc=1, device_id=(s, b, j), device_id_type=MESH)
+
+    def weight_copy(layer, e, which):
+        own, oth, dst, sem = ((win_a, win_b, win, wi_sem), (wdt_a, wdt_b, wdt, wd_sem))[which]
+        return own.at[e], oth.at[e], dst.at[e], sem.at[e]
+
+    def start_weight(layer, e, which):
+        own, oth, dst, sem = weight_copy(layer, e, which)
+
+        @pl.when(s == layer)
+        def _():
+            pltpu.make_async_copy(own, dst, sem).start()
+
+        @pl.when(s != layer)
+        def _():
+            pltpu.make_async_copy(oth, dst, sem).start()
+
+    def wait_weight(layer, e, which):
+        own, oth, dst, sem = weight_copy(layer, e, which)
+        pltpu.make_async_copy(own, dst, sem).wait()
+
+    def first_weights(e, c):
+        start_weight(0, e, 0)
+        start_weight(0, e, 1)
+        return c
+
+    lax.fori_loop(0, experts, first_weights, 0)
+
+    @pl.when(a == b)
+    def _():
+        pl.semaphore_wait(barrier, nx - 1 + ny - 1 + 1 + nx - 1)
+
+    @pl.when(a != b)
+    def _():
+        pl.semaphore_wait(barrier, nx - 1 + ny - 1 + 1 + nx)
+
+    def tokens_copy(i, slot, seq):
+        src = tin.at[:, :, pl.ds(pl.multiple_of(i * sub, sub), sub), :]
+        return remote(src, tbuf.at[slot], i_send.at[i], i_recv.at[slot], (s, i, seq))
+
+    def token_targets(do):
+        for c in range(nx):
+            i = lax.rem(a + c, nx)
+
+            @pl.when((i != a) | (a != b))
+            def _():
+                do(tokens_copy(i, b, a))
+
+    def routes_copy(src, slot):
+        return remote(routes.at[pl.ds(src * mbs, mbs)], rts.at[slot], q_send, q_recv, (1 - s, a, b))
+
+    token_targets(lambda copy: copy.start())
+    routes_copy(1 - s, s).start()
+    for share in entry_shares:
+        share.start()
+    rts[s] = routes[pl.ds(s * mbs, mbs)]
+
+    @pl.when(a == b)
+    def _():
+        tbuf[b] = tin[:, :, pl.ds(pl.multiple_of(a * sub, sub), sub), :]
+
+    routes_copy(0, 1 - s).wait()
+
+    def places():
+        t0 = lax.broadcasted_iota(jnp.int32, (tokens, tokens), 0)
+        t1 = lax.broadcasted_iota(jnp.int32, (tokens, tokens), 1)
+        before = bf((t1 < t0).astype(jnp.float32))
+        after = bf((t0 < t1).astype(jnp.float32))
+        er = lax.broadcasted_iota(jnp.int32, (experts, tokens), 0).astype(jnp.float32)
+        ec = lax.broadcasted_iota(jnp.int32, (tokens, 128), 1).astype(jnp.float32)
+        sub8 = lax.broadcasted_iota(jnp.int32, (128, tokens), 0)
+        for l in range(2):
+            for m in range(mbs):
+                r = rts[l, m].astype(jnp.float32)
+                rows = [r[c : c + 1] for c in range(2)]
+                hot = [(row == er).astype(jnp.float32) for row in rows]
+                count = mm(bf(hot[0] + hot[1]), after)
+                cols = jnp.where(sub8 == 0, rows[0], jnp.where(sub8 == 1, rows[1], 0.0)).T
+                cols = [cols[:, c : c + 1] for c in range(2)]
+                hot_t = [(col == ec).astype(jnp.float32) for col in cols]
+                count_t = mm(before, bf(hot_t[0] + hot_t[1]))
+                for c in range(2):
+                    rank = jnp.sum(hot[c] * count, axis=0, keepdims=True)
+                    place[l, m, c : c + 1] = (rows[c] * cap + rank).astype(jnp.int32)
+                    rank_t = jnp.sum(hot_t[c] * count_t, axis=1, keepdims=True)
+                    place_t[l, m, :, c : c + 1] = (cols[c] * cap + rank_t).astype(jnp.int32)
+
+    def tokens_ready():
+        for j in range(ny):
+            @pl.when((a != b) | (b != j))
+            def _():
+                tokens_copy(a, j, j).wait_recv()
+
+            for kind in range(2):
+                tok[kind, :, :, j * pw : (j + 1) * pw] = tbuf[j, kind]
+        token_targets(lambda copy: copy.wait_send())
+
+    def stream(l, m):
+        return (tok[0, m] if l == 0 else y[0, m]).astype(jnp.float32)
+
+    def copy_n(l, m, ai, slot):
+        return remote(nsend.at[l, m], nall.at[l, m, slot], n_send.at[l, m, ai], n_recv.at[l, m, slot], (s, ai, b))
+
+    def norm_first(l, m):
+        xv = stream(l, m)
+        nsend[l, m] = bf(xv * rms(xv, features) * small[l, experts + 1 : experts + 2])
+        pos.peers(lambda ai: copy_n(l, m, ai, a).start())
+        nall[l, m, a] = nsend[l, m]
+
+    def copy_o(l, m, ai, slot):
+        return remote(osend.at[l, m, ai], orecv.at[l, m, slot], o_send.at[l, m, ai], o_recv.at[l, m, slot], (s, ai, b))
+
+    def attention(l, m):
+        watt = watts[l]
+        pos.peers(lambda ai: copy_n(l, m, ai, ai).wait())
+        proj[...] = by_blocks(nall[l, m].reshape(length, d), watt, slice(0, 3 * pw), width, pw)
+        v[l, m] = bf(proj[:, 2 * pw : 3 * pw])
+        q[l, m] = turn(proj[:, :pw], cos[...], sin[...], rot[...], 1.0)
+        k[l, m] = turn(proj[:, pw : 2 * pw], cos[...], sin[...], rot[...], 1.0)
+        total = jnp.zeros((length, pw), jnp.float32)
+        for h in range(heads):
+            mask = head_mask(pw, h)
+            p = probs_of(jnp.where(mask, q[l, m], 0), k[l, m])
+            total = total + mm(bf(p), jnp.where(mask, v[l, m], 0))
+        att[l, m] = bf(total)
+        for j in range(ny):
+            part = mm(att[l, m], watt[j, :, 3 * pw : 4 * pw], ((1,), (1,)))
+            osend[l, m, :, :, j * pw : j * pw + width] = bf(part).reshape(nx, sub, width)
+        pos.peers(lambda ai: copy_o(l, m, ai, a).start())
+        orecv[l, m, a] = osend[l, m, a]
+
+    def copy_x(l, m, bi, slot):
+        return remote(xsend.at[l, m, bi], xline.at[l, m, slot], x_send.at[l, m, bi], x_recv.at[l, m, slot], (s, a, bi))
+
+    def copy_w(l, m, ai, slot):
+        return remote(xline.at[l, m], xall.at[l, m, :, slot], u_send.at[l, m, ai], u_recv.at[l, m, slot], (s, ai, b))
+
+    def copy_t(l, m, ai, slot):
+        return remote(n2.at[l, m], nrows.at[l, m, slot], t_send.at[l, m, ai], t_recv.at[l, m, slot], (s, ai, b))
+
+    def norm_second(l, m):
+        pos.peers(lambda ai: copy_o(l, m, ai, ai).wait())
+        mv = stream(l, m)
+        for ai in range(nx):
+            mv = mv + orecv[l, m, ai].astype(jnp.float32)
+        mid[l, m] = mv
+        n2v = bf(mv * rms(mv, features) * small[l, experts : experts + 1])
+        n2[l, m] = n2v
+        rv = mm(n2v, rwx[l], ((1,), (1,)))
+        hi = bf(rv)
+        lo = bf(rv - hi.astype(jnp.float32))
+        tail = jnp.where(lane < width + experts, hi, lo)
+        for j in range(ny):
+            xsend[l, m, j] = jnp.where(lane < width, n2v[:, j * pw : (j + 1) * pw], tail)
+        pos.line(lambda bi: copy_x(l, m, bi, b).start())
+        xline[l, m, b] = xsend[l, m, b]
+        pos.peers(lambda ai: copy_t(l, m, ai, a).start())
+        nrows[l, m, a] = n2[l, m]
+
+    def spread(l, m):
+        pos.line(lambda bi: copy_x(l, m, bi, bi).wait())
+        pos.peers(lambda ai: copy_w(l, m, ai, a).start())
+        xall[l, m, :, a] = xline[l, m]
+
+    def dispatch(l, m):
+        i0 = lax.broadcasted_iota(jnp.int32, (slots_n, tokens), 0)
+        pm[...] = bf(((place[l, m, 0:1] == i0) | (place[l, m, 1:2] == i0)).astype(jnp.float32))
+        pos.peers(lambda ai: copy_w(l, m, ai, ai).wait())
+        slots[l, m] = bf(mm(pm[...], xall[l, m].reshape(tokens, pw))).reshape(experts, cap, pw)
+
+    def shared_in_part(l, m):
+        pos.peers(lambda ai: copy_t(l, m, ai, ai).wait())
+        shw = shws[l]
+        gu_s = by_blocks(nrows[l, m].reshape(length, d), shw, slice(0, 2 * f), width, pw)
+        sgu[l, m] = bf(gu_s)
+        gate = gu_s[:, :f]
+        shid[l, m] = bf(gate * jax.nn.sigmoid(gate) * gu_s[:, f:])
+
+    def copy_s(l, m, ai, slot):
+        return remote(ssend.at[l, m, ai], srecv.at[l, m, slot], s_send.at[l, m, ai], s_recv.at[l, m, slot], (s, ai, b))
+
+    def shared_out_part(l, m):
+        for j in range(ny):
+            part = mm(shid[l, m], shws[l][j, :, 2 * f :], ((1,), (1,)))
+            ssend[l, m, :, :, j * pw : j * pw + width] = bf(part).reshape(nx, sub, width)
+        pos.peers(lambda ai: copy_s(l, m, ai, a).start())
+        srecv[l, m, a] = ssend[l, m, a]
+
+    def copy_g(l, m, ai, slot):
+        return remote(rsend.at[l, m, ai], rpeer.at[l, m, slot], g_send.at[l, m, ai], g_recv.at[l, m, slot], (s, ai, b))
+
+    def copy_r(l, m, bi, slot):
+        return remote(rline.at[l, m, bi], rrecv.at[l, m, slot], r_send.at[l, m, bi], r_recv.at[l, m, slot], (s, a, bi))
+
+    def combine(l, m):
+        i1 = lax.broadcasted_iota(jnp.int32, (tokens, slots_n), 1)
+        pt[...] = bf(((place_t[l, m, :, 0:1] == i1) | (place_t[l, m, :, 1:2] == i1)).astype(jnp.float32))
+        br = mm(pt[...], eo[m].reshape(slots_n, width))
+        for ai in range(nx):
+            rsend[l, m, ai, :, :, :width] = bf(br).reshape(ny, nx, sub, width)[:, ai]
+        pos.peers(lambda ai: copy_g(l, m, ai, a).start())
+        rpeer[l, m, a] = rsend[l, m, a]
+
+    def combine_line(l, m):
+        pos.peers(lambda ai: copy_g(l, m, ai, ai).wait())
+        total = rpeer[l, m, 0].astype(jnp.float32)
+        for ai in range(1, nx):
+            total = total + rpeer[l, m, ai].astype(jnp.float32)
+        rline[l, m] = bf(total)
+        pos.line(lambda bi: copy_r(l, m, bi, b).start())
+        rrecv[l, m, b] = rline[l, m, b]
+
+    def layer_out(l, m):
+        pos.peers(lambda ai: copy_s(l, m, ai, ai).wait())
+        pos.line(lambda bi: copy_r(l, m, bi, bi).wait())
+        total = mid[l, m]
+        for ai in range(nx):
+            total = total + srecv[l, m, ai].astype(jnp.float32)
+        for j in range(ny):
+            part = total[:, j * pw : (j + 1) * pw]
+            part = part + jnp.where(lane < width, rrecv[l, m, j].astype(jnp.float32), 0.0)
+            y[l, m, :, j * pw : (j + 1) * pw] = bf(part)
+
+    first = (b == ny - 1, b == 0)
+    last = (b == 0, b == ny - 1)
+    up = (ny - 1 - b, b)
+    down = (b, ny - 1 - b)
+    lag = (sk + ak) * (ny - 1)
+    apart = STAGE_STEPS
+    gap = max(half - 1 + lag + 6 * apart + 1 - 2 * half, 0)
+    starts = (0, half, 2 * half + gap, 3 * half + gap)
+    steps = starts[3] + half + lag
+
+    def unit(t, dd):
+        early = (t >= 0) & (t < 2 * half)
+        late = (t >= starts[2]) & (t < starts[2] + 2 * half)
+        u = jnp.clip(jnp.where(t < starts[2], jnp.minimum(t, 2 * half - 1), t - gap), 0, 4 * half - 1)
+        job = u // half
+        return early | late, job // 2, lax.rem(job, 2), lax.rem(u, half) + dd * half
+
+    def gu_copy(dd, l, m, e):
+        to = b - 1 if dd == 0 else b + 1
+        return remote(gu.at[l, m, e], gu.at[l, m, e], rs_send.at[l, m, e], rs_recv.at[l, m, e], (s, a, to))
+
+    def hid_copy(dd, l, m, e):
+        to = b + 1 if dd == 0 else b - 1
+        return remote(hid.at[l, m, e], hid.at[l, m, e], ag_send.at[l, m, e], ag_recv.at[l, m, e], (s, a, to))
+
+    def chain(i):
+        reduce = [unit(i - sk * up[dd], dd) for dd in range(2)]
+        spreads = [unit(i - sk * (ny - 1) - ak * down[dd], dd) for dd in range(2)]
+        for dd in range(2):
+            valid, l, m, e = reduce[dd]
+
+            @pl.when(valid)
+            def _():
+                @pl.when(m == 0)
+                def _():
+                    wait_weight(0, e, 0)
+
+                acc[dd] = mm(slots[l, m, e, :, :width], win[e])
+
+                @pl.when((l == 0) & (m == 1))
+                def _():
+                    start_weight(1, e, 0)
+
+        for dd in range(2):
+            valid, l, m, e = reduce[dd]
+
+            @pl.when(valid & first[dd])
+            def _():
+                gu[l, m, e] = bf(acc[dd])
+                gu_copy(dd, l, m, e).start()
+
+            @pl.when(valid & jnp.logical_not(first[dd] | last[dd]))
+            def _():
+                gu_copy(dd, l, m, e).wait_recv()
+                gu[l, m, e] = bf(acc[dd] + gu[l, m, e].astype(jnp.float32))
+                gu_copy(dd, l, m, e).start()
+
+            @pl.when(valid & last[dd])
+            def _():
+                gu_copy(dd, l, m, e).wait_recv()
+                total = acc[dd] + gu[l, m, e].astype(jnp.float32)
+                r = router_column(slots[l, m, e], e, width, experts)
+                gate = total[:, :f]
+                hid[l, m, e] = bf(gate * jax.nn.sigmoid(gate) * total[:, f:] * jax.nn.sigmoid(r))
+                hid_copy(dd, l, m, e).start()
+                gu[l, m, e] = bf(total)
+                pltpu.make_async_copy(gu.at[l, m, e], gu_o.at[l, m, e], g_sem.at[l, m, e]).start()
+
+        for dd in range(2):
+            valid, l, m, e = spreads[dd]
+
+            @pl.when(valid & jnp.logical_not(last[dd]))
+            def _():
+                hid_copy(dd, l, m, e).wait_recv()
+
+                @pl.when(jnp.logical_not(first[dd]))
+                def _():
+                    hid_copy(dd, l, m, e).start()
+
+        for dd in range(2):
+            valid, l, m, e = spreads[dd]
+
+            @pl.when(valid)
+            def _():
+                @pl.when(m == 0)
+                def _():
+                    wait_weight(0, e, 1)
+
+                eo[m, e] = bf(mm(hid[l, m, e], wdt[e], ((1,), (1,))))
+
+                @pl.when((l == 0) & (m == 1))
+                def _():
+                    start_weight(1, e, 1)
+
+    kept = [
+        (mid, mid_o), (n2, n2_o), (nall, rows_o), (q, q_o), (k, k_o), (v, v_o), (att, att_o), (slots, slots_o),
+        (hid, hid_o), (nrows, rows2_o), (sgu, sgu_o), (shid, shid_o), (y, y_o),
+    ]
+    stages = {}
+
+    def at(step, do):
+        stages.setdefault(step, []).append(do)
+
+    def stage(do, l, m):
+        return lambda: do(l, m)
+
+    osend[...] = jnp.zeros_like(osend)
+    ssend[...] = jnp.zeros_like(ssend)
+    rwx[...] = jnp.zeros_like(rwx)
+    for h in range(1, ny):
+        for share in entry_shares:
+            share.hop(h)
+    for share in entry_shares[:2]:
+        share.finish()
+    tokens_ready()
+    for l, full in enumerate((sm0, sm1)):
+        for j in range(ny):
+            small[l, :, j * pw : (j + 1) * pw] = full[j]
+    for l in range(2):
+        rwx[l, width : width + experts] = bf(small[l, :experts])
+        rwx[l, width + experts : width + 2 * experts] = bf(small[l, :experts])
+    norm_first(0, 0)
+    norm_first(0, 1)
+    places()
+    entry_shares[2].finish()
+    shares[0].start()
+    shares[1].start()
+    attention(0, 0)
+    norm_second(0, 0)
+    attention(0, 1)
+    spread(0, 0)
+    norm_second(0, 1)
+    dispatch(0, 0)
+    for h in range(1, ny):
+        at(h - 1, lambda h=h: (shares[0].hop(h), shares[1].hop(h)))
+    at(1, stage(spread, 0, 1))
+    at(3, stage(dispatch, 0, 1))
+    at(4, lambda: (shares[0].finish(), shares[1].finish()))
+    at(5, stage(shared_in_part, 0, 0))
+    at(6, stage(shared_out_part, 0, 0))
+    at(half, stage(shared_in_part, 0, 1))
+    at(half + 1, stage(shared_out_part, 0, 1))
+    for m in range(2):
+        done = starts[m] + half - 1 + lag
+        for c, do in enumerate((combine, combine_line)):
+            at(done + c * apart, stage(do, 0, m))
+        at(done + 2 * apart, stage(layer_out, 0, m))
+        for c, do in enumerate((norm_first, attention, norm_second, spread, dispatch)):
+            at(done + (2 + c) * apart, stage(do, 1, m))
+        at(starts[2 + m] + 2, stage(shared_in_part, 1, m))
+        at(starts[2 + m] + 4, stage(shared_out_part, 1, m))
+        done = starts[2 + m] + half - 1 + lag
+        for c, do in enumerate((combine, combine_line, layer_out)):
+            at(done + c * apart, stage(do, 1, m))
+    at(half + lag, shares[2].start)
+    for h in range(1, ny):
+        at(half + lag + h, lambda h=h: shares[2].hop(h))
+    at(half + lag + ny, shares[2].finish)
+
+    def step(i, c):
+        chain(i)
+        for when in sorted(stages):
+            if when < steps:
+                @pl.when(i == when)
+                def _():
+                    for do in stages[when]:
+                        do()
+
+        return c
+
+    lax.fori_loop(0, steps, step, 0)
+    for when in sorted(stages):
+        if when >= steps:
+            for do in stages[when]:
+                do()
+    kept += [(shw0, shw_o.at[0]), (shw1, shw_o.at[1]), (watt1, watt_o), (watt0, watt0_o), (tok, tok_o), (small, small_o)]
+    kept += [(place, place_o), (place_t, place_to)]
+    saves = [pltpu.make_async_copy(src, dst, k_sem.at[i]) for i, (src, dst) in enumerate(kept)]
+    for copy in saves:
+        copy.start()
+
+    def finish(index, c):
+        l = index // (mbs * half)
+        m = lax.rem(index // half, mbs)
+        for dd in range(2):
+            e = lax.rem(index, half) + dd * half
+
+            @pl.when(jnp.logical_not(last[dd]))
+            def _():
+                gu_copy(dd, l, m, e).wait_send()
+
+            @pl.when(jnp.logical_not(first[dd]))
+            def _():
+                hid_copy(dd, l, m, e).wait_send()
+
+            @pl.when(last[dd])
+            def _():
+                pltpu.make_async_copy(gu.at[l, m, e], gu_o.at[l, m, e], g_sem.at[l, m, e]).wait()
+
+        return c
+
+    lax.fori_loop(0, 2 * mbs * half, finish, 0)
+    for copy in saves:
+        copy.wait()
+
+
+def forward(tin, small_b, att_block, sh_block, routes, cos, sin, rot, win, wdt, dims, heads, features, ids):
+    width, pw, experts, cap = dims
+    nx, ny = lax.axis_size("gx"), lax.axis_size("gy")
+    mbs, length = tin.shape[1:3]
+    sub, d = length // nx, ny * pw
+    f = wdt[0].shape[-1]
+    length, tokens, n, slots = nx * sub, nx * ny * sub, nx * ny, experts * cap
+    b16, f32 = jnp.bfloat16, jnp.float32
+    vm = pl.BlockSpec(memory_space=pltpu.VMEM)
+    hbm = pl.BlockSpec(memory_space=pl.ANY)
+    lm = (2, mbs)
+    rows_shape = lm + (nx, sub, d)
+    spread_shape = lm + (ny, nx, sub, pw)
+    entry = (
+        ((2, mbs, sub, d), b16), ((2, small_b.shape[0], d), f32), (lm + (2, tokens), jnp.int32),
+        (lm + (tokens, 2), jnp.int32), ((ny,) + att_block.shape, b16),
+    )
+    kept = entry + (
+        (lm + (sub, d), b16), (lm + (sub, d), f32), (lm + (sub, d), b16), (rows_shape, b16),
+        (lm + (length, pw), b16), (lm + (length, pw), b16), (lm + (length, pw), b16), (lm + (length, pw), b16),
+        (lm + (experts, cap, pw), b16), (lm + (experts, cap, 2 * f), b16), (lm + (experts, cap, f), b16),
+        (rows_shape, b16), (lm + (length, 2 * f), b16), (lm + (length, f), b16),
+        ((2, ny) + sh_block.shape, b16), ((ny,) + att_block.shape, b16),
+    )
+    scratch = (
+        (lm + (sub, d), b16), (lm + (sub, d), f32), (lm + (sub, d), b16), None,
+        (lm + (sub, d), b16), (rows_shape, b16), ((length, 3 * pw), f32),
+        (lm + (length, pw), b16), (lm + (length, pw), b16), (lm + (length, pw), b16), (lm + (length, pw), b16),
+        (rows_shape, b16), (rows_shape, b16), ((2, pw, d), b16),
+        (lm + (ny, sub, pw), b16), (lm + (ny, sub, pw), b16), (spread_shape, b16), (rows_shape, b16),
+        ((slots, tokens), b16), ((tokens, slots), b16), (lm + (experts, cap, pw), b16), ((2, cap, 2 * f), f32),
+        (lm + (experts, cap, 2 * f), b16), (lm + (experts, cap, f), b16), ((mbs, experts, cap, width), b16),
+        (lm + (length, 2 * f), b16), (lm + (length, f), b16), (rows_shape, b16), (rows_shape, b16),
+        (lm + (nx, ny, sub, pw), b16), (lm + (nx, ny, sub, pw), b16), (lm + (ny, sub, pw), b16), (lm + (ny, sub, pw), b16),
+        ((experts, width, 2 * f), b16), ((experts, width, f), b16),
+        ((ny,) + sh_block.shape, b16), ((ny,) + sh_block.shape, b16), ((ny,) + att_block.shape, b16), ((ny,) + att_block.shape, b16),
+        ((ny, 2, mbs, sub, pw), b16), ((2, mbs, sub, d), b16), (lm + (2, tokens), jnp.int32),
+        (lm + (2, tokens), jnp.int32), (lm + (tokens, 2), jnp.int32),
+        ((ny,) + small_b.shape, f32), ((ny,) + small_b.shape, f32), ((2, small_b.shape[0], d), f32),
+    )
+    outs = pl.pallas_call(
+        functools.partial(forward_kernel, (nx, ny, mbs, sub, width, pw, heads, features, experts, cap, f, *FWD_SKEW)),
+        out_shape=tuple(jax.ShapeDtypeStruct(*v) for v in kept),
+        in_specs=[vm] * 8 + [hbm] * 4,
+        out_specs=(hbm,) * len(kept),
+        scratch_shapes=[pltpu.VMEM(*(v or ((8, 128), f32))) for v in scratch] + [
+            flags(lm + (nx,)), flags(lm + (nx,)), flags(lm + (nx,)), flags(lm + (nx,)),
+            flags(lm + (ny,)), flags(lm + (ny,)), flags(lm + (nx,)), flags(lm + (nx,)), flags(lm + (nx,)), flags(lm + (nx,)),
+            flags(lm + (nx,)), flags(lm + (nx,)), flags(lm + (nx,)), flags(lm + (nx,)), flags(lm + (ny,)), flags(lm + (ny,)),
+            flags(lm + (experts,)), flags(lm + (experts,)), flags(lm + (experts,)), flags(lm + (experts,)),
+            flags((experts,)), flags((experts,)), flags(lm + (experts,)), flags((24,)),
+            flags((nx,)), flags((ny,)), pltpu.SemaphoreType.DMA, pltpu.SemaphoreType.DMA,
+        ] + share_sems(ny) * 6,
+        compiler_params=params(ids),
+        cost_estimate=pl.CostEstimate(flops=10**10, bytes_accessed=8 * 10**7, transcendentals=10**6),
+        name="forward",
+    )(tin, small_b, att_block, sh_block, routes, cos, sin, rot, *win, *wdt)
+    names = ("tok", "small", "place", "place_t", "watt0", "y", "mid", "n2", "rows", "q", "k", "v", "att", "slots", "gu", "hid", "rows2", "sgu", "shid", "shw", "watt1")
+    return dict(zip(names, outs))
+
+
+FWD_SKEW = (1, 1)
+STAGE_STEPS = 1
+
+
+def backward_kernel(cfg, *refs):
+    layer, nx, ny, mbs, sub, width, pw, heads, features, experts, cap, f, sk, ak = cfg
+    n_by = 16
+    by_layer, refs = refs[:n_by], refs[n_by:]
+    (watt, cos, sin, rot, slots_i, gu_i, hid_i, win_a, win_b, wdt_a, wdt_b) = refs[:11]
+    refs = refs[11 + (0 if layer else 5) :]
+    (gx_o, win_g, wdt_g, att_g, sh_g, small_g,
+     win, wdt, xsend, xline, xall, grows, pm, pt, slots, gslots, gown, hid, acc, dh, dgu, deo, sti, std,
+     dsgu, ssend, srecv, rsend, rpeer, rline, rrecv, rwx, dm, msend, mall, datt, dqkv, dsend, drecv,
+     rw_p, gains, sh_p, att_p, small_p, sh_x, att_x, small_x, sh_r, att_r, small_r, sh_f, att_f, small_f, small_a,
+     x, g, small, mid, n2, rows, q, k, v, att, rows2, sgu, shid, shw, place, place_t,
+     w_sem, x_send, x_recv, u_send, u_recv, t_send, t_recv, s_send, s_recv, g_send, g_recv, r_send, r_recv,
+     m_send, m_recv, d_send, d_recv, rs_send, rs_recv, ag_send, ag_recv, wi_send, wi_recv, wd_send, wd_recv,
+     c_send, c_recv, e_send, e_recv, a_send, a_recv, l_sem, st_sem, f_sem, y_sem, free) = refs
+    resident = (g, small, place, place_t, x, mid, n2, rows, q, k, v, att, rows2, sgu, shid, shw)
+    pos = Position(nx, ny)
+    s, a, b = pos.s, pos.a, pos.b
+    keeper = s == layer
+    helper = jnp.logical_not(keeper)
+    slots_n = experts * cap
+    tokens = nx * ny * sub
+    d = ny * pw
+    length = nx * sub
+    half = experts // 2
+    scale = DH ** -0.5
+    lane = lax.broadcasted_iota(jnp.int32, (1, pw), 1)
+    first = (b == ny - 1, b == 0)
+    last = (b == 0, b == ny - 1)
+    up = (ny - 1 - b, b)
+    down = (b, ny - 1 - b)
+    barrier = pltpu.get_barrier_semaphore()
+    pos.peers(lambda ai: pl.semaphore_signal(barrier, inc=1, device_id=(s, ai, b), device_id_type=MESH))
+    pos.line(lambda bi: pl.semaphore_signal(barrier, inc=1, device_id=(s, a, bi), device_id_type=MESH))
+    pl.semaphore_signal(barrier, inc=1, device_id=(1 - s, a, b), device_id_type=MESH)
+
+    for j, (dst, own, oth) in enumerate(((win, win_a, win_b), (wdt, wdt_a, wdt_b))):
+        @pl.when(keeper)
+        def _():
+            pltpu.make_async_copy(own, dst, w_sem.at[j]).start()
+
+        @pl.when(helper)
+        def _():
+            pltpu.make_async_copy(oth, dst, w_sem.at[j]).start()
+
+    picks = (-1, layer, layer, layer, 0) + (layer,) * 11
+    fills = [
+        pltpu.make_async_copy(src.at[src.shape[0] - 1 if at < 0 else at], dst, y_sem.at[c])
+        for c, (src, dst, at) in enumerate(zip(by_layer, resident, picks))
+    ]
+    for copy in fills:
+        copy.start()
+    loads = fills[4:] + [pltpu.make_async_copy(slots_i.at[layer], slots, l_sem.at[0]), pltpu.make_async_copy(hid_i.at[layer], hid, l_sem.at[1])]
+    for copy in loads[-2:]:
+        copy.start()
+
+    def own_gates(dd):
+        part = pl.ds(dd * half, half)
+        return pltpu.make_async_copy(gu_i.at[layer, :, part], gown, l_sem.at[2])
+
+    for dd in range(2):
+        pl.when(last[dd])(own_gates(dd).start)
+
+    def copy_x(m, bi, slot):
+        return remote(xsend.at[m, bi], xline.at[m, slot], x_send.at[m, bi], x_recv.at[m, slot], (s, a, bi))
+
+    def copy_w(m, ai, slot):
+        return remote(xline.at[m], xall.at[m, :, slot], u_send.at[m, ai], u_recv.at[m, slot], (s, ai, b))
+
+    def copy_t(m, ai, slot):
+        return remote(g.at[m], grows.at[m, slot], t_send.at[m, ai], t_recv.at[m, slot], (s, ai, b))
+
+    for copy in fills[:4]:
+        copy.wait()
+    for m in range(mbs):
+        for j in range(ny):
+            xsend[m, j] = g[m, :, j * pw : (j + 1) * pw]
+    pl.semaphore_wait(barrier, nx - 1 + ny - 1 + 1)
+    for m in range(mbs):
+        pos.line(lambda bi: copy_x(m, bi, b).start())
+        xline[m, b] = xsend[m, b]
+    for m in range(mbs):
+        pos.peers(lambda ai: copy_t(m, ai, a).start())
+        grows[m, a] = g[m]
+    deo[...] = jnp.zeros_like(deo)
+    ssend[...] = jnp.zeros_like(ssend)
+    dsend[...] = jnp.zeros_like(dsend)
+    rwx[...] = jnp.zeros_like(rwx)
+    rwx[width : width + experts] = bf(small[:experts])
+    rwx[width + experts : width + 2 * experts] = bf(small[:experts])
+    rw_p[...] = jnp.zeros_like(rw_p)
+    gains[...] = jnp.zeros_like(gains)
+
+    def spread(m):
+        pos.line(lambda bi: copy_x(m, bi, bi).wait())
+        pos.peers(lambda ai: copy_w(m, ai, a).start())
+        xall[m, :, a] = xline[m]
+
+    def dispatch(m):
+        i0 = lax.broadcasted_iota(jnp.int32, (slots_n, tokens), 0)
+        pm[...] = bf(((place[m, 0:1] == i0) | (place[m, 1:2] == i0)).astype(jnp.float32))
+        pos.peers(lambda ai: copy_w(m, ai, ai).wait())
+        gslots[m] = bf(mm(pm[...], xall[m].reshape(tokens, pw))).reshape(experts, cap, pw)
+
+    def shared_act(m):
+        pos.peers(lambda ai: copy_t(m, ai, ai).wait())
+        dsh = by_blocks(grows[m].reshape(length, d), shw, slice(2 * f, 3 * f), width, pw)
+        dsg, dsu, _ = act_back(sgu[m, :, :f].astype(jnp.float32), sgu[m, :, f:].astype(jnp.float32), dsh, None)
+        dsgu[m, :, :f] = bf(dsg)
+        dsgu[m, :, f:] = bf(dsu)
+
+    def copy_s(m, ai, slot):
+        return remote(ssend.at[m, ai], srecv.at[m, slot], s_send.at[m, ai], s_recv.at[m, slot], (s, ai, b))
+
+    def shared_back(m):
+        for j in range(ny):
+            part = mm(dsgu[m], shw[j, :, : 2 * f], ((1,), (1,)))
+            ssend[m, :, :, j * pw : j * pw + width] = bf(part).reshape(nx, sub, width)
+        pos.peers(lambda ai: copy_s(m, ai, a).start())
+        srecv[m, a] = ssend[m, a]
+
+    crossing = ((sh_p, sh_x), (att_p, att_x), (small_p, small_x))
+    places = (sh_r, att_r, small_r)
+    finals = (sh_f, att_f, small_f)
+    results = (sh_g, att_g, small_g)
+
+    def cross(i):
+        return remote(crossing[i][0], crossing[i][1], c_send.at[i], c_recv.at[i], (layer, a, b))
+
+    def block(i, bi):
+        if i == 2:
+            return small_x.at[:, pl.ds(pl.multiple_of(bi * pw, pw), pw)]
+        return crossing[i][1].at[bi]
+
+    def along(i, bi, slot):
+        return remote(block(i, bi), places[i].at[slot], e_send.at[i, bi], e_recv.at[i, slot], (s, a, bi))
+
+    def give(i):
+        pl.when(helper)(cross(i).start)
+
+    def join(i):
+        @pl.when(keeper)
+        def _():
+            cross(i).wait_recv()
+            part, other = crossing[i]
+            other[...] = (part[...].astype(jnp.float32) + other[...].astype(jnp.float32)).astype(other.dtype)
+            pos.line(lambda bi: along(i, bi, b).start())
+
+    def settle(i):
+        @pl.when(keeper)
+        def _():
+            pos.line(lambda bi: along(i, bi, bi).wait())
+            total = block(i, b)[...].astype(jnp.float32)
+            for c in range(1, ny):
+                total = total + places[i][lax.rem(b + c, ny)].astype(jnp.float32)
+            finals[i][...] = total
+            if i < 2:
+                pltpu.make_async_copy(finals[i], results[i], f_sem.at[i]).start()
+
+    def shared_grads():
+        for j in range(ny):
+            rj = rows2[:, :, :, j * pw : j * pw + width].reshape(mbs * length, width)
+            sh_p[j, :, : 2 * f] = bf(mm(rj, dsgu[...].reshape(mbs * length, 2 * f), ((0,), (0,))))
+
+    def down_grads():
+        for j in range(ny):
+            gj = grows[:, :, :, j * pw : j * pw + width].reshape(mbs * length, width)
+            sh_p[j, :, 2 * f :] = bf(mm(gj, shid[...].reshape(mbs * length, f), ((0,), (0,))))
+        give(0)
+
+    def copy_g(m, ai, slot):
+        return remote(rsend.at[m, ai], rpeer.at[m, slot], g_send.at[m, ai], g_recv.at[m, slot], (s, ai, b))
+
+    def copy_r(m, bi, slot):
+        return remote(rline.at[m, bi], rrecv.at[m, slot], r_send.at[m, bi], r_recv.at[m, slot], (s, a, bi))
+
+    def combine(m):
+        i1 = lax.broadcasted_iota(jnp.int32, (tokens, slots_n), 1)
+        pt[...] = bf(((place_t[m, :, 0:1] == i1) | (place_t[m, :, 1:2] == i1)).astype(jnp.float32))
+        br = bf(mm(pt[...], deo[m].reshape(slots_n, pw))).reshape(ny, nx, sub, pw)
+        for ai in range(nx):
+            rsend[m, ai] = br[:, ai]
+        pos.peers(lambda ai: copy_g(m, ai, a).start())
+        rpeer[m, a] = rsend[m, a]
+
+    def combine_line(m):
+        pos.peers(lambda ai: copy_g(m, ai, ai).wait())
+        total = rpeer[m, 0].astype(jnp.float32)
+        for ai in range(1, nx):
+            total = total + rpeer[m, ai].astype(jnp.float32)
+        rline[m] = bf(total)
+        pos.line(lambda bi: copy_r(m, bi, b).start())
+        rrecv[m, b] = rline[m, b]
+
+    def copy_m(m, ai, slot):
+        return remote(msend.at[m], mall.at[m, slot], m_send.at[m, ai], m_recv.at[m, slot], (s, ai, b))
+
+    def second_norm(m):
+        pos.peers(lambda ai: copy_s(m, ai, ai).wait())
+        pos.line(lambda bi: copy_r(m, bi, bi).wait())
+        dlog = jnp.zeros((sub, pw), jnp.float32)
+        parts = []
+        for j in range(ny):
+            part = rrecv[m, j].astype(jnp.float32)
+            dlog = dlog + jnp.where(lane >= width, part, 0.0)
+            parts.append(jnp.where(lane < width, part, 0.0))
+        hi = bf(dlog)
+        lo = bf(dlog - hi.astype(jnp.float32))
+        dn2 = jnp.concatenate(parts, 1) + mm(hi, rwx[...]) + mm(lo, rwx[...])
+        for ai in range(nx):
+            dn2 = dn2 + srecv[m, ai].astype(jnp.float32)
+        rw_t = mm(hi, n2[m], ((0,), (0,))) + mm(lo, n2[m], ((0,), (0,)))
+        rw_p[...] += rw_t[width : width + experts] + rw_t[width + experts : width + 2 * experts]
+        mv = mid[m]
+        dx2, gain_g = norm_back(mv, rms(mv, features), small[experts : experts + 1], dn2, features)
+        gains[0:1] += gain_g
+        dm[m] = g[m].astype(jnp.float32) + dx2
+        msend[m] = bf(dm[m])
+        pos.peers(lambda ai: copy_m(m, ai, a).start())
+        mall[m, a] = msend[m]
+
+    def copy_d(m, ai, slot):
+        return remote(dsend.at[m, ai], drecv.at[m, slot], d_send.at[m, ai], d_recv.at[m, slot], (s, ai, b))
+
+    def attention(m):
+        pos.peers(lambda ai: copy_m(m, ai, ai).wait())
+        datt[...] = bf(by_blocks(mall[m].reshape(length, d), watt, slice(3 * pw, 4 * pw), width, pw))
+        dq = jnp.zeros((length, pw), jnp.float32)
+        dk = dq
+        dv = dq
+        for h in range(heads):
+            mask = head_mask(pw, h)
+            qh = jnp.where(mask, q[m], 0)
+            kh = jnp.where(mask, k[m], 0)
+            da = jnp.where(mask, datt[...], 0)
+            p = probs_of(qh, k[m])
+            dp = mm(da, v[m], ((1,), (1,)))
+            ds = bf(p * (dp - jnp.sum(dp * p, axis=1, keepdims=True)))
+            dv = dv + mm(bf(p), da, ((0,), (0,)))
+            dq = dq + mm(ds, kh)
+            dk = dk + mm(ds, qh, ((0,), (0,)))
+        dqkv[m, :, :pw] = turn(dq * scale, cos[...], sin[...], rot[...], -1.0)
+        dqkv[m, :, pw : 2 * pw] = turn(dk * scale, cos[...], sin[...], rot[...], -1.0)
+        dqkv[m, :, 2 * pw :] = bf(dv)
+        for j in range(ny):
+            part = mm(dqkv[m], watt[j, :, : 3 * pw], ((1,), (1,)))
+            dsend[m, :, :, j * pw : j * pw + width] = bf(part).reshape(nx, sub, width)
+        pos.peers(lambda ai: copy_d(m, ai, a).start())
+        drecv[m, a] = dsend[m, a]
+
+    def first_norm(m):
+        pos.peers(lambda ai: copy_d(m, ai, ai).wait())
+        dn1 = drecv[m, 0].astype(jnp.float32)
+        for ai in range(1, nx):
+            dn1 = dn1 + drecv[m, ai].astype(jnp.float32)
+        xv = x[m].astype(jnp.float32)
+        dx1, gain_g = norm_back(xv, rms(xv, features), small[experts + 1 : experts + 2], dn1, features)
+        gains[1:2] += gain_g
+        gx_o[m] = bf(dm[m] + dx1)
+
+    def attention_grads():
+        for j in range(ny):
+            cols = slice(j * pw, j * pw + width)
+            rj = rows[:, :, :, cols].reshape(mbs * length, width)
+            mj = mall[:, :, :, cols].reshape(mbs * length, width)
+            att_p[j, :, : 3 * pw] = bf(mm(rj, dqkv[...].reshape(mbs * length, 3 * pw), ((0,), (0,))))
+            att_p[j, :, 3 * pw :] = bf(mm(mj, att[...].reshape(mbs * length, pw), ((0,), (0,))))
+        give(1)
+
+    def small_grads():
+        small_p[:experts] = rw_p[...]
+        small_p[experts:] = gains[...]
+        give(2)
+
+    lag = (sk + ak) * (ny - 1)
+    apart = STAGE_STEPS
+    starts = (0, half)
+
+    def unit(t, dd):
+        u = jnp.clip(t, 0, mbs * half - 1)
+        return (t >= 0) & (t < mbs * half), u // half, lax.rem(u, half) + dd * half
+
+    def dh_copy(dd, m, e):
+        to = b - 1 if dd == 0 else b + 1
+        return remote(dh.at[m, e], dh.at[m, e], rs_send.at[m, e], rs_recv.at[m, e], (s, a, to))
+
+    def dgu_copy(dd, m, e):
+        to = b + 1 if dd == 0 else b - 1
+        return remote(dgu.at[m, e], dgu.at[m, e], ag_send.at[m, e], ag_recv.at[m, e], (s, a, to))
+
+    def wi_copy(e):
+        return remote(win.at[e], win.at[e], wi_send.at[e], wi_recv.at[e], (layer, a, b))
+
+    def wd_copy(e):
+        return remote(wdt.at[e], wdt.at[e], wd_send.at[e], wd_recv.at[e], (layer, a, b))
+
+    def st_copies(e, slot):
+        return (pltpu.make_async_copy(sti.at[slot], win_g.at[e], st_sem.at[0, slot]),
+                pltpu.make_async_copy(std.at[slot], wdt_g.at[e], st_sem.at[1, slot]))
+
+    def weight_grads(e):
+        gi = mm(slots[:, e, :, :width].reshape(mbs * cap, width), dgu[:, e].reshape(mbs * cap, 2 * f), ((0,), (0,)))
+        gd = mm(gslots[:, e, :, :width].reshape(mbs * cap, width), hid[:, e].reshape(mbs * cap, f), ((0,), (0,)))
+        return gi, gd
+
+    late = 2
+    steps = starts[1] + half + lag + late
+
+    def chain(i):
+        reduce = [unit(i - sk * up[dd], dd) for dd in range(2)]
+        spreads = [unit(i - sk * (ny - 1) - ak * down[dd], dd) for dd in range(2)]
+        for dd in range(2):
+            valid, m, e = reduce[dd]
+
+            @pl.when(valid)
+            def _():
+                acc[dd] = mm(gslots[m, e, :, :width], wdt[e])
+
+            @pl.when(valid & first[dd])
+            def _():
+                dh[m, e] = bf(acc[dd])
+                dh_copy(dd, m, e).start()
+
+            @pl.when(valid & jnp.logical_not(first[dd] | last[dd]))
+            def _():
+                dh_copy(dd, m, e).wait_recv()
+                dh[m, e] = bf(acc[dd] + dh[m, e].astype(jnp.float32))
+                dh_copy(dd, m, e).start()
+
+            @pl.when(valid & last[dd])
+            def _():
+                dh_copy(dd, m, e).wait_recv()
+                total = acc[dd] + dh[m, e].astype(jnp.float32)
+                r = router_column(slots[m, e], e, width, experts)
+                gate = gown[m, e - dd * half, :, :f].astype(jnp.float32)
+                upv = gown[m, e - dd * half, :, f:].astype(jnp.float32)
+                dgate, dup, dr = act_back(gate, upv, total, jax.nn.sigmoid(r))
+                dgu[m, e, :, :f] = bf(dgate)
+                dgu[m, e, :, f:] = bf(dup)
+                dgu_copy(dd, m, e).start()
+                hi = bf(dr).astype(jnp.float32)
+                deo[m, e] = bf(jnp.where(lane == width + e, hi, jnp.where(lane == width + experts + e, dr - hi, 0.0)))
+
+        for dd in range(2):
+            valid, m, e = spreads[dd]
+
+            @pl.when(valid & jnp.logical_not(last[dd]))
+            def _():
+                dgu_copy(dd, m, e).wait_recv()
+
+                @pl.when(jnp.logical_not(first[dd]))
+                def _():
+                    dgu_copy(dd, m, e).start()
+
+            @pl.when(valid)
+            def _():
+                deo[m, e, :, :width] = bf(mm(dgu[m, e], win[e], ((1,), (1,))))
+
+        u = i - half - lag
+
+        @pl.when((u >= 0) & (u < half) & keeper)
+        def _():
+            pl.semaphore_signal(free, inc=1, device_id=(1 - s, a, b), device_id_type=MESH)
+
+        @pl.when((u >= 0) & (u < half) & helper)
+        def _():
+            pl.semaphore_wait(free, 1)
+            for dd in range(2):
+                e = jnp.clip(u, 0, half - 1) + dd * half
+                gi, gd = weight_grads(e)
+                win[e] = bf(gi)
+                wi_copy(e).start()
+                wdt[e] = bf(gd)
+                wd_copy(e).start()
+
+        w = u - late
+
+        @pl.when((w >= 0) & (w < half) & keeper)
+        def _():
+            for dd in range(2):
+                e = jnp.clip(w, 0, half - 1) + dd * half
+
+                @pl.when(w >= 1)
+                def _():
+                    for copy in st_copies(e - 1, dd):
+                        copy.wait()
+
+                gi, gd = weight_grads(e)
+                wi_copy(e).wait_recv()
+                sti[dd] = gi + win[e].astype(jnp.float32)
+                wd_copy(e).wait_recv()
+                std[dd] = gd + wdt[e].astype(jnp.float32)
+                for copy in st_copies(e, dd):
+                    copy.start()
+
+    stages = {}
+
+    def at(step, do, *args):
+        stages.setdefault(step, []).append(lambda: do(*args))
+
+    spread(0)
+    spread(1)
+    dispatch(0)
+    for j, (dst, own) in enumerate(((win, win_a), (wdt, wdt_a))):
+        pltpu.make_async_copy(own, dst, w_sem.at[j]).wait()
+    for copy in loads:
+        copy.wait()
+    for dd in range(2):
+        pl.when(last[dd])(own_gates(dd).wait)
+    at(1, dispatch, 1)
+    at(2, shared_act, 0)
+    at(3, shared_act, 1)
+    at(4, shared_grads)
+    at(5, down_grads)
+    at(6, shared_back, 0)
+    at(7, join, 0)
+    at(8, shared_back, 1)
+    for m in range(2):
+        done = starts[m] + half - 1 + lag
+        for c, do in enumerate((combine, combine_line, second_norm, attention, first_norm)):
+            at(done + c * apart, do, m)
+    end = starts[1] + half - 1 + lag
+    at(end - 1, settle, 0)
+    at(end + 3 * apart, attention_grads)
+    at(end + 4 * apart, join, 1)
+    at(end + 4 * apart, small_grads)
+    at(end + 5 * apart, join, 2)
+    at(end + 5 * apart, settle, 1)
+    at(end + 5 * apart, settle, 2)
+
+    def step(i, c):
+        chain(i)
+        for when in sorted(stages):
+            if when < steps:
+                @pl.when(i == when)
+                def _():
+                    for do in stages[when]:
+                        do()
+
+        return c
+
+    lax.fori_loop(0, steps, step, 0)
+    for when in sorted(stages):
+        if when >= steps:
+            for do in stages[when]:
+                do()
+
+    def copy_a(ai, slot):
+        return remote(small_f, small_a.at[slot], a_send.at[ai], a_recv.at[slot], (s, ai, b))
+
+    @pl.when(helper)
+    def _():
+        for i in range(3):
+            cross(i).wait_send()
+
+    @pl.when(keeper)
+    def _():
+        pos.peers(lambda ai: copy_a(ai, a).start())
+        small_a[a] = small_f[...]
+        pos.peers(lambda ai: copy_a(ai, ai).wait())
+        total = small_a[0]
+        for ai in range(1, nx):
+            total = total + small_a[ai]
+        small_f[...] = total
+        pltpu.make_async_copy(small_f, small_g, f_sem.at[2]).start()
+        for i in range(3):
+            pltpu.make_async_copy(finals[i], results[i], f_sem.at[i]).wait()
+        for dd in range(2):
+            for copy in st_copies((dd + 1) * half - 1, dd):
+                copy.wait()
+
+    def finish(index, c):
+        m = index // half
+        for dd in range(2):
+            e = lax.rem(index, half) + dd * half
+
+            @pl.when(jnp.logical_not(last[dd]))
+            def _():
+                dh_copy(dd, m, e).wait_send()
+
+            @pl.when(jnp.logical_not(first[dd]))
+            def _():
+                dgu_copy(dd, m, e).wait_send()
+
+            @pl.when(helper & (m == 0))
+            def _():
+                wi_copy(e).wait_send()
+                wd_copy(e).wait_send()
+
+        return c
+
+    lax.fori_loop(0, mbs * half, finish, 0)
+
+
+def backward(layer, g, fwd, watt, cos, sin, rot, win, wdt, grads, dims, heads, features, ids):
+    width, pw, experts, cap = dims
+    nx, ny = lax.axis_size("gx"), lax.axis_size("gy")
+    mbs, sub, d = g.shape[-3:]
+    f = wdt[0].shape[-1]
+    length, tokens, slots = nx * sub, nx * ny * sub, experts * cap
+    b16, f32 = jnp.bfloat16, jnp.float32
+    vm = pl.BlockSpec(memory_space=pltpu.VMEM)
+    hbm = pl.BlockSpec(memory_space=pl.ANY)
+    ac, sc, n, half = watt.shape[2], fwd["shw"].shape[3], fwd["small"].shape[1], experts // 2
+    rows_shape = (mbs, nx, sub, d)
+    dense = lambda c: ((ny, width, c), b16)
+    scratch = (
+        ((experts, width, 2 * f), b16), ((experts, width, f), b16),
+        ((mbs, ny, sub, pw), b16), ((mbs, ny, sub, pw), b16), ((mbs, ny, nx, sub, pw), b16), (rows_shape, b16),
+        ((slots, tokens), b16), ((tokens, slots), b16),
+        ((mbs, experts, cap, pw), b16), ((mbs, experts, cap, pw), b16), ((mbs, half, cap, 2 * f), b16),
+        ((mbs, experts, cap, f), b16), ((2, cap, f), f32), ((mbs, experts, cap, f), b16),
+        ((mbs, experts, cap, 2 * f), b16), ((mbs, experts, cap, pw), b16),
+        ((2, width, 2 * f), f32), ((2, width, f), f32),
+        ((mbs, length, 2 * f), b16), (rows_shape, b16), (rows_shape, b16),
+        ((mbs, nx, ny, sub, pw), b16), ((mbs, nx, ny, sub, pw), b16), ((mbs, ny, sub, pw), b16), ((mbs, ny, sub, pw), b16),
+        ((pw, d), b16), ((mbs, sub, d), f32), ((mbs, sub, d), b16), (rows_shape, b16),
+        ((length, pw), b16), ((mbs, length, 3 * pw), b16), (rows_shape, b16), (rows_shape, b16),
+        ((experts, d), f32), ((8, d), f32),
+        dense(sc), dense(ac), ((n, d), f32), dense(sc), dense(ac), ((n, d), f32),
+        dense(sc), dense(ac), ((ny, n, pw), f32),
+        ((width, sc), f32), ((width, ac), f32), ((n, pw), f32), ((nx, n, pw), f32),
+    )
+    by_m = lambda c: flags((mbs, c))
+
+    names = ("mid", "n2", "rows", "q", "k", "v", "att", "rows2", "sgu", "shid", "shw")
+    by_layer = [g, fwd["small"], fwd["place"], fwd["place_t"], fwd["tok"] if layer == 0 else fwd["y"]]
+    by_layer += [fwd[name] for name in names]
+    order = [4, 0, 1, *range(5, 16), 2, 3]
+    resident = tuple((by_layer[c].shape[1:], by_layer[c].dtype) for c in order)
+    outs = pl.pallas_call(
+        functools.partial(
+            backward_kernel,
+            (layer, nx, ny, mbs, sub, width, pw, heads, features, experts, cap, f, *BWD_SKEW)),
+        out_shape=(
+            jax.ShapeDtypeStruct((mbs, sub, d), b16),
+            jax.ShapeDtypeStruct((experts, width, 2 * f), f32),
+            jax.ShapeDtypeStruct((experts, width, f), f32),
+            jax.ShapeDtypeStruct((width, ac), f32),
+            jax.ShapeDtypeStruct((width, sc), f32),
+            jax.ShapeDtypeStruct((n, pw), f32),
+        ),
+        in_specs=[hbm] * 16 + [vm] * 4 + [hbm] * (7 + len(grads)),
+        out_specs=(vm,) + (hbm,) * 5,
+        scratch_shapes=[pltpu.VMEM(*v) for v in scratch + resident] + [
+            flags((2,)), by_m(ny), by_m(ny), by_m(nx), by_m(nx), by_m(nx), by_m(nx), by_m(nx), by_m(nx),
+            by_m(nx), by_m(nx), by_m(ny), by_m(ny), by_m(nx), by_m(nx), by_m(nx), by_m(nx),
+            by_m(experts), by_m(experts), by_m(experts), by_m(experts),
+            flags((experts,)), flags((experts,)), flags((experts,)), flags((experts,)),
+            flags((3,)), flags((3,)), flags((3, ny)), flags((3, ny)), flags((nx,)), flags((nx,)),
+            flags((3,)), flags((2, 2)), flags((3,)), flags((16,)), pltpu.SemaphoreType.REGULAR,
+        ],
+        input_output_aliases={27 + i: 1 + i for i in range(len(grads))},
+        compiler_params=params(ids),
+        cost_estimate=pl.CostEstimate(flops=10**10, bytes_accessed=6 * 10**7, transcendentals=10**6),
+        name="backward",
+    )(
+        *by_layer, watt, cos, sin, rot,
+        *(fwd[name] for name in ("slots", "gu", "hid")), *win, *wdt, *grads,
+    )
+    return outs[0], outs[1:]
+
+
+BWD_SKEW = (1, 1)
+
+
+def fast_device(block_input, output_grad, attention_gain, attention_in, attention_out, feed_gain,
+                router_weight, expert_in, expert_down, shared_in, shared_down, routes):
+    s = lax.axis_index("section")
+    ny = lax.axis_size("gy")
+    nx = lax.axis_size("gx")
+    mbs = block_input.shape[0] // 2
+    width = block_input.shape[2]
+    features = width * ny
+    experts = expert_in.shape[1]
+    f = expert_in.shape[-1]
+    pw = lanes_up(width + 2 * experts)
+    tokens = routes.shape[2]
+    cap = 5 * tokens // (2 * experts)
+    length = tokens // ny
+    heads = attention_in.shape[-1] // DH
+    dims = (width, pw, experts, cap)
+
+    att_block = jnp.concatenate([
+        pad_to(attention_in[0], 2, pw).reshape(width, 3 * pw), pad_to(attention_out[0].T, 1, pw)], 1)
+    sh_block = jnp.concatenate([shared_in[0].reshape(width, 2 * f), shared_down[0].T], 1)
+    small = jnp.concatenate([
+        router_weight[0].T.astype(jnp.float32), feed_gain, attention_gain, jnp.zeros((6, width), jnp.float32)], 0)
+    tin = lax.dynamic_slice_in_dim(jnp.stack([block_input, output_grad]), s * mbs, mbs, 1)
+    tin = pad_to(tin, 3, pw)
+    small = pad_to(small, 1, pw)
+    win = expert_in[0].reshape(experts, width, 2 * f)
+    win = (win, pass_section(win))
+    wdt = expert_down[0].transpose(0, 2, 1)
+    wdt = (wdt, pass_section(wdt))
+    pairs = jnp.swapaxes(routes[0], 1, 2)
+    half = DH // 2
+    freq = 10000.0 ** (-jnp.arange(half, dtype=jnp.float32) / half)
+    ang = jnp.arange(length, dtype=jnp.float32)[:, None] * freq[None]
+    lanes = jnp.tile(ang, (1, 2 * heads))
+    cos = pad_to(jnp.cos(lanes), 1, pw)
+    sin = pad_to(jnp.sin(lanes), 1, pw)
+    rot = pad_to(pad_to(rot_columns(jnp.eye(heads * DH, dtype=jnp.float32)), 0, pw), 1, pw).astype(jnp.bfloat16)
+
+    fwd = forward(tin, small, att_block, sh_block, pairs, cos, sin, rot, win, wdt, dims, heads, features, 0)
+    outs, watt = fwd["y"], (fwd["watt0"], fwd["watt1"])
+    g, gouts, grads = fwd["tok"], [None, None], ()
+    for l in (1, 0):
+        gouts[l], grads = backward(l, g, fwd, watt[l], cos, sin, rot, win, wdt, grads, dims, heads, features, 1 + l)
+        g = gouts[l][None]
+
+    both = leave(jnp.stack([outs[0], gouts[0]]), jnp.stack([outs[1], gouts[1]]), pw, 3)[..., :width]
+    win_g, wdt_g, att_g, sh_g, small_g = grads
+    hd = heads * DH
+    return (
+        both[0][None],
+        both[1][None],
+        small_g[experts + 1 : experts + 2, :width],
+        att_g[:, : 3 * pw].reshape(width, 3, pw)[..., :hd][None],
+        att_g[:, 3 * pw : 3 * pw + hd].T[None],
+        small_g[experts : experts + 1, :width],
+        small_g[:experts, :width].T[None],
+        win_g.reshape(experts, width, 2, f)[None],
+        wdt_g.transpose(0, 2, 1)[None],
+        sh_g[:, : 2 * f].reshape(width, 2, f)[None],
+        sh_g[:, 2 * f :].T[None],
+    )
+
+
 def solution(mesh):
     in_specs = (
         P(None, "gx", "gy"),
@@ -538,6 +1973,7 @@
         P("section", "gy", None, "gx"),
         P("section", "gx", "gy"),
     )
+    fast = mesh.shape["gx"] == mesh.shape["gy"]
     return jax.shard_map(
-        on_device, mesh=mesh, in_specs=in_specs, out_specs=out_specs, check_vma=False
-    )
+        fast_device if fast else on_device, mesh=mesh, in_specs=in_specs, out_specs=out_specs, check_vma=False
+    )

time: 3400 us -> 829 us (0.24)
  waiting for transfers between devices: 1380 us -> 0.01 us
  blocking collectives: 862 us -> 0 us
  Pallas kernels: 0 us -> 750 us
  local copies, waits for them, and re-layouts: 458 us -> 61.2 us
  matrix products: 358 us -> 0 us
  other arithmetic: 290 us -> 4.7 us
    reduce_scatter x50 -> x0, waiting for transfers between devices: 1090 us -> none  [the longest x5 316 us: layer_forward(): lax.psum_scatter(expert_part.reshape(slot_count, -1), 'gy', scatter_dimen...]
    pallas_call x0 -> x4, Pallas kernels: none -> 750 us  [the longest x2 410 us: backward(): pl.pallas_call(functools.partial(backward_kernel, (layer, nx, ny, mbs, su...]
    all_gather x40 -> x0, blocking collectives: 520 us -> none  [the longest x10 193 us: gather_hidden(): lax.all_gather(shared_hidden, 'gy', axis=0, tiled=True)]
    dot_general x135 -> x0, matrix products: 358 us -> none  [the longest x5 55.1 us: layer_backward(): jnp.einsum('ecd,ecf->edf', grouped, gu_grouped, preferred_element_type=jn...]
    all_gather x20 -> x0, waiting for transfers between devices: 278 us -> none  [the longest x5 162 us: layer_backward(): lax.all_gather(grad_gu.astype(jnp.bfloat16), 'gy', axis=0, tiled=True)]
    psum x21 -> x0, blocking collectives: 247 us -> none  [the longest x20 230 us: width_sum(): return lax.psum(values, 'gy')]
    gather x55 -> x0, local copies, waits for them, and re-layouts: 183 us -> none  [the longest x10 28 us: layer_backward(): slot_back[route_slot[:, 1]]]
    unnamed x10 -> x0, blocking collectives: 95.5 us -> none
  transfers between devices with their start and end apart: 78 -> 2, of which waited for: 58 -> 0; matrix products, arithmetic and copies ran while one was open for 23% -> 2% of each run, Pallas kernels for 0% -> 0%
where the time goes in v4:
time: 829 us; the launch traced here: 818 us
  Pallas kernels  750 us (90%)
  local copies, waits for them, and re-layouts  61.2 us (7%)
    pallas_call x2, Pallas kernels, backward(): pl.pallas_call(functools.partial(backward_kernel, (layer, nx, ny, mbs, su...  410 us
    pallas_call x1, Pallas kernels, forward(): pl.pallas_call(functools.partial(forward_kernel, (nx, ny, mbs, sub, width...  326 us
    another operation x1, local copies, waits for them, and re-layouts, fast_device(): win_g.reshape(experts, width, 2, f)[None]  16.9 us
  transfers between devices with their start and end apart: 2, of which 0 were waited for; matrix products, arithmetic and copies ran while one was open for 2% of the time, Pallas kernels for 0%

profile of v4, /device:TPU:0, one launch (start us, length us, event | category | flops | bytes accessed | tf_op | source)
XLA Modules:
  0.0 817.7 jit_solution(12190020560966720074)
XLA Ops:
  0.6 0.0 copy-start
  0.7 11.1 %reshape_squeeze.7.refs_8_.refs_23_ = bf16[16,192,1024]{2,1,0:T(8,128)(2,1)} reshape(bf16[1,16,192,2,512]{4,3,2,1,0:T(2,128)(2,1)} %param.19) | data formatting | bytes 12582912 | tf_op jit(solution)/shard_map/reshape;squeeze | solution.py:1910
  11.8 0.5 collective-permute-start
  12.3 0.1 collective-permute-start.1
  12.3 0.1 pad.54.clone
  12.4 0.1 maximum_maximum_fusion
  12.5 0.6 pad.34.refs_1_
  13.1 0.1 fusion.5
  13.3 0.1 copy.41
  13.4 0.7 pad.38.refs_6_.refs_18_
  14.1 0.1 copy.40
  14.2 0.7 pad.37.refs_5_.refs_17_
  14.8 1.0 copy.39
  15.8 0.1 fusion.3
  16.0 0.7 copy.42
  16.7 1.1 copy.36
  17.8 1.8 copy.37
  19.6 1.6 pad.58.refs_7_.refs_19_
  21.2 0.9 fusion.2
  22.1 0.7 pad.33.refs_0_
  22.9 1.2 copy.47
  24.1 0.2 pad.35.clone
  24.3 1.0 copy.49
  25.4 0.8 fusion.1.refs_2_
  26.2 0.9 pad_maximum_fusion.refs_3_
  27.0 0.0 collective-permute-done.1.refs_11_.refs_26_
  27.1 326.4 %forward.1 = (bf16[2,2,32,1024]{3,2,1,0:T(8,128)(2,1)}, f32[2,24,1024]{2,1,0:T(8,128)}, s32[2,2,2,512]{3,2,1,0:T(2,128)}, s32[2,2,512,2]{3,2,1,0:T(8,128)}, bf16...) custom-call(bf16[2,2,128,256]{3,2,1,0:T(8,128)(2,1)} %pad.33.refs_0_, ...), custom_call_target="tpu_custom_call" | custom-call | flops 10000000000 | bytes 80000000 | tf_op jit(solution)/shard_map/forward/pallas_call | solution.py:1295
  353.5 1.0 fusion.8
  354.5 182.2 %backward.2 = (bf16[2,32,1024]{2,1,0:T(8,128)(2,1)}, f32[16,192,1024]{2,1,0:T(8,128)}, f32[16,192,512]{2,1,0:T(8,128)}, f32[192,1024]{1,0:T(8,128)}, f32[192,1536]{1,0:T(8,128)}, /*index=5*/f32[24,256]{1,0:T(8,128)}) custom-call(bf16[2,2,32,1024]{3,2,1,0:T(8,128)(2,1)} %get-tuple-element.45.refs_0_.refs_4_, f32[2,24,1024]{2,1,0:T(8,128)} %get-tuple-element.46.refs_1_, ...), custom_call_target="tpu_custom_call" | custom-call | flops 10000000000 | bytes 60000000 | tf_op jit(solution)/shard_map/backward/pallas_call | solution.py:1849
  536.7 228.0 %backward.3 = (bf16[2,32,1024]{2,1,0:T(8,128)(2,1)}, f32[16,192,1024]{2,1,0:T(8,128)}, f32[16,192,512]{2,1,0:T(8,128)}, f32[192,1024]{1,0:T(8,128)}, f32[192,1536]{1,0:T(8,128)}, /*index=5*/f32[24,256]{1,0:T(8,128)}) custom-call(bf16[1,2,32,1024]{3,2,1,0:T(8,128)(2,1)} %bitcast.57, ...), custom_call_target="tpu_custom_call", output_to_operand_aliasing={{1}: (27, {}), {2}: (28, {}), {3}: (29, {}), {4}: (30, {}),... | custom-call | flops 10000000000 | bytes 60000000 | tf_op jit(solution)/shard_map/backward/pallas_call | solution.py:1849
  764.7 1.3 fusion.9
  766.0 1.3 slice_bitcast_fusion.3
  767.4 0.9 slice_bitcast_fusion.2
  768.3 1.1 slice.53
  769.4 1.8 slice_bitcast_fusion.1
  771.2 1.2 slice.58
  772.4 1.7 pad_maximum_fusion.1
  774.1 13.4 %leave.1 = bf16[2,4,128,256]{3,2,1,0:T(8,128)(2,1)} custom-call(bf16[2,2,32,1024]{3,2,1,0:T(8,128)(2,1)} %get-tuple-element.107.pair0, bf16[2,2,32,1024]{3,2,1,0:T(8,128)(2,1)} %get-tuple-element.108.pair1), custom_call_target="tpu_custom_call" | custom-call | tf_op jit(solution)/shard_map/leave/pallas_call | solution.py:763
  787.5 1.1 fusion.7
  788.6 0.8 copy.44
  789.4 0.8 copy.43
  790.2 0.8 copy.46
  791.0 0.3 reshape.82
  791.4 0.1 slice_bitcast_fusion
  791.5 0.9 copy.45
  792.4 1.5 broadcast_in_dim_reshape.7
  794.0 16.9 %broadcast_in_dim_reshape.6 = f32[1,16,192,2,512]{4,3,2,1,0:T(2,128)} reshape(f32[16,192,1024]{2,1,0:T(8,128)} %get-tuple-element.74) | data formatting | bytes 25165824 | tf_op jit(solution)/shard_map/broadcast_in_dim;reshape | solution.py:1941
  810.8 6.5 copy.56
  (22 shorter events, 0.1 us)
Async XLA Ops:
  0.6 11.6 %copy-start = (bf16[1,16,512,192]{2,3,1,0:T(8,128)(2,1)S(1)}, bf16[1,16,512,192]{2,3,1,0:T(8,128)(2,1)}, u32[]{:S(2)}) copy-start(bf16[1,16,512,192]{2,3,1,0:T(8,128)(2,1)} %param.20) | copy-start | bytes 9437188
  0.7 11.7 %copy-start.3 = (bf16[1,192,16]{1,2,0:T(8,128)(2,1)S(1)}, bf16[1,192,16]{1,2,0:T(8,128)(2,1)}, u32[]{:S(2)}) copy-start(bf16[1,192,16]{1,2,0:T(8,128)(2,1)} %param.18) | copy-start | bytes 18436
  0.7 11.7 %copy-start.5 = (f32[1,192]{1,0:T(1,128)S(1)}, f32[1,192]{1,0:T(1,128)}, u32[]{:S(2)}) copy-start(f32[1,192]{1,0:T(1,128)} %param.17) | copy-start | bytes 2308
  0.7 11.7 %copy-start.4 = (f32[1,192]{1,0:T(1,128)S(1)}, f32[1,192]{1,0:T(1,128)}, u32[]{:S(2)}) copy-start(f32[1,192]{1,0:T(1,128)} %param.14) | copy-start | bytes 2308
  11.8 15.2 %collective-permute-start = (bf16[16,192,1024]{2,1,0:T(8,128)(2,1)}, bf16[16,192,1024]{2,1,0:T(8,128)(2,1)}, u32[]{:S(2)}, u32[]{:S(2)}) collective-permute-start(bf16[16,192,1024]{2,1,0:T(8,128)(2,1)} %reshape_squeeze.7.refs_8_.refs_23_), channel_id=1, source_target_pairs={{0,16},{16,0},{1,17},{17,1},{2,18},{18,2},{3,19},{19,3},{4,20},{20... | collective-permute-start | bytes 18874376 | tf_op jit(solution)/shard_map/ppermute | solution.py:18
  12.3 14.8 %collective-permute-start.1 = (bf16[16,192,512]{2,1,0:T(8,128)(2,1)S(1)}, bf16[16,192,512]{2,1,0:T(8,128)(2,1)}, u32[]{:S(2)}, u32[]{:S(2)}) collective-permute-start(bf16[16,192,512]{2,1,0:T(8,128)(2,1)S(1)} %bitcast.51), channel_id=1, source_target_pairs={{0,16},{16,0},{1,17},{17,1},{2,18},{18,2},{3,19},{19,3},{4,20},{20... | collective-permute-start | bytes 9437192 | tf_op jit(solution)/shard_map/ppermute | solution.py:18
  19.6 6.6 copy-start.2
  536.6 235.7 %copy-start.1 = (bf16[2,32,1024]{2,1,0:T(8,128)(2,1)S(1)}, bf16[2,32,1024]{2,1,0:T(8,128)(2,1)}, u32[]{:S(2)}) copy-start(bf16[2,32,1024]{2,1,0:T(8,128)(2,1)} %get-tuple-element.64) | copy-start | bytes 393220

commit v5 on v4

--- a/solution.py
+++ b/solution.py
@@ -1318,24 +1318,19 @@
 
 
 def backward_kernel(cfg, *refs):
-    layer, nx, ny, mbs, sub, width, pw, heads, features, experts, cap, f, sk, ak = cfg
-    n_by = 16
-    by_layer, refs = refs[:n_by], refs[n_by:]
-    (watt, cos, sin, rot, slots_i, gu_i, hid_i, win_a, win_b, wdt_a, wdt_b) = refs[:11]
-    refs = refs[11 + (0 if layer else 5) :]
+    nx, ny, mbs, sub, width, pw, heads, features, experts, cap, f, sk, ak = cfg
+    (tok_i, small_i, place_i, y_i, mid_i, n2_i, rows_i, q_i, k_i, v_i, att_i, rows2_i, sgu_i, shid_i, shw_i,
+     watt0_i, watt1_i, cos, sin, rot, slots_i, gu_i, hid_i, win_a, win_b, wdt_a, wdt_b) = refs[:27]
     (gx_o, win_g, wdt_g, att_g, sh_g, small_g,
      win, wdt, xsend, xline, xall, grows, pm, pt, slots, gslots, gown, hid, acc, dh, dgu, deo, sti, std,
      dsgu, ssend, srecv, rsend, rpeer, rline, rrecv, rwx, dm, msend, mall, datt, dqkv, dsend, drecv,
      rw_p, gains, sh_p, att_p, small_p, sh_x, att_x, small_x, sh_r, att_r, small_r, sh_f, att_f, small_f, small_a,
-     x, g, small, mid, n2, rows, q, k, v, att, rows2, sgu, shid, shw, place, place_t,
+     g, gx, small, place, x, mid, n2, rows, q, k, v, att, rows2, sgu, shid, shw, watt,
      w_sem, x_send, x_recv, u_send, u_recv, t_send, t_recv, s_send, s_recv, g_send, g_recv, r_send, r_recv,
      m_send, m_recv, d_send, d_recv, rs_send, rs_recv, ag_send, ag_recv, wi_send, wi_recv, wd_send, wd_recv,
-     c_send, c_recv, e_send, e_recv, a_send, a_recv, l_sem, st_sem, f_sem, y_sem, free) = refs
-    resident = (g, small, place, place_t, x, mid, n2, rows, q, k, v, att, rows2, sgu, shid, shw)
+     c_send, c_recv, e_send, e_recv, a_send, a_recv, l_sem, st_sem, f_sem, y_sem, free) = refs[27:]
     pos = Position(nx, ny)
     s, a, b = pos.s, pos.a, pos.b
-    keeper = s == layer
-    helper = jnp.logical_not(keeper)
     slots_n = experts * cap
     tokens = nx * ny * sub
     d = ny * pw
@@ -1352,32 +1347,57 @@
     pos.line(lambda bi: pl.semaphore_signal(barrier, inc=1, device_id=(s, a, bi), device_id_type=MESH))
     pl.semaphore_signal(barrier, inc=1, device_id=(1 - s, a, b), device_id_type=MESH)
 
-    for j, (dst, own, oth) in enumerate(((win, win_a, win_b), (wdt, wdt_a, wdt_b))):
-        @pl.when(keeper)
-        def _():
-            pltpu.make_async_copy(own, dst, w_sem.at[j]).start()
-
-        @pl.when(helper)
-        def _():
-            pltpu.make_async_copy(oth, dst, w_sem.at[j]).start()
-
-    picks = (-1, layer, layer, layer, 0) + (layer,) * 11
-    fills = [
-        pltpu.make_async_copy(src.at[src.shape[0] - 1 if at < 0 else at], dst, y_sem.at[c])
-        for c, (src, dst, at) in enumerate(zip(by_layer, resident, picks))
+    def weight_copy(l, e, which):
+        own, oth, dst = ((win_a, win_b, win), (wdt_a, wdt_b, wdt))[which]
+        sem = w_sem.at[which, e]
+        return pltpu.make_async_copy(own.at[e], dst.at[e], sem), pltpu.make_async_copy(oth.at[e], dst.at[e], sem)
+
+    def start_weights(l, e):
+        for which in range(2):
+            own, oth = weight_copy(l, e, which)
+            pl.when(s == l)(own.start)
+            pl.when(s != l)(oth.start)
+
+    def first_weights(e, c):
+        start_weights(1, e)
+        return c
+
+    lax.fori_loop(0, experts, first_weights, 0)
+
+    early = ((rows2_i, rows2), (sgu_i, sgu), (shid_i, shid), (shw_i, shw))
+    later = ((mid_i, mid), (n2_i, n2), (rows_i, rows), (q_i, q), (k_i, k), (v_i, v), (att_i, att))
+
+    def early_loads(l):
+        return [pltpu.make_async_copy(src.at[l], dst, y_sem.at[c]) for c, (src, dst) in enumerate(early)]
+
+    def later_loads(l):
+        copies = [pltpu.make_async_copy(src.at[l], dst, y_sem.at[4 + c]) for c, (src, dst) in enumerate(later)]
+        copies.append(pltpu.make_async_copy(y_i.at[0] if l else tok_i.at[0], x, y_sem.at[11]))
+        return copies + [pltpu.make_async_copy(watt1_i if l else watt0_i, watt, y_sem.at[12])]
+
+    def hid_load(l):
+        return pltpu.make_async_copy(hid_i.at[l], hid, l_sem.at[1])
+
+    def gates(l, m, dd):
+        return pltpu.make_async_copy(gu_i.at[l, m, pl.ds(dd * half, half)], gown.at[m], l_sem.at[2 + m])
+
+    def start_gates(l, m):
+        for dd in range(2):
+            pl.when(last[dd])(gates(l, m, dd).start)
+
+    def wait_gates(l, m):
+        for dd in range(2):
+            pl.when(last[dd])(gates(l, m, dd).wait)
+
+    first_loads = [
+        pltpu.make_async_copy(src, dst, y_sem.at[13 + c])
+        for c, (src, dst) in enumerate(((tok_i.at[1], g), (small_i, small), (place_i, place)))
     ]
-    for copy in fills:
+    slots_load = pltpu.make_async_copy(slots_i, slots, l_sem.at[0])
+    for copy in first_loads + [slots_load, hid_load(1)] + early_loads(1) + later_loads(1):
         copy.start()
-    loads = fills[4:] + [pltpu.make_async_copy(slots_i.at[layer], slots, l_sem.at[0]), pltpu.make_async_copy(hid_i.at[layer], hid, l_sem.at[1])]
-    for copy in loads[-2:]:
-        copy.start()
-
-    def own_gates(dd):
-        part = pl.ds(dd * half, half)
-        return pltpu.make_async_copy(gu_i.at[layer, :, part], gown, l_sem.at[2])
-
-    for dd in range(2):
-        pl.when(last[dd])(own_gates(dd).start)
+    for m in range(mbs):
+        start_gates(1, m)
 
     def copy_x(m, bi, slot):
         return remote(xsend.at[m, bi], xline.at[m, slot], x_send.at[m, bi], x_recv.at[m, slot], (s, a, bi))
@@ -1388,37 +1408,43 @@
     def copy_t(m, ai, slot):
         return remote(g.at[m], grows.at[m, slot], t_send.at[m, ai], t_recv.at[m, slot], (s, ai, b))
 
-    for copy in fills[:4]:
+    for copy in first_loads:
         copy.wait()
-    for m in range(mbs):
+    pl.semaphore_wait(barrier, nx - 1 + ny - 1 + 1)
+
+    def send_g(m):
         for j in range(ny):
             xsend[m, j] = g[m, :, j * pw : (j + 1) * pw]
-    pl.semaphore_wait(barrier, nx - 1 + ny - 1 + 1)
-    for m in range(mbs):
         pos.line(lambda bi: copy_x(m, bi, b).start())
         xline[m, b] = xsend[m, b]
-    for m in range(mbs):
         pos.peers(lambda ai: copy_t(m, ai, a).start())
         grows[m, a] = g[m]
+
+    send_g(0)
+    send_g(1)
     deo[...] = jnp.zeros_like(deo)
     ssend[...] = jnp.zeros_like(ssend)
     dsend[...] = jnp.zeros_like(dsend)
     rwx[...] = jnp.zeros_like(rwx)
-    rwx[width : width + experts] = bf(small[:experts])
-    rwx[width + experts : width + 2 * experts] = bf(small[:experts])
-    rw_p[...] = jnp.zeros_like(rw_p)
-    gains[...] = jnp.zeros_like(gains)
+
+    def new_layer(l):
+        rwx[width : width + experts] = bf(small[l, :experts])
+        rwx[width + experts : width + 2 * experts] = bf(small[l, :experts])
+        rw_p[...] = jnp.zeros_like(rw_p)
+        gains[...] = jnp.zeros_like(gains)
+
+    new_layer(1)
 
     def spread(m):
         pos.line(lambda bi: copy_x(m, bi, bi).wait())
         pos.peers(lambda ai: copy_w(m, ai, a).start())
         xall[m, :, a] = xline[m]
 
-    def dispatch(m):
+    def dispatch(l, m):
         i0 = lax.broadcasted_iota(jnp.int32, (slots_n, tokens), 0)
-        pm[...] = bf(((place[m, 0:1] == i0) | (place[m, 1:2] == i0)).astype(jnp.float32))
+        pm[...] = bf(((place[l, m, 0:1] == i0) | (place[l, m, 1:2] == i0)).astype(jnp.float32))
         pos.peers(lambda ai: copy_w(m, ai, ai).wait())
-        gslots[m] = bf(mm(pm[...], xall[m].reshape(tokens, pw))).reshape(experts, cap, pw)
+        gslots[l, m] = bf(mm(pm[...], xall[m].reshape(tokens, pw))).reshape(experts, cap, pw)
 
     def shared_act(m):
         pos.peers(lambda ai: copy_t(m, ai, ai).wait())
@@ -1442,8 +1468,8 @@
     finals = (sh_f, att_f, small_f)
     results = (sh_g, att_g, small_g)
 
-    def cross(i):
-        return remote(crossing[i][0], crossing[i][1], c_send.at[i], c_recv.at[i], (layer, a, b))
+    def cross(l, i):
+        return remote(crossing[i][0], crossing[i][1], c_send.at[i], c_recv.at[i], (l, a, b))
 
     def block(i, bi):
         if i == 2:
@@ -1453,24 +1479,28 @@
     def along(i, bi, slot):
         return remote(block(i, bi), places[i].at[slot], e_send.at[i, bi], e_recv.at[i, slot], (s, a, bi))
 
-    def give(i):
-        pl.when(helper)(cross(i).start)
-
-    def join(i):
-        @pl.when(keeper)
+    def give(l, i):
+        pl.when(s != l)(cross(l, i).start)
+
+    def given(l):
+        for i in range(3):
+            pl.when(s != l)(cross(l, i).wait_send)
+
+    def join(l, i):
+        @pl.when(s == l)
         def _():
-            cross(i).wait_recv()
+            cross(l, i).wait_recv()
             part, other = crossing[i]
             other[...] = (part[...].astype(jnp.float32) + other[...].astype(jnp.float32)).astype(other.dtype)
-            pos.line(lambda bi: along(i, bi, b).start())
-
-    def settle(i):
-        @pl.when(keeper)
+            pos.line(lambda bi: along(i, bi, lax.rem(b - bi + ny, ny) - 1).start())
+
+    def settle(l, i):
+        @pl.when(s == l)
         def _():
-            pos.line(lambda bi: along(i, bi, bi).wait())
+            pos.line(lambda bi: along(i, bi, lax.rem(bi - b + ny, ny) - 1).wait())
             total = block(i, b)[...].astype(jnp.float32)
             for c in range(1, ny):
-                total = total + places[i][lax.rem(b + c, ny)].astype(jnp.float32)
+                total = total + places[i][c - 1].astype(jnp.float32)
             finals[i][...] = total
             if i < 2:
                 pltpu.make_async_copy(finals[i], results[i], f_sem.at[i]).start()
@@ -1480,11 +1510,11 @@
             rj = rows2[:, :, :, j * pw : j * pw + width].reshape(mbs * length, width)
             sh_p[j, :, : 2 * f] = bf(mm(rj, dsgu[...].reshape(mbs * length, 2 * f), ((0,), (0,))))
 
-    def down_grads():
+    def down_grads(l):
         for j in range(ny):
             gj = grows[:, :, :, j * pw : j * pw + width].reshape(mbs * length, width)
             sh_p[j, :, 2 * f :] = bf(mm(gj, shid[...].reshape(mbs * length, f), ((0,), (0,))))
-        give(0)
+        give(l, 0)
 
     def copy_g(m, ai, slot):
         return remote(rsend.at[m, ai], rpeer.at[m, slot], g_send.at[m, ai], g_recv.at[m, slot], (s, ai, b))
@@ -1492,12 +1522,18 @@
     def copy_r(m, bi, slot):
         return remote(rline.at[m, bi], rrecv.at[m, slot], r_send.at[m, bi], r_recv.at[m, slot], (s, a, bi))
 
-    def combine(m):
-        i1 = lax.broadcasted_iota(jnp.int32, (tokens, slots_n), 1)
-        pt[...] = bf(((place_t[m, :, 0:1] == i1) | (place_t[m, :, 1:2] == i1)).astype(jnp.float32))
-        br = bf(mm(pt[...], deo[m].reshape(slots_n, pw))).reshape(ny, nx, sub, pw)
-        for ai in range(nx):
-            rsend[m, ai] = br[:, ai]
+    def combine(l, m):
+        row = lax.broadcasted_iota(jnp.int32, (128, tokens), 0)
+        pair = place[l, m].astype(jnp.float32)
+        cols = jnp.where(row == 0, pair[0:1], jnp.where(row == 1, pair[1:2], 0.0)).T.astype(jnp.int32)
+        part = tokens // 2
+        i1 = lax.broadcasted_iota(jnp.int32, (part, slots_n), 1)
+        for c in range(2):
+            these = cols[c * part : (c + 1) * part]
+            pt[...] = bf(((these[:, 0:1] == i1) | (these[:, 1:2] == i1)).astype(jnp.float32))
+            br = bf(mm(pt[...], deo[m].reshape(slots_n, pw))).reshape(ny // 2, nx, sub, pw)
+            for ai in range(nx):
+                rsend[m, ai, c * (ny // 2) : (c + 1) * (ny // 2)] = br[:, ai]
         pos.peers(lambda ai: copy_g(m, ai, a).start())
         rpeer[m, a] = rsend[m, a]
 
@@ -1513,7 +1549,7 @@
     def copy_m(m, ai, slot):
         return remote(msend.at[m], mall.at[m, slot], m_send.at[m, ai], m_recv.at[m, slot], (s, ai, b))
 
-    def second_norm(m):
+    def second_norm(l, m):
         pos.peers(lambda ai: copy_s(m, ai, ai).wait())
         pos.line(lambda bi: copy_r(m, bi, bi).wait())
         dlog = jnp.zeros((sub, pw), jnp.float32)
@@ -1530,7 +1566,7 @@
         rw_t = mm(hi, n2[m], ((0,), (0,))) + mm(lo, n2[m], ((0,), (0,)))
         rw_p[...] += rw_t[width : width + experts] + rw_t[width + experts : width + 2 * experts]
         mv = mid[m]
-        dx2, gain_g = norm_back(mv, rms(mv, features), small[experts : experts + 1], dn2, features)
+        dx2, gain_g = norm_back(mv, rms(mv, features), small[l, experts : experts + 1], dn2, features)
         gains[0:1] += gain_g
         dm[m] = g[m].astype(jnp.float32) + dx2
         msend[m] = bf(dm[m])
@@ -1566,185 +1602,253 @@
         pos.peers(lambda ai: copy_d(m, ai, a).start())
         drecv[m, a] = dsend[m, a]
 
-    def first_norm(m):
+    def first_norm(l, m):
         pos.peers(lambda ai: copy_d(m, ai, ai).wait())
         dn1 = drecv[m, 0].astype(jnp.float32)
         for ai in range(1, nx):
             dn1 = dn1 + drecv[m, ai].astype(jnp.float32)
         xv = x[m].astype(jnp.float32)
-        dx1, gain_g = norm_back(xv, rms(xv, features), small[experts + 1 : experts + 2], dn1, features)
+        dx1, gain_g = norm_back(xv, rms(xv, features), small[l, experts + 1 : experts + 2], dn1, features)
         gains[1:2] += gain_g
-        gx_o[m] = bf(dm[m] + dx1)
-
-    def attention_grads():
+        gx[l, m] = bf(dm[m] + dx1)
+        if l:
+            g[m] = gx[l, m]
+            send_g(m)
+
+    def attention_grads(l):
         for j in range(ny):
             cols = slice(j * pw, j * pw + width)
             rj = rows[:, :, :, cols].reshape(mbs * length, width)
             mj = mall[:, :, :, cols].reshape(mbs * length, width)
             att_p[j, :, : 3 * pw] = bf(mm(rj, dqkv[...].reshape(mbs * length, 3 * pw), ((0,), (0,))))
             att_p[j, :, 3 * pw :] = bf(mm(mj, att[...].reshape(mbs * length, pw), ((0,), (0,))))
-        give(1)
-
-    def small_grads():
+        give(l, 1)
+
+    def small_grads(l):
         small_p[:experts] = rw_p[...]
         small_p[experts:] = gains[...]
-        give(2)
+        give(l, 2)
 
     lag = (sk + ak) * (ny - 1)
-    apart = STAGE_STEPS
-    starts = (0, half)
+    gap = max(lag + 6 - half, 0)
+    starts = (0, half, 2 * half + gap, 3 * half + gap)
 
     def unit(t, dd):
-        u = jnp.clip(t, 0, mbs * half - 1)
-        return (t >= 0) & (t < mbs * half), u // half, lax.rem(u, half) + dd * half
-
-    def dh_copy(dd, m, e):
+        soon = (t >= 0) & (t < 2 * half)
+        then = (t >= starts[2]) & (t < starts[2] + 2 * half)
+        u = jnp.clip(jnp.where(t < starts[2], jnp.minimum(t, 2 * half - 1), t - gap), 0, 4 * half - 1)
+        job = u // half
+        return soon | then, 1 - job // 2, lax.rem(job, 2), lax.rem(u, half) + dd * half
+
+    def dh_copy(dd, l, m, e):
         to = b - 1 if dd == 0 else b + 1
-        return remote(dh.at[m, e], dh.at[m, e], rs_send.at[m, e], rs_recv.at[m, e], (s, a, to))
-
-    def dgu_copy(dd, m, e):
+        return remote(dh.at[m, e], dh.at[m, e], rs_send.at[l, m, e], rs_recv.at[l, m, e], (s, a, to))
+
+    def dgu_copy(dd, l, m, e):
         to = b + 1 if dd == 0 else b - 1
-        return remote(dgu.at[m, e], dgu.at[m, e], ag_send.at[m, e], ag_recv.at[m, e], (s, a, to))
-
-    def wi_copy(e):
-        return remote(win.at[e], win.at[e], wi_send.at[e], wi_recv.at[e], (layer, a, b))
-
-    def wd_copy(e):
-        return remote(wdt.at[e], wdt.at[e], wd_send.at[e], wd_recv.at[e], (layer, a, b))
-
-    def st_copies(e, slot):
-        return (pltpu.make_async_copy(sti.at[slot], win_g.at[e], st_sem.at[0, slot]),
-                pltpu.make_async_copy(std.at[slot], wdt_g.at[e], st_sem.at[1, slot]))
-
-    def weight_grads(e):
-        gi = mm(slots[:, e, :, :width].reshape(mbs * cap, width), dgu[:, e].reshape(mbs * cap, 2 * f), ((0,), (0,)))
-        gd = mm(gslots[:, e, :, :width].reshape(mbs * cap, width), hid[:, e].reshape(mbs * cap, f), ((0,), (0,)))
+        return remote(dgu.at[m, e], dgu.at[m, e], ag_send.at[l, m, e], ag_recv.at[l, m, e], (s, a, to))
+
+    def wi_copy(l, e):
+        return remote(win.at[e], win.at[e], wi_send.at[l, e], wi_recv.at[l, e], (l, a, b))
+
+    def wd_copy(l, e):
+        return remote(wdt.at[e], wdt.at[e], wd_send.at[l, e], wd_recv.at[l, e], (l, a, b))
+
+    def st_copies(e):
+        return (pltpu.make_async_copy(sti, win_g.at[e], st_sem.at[0]), pltpu.make_async_copy(std, wdt_g.at[e], st_sem.at[1]))
+
+    def weight_grads(l, e):
+        gi = mm(slots[l, :, e, :, :width].reshape(mbs * cap, width), dgu[:, e].reshape(mbs * cap, 2 * f), ((0,), (0,)))
+        gd = mm(gslots[l, :, e, :, :width].reshape(mbs * cap, width), hid[:, e].reshape(mbs * cap, f), ((0,), (0,)))
         return gi, gd
 
     late = 2
-    steps = starts[1] + half + lag + late
+    steps = starts[3] + half + lag + late
 
     def chain(i):
         reduce = [unit(i - sk * up[dd], dd) for dd in range(2)]
         spreads = [unit(i - sk * (ny - 1) - ak * down[dd], dd) for dd in range(2)]
         for dd in range(2):
-            valid, m, e = reduce[dd]
+            valid, l, m, e = reduce[dd]
 
             @pl.when(valid)
             def _():
-                acc[dd] = mm(gslots[m, e, :, :width], wdt[e])
+                @pl.when(m == 0)
+                def _():
+                    weight_copy(0, e, 1)[0].wait()
+
+                acc[dd] = mm(gslots[l, m, e, :, :width], wdt[e])
 
             @pl.when(valid & first[dd])
             def _():
                 dh[m, e] = bf(acc[dd])
-                dh_copy(dd, m, e).start()
+                dh_copy(dd, l, m, e).start()
 
             @pl.when(valid & jnp.logical_not(first[dd] | last[dd]))
             def _():
-                dh_copy(dd, m, e).wait_recv()
+                dh_copy(dd, l, m, e).wait_recv()
                 dh[m, e] = bf(acc[dd] + dh[m, e].astype(jnp.float32))
-                dh_copy(dd, m, e).start()
+                dh_copy(dd, l, m, e).start()
 
             @pl.when(valid & last[dd])
             def _():
-                dh_copy(dd, m, e).wait_recv()
+                dh_copy(dd, l, m, e).wait_recv()
                 total = acc[dd] + dh[m, e].astype(jnp.float32)
-                r = router_column(slots[m, e], e, width, experts)
+                r = router_column(slots[l, m, e], e, width, experts)
                 gate = gown[m, e - dd * half, :, :f].astype(jnp.float32)
                 upv = gown[m, e - dd * half, :, f:].astype(jnp.float32)
                 dgate, dup, dr = act_back(gate, upv, total, jax.nn.sigmoid(r))
                 dgu[m, e, :, :f] = bf(dgate)
                 dgu[m, e, :, f:] = bf(dup)
-                dgu_copy(dd, m, e).start()
+                dgu_copy(dd, l, m, e).start()
                 hi = bf(dr).astype(jnp.float32)
                 deo[m, e] = bf(jnp.where(lane == width + e, hi, jnp.where(lane == width + experts + e, dr - hi, 0.0)))
 
         for dd in range(2):
-            valid, m, e = spreads[dd]
+            valid, l, m, e = spreads[dd]
 
             @pl.when(valid & jnp.logical_not(last[dd]))
             def _():
-                dgu_copy(dd, m, e).wait_recv()
+                dgu_copy(dd, l, m, e).wait_recv()
 
                 @pl.when(jnp.logical_not(first[dd]))
                 def _():
-                    dgu_copy(dd, m, e).start()
+                    dgu_copy(dd, l, m, e).start()
 
             @pl.when(valid)
             def _():
+                @pl.when(m == 0)
+                def _():
+                    weight_copy(0, e, 0)[0].wait()
+
                 deo[m, e, :, :width] = bf(mm(dgu[m, e], win[e], ((1,), (1,))))
 
-        u = i - half - lag
-
-        @pl.when((u >= 0) & (u < half) & keeper)
+        for l in (1, 0):
+            u = i - starts[3 - 2 * l] - lag
+            weight_stage(l, u)
+
+    def chain_sent(l, e, dd):
+        for m in range(mbs):
+            pl.when(jnp.logical_not(last[dd]))(dh_copy(dd, l, m, e).wait_send)
+            pl.when(jnp.logical_not(first[dd]))(dgu_copy(dd, l, m, e).wait_send)
+
+    def weight_stage(l, u):
+        @pl.when((u >= 0) & (u < half))
         def _():
-            pl.semaphore_signal(free, inc=1, device_id=(1 - s, a, b), device_id_type=MESH)
-
-        @pl.when((u >= 0) & (u < half) & helper)
+            for dd in range(2):
+                chain_sent(l, jnp.clip(u, 0, half - 1) + dd * half, dd)
+
+        @pl.when((u >= 0) & (u < half) & (s == l))
         def _():
-            pl.semaphore_wait(free, 1)
+            pl.semaphore_signal(free.at[l], inc=1, device_id=(1 - s, a, b), device_id_type=MESH)
+
+        @pl.when((u >= 0) & (u < half) & (s != l))
+        def _():
+            pl.semaphore_wait(free.at[l], 1)
             for dd in range(2):
                 e = jnp.clip(u, 0, half - 1) + dd * half
-                gi, gd = weight_grads(e)
+                gi, gd = weight_grads(l, e)
                 win[e] = bf(gi)
-                wi_copy(e).start()
+                wi_copy(l, e).start()
                 wdt[e] = bf(gd)
-                wd_copy(e).start()
+                wd_copy(l, e).start()
 
         w = u - late
 
-        @pl.when((w >= 0) & (w < half) & keeper)
+        @pl.when((w >= 0) & (w < half) & (s != l))
         def _():
             for dd in range(2):
                 e = jnp.clip(w, 0, half - 1) + dd * half
-
-                @pl.when(w >= 1)
+                wi_copy(l, e).wait_send()
+                wd_copy(l, e).wait_send()
+                if l:
+                    start_weights(0, e)
+
+        @pl.when((w >= 0) & (w < half) & (s == l))
+        def _():
+            for dd in range(2):
+                e = jnp.clip(w, 0, half - 1) + dd * half
+
+                gi, gd = weight_grads(l, e)
+                wi_copy(l, e).wait_recv()
+                gi = gi + win[e].astype(jnp.float32)
+                wd_copy(l, e).wait_recv()
+                gd = gd + wdt[e].astype(jnp.float32)
+
+                @pl.when((w >= 1) | (dd == 1))
                 def _():
-                    for copy in st_copies(e - 1, dd):
+                    for copy in st_copies(e):
                         copy.wait()
 
-                gi, gd = weight_grads(e)
-                wi_copy(e).wait_recv()
-                sti[dd] = gi + win[e].astype(jnp.float32)
-                wd_copy(e).wait_recv()
-                std[dd] = gd + wdt[e].astype(jnp.float32)
-                for copy in st_copies(e, dd):
+                sti[...] = gi
+                std[...] = gd
+                for copy in st_copies(e):
                     copy.start()
+                if l:
+                    start_weights(0, e)
 
     stages = {}
 
     def at(step, do, *args):
         stages.setdefault(step, []).append(lambda: do(*args))
 
+    def shared_first(l, m):
+        if m == 0:
+            for copy in early_loads(l):
+                copy.wait()
+        shared_act(m)
+
+    def reload(copies):
+        for copy in copies:
+            copy.start()
+
+    def ready(copies):
+        for copy in copies:
+            copy.wait()
+
     spread(0)
     spread(1)
-    dispatch(0)
-    for j, (dst, own) in enumerate(((win, win_a), (wdt, wdt_a))):
-        pltpu.make_async_copy(own, dst, w_sem.at[j]).wait()
-    for copy in loads:
-        copy.wait()
-    for dd in range(2):
-        pl.when(last[dd])(own_gates(dd).wait)
-    at(1, dispatch, 1)
-    at(2, shared_act, 0)
-    at(3, shared_act, 1)
-    at(4, shared_grads)
-    at(5, down_grads)
-    at(6, shared_back, 0)
-    at(7, join, 0)
-    at(8, shared_back, 1)
-    for m in range(2):
-        done = starts[m] + half - 1 + lag
-        for c, do in enumerate((combine, combine_line, second_norm, attention, first_norm)):
-            at(done + c * apart, do, m)
+    dispatch(1, 0)
+    ready([slots_load, hid_load(1)] + later_loads(1))
+    for m in range(mbs):
+        wait_gates(1, m)
+    at(1, dispatch, 1, 1)
+    for l in (1, 0):
+        begin = starts[2 - 2 * l]
+        second = starts[3 - 2 * l]
+        at(begin + 2, shared_first, l, 0)
+        at(begin + 4, shared_back, 0)
+        at(second + (-5 if l else 1), shared_first, l, 1)
+        at(second + (-3 if l else 2), shared_back, 1)
+        at(second + (-2 if l else 3), shared_grads)
+        at(second + (-1 if l else 4), down_grads, l)
+        at(second + (1 if l else 6), join, l, 0)
+        for m in range(2):
+            done = starts[2 - 2 * l + m] + half - 1 + lag
+            for c, (do, *args) in enumerate((
+                    (combine, l, m), (combine_line, m), (second_norm, l, m), (attention, m), (first_norm, l, m))):
+                at(done + c, do, *args)
+            if l:
+                at(starts[m] + half + sk * (ny - 1), start_gates, 0, m)
+                at(done + 5, spread, m)
+                at(done + 6, dispatch, 0, m)
+                at(starts[2 + m] - 1, wait_gates, 0, m)
+        end = second + half - 1 + lag
+        at(end + 3, attention_grads, l)
+        at(end + 4, join, l, 1)
+        at(end + 4, small_grads, l)
+        at(end + 5, join, l, 2)
+        at(end + (2 if l else 4), settle, l, 0)
+        at(end + (9 if l else 5), settle, l, 1)
+        at(end + (9 if l else 5), settle, l, 2)
+        at(end + (9 if l else 5), given, l)
     end = starts[1] + half - 1 + lag
-    at(end - 1, settle, 0)
-    at(end + 3 * apart, attention_grads)
-    at(end + 4 * apart, join, 1)
-    at(end + 4 * apart, small_grads)
-    at(end + 5 * apart, join, 2)
-    at(end + 5 * apart, settle, 1)
-    at(end + 5 * apart, settle, 2)
+    at(starts[1] + 1, lambda: reload(early_loads(0)))
+    at(end + late + 1, lambda: reload([hid_load(0)]))
+    at(end + late + 4, lambda: ready([hid_load(0)]))
+    at(end + 5, lambda: reload(later_loads(0)))
+    at(end + 8, lambda: ready(later_loads(0)))
+    at(end + 10, new_layer, 0)
 
     def step(i, c):
         chain(i)
@@ -1766,13 +1870,7 @@
     def copy_a(ai, slot):
         return remote(small_f, small_a.at[slot], a_send.at[ai], a_recv.at[slot], (s, ai, b))
 
-    @pl.when(helper)
-    def _():
-        for i in range(3):
-            cross(i).wait_send()
-
-    @pl.when(keeper)
-    def _():
+    def gain_sums():
         pos.peers(lambda ai: copy_a(ai, a).start())
         small_a[a] = small_f[...]
         pos.peers(lambda ai: copy_a(ai, ai).wait())
@@ -1780,102 +1878,80 @@
         for ai in range(1, nx):
             total = total + small_a[ai]
         small_f[...] = total
-        pltpu.make_async_copy(small_f, small_g, f_sem.at[2]).start()
-        for i in range(3):
-            pltpu.make_async_copy(finals[i], results[i], f_sem.at[i]).wait()
-        for dd in range(2):
-            for copy in st_copies((dd + 1) * half - 1, dd):
-                copy.wait()
-
-    def finish(index, c):
-        m = index // half
-        for dd in range(2):
-            e = lax.rem(index, half) + dd * half
-
-            @pl.when(jnp.logical_not(last[dd]))
-            def _():
-                dh_copy(dd, m, e).wait_send()
-
-            @pl.when(jnp.logical_not(first[dd]))
-            def _():
-                dgu_copy(dd, m, e).wait_send()
-
-            @pl.when(helper & (m == 0))
-            def _():
-                wi_copy(e).wait_send()
-                wd_copy(e).wait_send()
-
-        return c
-
-    lax.fori_loop(0, mbs * half, finish, 0)
-
-
-def backward(layer, g, fwd, watt, cos, sin, rot, win, wdt, grads, dims, heads, features, ids):
+
+    gain_sums()
+    pltpu.make_async_copy(small_f, small_g, f_sem.at[2]).start()
+    gx_o[...] = gx[...]
+    for i in range(3):
+        pltpu.make_async_copy(finals[i], results[i], f_sem.at[i]).wait()
+    for copy in st_copies(experts - 1):
+        copy.wait()
+
+
+def backward(fwd, cos, sin, rot, win, wdt, dims, heads, features, ids):
     width, pw, experts, cap = dims
     nx, ny = lax.axis_size("gx"), lax.axis_size("gy")
-    mbs, sub, d = g.shape[-3:]
+    mbs, sub, d = fwd["tok"].shape[-3:]
     f = wdt[0].shape[-1]
     length, tokens, slots = nx * sub, nx * ny * sub, experts * cap
     b16, f32 = jnp.bfloat16, jnp.float32
     vm = pl.BlockSpec(memory_space=pltpu.VMEM)
     hbm = pl.BlockSpec(memory_space=pl.ANY)
-    ac, sc, n, half = watt.shape[2], fwd["shw"].shape[3], fwd["small"].shape[1], experts // 2
+    ac, sc, n, half = fwd["watt0"].shape[2], fwd["shw"].shape[3], fwd["small"].shape[1], experts // 2
     rows_shape = (mbs, nx, sub, d)
     dense = lambda c: ((ny, width, c), b16)
     scratch = (
         ((experts, width, 2 * f), b16), ((experts, width, f), b16),
         ((mbs, ny, sub, pw), b16), ((mbs, ny, sub, pw), b16), ((mbs, ny, nx, sub, pw), b16), (rows_shape, b16),
-        ((slots, tokens), b16), ((tokens, slots), b16),
-        ((mbs, experts, cap, pw), b16), ((mbs, experts, cap, pw), b16), ((mbs, half, cap, 2 * f), b16),
+        ((slots, tokens), b16), ((tokens // 2, slots), b16),
+        ((2, mbs, experts, cap, pw), b16), ((2, mbs, experts, cap, pw), b16), ((mbs, half, cap, 2 * f), b16),
         ((mbs, experts, cap, f), b16), ((2, cap, f), f32), ((mbs, experts, cap, f), b16),
         ((mbs, experts, cap, 2 * f), b16), ((mbs, experts, cap, pw), b16),
-        ((2, width, 2 * f), f32), ((2, width, f), f32),
+        ((width, 2 * f), f32), ((width, f), f32),
         ((mbs, length, 2 * f), b16), (rows_shape, b16), (rows_shape, b16),
         ((mbs, nx, ny, sub, pw), b16), ((mbs, nx, ny, sub, pw), b16), ((mbs, ny, sub, pw), b16), ((mbs, ny, sub, pw), b16),
         ((pw, d), b16), ((mbs, sub, d), f32), ((mbs, sub, d), b16), (rows_shape, b16),
         ((length, pw), b16), ((mbs, length, 3 * pw), b16), (rows_shape, b16), (rows_shape, b16),
         ((experts, d), f32), ((8, d), f32),
         dense(sc), dense(ac), ((n, d), f32), dense(sc), dense(ac), ((n, d), f32),
-        dense(sc), dense(ac), ((ny, n, pw), f32),
+        ((ny - 1, width, sc), b16), ((ny - 1, width, ac), b16), ((ny - 1, n, pw), f32),
         ((width, sc), f32), ((width, ac), f32), ((n, pw), f32), ((nx, n, pw), f32),
+        ((mbs, sub, d), b16), ((2, mbs, sub, d), b16),
+        *((fwd[name].shape, fwd[name].dtype) for name in ("small", "place")),
+        ((mbs, sub, d), b16),
+        *((fwd[name].shape[1:], fwd[name].dtype) for name in (
+            "mid", "n2", "rows", "q", "k", "v", "att", "rows2", "sgu", "shid", "shw")),
+        (fwd["watt0"].shape, b16),
     )
     by_m = lambda c: flags((mbs, c))
-
-    names = ("mid", "n2", "rows", "q", "k", "v", "att", "rows2", "sgu", "shid", "shw")
-    by_layer = [g, fwd["small"], fwd["place"], fwd["place_t"], fwd["tok"] if layer == 0 else fwd["y"]]
-    by_layer += [fwd[name] for name in names]
-    order = [4, 0, 1, *range(5, 16), 2, 3]
-    resident = tuple((by_layer[c].shape[1:], by_layer[c].dtype) for c in order)
+    by_lm = lambda c: flags((2, mbs, c))
+    names = ("tok", "small", "place", "y", "mid", "n2", "rows", "q", "k", "v", "att", "rows2", "sgu", "shid",
+             "shw", "watt0", "watt1")
     outs = pl.pallas_call(
         functools.partial(
-            backward_kernel,
-            (layer, nx, ny, mbs, sub, width, pw, heads, features, experts, cap, f, *BWD_SKEW)),
+            backward_kernel, (nx, ny, mbs, sub, width, pw, heads, features, experts, cap, f, *BWD_SKEW)),
         out_shape=(
-            jax.ShapeDtypeStruct((mbs, sub, d), b16),
+            jax.ShapeDtypeStruct((2, mbs, sub, d), b16),
             jax.ShapeDtypeStruct((experts, width, 2 * f), f32),
             jax.ShapeDtypeStruct((experts, width, f), f32),
             jax.ShapeDtypeStruct((width, ac), f32),
             jax.ShapeDtypeStruct((width, sc), f32),
             jax.ShapeDtypeStruct((n, pw), f32),
         ),
-        in_specs=[hbm] * 16 + [vm] * 4 + [hbm] * (7 + len(grads)),
+        in_specs=[hbm] * 17 + [vm] * 3 + [hbm] * 7,
         out_specs=(vm,) + (hbm,) * 5,
-        scratch_shapes=[pltpu.VMEM(*v) for v in scratch + resident] + [
-            flags((2,)), by_m(ny), by_m(ny), by_m(nx), by_m(nx), by_m(nx), by_m(nx), by_m(nx), by_m(nx),
+        scratch_shapes=[pltpu.VMEM(*v) for v in scratch] + [
+            flags((2, experts)), by_m(ny), by_m(ny), by_m(nx), by_m(nx), by_m(nx), by_m(nx), by_m(nx), by_m(nx),
             by_m(nx), by_m(nx), by_m(ny), by_m(ny), by_m(nx), by_m(nx), by_m(nx), by_m(nx),
-            by_m(experts), by_m(experts), by_m(experts), by_m(experts),
-            flags((experts,)), flags((experts,)), flags((experts,)), flags((experts,)),
+            by_lm(experts), by_lm(experts), by_lm(experts), by_lm(experts),
+            flags((2, experts)), flags((2, experts)), flags((2, experts)), flags((2, experts)),
             flags((3,)), flags((3,)), flags((3, ny)), flags((3, ny)), flags((nx,)), flags((nx,)),
-            flags((3,)), flags((2, 2)), flags((3,)), flags((16,)), pltpu.SemaphoreType.REGULAR,
+            flags((4,)), flags((2,)), flags((3,)), flags((20,)), pltpu.SemaphoreType.REGULAR((2,)),
         ],
-        input_output_aliases={27 + i: 1 + i for i in range(len(grads))},
         compiler_params=params(ids),
-        cost_estimate=pl.CostEstimate(flops=10**10, bytes_accessed=6 * 10**7, transcendentals=10**6),
+        cost_estimate=pl.CostEstimate(flops=2 * 10**10, bytes_accessed=10**8, transcendentals=10**6),
         name="backward",
-    )(
-        *by_layer, watt, cos, sin, rot,
-        *(fwd[name] for name in ("slots", "gu", "hid")), *win, *wdt, *grads,
-    )
+    )(*(fwd[name] for name in names), cos, sin, rot, *(fwd[name] for name in ("slots", "gu", "hid")), *win, *wdt)
     return outs[0], outs[1:]
 
 
@@ -1921,13 +1997,10 @@
     rot = pad_to(pad_to(rot_columns(jnp.eye(heads * DH, dtype=jnp.float32)), 0, pw), 1, pw).astype(jnp.bfloat16)
 
     fwd = forward(tin, small, att_block, sh_block, pairs, cos, sin, rot, win, wdt, dims, heads, features, 0)
-    outs, watt = fwd["y"], (fwd["watt0"], fwd["watt1"])
-    g, gouts, grads = fwd["tok"], [None, None], ()
-    for l in (1, 0):
-        gouts[l], grads = backward(l, g, fwd, watt[l], cos, sin, rot, win, wdt, grads, dims, heads, features, 1 + l)
-        g = gouts[l][None]
-
-    both = leave(jnp.stack([outs[0], gouts[0]]), jnp.stack([outs[1], gouts[1]]), pw, 3)[..., :width]
+    outs = fwd["y"]
+    gouts, grads = backward(fwd, cos, sin, rot, win, wdt, dims, heads, features, 1)
+
+    both = leave(jnp.stack([outs[0], gouts[0]]), jnp.stack([outs[1], gouts[1]]), pw, 2)[..., :width]
     win_g, wdt_g, att_g, sh_g, small_g = grads
     hd = heads * DH
     return (

time: 829 us -> 775 us (0.935)
  Pallas kernels: 750 us -> 697 us
    pallas_call x2 -> x1, Pallas kernels: 410 us -> 358 us  [backward(): pl.pallas_call(functools.partial(backward_kernel, (nx, ny, mbs, sub, widt...]
  transfers between devices with their start and end apart: 2 -> 2, of which waited for: 0 -> 1; matrix products, arithmetic and copies ran while one was open for 2% -> 1% of each run, Pallas kernels for 0% -> 0%
where the time goes in v5:
time: 775 us; the launch traced here: 764 us
  Pallas kernels  697 us (90%)
  local copies, waits for them, and re-layouts  55.1 us (7%)
    pallas_call x1, Pallas kernels, backward(): pl.pallas_call(functools.partial(backward_kernel, (nx, ny, mbs, sub, widt...  358 us
    pallas_call x1, Pallas kernels, forward(): pl.pallas_call(functools.partial(forward_kernel, (nx, ny, mbs, sub, width...  325 us
    another operation x1, local copies, waits for them, and re-layouts, fast_device(): win_g.reshape(experts, width, 2, f)[None]  16.9 us
  transfers between devices with their start and end apart: 2, of which 1 were waited for; matrix products, arithmetic and copies ran while one was open for 1% of the time, Pallas kernels for 0%

profile of v5, /device:TPU:0, one launch (start us, length us, event | category | flops | bytes accessed | tf_op | source)
XLA Modules:
  0.0 764.4 jit_solution(9700321785691081702)
XLA Ops:
  0.6 0.0 copy-start.6
  0.7 11.0 %reshape_squeeze.7.refs_8_.refs_23_ = bf16[16,192,1024]{2,1,0:T(8,128)(2,1)} reshape(bf16[1,16,192,2,512]{4,3,2,1,0:T(2,128)(2,1)} %param.19) | data formatting | bytes 12582912 | tf_op jit(solution)/shard_map/reshape;squeeze | solution.py:1986
  11.7 0.5 collective-permute-start
  12.3 0.1 collective-permute-start.1
  12.3 0.1 pad.54.clone
  12.4 0.1 maximum_maximum_fusion
  12.5 0.6 pad.34.refs_1_
  13.1 0.1 fusion.5
  13.3 0.1 copy.36
  13.4 0.7 pad.38.refs_6_.refs_18_
  14.1 0.1 copy.35
  14.2 0.7 pad.37.refs_5_.refs_17_
  14.9 0.0 copy-done.5
  14.9 0.1 copy.34
  15.0 0.1 fusion.3
  15.1 0.1 copy.37
  15.2 0.1 copy.31
  15.4 0.1 copy.32
  15.6 0.7 pad.58.refs_7_.refs_19_
  16.3 0.7 pad.33.refs_0_
  17.0 0.3 copy.42
  17.3 0.2 pad.35.clone
  17.6 0.8 fusion.1.refs_2_
  18.4 0.9 pad_maximum_fusion.refs_3_
  19.2 7.6 collective-permute-done.1.refs_11_.refs_26_
  26.9 0.0 collective-permute-done.refs_9_.refs_24_
  26.9 325.1 %forward.1 = (bf16[2,2,32,1024]{3,2,1,0:T(8,128)(2,1)}, f32[2,24,1024]{2,1,0:T(8,128)}, s32[2,2,2,512]{3,2,1,0:T(2,128)}, s32[2,2,512,2]{3,2,1,0:T(8,128)}, bf16...) custom-call(bf16[2,2,128,256]{3,2,1,0:T(8,128)(2,1)} %pad.33.refs_0_, ...), custom_call_target="tpu_custom_call" | custom-call | flops 10000000000 | bytes 80000000 | tf_op jit(solution)/shard_map/forward/pallas_call | solution.py:1295
  352.0 1.0 fusion.8
  353.0 357.9 %backward.1 = (bf16[2,2,32,1024]{3,2,1,0:T(8,128)(2,1)}, f32[16,192,1024]{2,1,0:T(8,128)}, f32[16,192,512]{2,1,0:T(8,128)}, f32[192,1024]{1,0:T(8,128)}, f32[192,1536]{1,0:T(8,128)}, /*index=5*/f32[24,256]{1,0:T(8,128)}) custom-call(bf16[2,2,32,1024]{3,2,1,0:T(8,128)(2,1)} %get-tuple-element.38.refs_0_, f32[2,24,1024]{2,1,0:T(8,128)} %get-tuple-element.39.refs_1_, ...), custom_call_target="tpu_custom_call" | custom-call | flops 20000000000 | bytes 100000000 | tf_op jit(solution)/shard_map/backward/pallas_call | solution.py:1930
  710.9 1.3 fusion.10
  712.2 1.3 slice_bitcast_fusion.3
  713.6 0.9 slice_bitcast_fusion.2
  714.5 1.1 slice.61
  715.6 1.8 slice_bitcast_fusion.1
  717.4 1.2 slice.66
  718.6 1.0 fusion.9
  719.6 0.8 pad_maximum_fusion.1
  720.4 13.8 %leave.1 = bf16[2,4,128,256]{3,2,1,0:T(8,128)(2,1)} custom-call(bf16[2,2,32,1024]{3,2,1,0:T(8,128)(2,1)} %get-tuple-element.95.pair0, bf16[2,2,32,1024]{3,2,1,0:T(8,128)(2,1)} %get-tuple-element.96.pair1), custom_call_target="tpu_custom_call" | custom-call | tf_op jit(solution)/shard_map/leave/pallas_call | solution.py:763
  734.3 1.1 fusion.7
  735.3 0.8 copy.39
  736.2 0.8 copy.38
  737.0 0.8 copy.41
  737.8 0.3 reshape.82
  738.1 0.1 slice_bitcast_fusion
  738.2 0.9 copy.40
  739.2 1.5 broadcast_in_dim_reshape.7
  740.7 16.9 %broadcast_in_dim_reshape.6 = f32[1,16,192,2,512]{4,3,2,1,0:T(2,128)} reshape(f32[16,192,1024]{2,1,0:T(8,128)} %get-tuple-element.60) | data formatting | bytes 25165824 | tf_op jit(solution)/shard_map/broadcast_in_dim;reshape | solution.py:2014
  757.6 6.5 copy.46
  (28 shorter events, 0.2 us)
Async XLA Ops:
  0.6 11.8 %copy-start.6 = (bf16[1,192,16]{1,2,0:T(8,128)(2,1)S(1)}, bf16[1,192,16]{1,2,0:T(8,128)(2,1)}, u32[]{:S(2)}) copy-start(bf16[1,192,16]{1,2,0:T(8,128)(2,1)} %param.18) | copy-start | bytes 18436
  0.7 11.8 %copy-start.8 = (f32[1,192]{1,0:T(1,128)S(1)}, f32[1,192]{1,0:T(1,128)}, u32[]{:S(2)}) copy-start(f32[1,192]{1,0:T(1,128)} %param.17) | copy-start | bytes 2308
  0.7 11.8 %copy-start.7 = (f32[1,192]{1,0:T(1,128)S(1)}, f32[1,192]{1,0:T(1,128)}, u32[]{:S(2)}) copy-start(f32[1,192]{1,0:T(1,128)} %param.14) | copy-start | bytes 2308
  0.7 14.2 %copy-start.5 = (bf16[1,192,192]{2,1,0:T(8,128)(2,1)S(1)}, bf16[1,192,192]{2,1,0:T(8,128)(2,1)}, u32[]{:S(2)}) copy-start(bf16[1,192,192]{2,1,0:T(8,128)(2,1)} %param.16) | copy-start | bytes 221188
  0.7 14.6 %copy-start.2 = (bf16[4,128,192]{1,2,0:T(8,128)(2,1)S(1)}, bf16[4,128,192]{1,2,0:T(8,128)(2,1)}, u32[]{:S(2)}) copy-start(bf16[4,128,192]{1,2,0:T(8,128)(2,1)} %param.12) | copy-start | bytes 589828
  0.7 14.7 %copy-start.3 = (bf16[4,128,192]{1,2,0:T(8,128)(2,1)S(1)}, bf16[4,128,192]{1,2,0:T(8,128)(2,1)}, u32[]{:S(2)}) copy-start(bf16[4,128,192]{1,2,0:T(8,128)(2,1)} %param.13) | copy-start | bytes 589828
  11.7 5.3 copy-start.1
  11.7 5.8 copy-start
  11.7 6.6 copy-start.4
  11.7 15.1 %collective-permute-start = (bf16[16,192,1024]{2,1,0:T(8,128)(2,1)}, bf16[16,192,1024]{2,1,0:T(8,128)(2,1)}, u32[]{:S(2)}, u32[]{:S(2)}) collective-permute-start(bf16[16,192,1024]{2,1,0:T(8,128)(2,1)} %reshape_squeeze.7.refs_8_.refs_23_), channel_id=1, source_target_pairs={{0,16},{16,0},{1,17},{17,1},{2,18},{18,2},{3,19},{19,3},{4,20},{20... | collective-permute-start | bytes 18874376 | tf_op jit(solution)/shard_map/ppermute | solution.py:18
  12.3 14.6 %collective-permute-start.1 = (bf16[16,192,512]{2,1,0:T(8,128)(2,1)}, bf16[16,192,512]{2,1,0:T(8,128)(2,1)}, u32[]{:S(2)}, u32[]{:S(2)}) collective-permute-start(bf16[16,192,512]{2,1,0:T(8,128)(2,1)} %bitcast.58), channel_id=1, source_target_pairs={{0,16},{16,0},{1,17},{17,1},{2,18},{18,2},{3,19},{19,3},{4,20},{20... | collective-permute-start | bytes 9437192 | tf_op jit(solution)/shard_map/ppermute | solution.py:18

commit v6 on v5

--- a/solution.py
+++ b/solution.py
@@ -2,6 +2,7 @@
 
 import jax
 import jax.numpy as jnp
+import numpy as np
 from jax import lax
 from jax.experimental import pallas as pl
 from jax.experimental.pallas import tpu as pltpu
@@ -705,75 +706,6 @@
     return pltpu.CompilerParams(collective_id=ids, has_side_effects=True, vmem_limit_bytes=VMEM_BYTES)
 
 
-def greet_all(pos):
-    barrier = pltpu.get_barrier_semaphore()
-    total = 2 * pos.n
-    mine = pos.s * pos.n + pos.me
-
-    def one(i, c):
-        index = lax.rem(mine + i, total)
-        rest = lax.rem(index, pos.n)
-        pl.semaphore_signal(
-            barrier, inc=1, device_id=(index // pos.n, rest // pos.ny, lax.rem(rest, pos.ny)), device_id_type=MESH)
-        return c
-
-    lax.fori_loop(1, total, one, 0)
-    pl.semaphore_wait(barrier, total - 1)
-
-
-def leave_kernel(cfg, pair0, pair1, out, buf, t_send, t_recv):
-    nx, ny, mbs, sub, pw = cfg
-    pos = Position(nx, ny)
-    s, a, b = pos.s, pos.a, pos.b
-    greet_all(pos)
-    pairs = (pair0, pair1)
-
-    def copy(l, j, s_slot, a_slot, seq):
-        src = pairs[l].at[:, :, :, pl.ds(pl.multiple_of(j * pw, pw), pw)]
-        return remote(src, buf.at[s_slot, a_slot], t_send.at[l, j], t_recv.at[s_slot, a_slot], (l, seq, j))
-
-    for l in range(2):
-        for j in range(ny):
-            @pl.when((l != s) | (a != b) | (j != b))
-            def _():
-                copy(l, j, s, a, b).start()
-
-        @pl.when((l == s) & (a == b))
-        def _():
-            buf[s, a] = pairs[l][:, :, :, pl.ds(pl.multiple_of(b * pw, pw), pw)]
-
-    for so in range(2):
-        for i in range(nx):
-            @pl.when((so != s) | (a != b) | (i != a))
-            def _():
-                copy(0, 0, so, i, i).wait_recv()
-
-            out[:, so * mbs : (so + 1) * mbs, i * sub : (i + 1) * sub, :] = buf[so, i]
-    for l in range(2):
-        for j in range(ny):
-            @pl.when((l != s) | (a != b) | (j != b))
-            def _():
-                copy(l, j, s, a, b).wait_send()
-
-
-def leave(pair0, pair1, pw, ids):
-    nx, ny = lax.axis_size("gx"), lax.axis_size("gy")
-    kinds, mbs, sub, d = pair0.shape
-    vm = pl.BlockSpec(memory_space=pltpu.VMEM)
-    return pl.pallas_call(
-        functools.partial(leave_kernel, (nx, ny, mbs, sub, pw)),
-        out_shape=jax.ShapeDtypeStruct((kinds, 2 * mbs, nx * sub, pw), jnp.bfloat16),
-        in_specs=[vm] * 2,
-        out_specs=vm,
-        scratch_shapes=[
-            pltpu.VMEM((2, nx, kinds, mbs, sub, pw), jnp.bfloat16),
-            flags((2, ny)), flags((2, nx)),
-        ],
-        compiler_params=params(ids),
-        name="leave",
-    )(pair0, pair1)
-
-
 def turn(t, cos, sin, rot, sign):
     hi = bf(t)
     lo = bf(t - hi.astype(jnp.float32))
@@ -790,20 +722,20 @@
 
 def forward_kernel(cfg, *refs):
     nx, ny, mbs, sub, width, pw, heads, features, experts, cap, f, sk, ak = cfg
-    (tin, small_b, att_b, sh_b, routes, cos, sin, rot, win_a, win_b, wdt_a, wdt_b,
-     tok_o, small_o, place_o, place_to, watt0_o, y_o, mid_o, n2_o, rows_o, q_o, k_o, v_o, att_o, slots_o, gu_o, hid_o, rows2_o, sgu_o, shid_o, shw_o, watt_o,
+    (tin, small_b, att_b, sh_b, routes, cos, sin, rot, win_a, wdt_a,
+     win_b, wdt_b, tok_o, small_o, place_o, place_to, watt0_o, y_o, mid_o, n2_o, rows_o, q_o, k_o, v_o, att_o, slots_o, gu_o, hid_o, rows2_o, sgu_o, shid_o, shw_o, watt_o,
      y, mid, n2, rx, nsend, nall, proj, q, k, v, att, osend, orecv, rwx,
      xsend, xline, xall, nrows, pm, pt, slots, acc, gu, hid, eo, sgu, shid, ssend, srecv, rsend, rpeer, rline, rrecv,
      win, wdt, shw0, shw1, watt0, watt1, tbuf, tok, rts, place, place_t, sm0, sm1, small,
      n_send, n_recv, o_send, o_recv, x_send, x_recv, u_send, u_recv, t_send, t_recv, s_send, s_recv, g_send, g_recv, r_send, r_recv,
-     rs_send, rs_recv, ag_send, ag_recv, wi_sem, wd_sem, g_sem, k_sem, i_send, i_recv, q_send, q_recv, *w_sems) = refs
+     rs_send, rs_recv, ag_send, ag_recv, wi_sem, wd_sem, g_sem, k_sem, i_send, i_recv, q_send, q_recv, v_send, v_recv, *w_sems) = refs
     pos = Position(nx, ny)
     s, a, b, me = pos.s, pos.a, pos.b, pos.me
     slots_n = experts * cap
     tokens = nx * ny * sub
     d = ny * pw
     length = nx * sub
-    half = experts // 2
+    half, hw = experts // 2, f // 2
     lane = lax.broadcasted_iota(jnp.int32, (1, pw), 1)
     shares = (
         Share(pos, 0, sh_b, shw0, w_sems[0:4]),
@@ -849,7 +781,14 @@
         start_weight(0, e, 1)
         return c
 
-    lax.fori_loop(0, experts, first_weights, 0)
+    def swap(c):
+        src, dst = ((win_a, win_b), (wdt_a, wdt_b))[c]
+        return remote(src, dst, v_send.at[c], v_recv.at[c], (1 - s, a, b))
+
+    def weights_ready():
+        for c in range(2):
+            swap(c).wait()
+        lax.fori_loop(0, experts, first_weights, 0)
 
     @pl.when(a == b)
     def _():
@@ -878,6 +817,8 @@
     routes_copy(1 - s, s).start()
     for share in entry_shares:
         share.start()
+    for c in range(2):
+        swap(c).start()
     rts[s] = routes[pl.ds(s * mbs, mbs)]
 
     @pl.when(a == b)
@@ -1052,89 +993,96 @@
     down = (b, ny - 1 - b)
     lag = (sk + ak) * (ny - 1)
     apart = STAGE_STEPS
-    gap = max(half - 1 + lag + 6 * apart + 1 - 2 * half, 0)
-    starts = (0, half, 2 * half + gap, 3 * half + gap)
-    steps = starts[3] + half + lag
+    units = 2 * half
+    gap = max(lag + 6 * apart - units, 0)
+    starts = (0, units, 2 * units + gap, 3 * units + gap)
+    steps = starts[3] + units + lag
 
     def unit(t, dd):
-        early = (t >= 0) & (t < 2 * half)
-        late = (t >= starts[2]) & (t < starts[2] + 2 * half)
-        u = jnp.clip(jnp.where(t < starts[2], jnp.minimum(t, 2 * half - 1), t - gap), 0, 4 * half - 1)
-        job = u // half
-        return early | late, job // 2, lax.rem(job, 2), lax.rem(u, half) + dd * half
-
-    def gu_copy(dd, l, m, e):
+        early = (t >= 0) & (t < 2 * units)
+        late = (t >= starts[2]) & (t < starts[2] + 2 * units)
+        u = jnp.clip(jnp.where(t < starts[2], jnp.minimum(t, 2 * units - 1), t - gap), 0, 4 * units - 1)
+        job, r = u // units, lax.rem(u, units)
+        return early | late, job // 2, lax.rem(job, 2), r // 2 + dd * half, lax.rem(r, 2)
+
+    def gu_copy(dd, l, m, e, c):
         to = b - 1 if dd == 0 else b + 1
-        return remote(gu.at[l, m, e], gu.at[l, m, e], rs_send.at[l, m, e], rs_recv.at[l, m, e], (s, a, to))
-
-    def hid_copy(dd, l, m, e):
+        return remote(gu.at[l, m, e, c], gu.at[l, m, e, c], rs_send.at[l, m, e, c], rs_recv.at[l, m, e, c], (s, a, to))
+
+    def hid_copy(dd, l, m, e, c):
         to = b + 1 if dd == 0 else b - 1
-        return remote(hid.at[l, m, e], hid.at[l, m, e], ag_send.at[l, m, e], ag_recv.at[l, m, e], (s, a, to))
+        return remote(hid.at[l, m, e, c], hid.at[l, m, e, c], ag_send.at[l, m, e, c], ag_recv.at[l, m, e, c], (s, a, to))
+
+    def save_gates(l, m, e, c):
+        return pltpu.make_async_copy(gu.at[l, m, e, c], gu_o.at[l, m, e, c], g_sem.at[l, m, e, c])
 
     def chain(i):
         reduce = [unit(i - sk * up[dd], dd) for dd in range(2)]
         spreads = [unit(i - sk * (ny - 1) - ak * down[dd], dd) for dd in range(2)]
         for dd in range(2):
-            valid, l, m, e = reduce[dd]
+            valid, l, m, e, c = reduce[dd]
 
             @pl.when(valid)
             def _():
-                @pl.when(m == 0)
+                @pl.when((m == 0) & (c == 0))
                 def _():
                     wait_weight(0, e, 0)
 
-                acc[dd] = mm(slots[l, m, e, :, :width], win[e])
-
-                @pl.when((l == 0) & (m == 1))
+                for plane in range(2):
+                    part = win[e, plane, :, pl.ds(pl.multiple_of(c * hw, hw), hw)]
+                    acc[dd, :, plane * hw : (plane + 1) * hw] = mm(slots[l, m, e, :, :width], part)
+
+                @pl.when((l == 0) & (m == 1) & (c == 1))
                 def _():
                     start_weight(1, e, 0)
 
         for dd in range(2):
-            valid, l, m, e = reduce[dd]
+            valid, l, m, e, c = reduce[dd]
 
             @pl.when(valid & first[dd])
             def _():
-                gu[l, m, e] = bf(acc[dd])
-                gu_copy(dd, l, m, e).start()
+                gu[l, m, e, c] = bf(acc[dd])
+                gu_copy(dd, l, m, e, c).start()
 
             @pl.when(valid & jnp.logical_not(first[dd] | last[dd]))
             def _():
-                gu_copy(dd, l, m, e).wait_recv()
-                gu[l, m, e] = bf(acc[dd] + gu[l, m, e].astype(jnp.float32))
-                gu_copy(dd, l, m, e).start()
+                gu_copy(dd, l, m, e, c).wait_recv()
+                gu[l, m, e, c] = bf(acc[dd] + gu[l, m, e, c].astype(jnp.float32))
+                gu_copy(dd, l, m, e, c).start()
 
             @pl.when(valid & last[dd])
             def _():
-                gu_copy(dd, l, m, e).wait_recv()
-                total = acc[dd] + gu[l, m, e].astype(jnp.float32)
+                gu_copy(dd, l, m, e, c).wait_recv()
+                total = acc[dd] + gu[l, m, e, c].astype(jnp.float32)
                 r = router_column(slots[l, m, e], e, width, experts)
-                gate = total[:, :f]
-                hid[l, m, e] = bf(gate * jax.nn.sigmoid(gate) * total[:, f:] * jax.nn.sigmoid(r))
-                hid_copy(dd, l, m, e).start()
-                gu[l, m, e] = bf(total)
-                pltpu.make_async_copy(gu.at[l, m, e], gu_o.at[l, m, e], g_sem.at[l, m, e]).start()
+                gate = total[:, :hw]
+                hid[l, m, e, c] = bf(gate * jax.nn.sigmoid(gate) * total[:, hw:] * jax.nn.sigmoid(r))
+                hid_copy(dd, l, m, e, c).start()
+                gu[l, m, e, c] = bf(total)
+                save_gates(l, m, e, c).start()
 
         for dd in range(2):
-            valid, l, m, e = spreads[dd]
+            valid, l, m, e, c = spreads[dd]
 
             @pl.when(valid & jnp.logical_not(last[dd]))
             def _():
-                hid_copy(dd, l, m, e).wait_recv()
+                hid_copy(dd, l, m, e, c).wait_recv()
 
                 @pl.when(jnp.logical_not(first[dd]))
                 def _():
-                    hid_copy(dd, l, m, e).start()
+                    hid_copy(dd, l, m, e, c).start()
 
         for dd in range(2):
-            valid, l, m, e = spreads[dd]
-
-            @pl.when(valid)
+            valid, l, m, e, c = spreads[dd]
+
+            @pl.when(valid & (c == 1))
             def _():
                 @pl.when(m == 0)
                 def _():
                     wait_weight(0, e, 1)
 
-                eo[m, e] = bf(mm(hid[l, m, e], wdt[e], ((1,), (1,))))
+                total = mm(hid[l, m, e, 0], wdt[e, :, :hw], ((1,), (1,)))
+                eo[m, e] = bf(total + mm(hid[l, m, e, 1], wdt[e, :, hw:], ((1,), (1,))))
 
                 @pl.when((l == 0) & (m == 1))
                 def _():
@@ -1156,8 +1104,10 @@
     ssend[...] = jnp.zeros_like(ssend)
     rwx[...] = jnp.zeros_like(rwx)
     for h in range(1, ny):
-        for share in entry_shares:
+        for share in entry_shares[:2]:
             share.hop(h)
+        if h == 2:
+            entry_shares[2].hop(1)
     for share in entry_shares[:2]:
         share.finish()
     tokens_ready()
@@ -1169,41 +1119,46 @@
         rwx[l, width + experts : width + 2 * experts] = bf(small[l, :experts])
     norm_first(0, 0)
     norm_first(0, 1)
+    entry_shares[2].hop(2)
     places()
+    entry_shares[2].hop(3)
     entry_shares[2].finish()
     shares[0].start()
     shares[1].start()
     attention(0, 0)
+    attention(0, 1)
     norm_second(0, 0)
-    attention(0, 1)
+    norm_second(0, 1)
+    weights_ready()
     spread(0, 0)
-    norm_second(0, 1)
+    shares[0].hop(1)
+    shares[1].hop(1)
+    spread(0, 1)
     dispatch(0, 0)
-    for h in range(1, ny):
-        at(h - 1, lambda h=h: (shares[0].hop(h), shares[1].hop(h)))
-    at(1, stage(spread, 0, 1))
-    at(3, stage(dispatch, 0, 1))
-    at(4, lambda: (shares[0].finish(), shares[1].finish()))
-    at(5, stage(shared_in_part, 0, 0))
-    at(6, stage(shared_out_part, 0, 0))
-    at(half, stage(shared_in_part, 0, 1))
-    at(half + 1, stage(shared_out_part, 0, 1))
+    for h in range(2, ny):
+        at(2 * (h - 2), lambda h=h: (shares[0].hop(h), shares[1].hop(h)))
+    at(units // 4, stage(dispatch, 0, 1))
+    at(2 * (ny - 2) + 1, lambda: (shares[0].finish(), shares[1].finish()))
+    at(units // 2, stage(shared_in_part, 0, 0))
+    at(units // 2 + 2, stage(shared_out_part, 0, 0))
+    at(units, stage(shared_in_part, 0, 1))
+    at(units + 2, stage(shared_out_part, 0, 1))
     for m in range(2):
-        done = starts[m] + half - 1 + lag
+        done = starts[m] + units - 1 + lag
         for c, do in enumerate((combine, combine_line)):
             at(done + c * apart, stage(do, 0, m))
         at(done + 2 * apart, stage(layer_out, 0, m))
         for c, do in enumerate((norm_first, attention, norm_second, spread, dispatch)):
             at(done + (2 + c) * apart, stage(do, 1, m))
-        at(starts[2 + m] + 2, stage(shared_in_part, 1, m))
-        at(starts[2 + m] + 4, stage(shared_out_part, 1, m))
-        done = starts[2 + m] + half - 1 + lag
+        at(starts[2 + m] + 4, stage(shared_in_part, 1, m))
+        at(starts[2 + m] + 8, stage(shared_out_part, 1, m))
+        done = starts[2 + m] + units - 1 + lag
         for c, do in enumerate((combine, combine_line, layer_out)):
             at(done + c * apart, stage(do, 1, m))
-    at(half + lag, shares[2].start)
+    at(units + lag - 1, shares[2].start)
     for h in range(1, ny):
-        at(half + lag + h, lambda h=h: shares[2].hop(h))
-    at(half + lag + ny, shares[2].finish)
+        at(units + lag - 1 + 2 * h, lambda h=h: shares[2].hop(h))
+    at(units + lag - 1 + 2 * ny, shares[2].finish)
 
     def step(i, c):
         chain(i)
@@ -1227,27 +1182,18 @@
     for copy in saves:
         copy.start()
 
-    def finish(index, c):
-        l = index // (mbs * half)
-        m = lax.rem(index // half, mbs)
+    def finish(index, carry):
+        l = index // (mbs * units)
+        m = lax.rem(index // units, mbs)
+        r = lax.rem(index, units)
         for dd in range(2):
-            e = lax.rem(index, half) + dd * half
-
-            @pl.when(jnp.logical_not(last[dd]))
-            def _():
-                gu_copy(dd, l, m, e).wait_send()
-
-            @pl.when(jnp.logical_not(first[dd]))
-            def _():
-                hid_copy(dd, l, m, e).wait_send()
-
-            @pl.when(last[dd])
-            def _():
-                pltpu.make_async_copy(gu.at[l, m, e], gu_o.at[l, m, e], g_sem.at[l, m, e]).wait()
-
-        return c
-
-    lax.fori_loop(0, 2 * mbs * half, finish, 0)
+            e, c = r // 2 + dd * half, lax.rem(r, 2)
+            pl.when(jnp.logical_not(last[dd]))(gu_copy(dd, l, m, e, c).wait_send)
+            pl.when(jnp.logical_not(first[dd]))(hid_copy(dd, l, m, e, c).wait_send)
+            pl.when(last[dd])(save_gates(l, m, e, c).wait)
+        return carry
+
+    lax.fori_loop(0, 2 * mbs * units, finish, 0)
     for copy in saves:
         copy.wait()
 
@@ -1257,7 +1203,7 @@
     nx, ny = lax.axis_size("gx"), lax.axis_size("gy")
     mbs, length = tin.shape[1:3]
     sub, d = length // nx, ny * pw
-    f = wdt[0].shape[-1]
+    f = wdt.shape[-1]
     length, tokens, n, slots = nx * sub, nx * ny * sub, nx * ny, experts * cap
     b16, f32 = jnp.bfloat16, jnp.float32
     vm = pl.BlockSpec(memory_space=pltpu.VMEM)
@@ -1266,13 +1212,14 @@
     rows_shape = lm + (nx, sub, d)
     spread_shape = lm + (ny, nx, sub, pw)
     entry = (
+        (win.shape, b16), (wdt.shape, b16),
         ((2, mbs, sub, d), b16), ((2, small_b.shape[0], d), f32), (lm + (2, tokens), jnp.int32),
         (lm + (tokens, 2), jnp.int32), ((ny,) + att_block.shape, b16),
     )
     kept = entry + (
         (lm + (sub, d), b16), (lm + (sub, d), f32), (lm + (sub, d), b16), (rows_shape, b16),
         (lm + (length, pw), b16), (lm + (length, pw), b16), (lm + (length, pw), b16), (lm + (length, pw), b16),
-        (lm + (experts, cap, pw), b16), (lm + (experts, cap, 2 * f), b16), (lm + (experts, cap, f), b16),
+        (lm + (experts, cap, pw), b16), (lm + (experts, 2, cap, f), b16), (lm + (experts, 2, cap, f // 2), b16),
         (rows_shape, b16), (lm + (length, 2 * f), b16), (lm + (length, f), b16),
         ((2, ny) + sh_block.shape, b16), ((ny,) + att_block.shape, b16),
     )
@@ -1282,11 +1229,11 @@
         (lm + (length, pw), b16), (lm + (length, pw), b16), (lm + (length, pw), b16), (lm + (length, pw), b16),
         (rows_shape, b16), (rows_shape, b16), ((2, pw, d), b16),
         (lm + (ny, sub, pw), b16), (lm + (ny, sub, pw), b16), (spread_shape, b16), (rows_shape, b16),
-        ((slots, tokens), b16), ((tokens, slots), b16), (lm + (experts, cap, pw), b16), ((2, cap, 2 * f), f32),
-        (lm + (experts, cap, 2 * f), b16), (lm + (experts, cap, f), b16), ((mbs, experts, cap, width), b16),
+        ((slots, tokens), b16), ((tokens, slots), b16), (lm + (experts, cap, pw), b16), ((2, cap, f), f32),
+        (lm + (experts, 2, cap, f), b16), (lm + (experts, 2, cap, f // 2), b16), ((mbs, experts, cap, width), b16),
         (lm + (length, 2 * f), b16), (lm + (length, f), b16), (rows_shape, b16), (rows_shape, b16),
         (lm + (nx, ny, sub, pw), b16), (lm + (nx, ny, sub, pw), b16), (lm + (ny, sub, pw), b16), (lm + (ny, sub, pw), b16),
-        ((experts, width, 2 * f), b16), ((experts, width, f), b16),
+        (win.shape, b16), (wdt.shape, b16),
         ((ny,) + sh_block.shape, b16), ((ny,) + sh_block.shape, b16), ((ny,) + att_block.shape, b16), ((ny,) + att_block.shape, b16),
         ((ny, 2, mbs, sub, pw), b16), ((2, mbs, sub, d), b16), (lm + (2, tokens), jnp.int32),
         (lm + (2, tokens), jnp.int32), (lm + (tokens, 2), jnp.int32),
@@ -1295,47 +1242,47 @@
     outs = pl.pallas_call(
         functools.partial(forward_kernel, (nx, ny, mbs, sub, width, pw, heads, features, experts, cap, f, *FWD_SKEW)),
         out_shape=tuple(jax.ShapeDtypeStruct(*v) for v in kept),
-        in_specs=[vm] * 8 + [hbm] * 4,
+        in_specs=[vm] * 8 + [hbm] * 2,
         out_specs=(hbm,) * len(kept),
         scratch_shapes=[pltpu.VMEM(*(v or ((8, 128), f32))) for v in scratch] + [
             flags(lm + (nx,)), flags(lm + (nx,)), flags(lm + (nx,)), flags(lm + (nx,)),
             flags(lm + (ny,)), flags(lm + (ny,)), flags(lm + (nx,)), flags(lm + (nx,)), flags(lm + (nx,)), flags(lm + (nx,)),
             flags(lm + (nx,)), flags(lm + (nx,)), flags(lm + (nx,)), flags(lm + (nx,)), flags(lm + (ny,)), flags(lm + (ny,)),
-            flags(lm + (experts,)), flags(lm + (experts,)), flags(lm + (experts,)), flags(lm + (experts,)),
-            flags((experts,)), flags((experts,)), flags(lm + (experts,)), flags((24,)),
-            flags((nx,)), flags((ny,)), pltpu.SemaphoreType.DMA, pltpu.SemaphoreType.DMA,
+            flags(lm + (experts, 2)), flags(lm + (experts, 2)), flags(lm + (experts, 2)), flags(lm + (experts, 2)),
+            flags((experts,)), flags((experts,)), flags(lm + (experts, 2)), flags((24,)),
+            flags((nx,)), flags((ny,)), pltpu.SemaphoreType.DMA, pltpu.SemaphoreType.DMA, flags((2,)), flags((2,)),
         ] + share_sems(ny) * 6,
         compiler_params=params(ids),
         cost_estimate=pl.CostEstimate(flops=10**10, bytes_accessed=8 * 10**7, transcendentals=10**6),
         name="forward",
-    )(tin, small_b, att_block, sh_block, routes, cos, sin, rot, *win, *wdt)
-    names = ("tok", "small", "place", "place_t", "watt0", "y", "mid", "n2", "rows", "q", "k", "v", "att", "slots", "gu", "hid", "rows2", "sgu", "shid", "shw", "watt1")
+    )(tin, small_b, att_block, sh_block, routes, cos, sin, rot, win, wdt)
+    names = ("win", "wdt", "tok", "small", "place", "place_t", "watt0", "y", "mid", "n2", "rows", "q", "k", "v", "att", "slots", "gu", "hid", "rows2", "sgu", "shid", "shw", "watt1")
     return dict(zip(names, outs))
 
 
-FWD_SKEW = (1, 1)
-STAGE_STEPS = 1
+FWD_SKEW = (2, 2)
+STAGE_STEPS = 2
 
 
 def backward_kernel(cfg, *refs):
     nx, ny, mbs, sub, width, pw, heads, features, experts, cap, f, sk, ak = cfg
     (tok_i, small_i, place_i, y_i, mid_i, n2_i, rows_i, q_i, k_i, v_i, att_i, rows2_i, sgu_i, shid_i, shw_i,
      watt0_i, watt1_i, cos, sin, rot, slots_i, gu_i, hid_i, win_a, win_b, wdt_a, wdt_b) = refs[:27]
-    (gx_o, win_g, wdt_g, att_g, sh_g, small_g,
+    (out_o, win_g, wdt_g, att_g, sh_g, small_g,
      win, wdt, xsend, xline, xall, grows, pm, pt, slots, gslots, gown, hid, acc, dh, dgu, deo, sti, std,
      dsgu, ssend, srecv, rsend, rpeer, rline, rrecv, rwx, dm, msend, mall, datt, dqkv, dsend, drecv,
-     rw_p, gains, sh_p, att_p, small_p, sh_x, att_x, small_x, sh_r, att_r, small_r, sh_f, att_f, small_f, small_a,
-     g, gx, small, place, x, mid, n2, rows, q, k, v, att, rows2, sgu, shid, shw, watt,
+     rw_p, gains, drs, sh_p, att_p, small_p, sh_x, att_x, small_x, sh_r, att_r, small_r, sh_f, att_f, small_f, small_a,
+     yv, obuf, g, gx, small, place, x, mid, n2, rows, q, k, v, att, rows2, sgu, shid, shw, watt,
      w_sem, x_send, x_recv, u_send, u_recv, t_send, t_recv, s_send, s_recv, g_send, g_recv, r_send, r_recv,
      m_send, m_recv, d_send, d_recv, rs_send, rs_recv, ag_send, ag_recv, wi_send, wi_recv, wd_send, wd_recv,
-     c_send, c_recv, e_send, e_recv, a_send, a_recv, l_sem, st_sem, f_sem, y_sem, free) = refs[27:]
+     c_send, c_recv, e_send, e_recv, a_send, a_recv, l_sem, st_sem, f_sem, y_sem, o_send, o_recv, free) = refs[27:]
     pos = Position(nx, ny)
     s, a, b = pos.s, pos.a, pos.b
     slots_n = experts * cap
     tokens = nx * ny * sub
     d = ny * pw
     length = nx * sub
-    half = experts // 2
+    half, hw = experts // 2, f // 2
     scale = DH ** -0.5
     lane = lax.broadcasted_iota(jnp.int32, (1, pw), 1)
     first = (b == ny - 1, b == 0)
@@ -1346,6 +1293,11 @@
     pos.peers(lambda ai: pl.semaphore_signal(barrier, inc=1, device_id=(s, ai, b), device_id_type=MESH))
     pos.line(lambda bi: pl.semaphore_signal(barrier, inc=1, device_id=(s, a, bi), device_id_type=MESH))
     pl.semaphore_signal(barrier, inc=1, device_id=(1 - s, a, b), device_id_type=MESH)
+    for so in range(2):
+        for i in range(nx):
+            @pl.when((so != s) | (i != a) | (a != b))
+            def _():
+                pl.semaphore_signal(barrier, inc=1, device_id=(so, i, a), device_id_type=MESH)
 
     def weight_copy(l, e, which):
         own, oth, dst = ((win_a, win_b, win), (wdt_a, wdt_b, wdt))[which]
@@ -1391,7 +1343,7 @@
 
     first_loads = [
         pltpu.make_async_copy(src, dst, y_sem.at[13 + c])
-        for c, (src, dst) in enumerate(((tok_i.at[1], g), (small_i, small), (place_i, place)))
+        for c, (src, dst) in enumerate(((tok_i.at[1], g), (small_i, small), (place_i, place), (y_i, yv)))
     ]
     slots_load = pltpu.make_async_copy(slots_i, slots, l_sem.at[0])
     for copy in first_loads + [slots_load, hid_load(1)] + early_loads(1) + later_loads(1):
@@ -1410,7 +1362,43 @@
 
     for copy in first_loads:
         copy.wait()
-    pl.semaphore_wait(barrier, nx - 1 + ny - 1 + 1)
+
+    @pl.when(a == b)
+    def _():
+        pl.semaphore_wait(barrier, nx - 1 + ny - 1 + 1 + 2 * ny - 1)
+
+    @pl.when(a != b)
+    def _():
+        pl.semaphore_wait(barrier, nx - 1 + ny - 1 + 1 + 2 * ny)
+
+    def out_copy(kind, l, j, s_slot, a_slot):
+        src = (yv, gx)[kind].at[l, :, :, pl.ds(j * pw, pw)]
+        return remote(src, obuf.at[kind, s_slot, a_slot], o_send.at[kind, l, j], o_recv.at[kind, s_slot, a_slot], (l, b, j))
+
+    def send_out(kind, l):
+        for j in range(ny):
+            @pl.when((l != s) | (a != b) | (j != b))
+            def _():
+                out_copy(kind, l, j, s, a).start()
+
+        @pl.when((l == s) & (a == b))
+        def _():
+            obuf[kind, s, a] = (yv, gx)[kind][l, :, :, pl.ds(pl.multiple_of(b * pw, pw), pw)]
+
+    def sent_out(kind, l):
+        for j in range(ny):
+            @pl.when((l != s) | (a != b) | (j != b))
+            def _():
+                out_copy(kind, l, j, s, a).wait_send()
+
+    def take_out(kind):
+        for so in range(2):
+            for i in range(nx):
+                @pl.when((so != s) | (a != b) | (i != a))
+                def _():
+                    out_copy(kind, 0, 0, so, i).wait_recv()
+
+                out_o[kind, so * mbs : (so + 1) * mbs, i * sub : (i + 1) * sub, :] = obuf[kind, so, i]
 
     def send_g(m):
         for j in range(ny):
@@ -1630,23 +1618,25 @@
         give(l, 2)
 
     lag = (sk + ak) * (ny - 1)
-    gap = max(lag + 6 - half, 0)
-    starts = (0, half, 2 * half + gap, 3 * half + gap)
+    apart = STAGE_STEPS
+    units = 2 * half
+    gap = max(lag + 6 * apart - units, 0)
+    starts = (0, units, 2 * units + gap, 3 * units + gap)
 
     def unit(t, dd):
-        soon = (t >= 0) & (t < 2 * half)
-        then = (t >= starts[2]) & (t < starts[2] + 2 * half)
-        u = jnp.clip(jnp.where(t < starts[2], jnp.minimum(t, 2 * half - 1), t - gap), 0, 4 * half - 1)
-        job = u // half
-        return soon | then, 1 - job // 2, lax.rem(job, 2), lax.rem(u, half) + dd * half
-
-    def dh_copy(dd, l, m, e):
+        soon = (t >= 0) & (t < 2 * units)
+        then = (t >= starts[2]) & (t < starts[2] + 2 * units)
+        u = jnp.clip(jnp.where(t < starts[2], jnp.minimum(t, 2 * units - 1), t - gap), 0, 4 * units - 1)
+        job, r = u // units, lax.rem(u, units)
+        return soon | then, 1 - job // 2, lax.rem(job, 2), r // 2 + dd * half, lax.rem(r, 2)
+
+    def dh_copy(dd, l, m, e, c):
         to = b - 1 if dd == 0 else b + 1
-        return remote(dh.at[m, e], dh.at[m, e], rs_send.at[l, m, e], rs_recv.at[l, m, e], (s, a, to))
-
-    def dgu_copy(dd, l, m, e):
+        return remote(dh.at[m, e, c], dh.at[m, e, c], rs_send.at[l, m, e, c], rs_recv.at[l, m, e, c], (s, a, to))
+
+    def dgu_copy(dd, l, m, e, c):
         to = b + 1 if dd == 0 else b - 1
-        return remote(dgu.at[m, e], dgu.at[m, e], ag_send.at[l, m, e], ag_recv.at[l, m, e], (s, a, to))
+        return remote(dgu.at[m, e, c], dgu.at[m, e, c], ag_send.at[l, m, e, c], ag_recv.at[l, m, e, c], (s, a, to))
 
     def wi_copy(l, e):
         return remote(win.at[e], win.at[e], wi_send.at[l, e], wi_recv.at[l, e], (l, a, b))
@@ -1658,104 +1648,125 @@
         return (pltpu.make_async_copy(sti, win_g.at[e], st_sem.at[0]), pltpu.make_async_copy(std, wdt_g.at[e], st_sem.at[1]))
 
     def weight_grads(l, e):
-        gi = mm(slots[l, :, e, :, :width].reshape(mbs * cap, width), dgu[:, e].reshape(mbs * cap, 2 * f), ((0,), (0,)))
-        gd = mm(gslots[l, :, e, :, :width].reshape(mbs * cap, width), hid[:, e].reshape(mbs * cap, f), ((0,), (0,)))
+        sl = slots[l, :, e, :, :width].reshape(mbs * cap, width)
+        gs = gslots[l, :, e, :, :width].reshape(mbs * cap, width)
+        gi = [mm(sl, dgu[:, e, c].reshape(mbs * cap, f), ((0,), (0,))) for c in range(2)]
+        gd = [mm(gs, hid[:, e, c].reshape(mbs * cap, hw), ((0,), (0,))) for c in range(2)]
         return gi, gd
 
     late = 2
-    steps = starts[3] + half + lag + late
+    steps = starts[3] + units + lag + 2 * late
 
     def chain(i):
         reduce = [unit(i - sk * up[dd], dd) for dd in range(2)]
         spreads = [unit(i - sk * (ny - 1) - ak * down[dd], dd) for dd in range(2)]
         for dd in range(2):
-            valid, l, m, e = reduce[dd]
+            valid, l, m, e, c = reduce[dd]
 
             @pl.when(valid)
             def _():
-                @pl.when(m == 0)
+                @pl.when((m == 0) & (c == 0))
                 def _():
                     weight_copy(0, e, 1)[0].wait()
 
-                acc[dd] = mm(gslots[l, m, e, :, :width], wdt[e])
+                acc[dd] = mm(gslots[l, m, e, :, :width], wdt[e, :, pl.ds(pl.multiple_of(c * hw, hw), hw)])
 
             @pl.when(valid & first[dd])
             def _():
-                dh[m, e] = bf(acc[dd])
-                dh_copy(dd, l, m, e).start()
+                dh[m, e, c] = bf(acc[dd])
+                dh_copy(dd, l, m, e, c).start()
 
             @pl.when(valid & jnp.logical_not(first[dd] | last[dd]))
             def _():
-                dh_copy(dd, l, m, e).wait_recv()
-                dh[m, e] = bf(acc[dd] + dh[m, e].astype(jnp.float32))
-                dh_copy(dd, l, m, e).start()
+                dh_copy(dd, l, m, e, c).wait_recv()
+                dh[m, e, c] = bf(acc[dd] + dh[m, e, c].astype(jnp.float32))
+                dh_copy(dd, l, m, e, c).start()
 
             @pl.when(valid & last[dd])
             def _():
-                dh_copy(dd, l, m, e).wait_recv()
-                total = acc[dd] + dh[m, e].astype(jnp.float32)
+                dh_copy(dd, l, m, e, c).wait_recv()
+                total = acc[dd] + dh[m, e, c].astype(jnp.float32)
                 r = router_column(slots[l, m, e], e, width, experts)
-                gate = gown[m, e - dd * half, :, :f].astype(jnp.float32)
-                upv = gown[m, e - dd * half, :, f:].astype(jnp.float32)
+                gate = gown[m, e - dd * half, c, :, :hw].astype(jnp.float32)
+                upv = gown[m, e - dd * half, c, :, hw:].astype(jnp.float32)
                 dgate, dup, dr = act_back(gate, upv, total, jax.nn.sigmoid(r))
-                dgu[m, e, :, :f] = bf(dgate)
-                dgu[m, e, :, f:] = bf(dup)
-                dgu_copy(dd, l, m, e).start()
+                dgu[m, e, c, :, :hw] = bf(dgate)
+                dgu[m, e, c, :, hw:] = bf(dup)
+                dgu_copy(dd, l, m, e, c).start()
+                dr = jnp.where(c == 0, 0.0, drs[dd][:, 0:1]) + dr
+                drs[dd] = jnp.broadcast_to(dr, (cap, 128))
                 hi = bf(dr).astype(jnp.float32)
                 deo[m, e] = bf(jnp.where(lane == width + e, hi, jnp.where(lane == width + experts + e, dr - hi, 0.0)))
 
         for dd in range(2):
-            valid, l, m, e = spreads[dd]
+            valid, l, m, e, c = spreads[dd]
 
             @pl.when(valid & jnp.logical_not(last[dd]))
             def _():
-                dgu_copy(dd, l, m, e).wait_recv()
+                dgu_copy(dd, l, m, e, c).wait_recv()
 
                 @pl.when(jnp.logical_not(first[dd]))
                 def _():
-                    dgu_copy(dd, l, m, e).start()
-
-            @pl.when(valid)
+                    dgu_copy(dd, l, m, e, c).start()
+
+        for dd in range(2):
+            valid, l, m, e, c = spreads[dd]
+
+            @pl.when(valid & (c == 1))
             def _():
                 @pl.when(m == 0)
                 def _():
                     weight_copy(0, e, 0)[0].wait()
 
-                deo[m, e, :, :width] = bf(mm(dgu[m, e], win[e], ((1,), (1,))))
+                total = None
+                for c2 in range(2):
+                    for plane in range(2):
+                        cols, hcols = slice(plane * hw, (plane + 1) * hw), slice(c2 * hw, (c2 + 1) * hw)
+                        part = mm(dgu[m, e, c2, :, cols], win[e, plane, :, hcols], ((1,), (1,)))
+                        total = part if total is None else total + part
+                deo[m, e, :, :width] = bf(total)
 
         for l in (1, 0):
-            u = i - starts[3 - 2 * l] - lag
-            weight_stage(l, u)
+            t = i - starts[3 - 2 * l] - lag
+            weight_stage(l, t)
 
     def chain_sent(l, e, dd):
         for m in range(mbs):
-            pl.when(jnp.logical_not(last[dd]))(dh_copy(dd, l, m, e).wait_send)
-            pl.when(jnp.logical_not(first[dd]))(dgu_copy(dd, l, m, e).wait_send)
-
-    def weight_stage(l, u):
-        @pl.when((u >= 0) & (u < half))
+            for c in range(2):
+                pl.when(jnp.logical_not(last[dd]))(dh_copy(dd, l, m, e, c).wait_send)
+                pl.when(jnp.logical_not(first[dd]))(dgu_copy(dd, l, m, e, c).wait_send)
+
+    def weight_stage(l, t):
+        u = t // 2
+        on = (t >= 0) & (t < units) & (lax.rem(t + 2, 2) == 1)
+
+        @pl.when(on)
         def _():
             for dd in range(2):
                 chain_sent(l, jnp.clip(u, 0, half - 1) + dd * half, dd)
 
-        @pl.when((u >= 0) & (u < half) & (s == l))
+        @pl.when(on & (s == l))
         def _():
             pl.semaphore_signal(free.at[l], inc=1, device_id=(1 - s, a, b), device_id_type=MESH)
 
-        @pl.when((u >= 0) & (u < half) & (s != l))
+        @pl.when(on & (s != l))
         def _():
             pl.semaphore_wait(free.at[l], 1)
             for dd in range(2):
                 e = jnp.clip(u, 0, half - 1) + dd * half
                 gi, gd = weight_grads(l, e)
-                win[e] = bf(gi)
+                for c in range(2):
+                    for plane in range(2):
+                        win[e, plane, :, c * hw : (c + 1) * hw] = bf(gi[c][:, plane * hw : (plane + 1) * hw])
+                    wdt[e, :, c * hw : (c + 1) * hw] = bf(gd[c])
                 wi_copy(l, e).start()
-                wdt[e] = bf(gd)
                 wd_copy(l, e).start()
 
-        w = u - late
-
-        @pl.when((w >= 0) & (w < half) & (s != l))
+        t2 = t - 2 * late
+        w = t2 // 2
+        on2 = (t2 >= 0) & (t2 < units) & (lax.rem(t2 + 8, 2) == 1)
+
+        @pl.when(on2 & (s != l))
         def _():
             for dd in range(2):
                 e = jnp.clip(w, 0, half - 1) + dd * half
@@ -1764,24 +1775,25 @@
                 if l:
                     start_weights(0, e)
 
-        @pl.when((w >= 0) & (w < half) & (s == l))
+        @pl.when(on2 & (s == l))
         def _():
             for dd in range(2):
                 e = jnp.clip(w, 0, half - 1) + dd * half
-
                 gi, gd = weight_grads(l, e)
                 wi_copy(l, e).wait_recv()
-                gi = gi + win[e].astype(jnp.float32)
                 wd_copy(l, e).wait_recv()
-                gd = gd + wdt[e].astype(jnp.float32)
 
                 @pl.when((w >= 1) | (dd == 1))
                 def _():
                     for copy in st_copies(e):
                         copy.wait()
 
-                sti[...] = gi
-                std[...] = gd
+                for c in range(2):
+                    hcols = slice(c * hw, (c + 1) * hw)
+                    for plane in range(2):
+                        part = gi[c][:, plane * hw : (plane + 1) * hw] + win[e, plane, :, hcols].astype(jnp.float32)
+                        sti[:, plane * f + c * hw : plane * f + (c + 1) * hw] = bf(part)
+                    std[:, hcols] = bf(gd[c] + wdt[e, :, hcols].astype(jnp.float32))
                 for copy in st_copies(e):
                     copy.start()
                 if l:
@@ -1816,39 +1828,44 @@
     for l in (1, 0):
         begin = starts[2 - 2 * l]
         second = starts[3 - 2 * l]
-        at(begin + 2, shared_first, l, 0)
-        at(begin + 4, shared_back, 0)
-        at(second + (-5 if l else 1), shared_first, l, 1)
-        at(second + (-3 if l else 2), shared_back, 1)
-        at(second + (-2 if l else 3), shared_grads)
-        at(second + (-1 if l else 4), down_grads, l)
-        at(second + (1 if l else 6), join, l, 0)
+        at(begin + 3, shared_first, l, 0)
+        at(begin + 5, shared_back, 0)
+        at(second + (-10 if l else 1), shared_first, l, 1)
+        at(second + (-8 if l else 3), shared_back, 1)
+        at(second + (-6 if l else 5), shared_grads)
+        at(second + (-4 if l else 6), down_grads, l)
+        at(second + (1 if l else 9), join, l, 0)
         for m in range(2):
-            done = starts[2 - 2 * l + m] + half - 1 + lag
+            done = starts[2 - 2 * l + m] + units - 1 + lag
             for c, (do, *args) in enumerate((
                     (combine, l, m), (combine_line, m), (second_norm, l, m), (attention, m), (first_norm, l, m))):
-                at(done + c, do, *args)
+                at(done + c * apart, do, *args)
             if l:
-                at(starts[m] + half + sk * (ny - 1), start_gates, 0, m)
-                at(done + 5, spread, m)
-                at(done + 6, dispatch, 0, m)
+                at(starts[m] + units + sk * (ny - 1), start_gates, 0, m)
+                at(done + 5 * apart, spread, m)
+                at(done + 6 * apart, dispatch, 0, m)
                 at(starts[2 + m] - 1, wait_gates, 0, m)
-        end = second + half - 1 + lag
-        at(end + 3, attention_grads, l)
-        at(end + 4, join, l, 1)
-        at(end + 4, small_grads, l)
-        at(end + 5, join, l, 2)
-        at(end + (2 if l else 4), settle, l, 0)
-        at(end + (9 if l else 5), settle, l, 1)
-        at(end + (9 if l else 5), settle, l, 2)
-        at(end + (9 if l else 5), given, l)
-    end = starts[1] + half - 1 + lag
+        end = second + units - 1 + lag
+        at(end + 3 * apart, attention_grads, l)
+        at(end + 4 * apart, join, l, 1)
+        at(end + 4 * apart, small_grads, l)
+        at(end + 5 * apart, join, l, 2)
+        at(end + (2 if l else 4) * apart, settle, l, 0)
+        at(end + (10 if l else 5) * apart, settle, l, 1)
+        at(end + (10 if l else 5) * apart, settle, l, 2)
+        at(end + (6 if l else 5) * apart, given, l)
+    at(units // 2 - 1, send_out, 0, 0)
+    at(units // 2 + 1, send_out, 0, 1)
+    at(2 * units, take_out, 0)
+    end = starts[1] + units - 1 + lag
+    at(end + 4 * apart + 1, send_out, 1, 1)
+    at(starts[3] + units - 1 + lag + 4 * apart, send_out, 1, 0)
     at(starts[1] + 1, lambda: reload(early_loads(0)))
-    at(end + late + 1, lambda: reload([hid_load(0)]))
-    at(end + late + 4, lambda: ready([hid_load(0)]))
-    at(end + 5, lambda: reload(later_loads(0)))
-    at(end + 8, lambda: ready(later_loads(0)))
-    at(end + 10, new_layer, 0)
+    at(end + 2 * late + 1, lambda: reload([hid_load(0)]))
+    at(end + 2 * late + 8, lambda: ready([hid_load(0)]))
+    at(end + 5 * apart, lambda: reload(later_loads(0)))
+    at(end + 10 * apart, lambda: ready(later_loads(0)))
+    at(end + 10 * apart, new_layer, 0)
 
     def step(i, c):
         chain(i)
@@ -1881,7 +1898,10 @@
 
     gain_sums()
     pltpu.make_async_copy(small_f, small_g, f_sem.at[2]).start()
-    gx_o[...] = gx[...]
+    take_out(1)
+    for l in range(2):
+        for kind in range(2):
+            sent_out(kind, l)
     for i in range(3):
         pltpu.make_async_copy(finals[i], results[i], f_sem.at[i]).wait()
     for copy in st_copies(experts - 1):
@@ -1892,7 +1912,7 @@
     width, pw, experts, cap = dims
     nx, ny = lax.axis_size("gx"), lax.axis_size("gy")
     mbs, sub, d = fwd["tok"].shape[-3:]
-    f = wdt[0].shape[-1]
+    f = wdt.shape[-1]
     length, tokens, slots = nx * sub, nx * ny * sub, experts * cap
     b16, f32 = jnp.bfloat16, jnp.float32
     vm = pl.BlockSpec(memory_space=pltpu.VMEM)
@@ -1901,21 +1921,22 @@
     rows_shape = (mbs, nx, sub, d)
     dense = lambda c: ((ny, width, c), b16)
     scratch = (
-        ((experts, width, 2 * f), b16), ((experts, width, f), b16),
+        (win.shape, b16), (wdt.shape, b16),
         ((mbs, ny, sub, pw), b16), ((mbs, ny, sub, pw), b16), ((mbs, ny, nx, sub, pw), b16), (rows_shape, b16),
         ((slots, tokens), b16), ((tokens // 2, slots), b16),
-        ((2, mbs, experts, cap, pw), b16), ((2, mbs, experts, cap, pw), b16), ((mbs, half, cap, 2 * f), b16),
-        ((mbs, experts, cap, f), b16), ((2, cap, f), f32), ((mbs, experts, cap, f), b16),
-        ((mbs, experts, cap, 2 * f), b16), ((mbs, experts, cap, pw), b16),
-        ((width, 2 * f), f32), ((width, f), f32),
+        ((2, mbs, experts, cap, pw), b16), ((2, mbs, experts, cap, pw), b16), ((mbs, half, 2, cap, f), b16),
+        ((mbs, experts, 2, cap, f // 2), b16), ((2, cap, f // 2), f32), ((mbs, experts, 2, cap, f // 2), b16),
+        ((mbs, experts, 2, cap, f), b16), ((mbs, experts, cap, pw), b16),
+        ((width, 2 * f), b16), ((width, f), b16),
         ((mbs, length, 2 * f), b16), (rows_shape, b16), (rows_shape, b16),
         ((mbs, nx, ny, sub, pw), b16), ((mbs, nx, ny, sub, pw), b16), ((mbs, ny, sub, pw), b16), ((mbs, ny, sub, pw), b16),
         ((pw, d), b16), ((mbs, sub, d), f32), ((mbs, sub, d), b16), (rows_shape, b16),
         ((length, pw), b16), ((mbs, length, 3 * pw), b16), (rows_shape, b16), (rows_shape, b16),
-        ((experts, d), f32), ((8, d), f32),
+        ((experts, d), f32), ((8, d), f32), ((2, cap, 128), f32),
         dense(sc), dense(ac), ((n, d), f32), dense(sc), dense(ac), ((n, d), f32),
         ((ny - 1, width, sc), b16), ((ny - 1, width, ac), b16), ((ny - 1, n, pw), f32),
         ((width, sc), f32), ((width, ac), f32), ((n, pw), f32), ((nx, n, pw), f32),
+        ((2, mbs, sub, d), b16), ((2, 2, nx, mbs, sub, pw), b16),
         ((mbs, sub, d), b16), ((2, mbs, sub, d), b16),
         *((fwd[name].shape, fwd[name].dtype) for name in ("small", "place")),
         ((mbs, sub, d), b16),
@@ -1924,16 +1945,16 @@
         (fwd["watt0"].shape, b16),
     )
     by_m = lambda c: flags((mbs, c))
-    by_lm = lambda c: flags((2, mbs, c))
+    by_half = flags((2, mbs, experts, 2))
     names = ("tok", "small", "place", "y", "mid", "n2", "rows", "q", "k", "v", "att", "rows2", "sgu", "shid",
              "shw", "watt0", "watt1")
     outs = pl.pallas_call(
         functools.partial(
             backward_kernel, (nx, ny, mbs, sub, width, pw, heads, features, experts, cap, f, *BWD_SKEW)),
         out_shape=(
-            jax.ShapeDtypeStruct((2, mbs, sub, d), b16),
-            jax.ShapeDtypeStruct((experts, width, 2 * f), f32),
-            jax.ShapeDtypeStruct((experts, width, f), f32),
+            jax.ShapeDtypeStruct((2, 2 * mbs, length, pw), b16),
+            jax.ShapeDtypeStruct((experts, width, 2 * f), b16),
+            jax.ShapeDtypeStruct((experts, width, f), b16),
             jax.ShapeDtypeStruct((width, ac), f32),
             jax.ShapeDtypeStruct((width, sc), f32),
             jax.ShapeDtypeStruct((n, pw), f32),
@@ -1943,19 +1964,19 @@
         scratch_shapes=[pltpu.VMEM(*v) for v in scratch] + [
             flags((2, experts)), by_m(ny), by_m(ny), by_m(nx), by_m(nx), by_m(nx), by_m(nx), by_m(nx), by_m(nx),
             by_m(nx), by_m(nx), by_m(ny), by_m(ny), by_m(nx), by_m(nx), by_m(nx), by_m(nx),
-            by_lm(experts), by_lm(experts), by_lm(experts), by_lm(experts),
+            by_half, by_half, by_half, by_half,
             flags((2, experts)), flags((2, experts)), flags((2, experts)), flags((2, experts)),
             flags((3,)), flags((3,)), flags((3, ny)), flags((3, ny)), flags((nx,)), flags((nx,)),
-            flags((4,)), flags((2,)), flags((3,)), flags((20,)), pltpu.SemaphoreType.REGULAR((2,)),
+            flags((4,)), flags((2,)), flags((3,)), flags((20,)), flags((2, 2, ny)), flags((2, 2, nx)), pltpu.SemaphoreType.REGULAR((2,)),
         ],
         compiler_params=params(ids),
         cost_estimate=pl.CostEstimate(flops=2 * 10**10, bytes_accessed=10**8, transcendentals=10**6),
         name="backward",
-    )(*(fwd[name] for name in names), cos, sin, rot, *(fwd[name] for name in ("slots", "gu", "hid")), *win, *wdt)
+    )(*(fwd[name] for name in names), cos, sin, rot, *(fwd[name] for name in ("slots", "gu", "hid")), win, fwd["win"], wdt, fwd["wdt"])
     return outs[0], outs[1:]
 
 
-BWD_SKEW = (1, 1)
+BWD_SKEW = (2, 2)
 
 
 def fast_device(block_input, output_grad, attention_gain, attention_in, attention_out, feed_gain,
@@ -1983,24 +2004,26 @@
     tin = lax.dynamic_slice_in_dim(jnp.stack([block_input, output_grad]), s * mbs, mbs, 1)
     tin = pad_to(tin, 3, pw)
     small = pad_to(small, 1, pw)
-    win = expert_in[0].reshape(experts, width, 2 * f)
-    win = (win, pass_section(win))
+    win = jnp.swapaxes(expert_in[0], 1, 2)
     wdt = expert_down[0].transpose(0, 2, 1)
-    wdt = (wdt, pass_section(wdt))
     pairs = jnp.swapaxes(routes[0], 1, 2)
     half = DH // 2
-    freq = 10000.0 ** (-jnp.arange(half, dtype=jnp.float32) / half)
-    ang = jnp.arange(length, dtype=jnp.float32)[:, None] * freq[None]
-    lanes = jnp.tile(ang, (1, 2 * heads))
-    cos = pad_to(jnp.cos(lanes), 1, pw)
-    sin = pad_to(jnp.sin(lanes), 1, pw)
-    rot = pad_to(pad_to(rot_columns(jnp.eye(heads * DH, dtype=jnp.float32)), 0, pw), 1, pw).astype(jnp.bfloat16)
+    freq = 10000.0 ** (-np.arange(half, dtype=np.float64) / half)
+    lanes = np.tile(np.arange(length)[:, None] * freq[None], (1, 2 * heads))
+    cos = np.zeros((length, pw), np.float32)
+    sin = np.zeros((length, pw), np.float32)
+    cos[:, : heads * DH] = np.cos(lanes)
+    sin[:, : heads * DH] = np.sin(lanes)
+    rot = np.zeros((pw, pw), np.float32)
+    for lead in range(0, heads * DH, DH):
+        at = lead + np.arange(half)
+        rot[at + half, at] = -1.0
+        rot[at, at + half] = 1.0
+    cos, sin, rot = jnp.asarray(cos), jnp.asarray(sin), jnp.asarray(rot, jnp.bfloat16)
 
     fwd = forward(tin, small, att_block, sh_block, pairs, cos, sin, rot, win, wdt, dims, heads, features, 0)
-    outs = fwd["y"]
-    gouts, grads = backward(fwd, cos, sin, rot, win, wdt, dims, heads, features, 1)
-
-    both = leave(jnp.stack([outs[0], gouts[0]]), jnp.stack([outs[1], gouts[1]]), pw, 2)[..., :width]
+    both, grads = backward(fwd, cos, sin, rot, win, wdt, dims, heads, features, 1)
+    both = both[..., :width]
     win_g, wdt_g, att_g, sh_g, small_g = grads
     hd = heads * DH
     return (
@@ -2011,8 +2034,8 @@
         att_g[:, 3 * pw : 3 * pw + hd].T[None],
         small_g[experts : experts + 1, :width],
         small_g[:experts, :width].T[None],
-        win_g.reshape(experts, width, 2, f)[None],
-        wdt_g.transpose(0, 2, 1)[None],
+        win_g.astype(jnp.float32).reshape(experts, width, 2, f)[None],
+        wdt_g.astype(jnp.float32).transpose(0, 2, 1)[None],
         sh_g[:, : 2 * f].reshape(width, 2, f)[None],
         sh_g[:, 2 * f :].T[None],
     )

time: 775 us -> 743 us (0.959)
  local copies, waits for them, and re-layouts: 55.1 us -> 41.4 us
  Pallas kernels: 697 us -> 684 us
    pallas_call x1 -> x0, Pallas kernels: 13.8 us -> none  [leave(): pl.pallas_call(functools.partial(leave_kernel, (nx, ny, mbs, sub, pw)), o...]
    another operation x4 -> x1, local copies, waits for them, and re-layouts: 27.9 us -> 16.4 us  [fast_device(): win_g.astype(jnp.float32).reshape(experts, width, 2, f)[None]]
  transfers between devices with their start and end apart: 2 -> 0, of which waited for: 1 -> 0; matrix products, arithmetic and copies ran while one was open for 1% -> 0% of each run, Pallas kernels for 0% -> 0%
where the time goes in v6:
time: 743 us; the launch traced here: 735 us
  Pallas kernels  684 us (92%)
  local copies, waits for them, and re-layouts  41.4 us (6%)
  other arithmetic  8.67 us (1%)
    pallas_call x1, Pallas kernels, backward(): pl.pallas_call(functools.partial(backward_kernel, (nx, ny, mbs, sub, widt...  363 us
    pallas_call x1, Pallas kernels, forward(): pl.pallas_call(functools.partial(forward_kernel, (nx, ny, mbs, sub, width...  321 us
    another operation x1, local copies, waits for them, and re-layouts, fast_device(): win_g.astype(jnp.float32).reshape(experts, width, 2, f)[None]  16.4 us

profile of v6, /device:TPU:0, one launch (start us, length us, event | category | flops | bytes accessed | tf_op | source)
XLA Modules:
  0.0 735.4 jit_solution(5861822338920450772)
XLA Ops:
  0.6 0.0 copy-start.1
  0.7 0.1 pad.27.clone
  0.7 0.0 copy-start.2
  0.7 0.7 convert_bitcast_fusion.1
  1.5 0.8 maximum_maximum_fusion
  2.3 0.6 pad.17.refs_1_
  2.9 1.0 copy.38
  3.9 1.1 copy.35
  4.9 1.1 copy.36
  6.0 0.1 fusion.2
  6.1 0.7 pad.16.refs_0_
  6.8 1.2 copy.44
  8.0 0.2 pad.18.clone
  8.3 0.8 fusion.1.refs_2_
  9.1 0.0 copy-done.1
  9.1 0.0 copy-done.2
  9.1 0.9 pad_maximum_fusion.refs_3_
  10.0 6.9 copy.48
  16.9 321.0 %forward.1 = (bf16[16,2,192,512]{3,2,1,0:T(8,128)(2,1)}, bf16[16,192,512]{2,1,0:T(8,128)(2,1)}, bf16[2,2,32,1024]{3,2,1,0:T(8,128)(2,1)}, f32[2,24,1024]{2,1,0:T...) custom-call(bf16[2,2,128,256]{3,2,1,0:T(8,128)(2,1)} %pad.16.refs_0_, ...), custom_call_target="tpu_custom_call" | custom-call | flops 10000000000 | bytes 80000000 | tf_op jit(solution)/shard_map/forward/pallas_call | solution.py:1242
  337.9 363.2 %backward.1 = (bf16[2,4,128,256]{3,2,1,0:T(8,128)(2,1)}, bf16[16,192,1024]{2,1,0:T(8,128)(2,1)}, bf16[16,192,512]{2,1,0:T(8,128)(2,1)}, f32[192,1024]{1,0:T(8,12...) custom-call(bf16[2,2,32,1024]{3,2,1,0:T(8,128)(2,1)} %get-tuple-element.39.refs_0_, ...), custom_call_target="tpu_custom_call" | custom-call | flops 20000000000 | bytes 100000000 | tf_op jit(solution)/shard_map/backward/pallas_call | solution.py:1951
  701.1 1.1 fusion.3
  702.1 0.8 copy.41
  703.0 1.3 fusion.4
  704.3 1.3 slice_bitcast_fusion.3
  705.6 0.8 copy.40
  706.4 0.0 copy-start
  706.4 1.0 slice_bitcast_fusion.2
  707.5 1.1 slice.36
  708.6 0.8 copy.43
  709.4 0.3 reshape.31
  709.7 0.1 slice_bitcast_fusion
  709.8 0.9 copy.42
  710.8 0.0 copy-done
  710.8 0.8 slice_bitcast_fusion.1
  711.5 0.1 slice.41
  711.6 1.5 broadcast_in_dim_reshape.11
  713.2 5.5 convert_bitcast_fusion
  718.6 16.4 %reshape.32 = f32[1,16,192,2,512]{4,3,2,1,0:T(2,128)} reshape(bf16[16,192,1024]{2,1,0:T(8,128)(2,1)} %get-tuple-element.64) | data formatting | bytes 18874368 | tf_op jit(solution)/shard_map/broadcast_in_dim;reshape | solution.py:2037
  (3 shorter events, 0.1 us)
Async XLA Ops:
  0.6 8.4 %copy-start.1 = (bf16[1,192,2,512]{3,2,1,0:T(2,128)(2,1)S(1)}, bf16[1,192,2,512]{3,2,1,0:T(2,128)(2,1)}, u32[]{:S(2)}) copy-start(bf16[1,192,2,512]{3,2,1,0:T(2,128)(2,1)} %param.24) | copy-start | bytes 1179652
  0.7 8.4 %copy-start.2 = (bf16[1,512,192]{1,2,0:T(8,128)(2,1)S(1)}, bf16[1,512,192]{1,2,0:T(8,128)(2,1)}, u32[]{:S(2)}) copy-start(bf16[1,512,192]{1,2,0:T(8,128)(2,1)} %param.25) | copy-start | bytes 589828
  706.4 4.3 copy-start

commit v7 on v6

--- a/solution.py
+++ b/solution.py
@@ -635,8 +635,11 @@
 
 
 class Share:
-    def __init__(self, pos, layer, block, full, sems):
-        self.pos, self.layer, self.block, self.full = pos, layer, block, full
+    def __init__(self, pos, layer, block, full, sems, cols=None):
+        if cols is None:
+            cols = pl.ds(0, block.shape[1])
+        self.pos, self.layer, self.cols = pos, layer, cols
+        self.block, self.full = block.at[:, cols], full.at[:, :, cols]
         self.sems = sems
         self.source = pos.s == layer
 
@@ -720,15 +723,67 @@
     return total
 
 
+def finish_kernel(cfg, win, wdt, both, att, sh, small, win_o, wdt_o, y_o, gx_o, ain_o, aout_o, sin_o, sdn_o, gain_o, fgain_o, rw_o):
+    width, pw, hd, experts = cfg
+    f = wdt.shape[-1]
+    value = win[0].astype(jnp.float32)
+    win_o[0, :, 0, :] = value[:, :f]
+    win_o[0, :, 1, :] = value[:, f:]
+    wdt_o[0] = wdt[0].astype(jnp.float32)
+
+    @pl.when(pl.program_id(0) == 0)
+    def _():
+        for kind, dst in enumerate((y_o, gx_o)):
+            for m in range(both.shape[1]):
+                dst[m] = both[kind, m].astype(jnp.float32).T[:width].astype(dst.dtype)
+        for c in range(3):
+            ain_o[c] = att[:, c * pw : c * pw + hd]
+        square = jnp.concatenate([att[:, 3 * pw :], jnp.zeros((pw - width, pw), jnp.float32)], 0)
+        aout_o[...] = square.T[:hd, :width]
+        value = sh[:, : 2 * f]
+        sin_o[:, 0, :] = value[:, :f]
+        sin_o[:, 1, :] = value[:, f:]
+        sdn_o[...] = sh[:, 2 * f :]
+        rw_o[...] = small[:experts, :width]
+        fgain_o[...] = small[experts : experts + 1, :width]
+        gain_o[...] = small[experts + 1 : experts + 2, :width]
+
+
+def finish_outputs(win, wdt, both, att, sh, small, pw, hd):
+    experts, width, f = wdt.shape
+    mbs, tokens = both.shape[1:3]
+    f32 = jnp.float32
+    each = lambda *shape: pl.BlockSpec((1,) + shape, lambda e: (e,) + (0,) * len(shape))
+    once = lambda *shape: pl.BlockSpec(shape, lambda e: (0,) * len(shape))
+    shapes = (
+        ((mbs, width, tokens), both.dtype), ((mbs, width, tokens), both.dtype),
+        ((3, width, hd), f32), ((hd, width), f32), ((width, 2, f), f32), ((width, f), f32),
+        ((1, width), f32), ((1, width), f32), ((experts, width), f32),
+    )
+    return pl.pallas_call(
+        functools.partial(finish_kernel, (width, pw, hd, experts)),
+        grid=(experts,),
+        out_shape=(
+            jax.ShapeDtypeStruct((experts, width, 2, f), f32),
+            jax.ShapeDtypeStruct((experts, width, f), f32),
+            *(jax.ShapeDtypeStruct(*v) for v in shapes),
+        ),
+        in_specs=[each(width, 2 * f), each(width, f)] + [once(*v.shape) for v in (both, att, sh, small)],
+        out_specs=(each(width, 2, f), each(width, f), *(once(*v[0]) for v in shapes)),
+        compiler_params=pltpu.CompilerParams(vmem_limit_bytes=VMEM_BYTES),
+        name="finish",
+    )(win, wdt, both, att, sh, small)
+
+
 def forward_kernel(cfg, *refs):
     nx, ny, mbs, sub, width, pw, heads, features, experts, cap, f, sk, ak = cfg
     (tin, small_b, att_b, sh_b, routes, cos, sin, rot, win_a, wdt_a,
-     win_b, wdt_b, tok_o, small_o, place_o, place_to, watt0_o, y_o, mid_o, n2_o, rows_o, q_o, k_o, v_o, att_o, slots_o, gu_o, hid_o, rows2_o, sgu_o, shid_o, shw_o, watt_o,
+     win_b, wdt_b, tok_o, small_o, place_o, place_to, watt0_o, y_o, mid_o, n2_o, rows_o, q_o, k_o, v_o, att_o, slots_o, gu_o, hid_o, rows2_o, sgu_o, shid_o, shw_o, watt_o, gslots_o,
      y, mid, n2, rx, nsend, nall, proj, q, k, v, att, osend, orecv, rwx,
      xsend, xline, xall, nrows, pm, pt, slots, acc, gu, hid, eo, sgu, shid, ssend, srecv, rsend, rpeer, rline, rrecv,
-     win, wdt, shw0, shw1, watt0, watt1, tbuf, tok, rts, place, place_t, sm0, sm1, small,
+     win, wdt, shw0, shw1, watt0, watt1, tbuf, tok, rts, place, place_t, sm0, sm1, small, gall, gslots,
      n_send, n_recv, o_send, o_recv, x_send, x_recv, u_send, u_recv, t_send, t_recv, s_send, s_recv, g_send, g_recv, r_send, r_recv,
-     rs_send, rs_recv, ag_send, ag_recv, wi_sem, wd_sem, g_sem, k_sem, i_send, i_recv, q_send, q_recv, v_send, v_recv, *w_sems) = refs
+     rs_send, rs_recv, ag_send, ag_recv, wi_sem, wd_sem, g_sem, k_sem, i_send, i_recv, q_send, q_recv, v_send, v_recv, gu_send, gu_recv, *w_sems) = refs
     pos = Position(nx, ny)
     s, a, b, me = pos.s, pos.a, pos.b, pos.me
     slots_n = experts * cap
@@ -745,7 +800,8 @@
     entry_shares = (
         Share(pos, 0, small_b, sm0, w_sems[12:16]),
         Share(pos, 1, small_b, sm1, w_sems[16:20]),
-        Share(pos, 0, att_b, watt0, w_sems[20:24]),
+        Share(pos, 0, att_b, watt0, w_sems[20:24], pl.ds(0, 2 * pw)),
+        Share(pos, 0, att_b, watt0, w_sems[24:28], pl.ds(2 * pw, 2 * pw)),
     )
     watts, shws = (watt0, watt1), (shw0, shw1)
     barrier = pltpu.get_barrier_semaphore()
@@ -934,6 +990,26 @@
         pos.peers(lambda ai: copy_w(l, m, ai, ai).wait())
         slots[l, m] = bf(mm(pm[...], xall[l, m].reshape(tokens, pw))).reshape(experts, cap, pw)
 
+    def grad_send(m):
+        for j in range(ny):
+            xsend[0, m, j] = tok[1, m, :, j * pw : (j + 1) * pw]
+        pos.line(lambda bi: copy_x(0, m, bi, b).start())
+        xline[0, m, b] = xsend[0, m, b]
+
+    def copy_gw(m, ai, slot):
+        return remote(xline.at[0, m], gall.at[m, :, slot], gu_send.at[m, ai], gu_recv.at[m, slot], (s, ai, b))
+
+    def grad_spread(m):
+        pos.line(lambda bi: copy_x(0, m, bi, bi).wait())
+        pos.peers(lambda ai: copy_gw(m, ai, a).start())
+        gall[m, :, a] = xline[0, m]
+
+    def grad_dispatch(m):
+        i0 = lax.broadcasted_iota(jnp.int32, (slots_n, tokens), 0)
+        pm[...] = bf(((place[1, m, 0:1] == i0) | (place[1, m, 1:2] == i0)).astype(jnp.float32))
+        pos.peers(lambda ai: copy_gw(m, ai, ai).wait())
+        gslots[m] = bf(mm(pm[...], gall[m].reshape(tokens, pw))).reshape(experts, cap, pw)
+
     def shared_in_part(l, m):
         pos.peers(lambda ai: copy_t(l, m, ai, ai).wait())
         shw = shws[l]
@@ -1088,10 +1164,18 @@
                 def _():
                     start_weight(1, e, 1)
 
-    kept = [
-        (mid, mid_o), (n2, n2_o), (nall, rows_o), (q, q_o), (k, k_o), (v, v_o), (att, att_o), (slots, slots_o),
-        (hid, hid_o), (nrows, rows2_o), (sgu, sgu_o), (shid, shid_o), (y, y_o),
-    ]
+    kept = (
+        (slots, slots_o), (nall, rows_o), (q, q_o), (k, k_o), (v, v_o), (att, att_o), (mid, mid_o), (n2, n2_o),
+        (nrows, rows2_o), (sgu, sgu_o), (shid, shid_o), (shw0, shw_o.at[0]), (shw1, shw_o.at[1]), (watt1, watt_o),
+        (watt0, watt0_o), (tok, tok_o), (small, small_o), (place, place_o), (place_t, place_to),
+        (gslots, gslots_o), (hid, hid_o), (y, y_o),
+    )
+    saves = [pltpu.make_async_copy(src, dst, k_sem.at[c]) for c, (src, dst) in enumerate(kept)]
+
+    def save(copies):
+        for copy in copies:
+            copy.start()
+
     stages = {}
 
     def at(step, do):
@@ -1108,6 +1192,7 @@
             share.hop(h)
         if h == 2:
             entry_shares[2].hop(1)
+            entry_shares[3].hop(1)
     for share in entry_shares[:2]:
         share.finish()
     tokens_ready()
@@ -1120,9 +1205,12 @@
     norm_first(0, 0)
     norm_first(0, 1)
     entry_shares[2].hop(2)
+    entry_shares[3].hop(2)
     places()
     entry_shares[2].hop(3)
+    entry_shares[3].hop(3)
     entry_shares[2].finish()
+    entry_shares[3].finish()
     shares[0].start()
     shares[1].start()
     attention(0, 0)
@@ -1155,6 +1243,12 @@
         done = starts[2 + m] + units - 1 + lag
         for c, do in enumerate((combine, combine_line, layer_out)):
             at(done + c * apart, stage(do, 1, m))
+    at(starts[3] + 9, lambda: save(saves[:-2]))
+    at(starts[3] + units - 1 + lag, lambda: save(saves[-2:-1]))
+    for m in range(2):
+        at(units + 4 + m, lambda m=m: grad_send(m))
+        at(units + 6 + m, lambda m=m: grad_spread(m))
+        at(units + 8 + m, lambda m=m: grad_dispatch(m))
     at(units + lag - 1, shares[2].start)
     for h in range(1, ny):
         at(units + lag - 1 + 2 * h, lambda h=h: shares[2].hop(h))
@@ -1176,11 +1270,7 @@
         if when >= steps:
             for do in stages[when]:
                 do()
-    kept += [(shw0, shw_o.at[0]), (shw1, shw_o.at[1]), (watt1, watt_o), (watt0, watt0_o), (tok, tok_o), (small, small_o)]
-    kept += [(place, place_o), (place_t, place_to)]
-    saves = [pltpu.make_async_copy(src, dst, k_sem.at[i]) for i, (src, dst) in enumerate(kept)]
-    for copy in saves:
-        copy.start()
+    saves[-1].start()
 
     def finish(index, carry):
         l = index // (mbs * units)
@@ -1221,7 +1311,7 @@
         (lm + (length, pw), b16), (lm + (length, pw), b16), (lm + (length, pw), b16), (lm + (length, pw), b16),
         (lm + (experts, cap, pw), b16), (lm + (experts, 2, cap, f), b16), (lm + (experts, 2, cap, f // 2), b16),
         (rows_shape, b16), (lm + (length, 2 * f), b16), (lm + (length, f), b16),
-        ((2, ny) + sh_block.shape, b16), ((ny,) + att_block.shape, b16),
+        ((2, ny) + sh_block.shape, b16), ((ny,) + att_block.shape, b16), ((mbs, experts, cap, pw), b16),
     )
     scratch = (
         (lm + (sub, d), b16), (lm + (sub, d), f32), (lm + (sub, d), b16), None,
@@ -1238,6 +1328,7 @@
         ((ny, 2, mbs, sub, pw), b16), ((2, mbs, sub, d), b16), (lm + (2, tokens), jnp.int32),
         (lm + (2, tokens), jnp.int32), (lm + (tokens, 2), jnp.int32),
         ((ny,) + small_b.shape, f32), ((ny,) + small_b.shape, f32), ((2, small_b.shape[0], d), f32),
+        ((mbs, ny, nx, sub, pw), b16), ((mbs, experts, cap, pw), b16),
     )
     outs = pl.pallas_call(
         functools.partial(forward_kernel, (nx, ny, mbs, sub, width, pw, heads, features, experts, cap, f, *FWD_SKEW)),
@@ -1250,13 +1341,13 @@
             flags(lm + (nx,)), flags(lm + (nx,)), flags(lm + (nx,)), flags(lm + (nx,)), flags(lm + (ny,)), flags(lm + (ny,)),
             flags(lm + (experts, 2)), flags(lm + (experts, 2)), flags(lm + (experts, 2)), flags(lm + (experts, 2)),
             flags((experts,)), flags((experts,)), flags(lm + (experts, 2)), flags((24,)),
-            flags((nx,)), flags((ny,)), pltpu.SemaphoreType.DMA, pltpu.SemaphoreType.DMA, flags((2,)), flags((2,)),
-        ] + share_sems(ny) * 6,
+            flags((nx,)), flags((ny,)), pltpu.SemaphoreType.DMA, pltpu.SemaphoreType.DMA, flags((2,)), flags((2,)), flags((mbs, nx)), flags((mbs, nx)),
+        ] + share_sems(ny) * 7,
         compiler_params=params(ids),
         cost_estimate=pl.CostEstimate(flops=10**10, bytes_accessed=8 * 10**7, transcendentals=10**6),
         name="forward",
     )(tin, small_b, att_block, sh_block, routes, cos, sin, rot, win, wdt)
-    names = ("win", "wdt", "tok", "small", "place", "place_t", "watt0", "y", "mid", "n2", "rows", "q", "k", "v", "att", "slots", "gu", "hid", "rows2", "sgu", "shid", "shw", "watt1")
+    names = ("win", "wdt", "tok", "small", "place", "place_t", "watt0", "y", "mid", "n2", "rows", "q", "k", "v", "att", "slots", "gu", "hid", "rows2", "sgu", "shid", "shw", "watt1", "gslots")
     return dict(zip(names, outs))
 
 
@@ -1267,7 +1358,7 @@
 def backward_kernel(cfg, *refs):
     nx, ny, mbs, sub, width, pw, heads, features, experts, cap, f, sk, ak = cfg
     (tok_i, small_i, place_i, y_i, mid_i, n2_i, rows_i, q_i, k_i, v_i, att_i, rows2_i, sgu_i, shid_i, shw_i,
-     watt0_i, watt1_i, cos, sin, rot, slots_i, gu_i, hid_i, win_a, win_b, wdt_a, wdt_b) = refs[:27]
+     watt0_i, watt1_i, cos, sin, rot, slots_i, gu_i, hid_i, gslots_i, win_a, win_b, wdt_a, wdt_b) = refs[:28]
     (out_o, win_g, wdt_g, att_g, sh_g, small_g,
      win, wdt, xsend, xline, xall, grows, pm, pt, slots, gslots, gown, hid, acc, dh, dgu, deo, sti, std,
      dsgu, ssend, srecv, rsend, rpeer, rline, rrecv, rwx, dm, msend, mall, datt, dqkv, dsend, drecv,
@@ -1275,7 +1366,7 @@
      yv, obuf, g, gx, small, place, x, mid, n2, rows, q, k, v, att, rows2, sgu, shid, shw, watt,
      w_sem, x_send, x_recv, u_send, u_recv, t_send, t_recv, s_send, s_recv, g_send, g_recv, r_send, r_recv,
      m_send, m_recv, d_send, d_recv, rs_send, rs_recv, ag_send, ag_recv, wi_send, wi_recv, wd_send, wd_recv,
-     c_send, c_recv, e_send, e_recv, a_send, a_recv, l_sem, st_sem, f_sem, y_sem, o_send, o_recv, free) = refs[27:]
+     c_send, c_recv, e_send, e_recv, a_send, a_recv, l_sem, st_sem, f_sem, y_sem, o_send, o_recv, free) = refs[28:]
     pos = Position(nx, ny)
     s, a, b = pos.s, pos.a, pos.b
     slots_n = experts * cap
@@ -1346,7 +1437,8 @@
         for c, (src, dst) in enumerate(((tok_i.at[1], g), (small_i, small), (place_i, place), (y_i, yv)))
     ]
     slots_load = pltpu.make_async_copy(slots_i, slots, l_sem.at[0])
-    for copy in first_loads + [slots_load, hid_load(1)] + early_loads(1) + later_loads(1):
+    gslots_load = pltpu.make_async_copy(gslots_i, gslots.at[1], l_sem.at[4])
+    for copy in first_loads + [slots_load, gslots_load, hid_load(1)] + early_loads(1) + later_loads(1):
         copy.start()
     for m in range(mbs):
         start_gates(1, m)
@@ -1400,16 +1492,17 @@
 
                 out_o[kind, so * mbs : (so + 1) * mbs, i * sub : (i + 1) * sub, :] = obuf[kind, so, i]
 
-    def send_g(m):
-        for j in range(ny):
-            xsend[m, j] = g[m, :, j * pw : (j + 1) * pw]
-        pos.line(lambda bi: copy_x(m, bi, b).start())
-        xline[m, b] = xsend[m, b]
+    def send_g(m, slots_too=True):
+        if slots_too:
+            for j in range(ny):
+                xsend[m, j] = g[m, :, j * pw : (j + 1) * pw]
+            pos.line(lambda bi: copy_x(m, bi, b).start())
+            xline[m, b] = xsend[m, b]
         pos.peers(lambda ai: copy_t(m, ai, a).start())
         grows[m, a] = g[m]
 
-    send_g(0)
-    send_g(1)
+    send_g(0, False)
+    send_g(1, False)
     deo[...] = jnp.zeros_like(deo)
     ssend[...] = jnp.zeros_like(ssend)
     dsend[...] = jnp.zeros_like(dsend)
@@ -1818,13 +1911,9 @@
         for copy in copies:
             copy.wait()
 
-    spread(0)
-    spread(1)
-    dispatch(1, 0)
-    ready([slots_load, hid_load(1)] + later_loads(1))
+    ready([slots_load, gslots_load, hid_load(1)] + later_loads(1))
     for m in range(mbs):
         wait_gates(1, m)
-    at(1, dispatch, 1, 1)
     for l in (1, 0):
         begin = starts[2 - 2 * l]
         second = starts[3 - 2 * l]
@@ -1959,7 +2048,7 @@
             jax.ShapeDtypeStruct((width, sc), f32),
             jax.ShapeDtypeStruct((n, pw), f32),
         ),
-        in_specs=[hbm] * 17 + [vm] * 3 + [hbm] * 7,
+        in_specs=[hbm] * 17 + [vm] * 3 + [hbm] * 8,
         out_specs=(vm,) + (hbm,) * 5,
         scratch_shapes=[pltpu.VMEM(*v) for v in scratch] + [
             flags((2, experts)), by_m(ny), by_m(ny), by_m(nx), by_m(nx), by_m(nx), by_m(nx), by_m(nx), by_m(nx),
@@ -1967,12 +2056,12 @@
             by_half, by_half, by_half, by_half,
             flags((2, experts)), flags((2, experts)), flags((2, experts)), flags((2, experts)),
             flags((3,)), flags((3,)), flags((3, ny)), flags((3, ny)), flags((nx,)), flags((nx,)),
-            flags((4,)), flags((2,)), flags((3,)), flags((20,)), flags((2, 2, ny)), flags((2, 2, nx)), pltpu.SemaphoreType.REGULAR((2,)),
+            flags((5,)), flags((2,)), flags((3,)), flags((20,)), flags((2, 2, ny)), flags((2, 2, nx)), pltpu.SemaphoreType.REGULAR((2,)),
         ],
         compiler_params=params(ids),
         cost_estimate=pl.CostEstimate(flops=2 * 10**10, bytes_accessed=10**8, transcendentals=10**6),
         name="backward",
-    )(*(fwd[name] for name in names), cos, sin, rot, *(fwd[name] for name in ("slots", "gu", "hid")), win, fwd["win"], wdt, fwd["wdt"])
+    )(*(fwd[name] for name in names), cos, sin, rot, *(fwd[name] for name in ("slots", "gu", "hid", "gslots")), win, fwd["win"], wdt, fwd["wdt"])
     return outs[0], outs[1:]
 
 
@@ -2023,21 +2112,21 @@
 
     fwd = forward(tin, small, att_block, sh_block, pairs, cos, sin, rot, win, wdt, dims, heads, features, 0)
     both, grads = backward(fwd, cos, sin, rot, win, wdt, dims, heads, features, 1)
-    both = both[..., :width]
     win_g, wdt_g, att_g, sh_g, small_g = grads
-    hd = heads * DH
+    win_g, wdt_g, y, gx, ain, aout, sin_g, sdn, gain_g, fgain_g, rw = finish_outputs(
+        win_g, wdt_g, both, att_g, sh_g, small_g, pw, heads * DH)
     return (
-        both[0][None],
-        both[1][None],
-        small_g[experts + 1 : experts + 2, :width],
-        att_g[:, : 3 * pw].reshape(width, 3, pw)[..., :hd][None],
-        att_g[:, 3 * pw : 3 * pw + hd].T[None],
-        small_g[experts : experts + 1, :width],
-        small_g[:experts, :width].T[None],
-        win_g.astype(jnp.float32).reshape(experts, width, 2, f)[None],
-        wdt_g.astype(jnp.float32).transpose(0, 2, 1)[None],
-        sh_g[:, : 2 * f].reshape(width, 2, f)[None],
-        sh_g[:, 2 * f :].T[None],
+        jnp.swapaxes(y, 1, 2)[None],
+        jnp.swapaxes(gx, 1, 2)[None],
+        gain_g,
+        jnp.swapaxes(ain, 0, 1)[None],
+        aout[None],
+        fgain_g,
+        rw.T[None],
+        win_g[None],
+        jnp.swapaxes(wdt_g, 1, 2)[None],
+        sin_g[None],
+        sdn.T[None],
     )
 
 

time: 743 us -> 716 us (0.964)
  local copies, waits for them, and re-layouts: 41.4 us -> 12.9 us
    another operation x2 -> x0, local copies, waits for them, and re-layouts: 18 us -> none  [the longest x1 16.4 us: fast_device(): win_g.astype(jnp.float32).reshape(experts, width, 2, f)[None]]
    pallas_call x0 -> x1, Pallas kernels: none -> 17.3 us  [finish_outputs(): pl.pallas_call(functools.partial(finish_kernel, (width, pw, hd, experts))...]
where the time goes in v7:
time: 716 us; the launch traced here: 709 us
  Pallas kernels  691 us (97%)
  local copies, waits for them, and re-layouts  12.9 us (2%)
    pallas_call x1, Pallas kernels, backward(): pl.pallas_call(functools.partial(backward_kernel, (nx, ny, mbs, sub, widt...  356 us
    pallas_call x1, Pallas kernels, forward(): pl.pallas_call(functools.partial(forward_kernel, (nx, ny, mbs, sub, width...  318 us
    pallas_call x1, Pallas kernels, finish_outputs(): pl.pallas_call(functools.partial(finish_kernel, (width, pw, hd, experts))...  17.3 us

profile of v7, /device:TPU:0, one launch (start us, length us, event | category | flops | bytes accessed | tf_op | source)
XLA Modules:
  0.0 708.6 jit_solution(10674498989931888000)
XLA Ops:
  0.6 0.0 copy-start
  0.7 0.1 pad.27.clone
  0.7 0.0 copy-start.1
  0.7 0.7 convert_bitcast_fusion
  1.5 0.8 maximum_maximum_fusion
  2.3 0.6 pad.17.refs_1_
  2.9 1.0 copy.34
  3.9 1.1 copy.31
  4.9 1.1 copy.32
  6.0 0.1 fusion.2
  6.1 0.7 pad.16.refs_0_
  6.8 1.2 copy.36
  8.0 0.2 pad.18.clone
  8.3 0.8 fusion.1.refs_2_
  9.1 0.0 copy-done
  9.1 0.0 copy-done.1
  9.1 0.9 pad_maximum_fusion.refs_3_
  10.0 6.9 copy.40
  16.9 317.8 %forward.1 = (bf16[16,2,192,512]{3,2,1,0:T(8,128)(2,1)}, bf16[16,192,512]{2,1,0:T(8,128)(2,1)}, bf16[2,2,32,1024]{3,2,1,0:T(8,128)(2,1)}, f32[2,24,1024]{2,1,0:T...) custom-call(bf16[2,2,128,256]{3,2,1,0:T(8,128)(2,1)} %pad.16.refs_0_, ...), custom_call_target="tpu_custom_call" | custom-call | flops 10000000000 | bytes 80000000 | tf_op jit(solution)/shard_map/forward/pallas_call | solution.py:1333
  334.7 356.2 %backward.1 = (bf16[2,4,128,256]{3,2,1,0:T(8,128)(2,1)}, bf16[16,192,1024]{2,1,0:T(8,128)(2,1)}, bf16[16,192,512]{2,1,0:T(8,128)(2,1)}, f32[192,1024]{1,0:T(8,12...) custom-call(bf16[2,2,32,1024]{3,2,1,0:T(8,128)(2,1)} %get-tuple-element.51.refs_0_, ...), custom_call_target="tpu_custom_call" | custom-call | flops 20000000000 | bytes 100000000 | tf_op jit(solution)/shard_map/backward/pallas_call | solution.py:2040
  690.9 17.3 %finish.1 = (f32[16,192,2,512]{3,2,1,0:T(2,128)}, f32[16,192,512]{2,1,0:T(8,128)}, bf16[4,192,128]{2,1,0:T(8,128)(2,1)}, bf16[4,192,128]{2,1,0:T(8,128)(2,1)}, f...) custom-call(bf16[16,192,1024]{2,1,0:T(8,128)(2,1)} %get-tuple-elemen, ...), custom_call_target="tpu_custom_call" | custom-call | tf_op jit(solution)/shard_map/finish/pallas_call | solution.py:763
  (3 shorter events, 0.1 us)
Async XLA Ops:
  0.6 8.4 %copy-start = (bf16[1,192,2,512]{3,2,1,0:T(2,128)(2,1)S(1)}, bf16[1,192,2,512]{3,2,1,0:T(2,128)(2,1)}, u32[]{:S(2)}) copy-start(bf16[1,192,2,512]{3,2,1,0:T(2,128)(2,1)} %param.24) | copy-start | bytes 1179652
  0.7 8.4 %copy-start.1 = (bf16[1,512,192]{1,2,0:T(8,128)(2,1)S(1)}, bf16[1,512,192]{1,2,0:T(8,128)(2,1)}, u32[]{:S(2)}) copy-start(bf16[1,512,192]{1,2,0:T(8,128)(2,1)} %param.25) | copy-start | bytes 589828

commit v8 on v7

--- a/solution.py
+++ b/solution.py
@@ -736,9 +736,16 @@
         for kind, dst in enumerate((y_o, gx_o)):
             for m in range(both.shape[1]):
                 dst[m] = both[kind, m].astype(jnp.float32).T[:width].astype(dst.dtype)
+        lane = lax.broadcasted_iota(jnp.int32, (width, 128), 1)
+        parts = []
+        for c in range(4):
+            pair = att[:, (4 + c // 2) * 128 : (5 + c // 2) * 128]
+            pair = pltpu.roll(pair, 64, 1) if c % 2 else pair
+            parts.append((att[:, c * 128 : (c + 1) * 128], jnp.where(lane < 64, pair, 0.0)))
         for c in range(3):
-            ain_o[c] = att[:, c * pw : c * pw + hd]
-        square = jnp.concatenate([att[:, 3 * pw :], jnp.zeros((pw - width, pw), jnp.float32)], 0)
+            ain_o[c, :, :128] = parts[c][0]
+            ain_o[c, :, 128:] = parts[c][1][:, : hd - 128]
+        square = jnp.concatenate([jnp.concatenate(parts[3], 1), jnp.zeros((pw - width, pw), jnp.float32)], 0)
         aout_o[...] = square.T[:hd, :width]
         value = sh[:, : 2 * f]
         sin_o[:, 0, :] = value[:, :f]
@@ -1701,8 +1708,14 @@
             cols = slice(j * pw, j * pw + width)
             rj = rows[:, :, :, cols].reshape(mbs * length, width)
             mj = mall[:, :, :, cols].reshape(mbs * length, width)
-            att_p[j, :, : 3 * pw] = bf(mm(rj, dqkv[...].reshape(mbs * length, 3 * pw), ((0,), (0,))))
-            att_p[j, :, 3 * pw :] = bf(mm(mj, att[...].reshape(mbs * length, pw), ((0,), (0,))))
+            qkv = mm(rj, dqkv[...].reshape(mbs * length, 3 * pw), ((0,), (0,)))
+            rest = mm(mj, att[...].reshape(mbs * length, pw), ((0,), (0,)))
+            parts = [qkv[:, c * pw : (c + 1) * pw] for c in range(3)] + [rest]
+            for c in range(4):
+                att_p[j, :, c * 128 : (c + 1) * 128] = bf(parts[c][:, :128])
+            for c in range(2):
+                joined = parts[2 * c][:, 128:] + pltpu.roll(parts[2 * c + 1][:, 128:], 64, 1)
+                att_p[j, :, (4 + c) * 128 : (5 + c) * 128] = bf(joined)
         give(l, 1)
 
     def small_grads(l):
@@ -1936,13 +1949,14 @@
                 at(starts[2 + m] - 1, wait_gates, 0, m)
         end = second + units - 1 + lag
         at(end + 3 * apart, attention_grads, l)
-        at(end + 4 * apart, join, l, 1)
+        at(end + 4 * apart - (0 if l else 1), join, l, 1)
         at(end + 4 * apart, small_grads, l)
         at(end + 5 * apart, join, l, 2)
         at(end + (2 if l else 4) * apart, settle, l, 0)
-        at(end + (10 if l else 5) * apart, settle, l, 1)
         at(end + (10 if l else 5) * apart, settle, l, 2)
-        at(end + (6 if l else 5) * apart, given, l)
+        if l:
+            at(end + 10 * apart, settle, l, 1)
+            at(end + 6 * apart, given, l)
     at(units // 2 - 1, send_out, 0, 0)
     at(units // 2 + 1, send_out, 0, 1)
     at(2 * units, take_out, 0)
@@ -1991,6 +2005,8 @@
     for l in range(2):
         for kind in range(2):
             sent_out(kind, l)
+    settle(0, 1)
+    given(0)
     for i in range(3):
         pltpu.make_async_copy(finals[i], results[i], f_sem.at[i]).wait()
     for copy in st_copies(experts - 1):
@@ -2006,7 +2022,7 @@
     b16, f32 = jnp.bfloat16, jnp.float32
     vm = pl.BlockSpec(memory_space=pltpu.VMEM)
     hbm = pl.BlockSpec(memory_space=pl.ANY)
-    ac, sc, n, half = fwd["watt0"].shape[2], fwd["shw"].shape[3], fwd["small"].shape[1], experts // 2
+    ac, sc, n, half = 6 * 128, fwd["shw"].shape[3], fwd["small"].shape[1], experts // 2
     rows_shape = (mbs, nx, sub, d)
     dense = lambda c: ((ny, width, c), b16)
     scratch = (
@@ -2130,6 +2146,22 @@
     )
 
 
+def any_device(*arrays):
+    block_input, attention_in, routes = arrays[0], arrays[3], arrays[-1]
+    batches, rows, width = block_input.shape
+    fits = (
+        lax.axis_size("gx") == lax.axis_size("gy")
+        and lax.axis_size("section") == 2
+        and batches == 4
+        and rows == 128
+        and routes.shape[2] == rows * lax.axis_size("gy")
+        and 128 < width <= 192
+        and attention_in.shape[-1] == width
+        and lanes_up(width + 2 * arrays[7].shape[1]) == 256
+    )
+    return fast_device(*arrays) if fits else on_device(*arrays)
+
+
 def solution(mesh):
     in_specs = (
         P(None, "gx", "gy"),
@@ -2158,7 +2190,6 @@
         P("section", "gy", None, "gx"),
         P("section", "gx", "gy"),
     )
-    fast = mesh.shape["gx"] == mesh.shape["gy"]
     return jax.shard_map(
-        fast_device if fast else on_device, mesh=mesh, in_specs=in_specs, out_specs=out_specs, check_vma=False
-    )
+        any_device, mesh=mesh, in_specs=in_specs, out_specs=out_specs, check_vma=False
+    )

time: 716 us -> 702 us (0.980)
  Pallas kernels: 691 us -> 678 us
    pallas_call x1, Pallas kernels: 356 us -> 343 us  [backward(): pl.pallas_call(functools.partial(backward_kernel, (nx, ny, mbs, sub, widt...]
where the time goes in v8:
time: 702 us; the launch traced here: 695 us
  Pallas kernels  678 us (97%)
  local copies, waits for them, and re-layouts  12.9 us (2%)
    pallas_call x1, Pallas kernels, backward(): pl.pallas_call(functools.partial(backward_kernel, (nx, ny, mbs, sub, widt...  343 us
    pallas_call x1, Pallas kernels, forward(): pl.pallas_call(functools.partial(forward_kernel, (nx, ny, mbs, sub, width...  318 us
    pallas_call x1, Pallas kernels, finish_outputs(): pl.pallas_call(functools.partial(finish_kernel, (width, pw, hd, experts))...  17.3 us

profile of v8, /device:TPU:0, one launch (start us, length us, event | category | flops | bytes accessed | tf_op | source)
XLA Modules:
  0.0 695.0 jit_solution(11390827732069066154)
XLA Ops:
  0.6 0.0 copy-start
  0.7 0.1 pad.27.clone
  0.7 0.0 copy-start.1
  0.7 0.7 convert_bitcast_fusion
  1.5 0.8 maximum_maximum_fusion
  2.3 0.6 pad.17.refs_1_
  2.9 1.0 copy.34
  3.9 1.1 copy.31
  4.9 1.1 copy.32
  6.0 0.1 fusion.2
  6.1 0.7 pad.16.refs_0_
  6.8 1.2 copy.36
  8.0 0.2 pad.18.clone
  8.3 0.8 fusion.1.refs_2_
  9.1 0.0 copy-done
  9.1 0.0 copy-done.1
  9.1 0.9 pad_maximum_fusion.refs_3_
  10.0 6.9 copy.40
  16.9 317.8 %forward.1 = (bf16[16,2,192,512]{3,2,1,0:T(8,128)(2,1)}, bf16[16,192,512]{2,1,0:T(8,128)(2,1)}, bf16[2,2,32,1024]{3,2,1,0:T(8,128)(2,1)}, f32[2,24,1024]{2,1,0:T...) custom-call(bf16[2,2,128,256]{3,2,1,0:T(8,128)(2,1)} %pad.16.refs_0_, ...), custom_call_target="tpu_custom_call" | custom-call | flops 10000000000 | bytes 80000000 | tf_op jit(solution)/shard_map/forward/pallas_call | solution.py:1340
  334.7 342.6 %backward.1 = (bf16[2,4,128,256]{3,2,1,0:T(8,128)(2,1)}, bf16[16,192,1024]{2,1,0:T(8,128)(2,1)}, bf16[16,192,512]{2,1,0:T(8,128)(2,1)}, f32[192,768]{1,0:T(8,128...) custom-call(bf16[2,2,32,1024]{3,2,1,0:T(8,128)(2,1)} %get-tuple-element.51.refs_0_, f32[2,24,1024]{2,1,0:T(8,128)} %get-tuple-element.52.refs_1_, ...), custom_call_target="tpu_custom_call" | custom-call | flops 20000000000 | bytes 100000000 | tf_op jit(solution)/shard_map/backward/pallas_call | solution.py:2056
  677.3 17.3 %finish.1 = (f32[16,192,2,512]{3,2,1,0:T(2,128)}, f32[16,192,512]{2,1,0:T(8,128)}, bf16[4,192,128]{2,1,0:T(8,128)(2,1)}, bf16[4,192,128]{2,1,0:T(8,128)(2,1)}, f...) custom-call(bf16[16,192,1024]{2,1,0:T(8,128)(2,1)} %get-tuple-elemen, ...), custom_call_target="tpu_custom_call" | custom-call | tf_op jit(solution)/shard_map/finish/pallas_call | solution.py:770
  (3 shorter events, 0.1 us)
Async XLA Ops:
  0.6 8.4 %copy-start = (bf16[1,192,2,512]{3,2,1,0:T(2,128)(2,1)S(1)}, bf16[1,192,2,512]{3,2,1,0:T(2,128)(2,1)}, u32[]{:S(2)}) copy-start(bf16[1,192,2,512]{3,2,1,0:T(2,128)(2,1)} %param.24) | copy-start | bytes 1179652
  0.7 8.4 %copy-start.1 = (bf16[1,512,192]{1,2,0:T(8,128)(2,1)S(1)}, bf16[1,512,192]{1,2,0:T(8,128)(2,1)}, u32[]{:S(2)}) copy-start(bf16[1,512,192]{1,2,0:T(8,128)(2,1)} %param.25) | copy-start | bytes 589828

commit v9 on v8

--- a/solution.py
+++ b/solution.py
@@ -1760,7 +1760,7 @@
         gd = [mm(gs, hid[:, e, c].reshape(mbs * cap, hw), ((0,), (0,))) for c in range(2)]
         return gi, gd
 
-    late = 2
+    late = 1
     steps = starts[3] + units + lag + 2 * late
 
     def chain(i):

time: 702 us -> 702 us (level)
  no operation moved by 1% of the time
where the time goes in v9:
time: 702 us; the launch traced here: 695 us
  Pallas kernels  678 us (97%)
  local copies, waits for them, and re-layouts  12.9 us (2%)
    pallas_call x1, Pallas kernels, backward(): pl.pallas_call(functools.partial(backward_kernel, (nx, ny, mbs, sub, widt...  343 us
    pallas_call x1, Pallas kernels, forward(): pl.pallas_call(functools.partial(forward_kernel, (nx, ny, mbs, sub, width...  318 us
    pallas_call x1, Pallas kernels, finish_outputs(): pl.pallas_call(functools.partial(finish_kernel, (width, pw, hd, experts))...  17.3 us

profile of v9, /device:TPU:0, one launch (start us, length us, event | category | flops | bytes accessed | tf_op | source)
XLA Modules:
  0.0 695.0 jit_solution(17661481244738176033)
XLA Ops:
  0.6 0.0 copy-start
  0.7 0.1 pad.27.clone
  0.7 0.0 copy-start.1
  0.7 0.7 convert_bitcast_fusion
  1.5 0.8 maximum_maximum_fusion
  2.3 0.6 pad.17.refs_1_
  2.9 1.0 copy.34
  3.9 1.1 copy.31
  4.9 1.1 copy.32
  6.0 0.1 fusion.2
  6.1 0.7 pad.16.refs_0_
  6.8 1.2 copy.36
  8.0 0.2 pad.18.clone
  8.3 0.8 fusion.1.refs_2_
  9.1 0.0 copy-done
  9.1 0.0 copy-done.1
  9.1 0.9 pad_maximum_fusion.refs_3_
  10.0 6.9 copy.40
  16.9 317.8 %forward.1 = (bf16[16,2,192,512]{3,2,1,0:T(8,128)(2,1)}, bf16[16,192,512]{2,1,0:T(8,128)(2,1)}, bf16[2,2,32,1024]{3,2,1,0:T(8,128)(2,1)}, f32[2,24,1024]{2,1,0:T...) custom-call(bf16[2,2,128,256]{3,2,1,0:T(8,128)(2,1)} %pad.16.refs_0_, ...), custom_call_target="tpu_custom_call" | custom-call | flops 10000000000 | bytes 80000000 | tf_op jit(solution)/shard_map/forward/pallas_call | solution.py:1340
  334.7 342.7 %backward.1 = (bf16[2,4,128,256]{3,2,1,0:T(8,128)(2,1)}, bf16[16,192,1024]{2,1,0:T(8,128)(2,1)}, bf16[16,192,512]{2,1,0:T(8,128)(2,1)}, f32[192,768]{1,0:T(8,128...) custom-call(bf16[2,2,32,1024]{3,2,1,0:T(8,128)(2,1)} %get-tuple-element.51.refs_0_, f32[2,24,1024]{2,1,0:T(8,128)} %get-tuple-element.52.refs_1_, ...), custom_call_target="tpu_custom_call" | custom-call | flops 20000000000 | bytes 100000000 | tf_op jit(solution)/shard_map/backward/pallas_call | solution.py:2056
  677.3 17.3 %finish.1 = (f32[16,192,2,512]{3,2,1,0:T(2,128)}, f32[16,192,512]{2,1,0:T(8,128)}, bf16[4,192,128]{2,1,0:T(8,128)(2,1)}, bf16[4,192,128]{2,1,0:T(8,128)(2,1)}, f...) custom-call(bf16[16,192,1024]{2,1,0:T(8,128)(2,1)} %get-tuple-elemen, ...), custom_call_target="tpu_custom_call" | custom-call | tf_op jit(solution)/shard_map/finish/pallas_call | solution.py:770
  (3 shorter events, 0.1 us)
Async XLA Ops:
  0.6 8.4 %copy-start = (bf16[1,192,2,512]{3,2,1,0:T(2,128)(2,1)S(1)}, bf16[1,192,2,512]{3,2,1,0:T(2,128)(2,1)}, u32[]{:S(2)}) copy-start(bf16[1,192,2,512]{3,2,1,0:T(2,128)(2,1)} %param.24) | copy-start | bytes 1179652
  0.7 8.4 %copy-start.1 = (bf16[1,512,192]{1,2,0:T(8,128)(2,1)S(1)}, bf16[1,512,192]{1,2,0:T(8,128)(2,1)}, u32[]{:S(2)}) copy-start(bf16[1,512,192]{1,2,0:T(8,128)(2,1)} %param.25) | copy-start | bytes 589828
